TPU v7x, 32 devices: a whole 2x2x4 slice. The times are simulated.
32 devices in a mesh: dp: 4 (over y, x), ctx: 2 (over core), expert: 4 (over z).
Axes of the slice: x: 2, y: 2, z: 4, core: 2. Of those that a mesh axis runs over, the one named last changes fastest.
Arguments:
- tokens: bfloat16 [32, 1024, 768], P(('dp', 'expert'), 'ctx'), may hold values from -6 to 6
- cotangent: bfloat16 [32, 1024, 768], P(('dp', 'expert'), 'ctx'), may hold values from -6 to 6
- routes: int32 [32, 1024], P(('dp', 'expert'), 'ctx'), may hold values from 0 to 3, as said below
- norm1_gain: float32 [768], replicated, may hold values from 0.1 to 1.9
- query_weight: bfloat16 [768, 768], replicated, may hold values from -0.109375 to 0.109375
- key_weight: bfloat16 [768, 768], replicated, may hold values from -0.109375 to 0.109375
- value_weight: bfloat16 [768, 768], replicated, may hold values from -0.21875 to 0.21875
- output_weight: bfloat16 [768, 768], replicated, may hold values from -0.875 to 0.875
- bias_table: float32 [32, 12], replicated, may hold values from -4 to 4
- norm2_gain: float32 [768], replicated, may hold values from 0.1 to 1.9
- router_weight: bfloat16 [768, 4], replicated, may hold values from -0.15625 to 0.15625
- w_in: bfloat16 [4, 768, 3072], P('expert'), may hold values from -0.21875 to 0.21875
- w_out: bfloat16 [4, 3072, 768], P('expert'), may hold values from -0.4375 to 0.4375
Outputs:
- block_out: bfloat16 [32, 1024, 768], P(('dp', 'expert'), 'ctx')
- d_tokens: float32 [32, 1024, 768], P(('dp', 'expert'), 'ctx')
- d_norm1_gain: float32 [768], replicated
- d_w_query: float32 [768, 768], replicated
- d_w_key: float32 [768, 768], replicated
- d_w_value: float32 [768, 768], replicated
- d_w_output: float32 [768, 768], replicated
- d_bias_table: float32 [32, 12], replicated
- d_norm2_gain: float32 [768], replicated
- d_w_router: float32 [768, 4], replicated
- d_w_in: float32 [4, 768, 3072], P('expert', None, ('dp', 'ctx'))
- d_w_out: float32 [4, 3072, 768], P('expert', ('dp', 'ctx'))
Inputs may be any that keep to these rules, and one draw needn't show every extreme that they name: `routes`: within the 512 tokens of one sequence on one device no expert is named more than 256 times; one expert, the same for every such block, is named exactly 256 times in each.
All inputs are finite; a program needn't handle non-finite values.
Results may differ from a plain program's by a relative error of at most 0.018.
Values may be sent and summed in bfloat16 or wider, within the bound.
No kernel may reach another device: no remote copies, remote signals or barrier semaphores. Data moves between devices by JAX's collectives and lax.ppermute only.
A program may use at most 256 MiB of HBM per device.

v0:
```python
import jax
import jax.numpy as jnp
from jax import lax
from jax.sharding import PartitionSpec as P

DH = 64


bucket_edges = (1, 2, 3, 4, 5, 6, 7, 8, 12, 16, 23, 32, 46, 64, 91)
norm_eps = 1e-06
precise_result = lax.Precision.HIGHEST


def bucket_of(relative):
    distance = jnp.abs(relative)
    half_bucket = jnp.zeros(relative.shape, jnp.int32)
    for threshold in bucket_edges:
        half_bucket = half_bucket + (distance >= threshold).astype(jnp.int32)
    return half_bucket + 16 * (relative > 0).astype(jnp.int32)


def bucket_grid(row_start, row_count, col_count):
    row_pos = row_start + jnp.arange(row_count, dtype=jnp.int32)
    col_pos = jnp.arange(col_count, dtype=jnp.int32)
    return bucket_of(col_pos[None, :] - row_pos[:, None])


def bias_grid(buckets, table_column, bucket_count):
    result = jnp.zeros(buckets.shape, jnp.float32)
    for label in range(bucket_count):
        result = result + jnp.where(buckets == label, table_column[label], 0.0)
    return result


def fold_buckets(buckets, grad_sum, bucket_count):
    return jnp.stack(
        [jnp.sum(jnp.where(buckets == label, grad_sum, 0.0)) for label in range(bucket_count)]
    )


def rms_norm(value_rows, gain_vector):
    inv_scale = lax.rsqrt(jnp.mean(value_rows * value_rows, axis=-1, keepdims=True) + norm_eps)
    return value_rows * inv_scale * gain_vector


def gelu_tanh(value_rows):
    return jax.nn.gelu(value_rows, approximate=True)


def head_slice(value_rows, head_index, head_size):
    return lax.dynamic_slice_in_dim(value_rows, head_index * head_size, head_size, 2)


def put_head(target, portion, head_index, head_size):
    return lax.dynamic_update_slice_in_dim(target, portion, head_index * head_size, 2)


def head_scores(q_head, k_head, buckets, bias_table, head_index):
    table_column = lax.dynamic_index_in_dim(bias_table, head_index, 1, keepdims=False)
    scores = jnp.einsum("sqd,skd->sqk", q_head, k_head, preferred_element_type=jnp.float32)
    return scores + bias_grid(buckets, table_column, bias_table.shape[0])[None]


def attend(query_matrix, keys_whole, values_whole, buckets, bias_table, head_size):
    seq_count, row_count, feature_width = query_matrix.shape
    head_count = feature_width // head_size

    def one_head(head_index, running):
        attention_result, log_totals = running
        scores = head_scores(
            head_slice(query_matrix, head_index, head_size),
            head_slice(keys_whole, head_index, head_size),
            buckets,
            bias_table,
            head_index,
        )
        row_max = jnp.max(scores, axis=-1, keepdims=True)
        log_total = row_max + jnp.log(jnp.sum(jnp.exp(scores - row_max), axis=-1, keepdims=True))
        weights_low = jnp.exp(scores - log_total).astype(jnp.bfloat16)
        portion = jnp.einsum(
            "sqk,skd->sqd",
            weights_low,
            head_slice(values_whole, head_index, head_size),
            preferred_element_type=jnp.float32,
        )
        attention_result = put_head(attention_result, portion, head_index, head_size)
        log_totals = lax.dynamic_update_index_in_dim(log_totals, log_total[..., 0], head_index, 0)
        return (attention_result, log_totals)

    initial = (
        jnp.zeros((seq_count, row_count, feature_width), jnp.float32),
        jnp.zeros((head_count, seq_count, row_count), jnp.float32),
    )
    return lax.fori_loop(0, head_count, one_head, initial)


def attend_back_rows(
    query_matrix, keys_whole, values_whole, mixed_grad, log_totals, buckets, bias_table, head_size
):
    seq_count, row_count, feature_width = query_matrix.shape
    col_count = keys_whole.shape[1]
    head_count = feature_width // head_size
    bucket_count = bias_table.shape[0]

    def one_head(head_index, running):
        query_grad, deltas, diag_grad, key_part, value_part = running
        q_head = head_slice(query_matrix, head_index, head_size)
        k_head = head_slice(keys_whole, head_index, head_size)
        v_head = head_slice(values_whole, head_index, head_size)
        g_head = head_slice(mixed_grad, head_index, head_size)
        scores = head_scores(q_head, k_head, buckets, bias_table, head_index)
        weights = jnp.exp(scores - log_totals[head_index][..., None])
        weight_grad = jnp.einsum("sqd,skd->sqk", g_head, v_head, preferred_element_type=jnp.float32)
        delta_row = jnp.sum(weights * weight_grad, axis=-1)
        score_grad = (weights * (weight_grad - delta_row[..., None])).astype(jnp.bfloat16)
        query_grad = put_head(
            query_grad,
            jnp.einsum("sqk,skd->sqd", score_grad, k_head, preferred_element_type=jnp.float32),
            head_index,
            head_size,
        )
        deltas = lax.dynamic_update_index_in_dim(deltas, delta_row, head_index, 0)
        folded = fold_buckets(
            buckets, jnp.sum(score_grad.astype(jnp.float32), axis=0), bucket_count
        )
        diag_grad = lax.dynamic_update_index_in_dim(diag_grad, folded, head_index, 0)
        key_part = put_head(
            key_part,
            jnp.einsum("sqk,sqd->skd", score_grad, q_head, preferred_element_type=jnp.float32),
            head_index,
            head_size,
        )
        value_part = put_head(
            value_part,
            jnp.einsum(
                "sqk,sqd->skd",
                weights.astype(jnp.bfloat16),
                g_head,
                preferred_element_type=jnp.float32,
            ),
            head_index,
            head_size,
        )
        return (query_grad, deltas, diag_grad, key_part, value_part)

    key_shape = (seq_count, col_count, feature_width)
    initial = (
        jnp.zeros((seq_count, row_count, feature_width), jnp.float32),
        jnp.zeros((head_count, seq_count, row_count), jnp.float32),
        jnp.zeros((head_count, bucket_count), jnp.float32),
        jnp.zeros(key_shape, jnp.float32),
        jnp.zeros(key_shape, jnp.float32),
    )
    return lax.fori_loop(0, head_count, one_head, initial)


def make_dispatch(routes, expert_count, capacity):
    labels = jnp.arange(expert_count, dtype=jnp.int32)
    expert_hits = (routes[..., None] == labels).astype(jnp.int32)
    places = jnp.sum((jnp.cumsum(expert_hits, axis=1) - 1) * expert_hits, axis=-1)
    expert_match = routes[:, None, None, :] == labels[None, :, None, None]
    slot_match = (
        places[:, None, None, :] == jnp.arange(capacity, dtype=jnp.int32)[None, None, :, None]
    )
    return (expert_match & slot_match).astype(jnp.bfloat16)


def to_rows(arrived, owners, local_experts):
    feature_width = arrived.shape[-1]
    grouped = arrived.reshape(owners, local_experts, -1, feature_width)
    return jnp.swapaxes(grouped, 0, 1).reshape(local_experts, -1, feature_width)


def from_rows(expert_rows, owners, seq_count, capacity):
    local_experts, _, feature_width = expert_rows.shape
    grouped = expert_rows.reshape(local_experts, owners, seq_count * capacity, feature_width)
    return jnp.swapaxes(grouped, 0, 1).reshape(
        owners * local_experts, seq_count, capacity, feature_width
    )


def per_device(
    tokens,
    cotangent,
    routes,
    norm1_gain,
    query_weight,
    key_weight,
    value_weight,
    output_weight,
    bias_table,
    norm2_gain,
    router_weight,
    w_in,
    w_out,
):
    seq_count, local_len, model_width = tokens.shape
    head_size = DH
    expert_count = router_weight.shape[1]
    local_experts = w_in.shape[0]
    owners = lax.axis_size("expert")
    capacity = local_len // 2
    full_len = local_len * lax.axis_size("ctx")
    first_pos = lax.axis_index("ctx") * local_len
    input_tokens = tokens.astype(jnp.float32)
    normed1, norm1_pull = jax.vjp(rms_norm, input_tokens, norm1_gain)
    attention_input = normed1.astype(jnp.bfloat16)
    query_matrix = jnp.einsum(
        "sxd,de->sxe", attention_input, query_weight, preferred_element_type=jnp.float32
    ).astype(jnp.bfloat16)
    keys_local = jnp.einsum(
        "sxd,de->sxe", attention_input, key_weight, preferred_element_type=jnp.float32
    ).astype(jnp.bfloat16)
    values_local = jnp.einsum(
        "sxd,de->sxe", attention_input, value_weight, preferred_element_type=jnp.float32
    ).astype(jnp.bfloat16)
    keys_whole, values_whole = (
        lax.all_gather(keys_local, "ctx", axis=1, tiled=True),
        lax.all_gather(values_local, "ctx", axis=1, tiled=True),
    )
    near_buckets = bucket_grid(first_pos, local_len, full_len)
    attention_result, log_totals = attend(
        query_matrix, keys_whole, values_whole, near_buckets, bias_table, head_size
    )
    attn_mixed = attention_result.astype(jnp.bfloat16)
    first_residual1 = input_tokens + jnp.einsum(
        "sxd,de->sxe", attn_mixed, output_weight, preferred_element_type=jnp.float32
    )
    normed2, norm2_pull = jax.vjp(rms_norm, first_residual1, norm2_gain)
    router_input = normed2.astype(jnp.bfloat16)
    router_scores = jnp.einsum(
        "sxd,de->sxe", router_input, router_weight, preferred_element_type=jnp.float32
    )
    expert_onehot = (routes[..., None] == jnp.arange(expert_count, dtype=jnp.int32)).astype(
        jnp.float32
    )

    def gate_of(logit_values):
        return jnp.sum(jax.nn.softmax(logit_values, axis=-1) * expert_onehot, axis=-1)

    gates, gate_pull = jax.vjp(gate_of, router_scores)
    dispatch = make_dispatch(routes, expert_count, capacity)
    outgoing = jnp.einsum(
        "secx,sxd->escd", dispatch, router_input, preferred_element_type=jnp.float32
    ).astype(jnp.bfloat16)
    arrived = lax.all_to_all(outgoing, "expert", split_axis=0, concat_axis=0, tiled=True)
    expert_rows = to_rows(arrived, owners, local_experts)
    pre_act = jnp.einsum("erd,edf->erf", expert_rows, w_in, preferred_element_type=jnp.float32)
    hidden, gelu_pull = jax.vjp(gelu_tanh, pre_act)
    hidden_low = hidden.astype(jnp.bfloat16)
    expert_out = jnp.einsum(
        "erf,efd->erd", hidden_low, w_out, preferred_element_type=jnp.float32
    ).astype(jnp.bfloat16)
    returned = lax.all_to_all(
        from_rows(expert_out, owners, seq_count, capacity),
        "expert",
        split_axis=0,
        concat_axis=0,
        tiled=True,
    )
    expert_tok = jnp.einsum(
        "secx,escd->sxd", dispatch, returned, preferred_element_type=jnp.float32
    )
    block_out = (first_residual1 + gates[..., None] * expert_tok).astype(jnp.bfloat16)
    upstream = cotangent.astype(jnp.float32)
    gate_grad = jnp.sum(upstream * expert_tok, axis=-1)
    logit_grad = gate_pull(gate_grad)[0]
    grad_tok = (gates[..., None] * upstream).astype(jnp.bfloat16)
    grad_out = jnp.einsum(
        "secx,sxd->escd", dispatch, grad_tok, preferred_element_type=jnp.float32
    ).astype(jnp.bfloat16)
    grad_rows = to_rows(
        lax.all_to_all(grad_out, "expert", split_axis=0, concat_axis=0, tiled=True),
        owners,
        local_experts,
    )
    hidden_grad = jnp.einsum(
        "erd,efd->erf", grad_rows, w_out, preferred_element_type=jnp.float32
    ).astype(jnp.bfloat16)
    grad_w_out = jnp.einsum(
        "erf,erd->efd", hidden_low, grad_rows, preferred_element_type=jnp.float32
    )
    pre_grad = gelu_pull(hidden_grad.astype(jnp.float32))[0].astype(jnp.bfloat16)
    grad_w_in = jnp.einsum(
        "erd,erf->edf", expert_rows, pre_grad, preferred_element_type=jnp.float32
    )
    row_grad = jnp.einsum(
        "erf,edf->erd", pre_grad, w_in, preferred_element_type=jnp.float32
    ).astype(jnp.bfloat16)
    back_grad = lax.all_to_all(
        from_rows(row_grad, owners, seq_count, capacity),
        "expert",
        split_axis=0,
        concat_axis=0,
        tiled=True,
    )
    router_in_grad = jnp.einsum(
        "secx,escd->sxd", dispatch, back_grad, preferred_element_type=jnp.float32
    )
    router_in_grad = router_in_grad + jnp.einsum(
        "sxe,de->sxd", logit_grad, router_weight.astype(jnp.float32), precision=precise_result
    )
    grad_w_router = jnp.einsum(
        "sxd,sxe->de", router_input.astype(jnp.float32), logit_grad, precision=precise_result
    )
    norm2_back, grad_norm2 = norm2_pull(router_in_grad)
    resid_grad = upstream + norm2_back
    attn_grad = resid_grad.astype(jnp.bfloat16)
    grad_w_output = jnp.einsum(
        "sxd,sxe->de", attn_mixed, attn_grad, preferred_element_type=jnp.float32
    )
    mixed_grad = jnp.einsum(
        "sxe,de->sxd", attn_grad, output_weight, preferred_element_type=jnp.float32
    ).astype(jnp.bfloat16)
    keys_back, values_back = (keys_whole, values_whole)
    query_grad, deltas, diag_grad, key_part, value_part = attend_back_rows(
        query_matrix,
        keys_back,
        values_back,
        mixed_grad,
        log_totals,
        near_buckets,
        bias_table,
        head_size,
    )
    key_grad, value_grad = (
        lax.psum_scatter(key_part, "ctx", scatter_dimension=1, tiled=True),
        lax.psum_scatter(value_part, "ctx", scatter_dimension=1, tiled=True),
    )
    query_low = query_grad.astype(jnp.bfloat16)
    key_low = key_grad.astype(jnp.bfloat16)
    value_low = value_grad.astype(jnp.bfloat16)
    grad_w_query = jnp.einsum(
        "sxd,sxe->de", attention_input, query_low, preferred_element_type=jnp.float32
    )
    grad_w_key = jnp.einsum(
        "sxd,sxe->de", attention_input, key_low, preferred_element_type=jnp.float32
    )
    grad_w_value = jnp.einsum(
        "sxd,sxe->de", attention_input, value_low, preferred_element_type=jnp.float32
    )
    norm_in_grad = jnp.einsum(
        "sxe,de->sxd", query_low, query_weight, preferred_element_type=jnp.float32
    )
    norm_in_grad = norm_in_grad + jnp.einsum(
        "sxe,de->sxd", key_low, key_weight, preferred_element_type=jnp.float32
    )
    norm_in_grad = norm_in_grad + jnp.einsum(
        "sxe,de->sxd", value_low, value_weight, preferred_element_type=jnp.float32
    )
    norm1_back, grad_norm1 = norm1_pull(norm_in_grad)
    d_tokens = resid_grad + norm1_back
    grad_bias = diag_grad.T
    summed = lax.psum(
        (
            grad_w_query,
            grad_w_key,
            grad_w_value,
            grad_w_output,
            grad_bias,
            grad_norm1,
            grad_norm2,
            grad_w_router,
        ),
        ("dp", "ctx", "expert"),
    )
    expert_sums = (
        lax.psum_scatter(grad_w_in, ("dp", "ctx"), scatter_dimension=2, tiled=True),
        lax.psum_scatter(grad_w_out, ("dp", "ctx"), scatter_dimension=1, tiled=True),
    )
    return (
        block_out,
        d_tokens,
        summed[5],
        summed[0],
        summed[1],
        summed[2],
        summed[3],
        summed[4],
        summed[6],
        summed[7],
        expert_sums[0],
        expert_sums[1],
    )


def solution(mesh):
    in_specs = (
        P(("dp", "expert"), "ctx", None),
        P(("dp", "expert"), "ctx", None),
        P(("dp", "expert"), "ctx"),
        P(),
        P(),
        P(),
        P(),
        P(),
        P(),
        P(),
        P(),
        P("expert", None, None),
        P("expert", None, None),
    )
    out_specs = (
        P(("dp", "expert"), "ctx", None),
        P(("dp", "expert"), "ctx", None),
        P(),
        P(),
        P(),
        P(),
        P(),
        P(),
        P(),
        P(),
        P("expert", None, ("dp", "ctx")),
        P("expert", ("dp", "ctx"), None),
    )
    return jax.shard_map(
        per_device, mesh=mesh, in_specs=in_specs, out_specs=out_specs, check_vma=False
    )
```

profile of v0, /device:TPU:0, one launch (start us, length us, event | category | flops | bytes accessed | tf_op | source)
XLA Modules:
  0.0 2293.2 jit_solution(1817428912164469579)
XLA Ops:
  50.6 458.8 %while.36 = (s32[]{:T(128)}, bf16[2,512,768]{1,2,0:T(8,128)(2,1)}, f32[12,2,512]{2,1,0:T(2,128)}, bf16[2,512,768]{1,2,0:T(8,128)(2,1)}, bf16[2,1024,768]{1,2,0:T...) while((s32[]{:T(128)}, bf16[2,512,768]{1,2,0:T(8,128)(2,1)}, ...), condition=%wide.region_4.5_spmd.clone, body=%wide.region_1.4_spmd.clone.sunk | while | flops 352320512 | bytes 21926708 | solution.py:94
  53.2 30.0 %select_add_fusion.6 = f32[512,1024]{1,0:T(8,128)S(1)} fusion(s32[512]{0:T(512)S(1)} %get-tuple-element.995, f32[]{:T(128)} %bitcast.313, f32[]{:T(128)} %bitcast.314, f32[]{:T(128)} %bitcast.315, f32[]{:T(128)} %bitcast.316, f32[]{:T(128)} %bitcast.317, f32[]{:T(128)} %bitcast.318, f32[]{:T(128)} %bitcast.319, f32[]{:T(128)} %bitcast.320, ...), kind=kLoop, calls=%fused_computation.24.clone.1 | loop fusion | flops 75497472 | bytes 2099328 | tf_op jit(solution)/shard_map/while/body/eval_jaxpr/add | solution.py:31
  91.4 30.0 %select_add_fusion.6 = f32[512,1024]{1,0:T(8,128)S(1)} fusion(s32[512]{0:T(512)S(1)} %get-tuple-element.995, f32[]{:T(128)} %bitcast.313, f32[]{:T(128)} %bitcast.314, f32[]{:T(128)} %bitcast.315, f32[]{:T(128)} %bitcast.316, f32[]{:T(128)} %bitcast.317, f32[]{:T(128)} %bitcast.318, f32[]{:T(128)} %bitcast.319, f32[]{:T(128)} %bitcast.320, ...), kind=kLoop, calls=%fused_computation.24.clone.1 | loop fusion | flops 75497472 | bytes 2099328 | tf_op jit(solution)/shard_map/while/body/eval_jaxpr/add | solution.py:31
  129.5 30.0 %select_add_fusion.6 = f32[512,1024]{1,0:T(8,128)S(1)} fusion(s32[512]{0:T(512)S(1)} %get-tuple-element.995, f32[]{:T(128)} %bitcast.313, f32[]{:T(128)} %bitcast.314, f32[]{:T(128)} %bitcast.315, f32[]{:T(128)} %bitcast.316, f32[]{:T(128)} %bitcast.317, f32[]{:T(128)} %bitcast.318, f32[]{:T(128)} %bitcast.319, f32[]{:T(128)} %bitcast.320, ...), kind=kLoop, calls=%fused_computation.24.clone.1 | loop fusion | flops 75497472 | bytes 2099328 | tf_op jit(solution)/shard_map/while/body/eval_jaxpr/add | solution.py:31
  167.7 30.0 %select_add_fusion.6 = f32[512,1024]{1,0:T(8,128)S(1)} fusion(s32[512]{0:T(512)S(1)} %get-tuple-element.995, f32[]{:T(128)} %bitcast.313, f32[]{:T(128)} %bitcast.314, f32[]{:T(128)} %bitcast.315, f32[]{:T(128)} %bitcast.316, f32[]{:T(128)} %bitcast.317, f32[]{:T(128)} %bitcast.318, f32[]{:T(128)} %bitcast.319, f32[]{:T(128)} %bitcast.320, ...), kind=kLoop, calls=%fused_computation.24.clone.1 | loop fusion | flops 75497472 | bytes 2099328 | tf_op jit(solution)/shard_map/while/body/eval_jaxpr/add | solution.py:31
  205.9 30.0 %select_add_fusion.6 = f32[512,1024]{1,0:T(8,128)S(1)} fusion(s32[512]{0:T(512)S(1)} %get-tuple-element.995, f32[]{:T(128)} %bitcast.313, f32[]{:T(128)} %bitcast.314, f32[]{:T(128)} %bitcast.315, f32[]{:T(128)} %bitcast.316, f32[]{:T(128)} %bitcast.317, f32[]{:T(128)} %bitcast.318, f32[]{:T(128)} %bitcast.319, f32[]{:T(128)} %bitcast.320, ...), kind=kLoop, calls=%fused_computation.24.clone.1 | loop fusion | flops 75497472 | bytes 2099328 | tf_op jit(solution)/shard_map/while/body/eval_jaxpr/add | solution.py:31
  244.1 30.0 %select_add_fusion.6 = f32[512,1024]{1,0:T(8,128)S(1)} fusion(s32[512]{0:T(512)S(1)} %get-tuple-element.995, f32[]{:T(128)} %bitcast.313, f32[]{:T(128)} %bitcast.314, f32[]{:T(128)} %bitcast.315, f32[]{:T(128)} %bitcast.316, f32[]{:T(128)} %bitcast.317, f32[]{:T(128)} %bitcast.318, f32[]{:T(128)} %bitcast.319, f32[]{:T(128)} %bitcast.320, ...), kind=kLoop, calls=%fused_computation.24.clone.1 | loop fusion | flops 75497472 | bytes 2099328 | tf_op jit(solution)/shard_map/while/body/eval_jaxpr/add | solution.py:31
  282.3 30.0 %select_add_fusion.6 = f32[512,1024]{1,0:T(8,128)S(1)} fusion(s32[512]{0:T(512)S(1)} %get-tuple-element.995, f32[]{:T(128)} %bitcast.313, f32[]{:T(128)} %bitcast.314, f32[]{:T(128)} %bitcast.315, f32[]{:T(128)} %bitcast.316, f32[]{:T(128)} %bitcast.317, f32[]{:T(128)} %bitcast.318, f32[]{:T(128)} %bitcast.319, f32[]{:T(128)} %bitcast.320, ...), kind=kLoop, calls=%fused_computation.24.clone.1 | loop fusion | flops 75497472 | bytes 2099328 | tf_op jit(solution)/shard_map/while/body/eval_jaxpr/add | solution.py:31
  320.4 30.0 %select_add_fusion.6 = f32[512,1024]{1,0:T(8,128)S(1)} fusion(s32[512]{0:T(512)S(1)} %get-tuple-element.995, f32[]{:T(128)} %bitcast.313, f32[]{:T(128)} %bitcast.314, f32[]{:T(128)} %bitcast.315, f32[]{:T(128)} %bitcast.316, f32[]{:T(128)} %bitcast.317, f32[]{:T(128)} %bitcast.318, f32[]{:T(128)} %bitcast.319, f32[]{:T(128)} %bitcast.320, ...), kind=kLoop, calls=%fused_computation.24.clone.1 | loop fusion | flops 75497472 | bytes 2099328 | tf_op jit(solution)/shard_map/while/body/eval_jaxpr/add | solution.py:31
  358.6 30.0 %select_add_fusion.6 = f32[512,1024]{1,0:T(8,128)S(1)} fusion(s32[512]{0:T(512)S(1)} %get-tuple-element.995, f32[]{:T(128)} %bitcast.313, f32[]{:T(128)} %bitcast.314, f32[]{:T(128)} %bitcast.315, f32[]{:T(128)} %bitcast.316, f32[]{:T(128)} %bitcast.317, f32[]{:T(128)} %bitcast.318, f32[]{:T(128)} %bitcast.319, f32[]{:T(128)} %bitcast.320, ...), kind=kLoop, calls=%fused_computation.24.clone.1 | loop fusion | flops 75497472 | bytes 2099328 | tf_op jit(solution)/shard_map/while/body/eval_jaxpr/add | solution.py:31
  396.8 30.0 %select_add_fusion.6 = f32[512,1024]{1,0:T(8,128)S(1)} fusion(s32[512]{0:T(512)S(1)} %get-tuple-element.995, f32[]{:T(128)} %bitcast.313, f32[]{:T(128)} %bitcast.314, f32[]{:T(128)} %bitcast.315, f32[]{:T(128)} %bitcast.316, f32[]{:T(128)} %bitcast.317, f32[]{:T(128)} %bitcast.318, f32[]{:T(128)} %bitcast.319, f32[]{:T(128)} %bitcast.320, ...), kind=kLoop, calls=%fused_computation.24.clone.1 | loop fusion | flops 75497472 | bytes 2099328 | tf_op jit(solution)/shard_map/while/body/eval_jaxpr/add | solution.py:31
  435.0 30.0 %select_add_fusion.6 = f32[512,1024]{1,0:T(8,128)S(1)} fusion(s32[512]{0:T(512)S(1)} %get-tuple-element.995, f32[]{:T(128)} %bitcast.313, f32[]{:T(128)} %bitcast.314, f32[]{:T(128)} %bitcast.315, f32[]{:T(128)} %bitcast.316, f32[]{:T(128)} %bitcast.317, f32[]{:T(128)} %bitcast.318, f32[]{:T(128)} %bitcast.319, f32[]{:T(128)} %bitcast.320, ...), kind=kLoop, calls=%fused_computation.24.clone.1 | loop fusion | flops 75497472 | bytes 2099328 | tf_op jit(solution)/shard_map/while/body/eval_jaxpr/add | solution.py:31
  473.2 30.0 %select_add_fusion.6 = f32[512,1024]{1,0:T(8,128)S(1)} fusion(s32[512]{0:T(512)S(1)} %get-tuple-element.995, f32[]{:T(128)} %bitcast.313, f32[]{:T(128)} %bitcast.314, f32[]{:T(128)} %bitcast.315, f32[]{:T(128)} %bitcast.316, f32[]{:T(128)} %bitcast.317, f32[]{:T(128)} %bitcast.318, f32[]{:T(128)} %bitcast.319, f32[]{:T(128)} %bitcast.320, ...), kind=kLoop, calls=%fused_computation.24.clone.1 | loop fusion | flops 75497472 | bytes 2099328 | tf_op jit(solution)/shard_map/while/body/eval_jaxpr/add | solution.py:31
  517.3 75.9 %all_to_all.20 = bf16[4,2,256,768]{2,3,1,0:T(8,128)(2,1)} all-to-all(bf16[4,2,256,768]{2,3,1,0:T(8,128)(2,1)S(1)} %copy.79), channel_id=1, replica_groups=mesh['dp'=4,'ctx'=2,'expert'=4] {'expert'}, dimensions={0} | all-to-all | bytes 6291456 | tf_op jit(solution)/shard_map/all_to_all | solution.py:246
  615.3 21.7 fusion.119
  642.7 69.8 %all-to-all-done.1 = bf16[4,2,256,768]{3,2,1,0:T(8,128)(2,1)} async-done(((bf16[4,2,256,768]{3,2,1,0:T(8,128)(2,1)}), bf16[4,2,256,768]{3,2,1,0:T(8,128)(2,1)}, u32[]{:S(2)}, u32[]{:S(2)}) %all-to-all-start.1) | async-done | bytes 3145760 | tf_op jit(solution)/shard_map/all_to_all | solution.py:254
  720.0 73.6 %all_to_all.21 = bf16[4,2,256,768]{2,3,1,0:T(8,128)(2,1)} all-to-all(bf16[4,2,256,768]{2,3,1,0:T(8,128)(2,1)S(1)} %copy.84), channel_id=1, replica_groups=mesh['dp'=4,'ctx'=2,'expert'=4] {'expert'}, dimensions={0} | all-to-all | bytes 6291456 | tf_op jit(solution)/shard_map/all_to_all | solution.py:273
  798.4 31.1 %fusion.91 = bf16[2048,3072]{1,0:T(8,128)(2,1)} fusion(f32[2048,3072]{1,0:T(8,128)} %fusion.112, bf16[2048,768]{1,0:T(8,128)(2,1)} %bitcast.415, bf16[1,3072,768]{2,1,0:T(8,128)(2,1)} %param.29), kind=kOutput, calls=%fused_computation.154 | convolution fusion | flops 9802088448 | bytes 45613056 | tf_op jit(solution)/shard_map/erd,efd->erf/dot_general | solution.py:277
  849.6 69.7 %all-to-all-done.3 = bf16[4,2,256,768]{3,2,1,0:T(8,128)(2,1)} async-done(((bf16[4,2,256,768]{3,2,1,0:T(8,128)(2,1)}), bf16[4,2,256,768]{3,2,1,0:T(8,128)(2,1)}, u32[]{:S(2)}, u32[]{:S(2)}) %all-to-all-start.3) | async-done | bytes 3145760 | tf_op jit(solution)/shard_map/all_to_all | solution.py:290
  941.3 941.3 %while.37 = (s32[]{:T(128)}, bf16[2,512,768]{1,2,0:T(8,128)(2,1)}, f32[12,32]{1,0:T(8,128)S(1)}, f32[2,1024,768]{1,2,0:T(8,128)}, f32[2,1024,768]{1,2,0:T(8,128)...) while((s32[]{:T(128)}, bf16[2,512,768]{1,2,0:T(8,128)(2,1)}, ...), condition=%wide.region_50.51_spmd.clone, body=%wide.region_15.50_spmd.clone.sunk | while | flops 836762624 | bytes 46701012 | solution.py:154
  944.3 30.2 %select_add_fusion.7 = f32[512,1024]{1,0:T(8,128)S(1)} fusion(s32[512]{0:T(512)S(1)} %get-tuple-element.1043, f32[]{:T(128)} %bitcast.348, f32[]{:T(128)} %bitcast.349, f32[]{:T(128)} %bitcast.350, f32[]{:T(128)} %bitcast.351, f32[]{:T(128)} %bitcast.352, f32[]{:T(128)} %bitcast.353, f32[]{:T(128)} %bitcast.354, f32[]{:T(128)} %bitcast.355, ...), kind=kLoop, calls=%fused_computation.95.clone.1 | loop fusion | flops 75497472 | bytes 2099328 | tf_op jit(solution)/shard_map/while/body/eval_jaxpr/add | solution.py:31
  994.5 20.8 stack.265
  1022.7 30.2 %select_add_fusion.7 = f32[512,1024]{1,0:T(8,128)S(1)} fusion(s32[512]{0:T(512)S(1)} %get-tuple-element.1043, f32[]{:T(128)} %bitcast.348, f32[]{:T(128)} %bitcast.349, f32[]{:T(128)} %bitcast.350, f32[]{:T(128)} %bitcast.351, f32[]{:T(128)} %bitcast.352, f32[]{:T(128)} %bitcast.353, f32[]{:T(128)} %bitcast.354, f32[]{:T(128)} %bitcast.355, ...), kind=kLoop, calls=%fused_computation.95.clone.1 | loop fusion | flops 75497472 | bytes 2099328 | tf_op jit(solution)/shard_map/while/body/eval_jaxpr/add | solution.py:31
  1072.9 20.8 stack.265
  1101.1 30.2 %select_add_fusion.7 = f32[512,1024]{1,0:T(8,128)S(1)} fusion(s32[512]{0:T(512)S(1)} %get-tuple-element.1043, f32[]{:T(128)} %bitcast.348, f32[]{:T(128)} %bitcast.349, f32[]{:T(128)} %bitcast.350, f32[]{:T(128)} %bitcast.351, f32[]{:T(128)} %bitcast.352, f32[]{:T(128)} %bitcast.353, f32[]{:T(128)} %bitcast.354, f32[]{:T(128)} %bitcast.355, ...), kind=kLoop, calls=%fused_computation.95.clone.1 | loop fusion | flops 75497472 | bytes 2099328 | tf_op jit(solution)/shard_map/while/body/eval_jaxpr/add | solution.py:31
  1151.3 20.8 stack.265
  1179.5 30.2 %select_add_fusion.7 = f32[512,1024]{1,0:T(8,128)S(1)} fusion(s32[512]{0:T(512)S(1)} %get-tuple-element.1043, f32[]{:T(128)} %bitcast.348, f32[]{:T(128)} %bitcast.349, f32[]{:T(128)} %bitcast.350, f32[]{:T(128)} %bitcast.351, f32[]{:T(128)} %bitcast.352, f32[]{:T(128)} %bitcast.353, f32[]{:T(128)} %bitcast.354, f32[]{:T(128)} %bitcast.355, ...), kind=kLoop, calls=%fused_computation.95.clone.1 | loop fusion | flops 75497472 | bytes 2099328 | tf_op jit(solution)/shard_map/while/body/eval_jaxpr/add | solution.py:31
  1229.7 20.8 stack.265
  1258.0 30.2 %select_add_fusion.7 = f32[512,1024]{1,0:T(8,128)S(1)} fusion(s32[512]{0:T(512)S(1)} %get-tuple-element.1043, f32[]{:T(128)} %bitcast.348, f32[]{:T(128)} %bitcast.349, f32[]{:T(128)} %bitcast.350, f32[]{:T(128)} %bitcast.351, f32[]{:T(128)} %bitcast.352, f32[]{:T(128)} %bitcast.353, f32[]{:T(128)} %bitcast.354, f32[]{:T(128)} %bitcast.355, ...), kind=kLoop, calls=%fused_computation.95.clone.1 | loop fusion | flops 75497472 | bytes 2099328 | tf_op jit(solution)/shard_map/while/body/eval_jaxpr/add | solution.py:31
  1308.1 20.8 stack.265
  1336.3 30.2 %select_add_fusion.7 = f32[512,1024]{1,0:T(8,128)S(1)} fusion(s32[512]{0:T(512)S(1)} %get-tuple-element.1043, f32[]{:T(128)} %bitcast.348, f32[]{:T(128)} %bitcast.349, f32[]{:T(128)} %bitcast.350, f32[]{:T(128)} %bitcast.351, f32[]{:T(128)} %bitcast.352, f32[]{:T(128)} %bitcast.353, f32[]{:T(128)} %bitcast.354, f32[]{:T(128)} %bitcast.355, ...), kind=kLoop, calls=%fused_computation.95.clone.1 | loop fusion | flops 75497472 | bytes 2099328 | tf_op jit(solution)/shard_map/while/body/eval_jaxpr/add | solution.py:31
  1386.5 20.8 stack.265
  1414.7 30.2 %select_add_fusion.7 = f32[512,1024]{1,0:T(8,128)S(1)} fusion(s32[512]{0:T(512)S(1)} %get-tuple-element.1043, f32[]{:T(128)} %bitcast.348, f32[]{:T(128)} %bitcast.349, f32[]{:T(128)} %bitcast.350, f32[]{:T(128)} %bitcast.351, f32[]{:T(128)} %bitcast.352, f32[]{:T(128)} %bitcast.353, f32[]{:T(128)} %bitcast.354, f32[]{:T(128)} %bitcast.355, ...), kind=kLoop, calls=%fused_computation.95.clone.1 | loop fusion | flops 75497472 | bytes 2099328 | tf_op jit(solution)/shard_map/while/body/eval_jaxpr/add | solution.py:31
  1464.9 20.8 stack.265
  1493.1 30.2 %select_add_fusion.7 = f32[512,1024]{1,0:T(8,128)S(1)} fusion(s32[512]{0:T(512)S(1)} %get-tuple-element.1043, f32[]{:T(128)} %bitcast.348, f32[]{:T(128)} %bitcast.349, f32[]{:T(128)} %bitcast.350, f32[]{:T(128)} %bitcast.351, f32[]{:T(128)} %bitcast.352, f32[]{:T(128)} %bitcast.353, f32[]{:T(128)} %bitcast.354, f32[]{:T(128)} %bitcast.355, ...), kind=kLoop, calls=%fused_computation.95.clone.1 | loop fusion | flops 75497472 | bytes 2099328 | tf_op jit(solution)/shard_map/while/body/eval_jaxpr/add | solution.py:31
  1543.3 20.8 stack.265
  1571.4 30.2 %select_add_fusion.7 = f32[512,1024]{1,0:T(8,128)S(1)} fusion(s32[512]{0:T(512)S(1)} %get-tuple-element.1043, f32[]{:T(128)} %bitcast.348, f32[]{:T(128)} %bitcast.349, f32[]{:T(128)} %bitcast.350, f32[]{:T(128)} %bitcast.351, f32[]{:T(128)} %bitcast.352, f32[]{:T(128)} %bitcast.353, f32[]{:T(128)} %bitcast.354, f32[]{:T(128)} %bitcast.355, ...), kind=kLoop, calls=%fused_computation.95.clone.1 | loop fusion | flops 75497472 | bytes 2099328 | tf_op jit(solution)/shard_map/while/body/eval_jaxpr/add | solution.py:31
  1621.6 20.8 stack.265
  1649.8 30.2 %select_add_fusion.7 = f32[512,1024]{1,0:T(8,128)S(1)} fusion(s32[512]{0:T(512)S(1)} %get-tuple-element.1043, f32[]{:T(128)} %bitcast.348, f32[]{:T(128)} %bitcast.349, f32[]{:T(128)} %bitcast.350, f32[]{:T(128)} %bitcast.351, f32[]{:T(128)} %bitcast.352, f32[]{:T(128)} %bitcast.353, f32[]{:T(128)} %bitcast.354, f32[]{:T(128)} %bitcast.355, ...), kind=kLoop, calls=%fused_computation.95.clone.1 | loop fusion | flops 75497472 | bytes 2099328 | tf_op jit(solution)/shard_map/while/body/eval_jaxpr/add | solution.py:31
  1700.0 20.8 stack.265
  1728.2 30.2 %select_add_fusion.7 = f32[512,1024]{1,0:T(8,128)S(1)} fusion(s32[512]{0:T(512)S(1)} %get-tuple-element.1043, f32[]{:T(128)} %bitcast.348, f32[]{:T(128)} %bitcast.349, f32[]{:T(128)} %bitcast.350, f32[]{:T(128)} %bitcast.351, f32[]{:T(128)} %bitcast.352, f32[]{:T(128)} %bitcast.353, f32[]{:T(128)} %bitcast.354, f32[]{:T(128)} %bitcast.355, ...), kind=kLoop, calls=%fused_computation.95.clone.1 | loop fusion | flops 75497472 | bytes 2099328 | tf_op jit(solution)/shard_map/while/body/eval_jaxpr/add | solution.py:31
  1778.4 20.8 stack.265
  1806.6 30.2 %select_add_fusion.7 = f32[512,1024]{1,0:T(8,128)S(1)} fusion(s32[512]{0:T(512)S(1)} %get-tuple-element.1043, f32[]{:T(128)} %bitcast.348, f32[]{:T(128)} %bitcast.349, f32[]{:T(128)} %bitcast.350, f32[]{:T(128)} %bitcast.351, f32[]{:T(128)} %bitcast.352, f32[]{:T(128)} %bitcast.353, f32[]{:T(128)} %bitcast.354, f32[]{:T(128)} %bitcast.355, ...), kind=kLoop, calls=%fused_computation.95.clone.1 | loop fusion | flops 75497472 | bytes 2099328 | tf_op jit(solution)/shard_map/while/body/eval_jaxpr/add | solution.py:31
  1856.8 20.8 stack.265
  1883.3 22.5 convolution_bitcast_fusion
  1955.2 39.3 %all-reduce = (f32[768]{0:T(1024)}, f32[32,12]{0,1:T(8,128)}, f32[768]{0:T(1024)}, f32[768,4]{0,1:T(4,128)}) all-reduce(f32[768]{0:T(1024)S(1)} %get-tuple-element.500, f32[32,12]{0,1:T(8,128)S(1)} %bitcast.421, f32[768]{0:T(1024)S(1)} %copy-done.33, ...), channel_id=1, replica_groups=mesh['dp'=4,'ctx'=2,'expert'=4] {'dp','ctx','expert'}, use_global_device_ids=true, to_apply=%region_55.56 | all-reduce | flops 4992 | bytes 39936 | tf_op jit(solution)/shard_map/psum | solution.py:354
  1999.8 77.8 %reduce-scatter.9.cloned.1.call-done = f32[1,768,384]{2,1,0:T(8,128)} async-done(((f32[1,768,3072]{2,1,0:T(8,128)}), f32[1,768,384]{2,1,0:T(8,128)}) %reduce-scatter.9.cloned.1.call-update) | async-done | bytes 1179664 | tf_op jit(solution)/shard_map/reduce_scatter | solution.py:368
  2077.6 198.8 %all-reduce.4.cloned.1.call-done = (f32[768,768]{1,0:T(8,128)}, f32[768,768]{1,0:T(8,128)}, f32[768,768]{1,0:T(8,128)}, f32[768,768]{1,0:T(8,128)}) async-done(((f32[768,768]{1,0:T(8,128)}, f32[768,768]{1,0:T(8,128)}, f32[768,768]{1,0:T(8,128)}, f32[768,768]{1,0:T(8,128)}), (f32[768,768]{1,0:T(8,128)}, f32[768,768]{1,0:T(8,128)}, f32[768,768]{1,0:T(8,128)}, ...) | async-done | bytes 9437200 | tf_op jit(solution)/shard_map/psum | solution.py:354
  (385 shorter events, 625.2 us)
Async XLA Ops:
  7.2 7.1 copy-start
  7.2 22.0 all-gather.3.cloned.1.call-start
  9.1 0.6 copy-start.30
  9.7 10.5 copy-start.24
  9.7 4.6 copy-start.5
  9.7 4.6 copy-start.28
  14.2 2.7 copy-start.21
  14.3 30.4 %all-gather.5.cloned.1.call-start = ((), (), s32[]{:S(2)}) async-start(), calls=%async_computation.9 | async-start | bytes 4718592 | tf_op jit(solution)/shard_map/all_gather | solution.py:219
  509.4 3.4 copy-start.19
  509.4 5.1 copy-start.26
  512.8 1.6 copy-start.1
  512.9 2.0 copy-start.34
  512.9 2.0 copy-start.22
  514.8 127.2 %copy-start.3 = (bf16[2,512,768]{2,1,0:T(8,128)(2,1)}, bf16[2,512,768]{2,1,0:T(8,128)(2,1)S(1)}, u32[]{:S(2)}) copy-start(bf16[2,512,768]{2,1,0:T(8,128)(2,1)S(1)} %multiply_convert_fusion.2) | copy-start | bytes 4718596
  637.0 5.1 copy-start.32
  637.0 75.4 %all-to-all-start.1 = ((bf16[4,2,256,768]{3,2,1,0:T(8,128)(2,1)}), bf16[4,2,256,768]{3,2,1,0:T(8,128)(2,1)}, u32[]{:S(2)}, u32[]{:S(2)}) async-start(bf16[4,2,256,768]{3,2,1,0:T(8,128)(2,1)} %bitcast.418), calls=%async_computation.1 | async-start | bytes 6291456 | tf_op jit(solution)/shard_map/all_to_all | solution.py:254
  642.6 74.8 %copy-start.16 = (bf16[2,512,768]{2,1,0:T(8,128)(2,1)S(1)}, bf16[2,512,768]{2,1,0:T(8,128)(2,1)}, u32[]{:S(2)}) copy-start(bf16[2,512,768]{2,1,0:T(8,128)(2,1)} %param.18) | copy-start | bytes 4718596
  844.9 74.4 %all-to-all-start.3 = ((bf16[4,2,256,768]{3,2,1,0:T(8,128)(2,1)}), bf16[4,2,256,768]{3,2,1,0:T(8,128)(2,1)}, u32[]{:S(2)}, u32[]{:S(2)}) async-start(bf16[4,2,256,768]{3,2,1,0:T(8,128)(2,1)} %bitcast.417), calls=%async_computation.3 | async-start | bytes 6291456 | tf_op jit(solution)/shard_map/all_to_all | solution.py:290
  849.5 1083.2 %reduce-scatter.5.cloned.1.call-start = ((), (), s32[]{:S(2)}) async-start(), calls=%async_computation.10 | async-start | bytes 9437184 | tf_op jit(solution)/shard_map/reduce_scatter | solution.py:327
  849.6 73.9 %copy-start.23 = (f32[2,512]{1,0:T(2,128)S(1)}, f32[2,512]{1,0:T(2,128)}, u32[]{:S(2)}) copy-start(f32[2,512]{1,0:T(2,128)} %copy-done.22) | copy-start | bytes 12292
  849.6 73.9 %copy-start.27 = (f32[768]{0:T(1024)S(1)}, f32[768]{0:T(1024)}, u32[]{:S(2)}) copy-start(f32[768]{0:T(1024)} %param.26) | copy-start | bytes 9220
  919.3 4.2 copy-start.2
  923.6 3.0 copy-start.35
  923.6 3.0 copy-start.12
  926.6 3.7 copy-start.36
  928.6 1.6 copy-start.8
  937.9 3.4 copy-start.20
  1882.6 55.7 %reduce-scatter.7.cloned.1.call-start = ((), (), s32[]{:S(2)}) async-start(), calls=%async_computation.11 | async-start | bytes 9437184 | tf_op jit(solution)/shard_map/reduce_scatter | solution.py:328
  1883.2 116.6 %reduce-scatter.11.cloned.1.call-start = ((), (), s32[]{:S(2)}) async-start(), calls=%async_computation.13 | async-start | bytes 10616832 | tf_op jit(solution)/shard_map/reduce_scatter | solution.py:369
  1905.8 171.8 %reduce-scatter.9.cloned.1.call-start = ((), (), s32[]{:S(2)}) async-start(), calls=%async_computation.12 | async-start | bytes 10616832 | tf_op jit(solution)/shard_map/reduce_scatter | solution.py:368
  1923.6 1.7 copy-start.6
  1923.6 1.7 copy-start.25
  1923.6 1.7 copy-start.29
  1923.6 352.7 %all-reduce.4.cloned.1.call-start = ((), (), s32[]{:S(2)}) async-start(), calls=%async_computation.14 | async-start | bytes 18874368 | tf_op jit(solution)/shard_map/psum | solution.py:354
  1925.3 4.6 copy-start.9
  1925.3 4.6 copy-start.17
  1943.2 1.4 copy-start.4
  1945.4 3.4 copy-start.10
  1945.4 3.4 copy-start.18
  1948.8 1.5 copy-start.7
  1948.8 2.4 copy-start.11
  1951.2 4.0 copy-start.33
  1951.2 43.3 %copy-start.31 = (f32[2,512]{1,0:T(2,128)S(1)}, f32[2,512]{1,0:T(2,128)}, u32[]{:S(2)}) copy-start(f32[2,512]{1,0:T(2,128)} %copy-done.30) | copy-start | bytes 12292
  2276.4 3.4 copy-start.15
  2279.8 2.5 copy-start.14
  2282.3 2.5 copy-start.13
Sparse Core Ops, SparseCore 0:
  14.4 14.8 all-gather.2
  31.3 13.2 all-gather.4
  1882.8 13.5 reduce-scatter.4
  1898.6 15.6 reduce-scatter.6
  1918.2 78.9 reduce-scatter.10
  2001.1 76.4 reduce-scatter.8
  2084.4 191.9 all-reduce.3
where the time goes:
time: 2310 us; the launch traced here: 2290 us
  other arithmetic  912 us (39%)
  waiting for transfers between devices  430 us (19%)
  matrix products  377 us (16%)
  local copies, waits for them, and re-layouts  359 us (16%)
  blocking collectives  189 us (8%)
    add x24, other arithmetic, bias_grid(): result = result + jnp.where(buckets == label, table_column[label], 0.0)  722 us
    another operation x12, local copies, waits for them, and re-layouts, fold_buckets(): jnp.stack([jnp.sum(jnp.where(buckets == label, grad_sum, 0.0)) for label...  249 us
    psum x1, waiting for transfers between devices, per_device(): lax.psum((grad_w_query, grad_w_key, grad_w_value, grad_w_output, grad_bia...  199 us
    reduce_sum x12, other arithmetic, fold_buckets(): jnp.sum(jnp.where(buckets == label, grad_sum, 0.0))  142 us
    reduce_scatter x1, waiting for transfers between devices, per_device(): lax.psum_scatter(grad_w_in, ('dp', 'ctx'), scatter_dimension=2, tiled=True)  77.8 us
    all_to_all x1, blocking collectives, per_device(): lax.all_to_all(outgoing, 'expert', split_axis=0, concat_axis=0, tiled=True)  75.9 us
    all_to_all x1, blocking collectives, per_device(): lax.all_to_all(grad_out, 'expert', split_axis=0, concat_axis=0, tiled=True)  73.6 us
    all_to_all x1, waiting for transfers between devices, per_device(): lax.all_to_all(from_rows(expert_out, owners, seq_count, capacity), 'exper...  69.8 us
  transfers between devices with their start and end apart: 9, of which 6 were waited for; matrix products, arithmetic and copies ran while one was open for 4% of the time, Pallas kernels for 0%

commit v1 on v0

v1 whole, which is shorter than its diff:
```python
import jax
import jax.numpy as jnp
import numpy as np
from jax import lax
from jax.experimental import pallas as pl
from jax.experimental.pallas import tpu as pltpu
from jax.sharding import PartitionSpec as P

DH = 64
QB = 256

bucket_edges = (1, 2, 3, 4, 5, 6, 7, 8, 12, 16, 23, 32, 46, 64, 91)
norm_eps = 1e-06
precise_result = lax.Precision.HIGHEST


def bucket_of(relative):
    distance = jnp.abs(relative)
    half_bucket = jnp.zeros(relative.shape, jnp.int32)
    for threshold in bucket_edges:
        half_bucket = half_bucket + (distance >= threshold).astype(jnp.int32)
    return half_bucket + 16 * (relative > 0).astype(jnp.int32)


def bucket_grid(row_start, row_count, col_count):
    row_pos = row_start + jnp.arange(row_count, dtype=jnp.int32)
    col_pos = jnp.arange(col_count, dtype=jnp.int32)
    return bucket_of(col_pos[None, :] - row_pos[:, None])


def bias_grid(buckets, table_column, bucket_count):
    result = jnp.zeros(buckets.shape, jnp.float32)
    for label in range(bucket_count):
        result = result + jnp.where(buckets == label, table_column[label], 0.0)
    return result


def fold_buckets(buckets, grad_sum, bucket_count):
    return jnp.stack(
        [jnp.sum(jnp.where(buckets == label, grad_sum, 0.0)) for label in range(bucket_count)]
    )


def head_slice(value_rows, head_index, head_size):
    return lax.dynamic_slice_in_dim(value_rows, head_index * head_size, head_size, 2)


def put_head(target, portion, head_index, head_size):
    return lax.dynamic_update_slice_in_dim(target, portion, head_index * head_size, 2)


def head_scores(q_head, k_head, buckets, bias_table, head_index):
    table_column = lax.dynamic_index_in_dim(bias_table, head_index, 1, keepdims=False)
    scores = jnp.einsum("sqd,skd->sqk", q_head, k_head, preferred_element_type=jnp.float32)
    return scores + bias_grid(buckets, table_column, bias_table.shape[0])[None]


def attend_rows(query_matrix, keys_whole, values_whole, buckets, bias_table, head_size):
    seq_count, row_count, feature_width = query_matrix.shape
    head_count = feature_width // head_size

    def one_head(head_index, running):
        attention_result, log_totals = running
        scores = head_scores(
            head_slice(query_matrix, head_index, head_size),
            head_slice(keys_whole, head_index, head_size),
            buckets,
            bias_table,
            head_index,
        )
        row_max = jnp.max(scores, axis=-1, keepdims=True)
        log_total = row_max + jnp.log(jnp.sum(jnp.exp(scores - row_max), axis=-1, keepdims=True))
        weights_low = jnp.exp(scores - log_total).astype(jnp.bfloat16)
        portion = jnp.einsum(
            "sqk,skd->sqd",
            weights_low,
            head_slice(values_whole, head_index, head_size),
            preferred_element_type=jnp.float32,
        )
        attention_result = put_head(attention_result, portion, head_index, head_size)
        log_totals = lax.dynamic_update_index_in_dim(log_totals, log_total[..., 0], head_index, 0)
        return (attention_result, log_totals)

    initial = (
        jnp.zeros((seq_count, row_count, feature_width), jnp.float32),
        jnp.zeros((head_count, seq_count, row_count), jnp.float32),
    )
    return lax.fori_loop(0, head_count, one_head, initial)


def attend_back_rows(
    query_matrix, keys_whole, values_whole, mixed_grad, log_totals, buckets, bias_table, head_size
):
    seq_count, row_count, feature_width = query_matrix.shape
    col_count = keys_whole.shape[1]
    head_count = feature_width // head_size
    bucket_count = bias_table.shape[0]

    def one_head(head_index, running):
        query_grad, deltas, diag_grad, key_part, value_part = running
        q_head = head_slice(query_matrix, head_index, head_size)
        k_head = head_slice(keys_whole, head_index, head_size)
        v_head = head_slice(values_whole, head_index, head_size)
        g_head = head_slice(mixed_grad, head_index, head_size)
        scores = head_scores(q_head, k_head, buckets, bias_table, head_index)
        weights = jnp.exp(scores - log_totals[head_index][..., None])
        weight_grad = jnp.einsum("sqd,skd->sqk", g_head, v_head, preferred_element_type=jnp.float32)
        delta_row = jnp.sum(weights * weight_grad, axis=-1)
        score_grad = (weights * (weight_grad - delta_row[..., None])).astype(jnp.bfloat16)
        query_grad = put_head(
            query_grad,
            jnp.einsum("sqk,skd->sqd", score_grad, k_head, preferred_element_type=jnp.float32),
            head_index,
            head_size,
        )
        deltas = lax.dynamic_update_index_in_dim(deltas, delta_row, head_index, 0)
        folded = fold_buckets(
            buckets, jnp.sum(score_grad.astype(jnp.float32), axis=0), bucket_count
        )
        diag_grad = lax.dynamic_update_index_in_dim(diag_grad, folded, head_index, 0)
        key_part = put_head(
            key_part,
            jnp.einsum("sqk,sqd->skd", score_grad, q_head, preferred_element_type=jnp.float32),
            head_index,
            head_size,
        )
        value_part = put_head(
            value_part,
            jnp.einsum(
                "sqk,sqd->skd",
                weights.astype(jnp.bfloat16),
                g_head,
                preferred_element_type=jnp.float32,
            ),
            head_index,
            head_size,
        )
        return (query_grad, deltas, diag_grad, key_part, value_part)

    key_shape = (seq_count, col_count, feature_width)
    initial = (
        jnp.zeros((seq_count, row_count, feature_width), jnp.float32),
        jnp.zeros((head_count, seq_count, row_count), jnp.float32),
        jnp.zeros((head_count, bucket_count), jnp.float32),
        jnp.zeros(key_shape, jnp.float32),
        jnp.zeros(key_shape, jnp.float32),
    )
    return lax.fori_loop(0, head_count, one_head, initial)


def bucket_np(relative):
    half_bucket = np.zeros(relative.shape, np.int32)
    for threshold in bucket_edges:
        half_bucket = half_bucket + (np.abs(relative) >= threshold)
    return half_bucket + 16 * (relative > 0)


def bias_lines(bias_table):
    lane = np.arange(4 * QB)
    both = np.stack([lane - 2 * QB, 2 * QB - lane])
    onehot = (bucket_np(both)[..., None] == np.arange(32)).astype(np.float32)
    return jnp.einsum("lcb,bh->hlc", jnp.asarray(onehot), bias_table, precision=lax.Precision.HIGHEST)

def fwd_kernel(lines_ref, q_ref, k_ref, v_ref, o_ref, band_ref):
    n = q_ref.shape[0] // QB
    lane = lax.broadcasted_iota(jnp.int32, (QB, 128), 1)
    for h in range(2):
        line = lines_ref[h, 0:1, :]
        spread = pltpu.roll(jnp.broadcast_to(line, (QB, 4 * QB)), 0, 1, stride=1, stride_axis=0)
        band_ref[h] = spread[:, QB:]
    for i in range(n):
        rows = slice(i * QB, (i + 1) * QB)
        outs = []
        for h in range(2):
            low_bias = lines_ref[h, 0:1, 0:1]
            high_bias = lines_ref[h, 0:1, 4 * QB - 1:]
            q = jnp.where((lane < 64) == (h == 0), q_ref[rows, :], 0)
            s = lax.dot_general(q, k_ref[...], (((1,), (1,)), ((), ())), preferred_element_type=jnp.float32)
            parts = []
            for j in range(n):
                d = j - i
                b = band_ref[h, :, (d + 1) * QB:(d + 2) * QB] if abs(d) <= 1 else (low_bias if d < 0 else high_bias)
                parts.append(s[:, j * QB:(j + 1) * QB] + b)
            s = jnp.concatenate(parts, axis=1)
            m = jnp.max(s, axis=1, keepdims=True)
            p = jnp.exp(s - m)
            l = jnp.sum(p, axis=1, keepdims=True)
            o = jnp.dot(p.astype(jnp.bfloat16), v_ref[...], preferred_element_type=jnp.float32)
            outs.append(o * (1.0 / l))
        o_ref[rows, :] = jnp.where(lane < 64, outs[0], outs[1]).astype(jnp.bfloat16)

def attend(q, k, v, lines):
    length, width = q.shape
    col = pl.BlockSpec((length, 128), lambda h: (0, h))
    return pl.pallas_call(
        fwd_kernel,
        grid=(width // 128,),
        in_specs=[pl.BlockSpec((2, 2, 4 * QB), lambda h: (h, 0, 0)), col, col, col],
        out_specs=col,
        out_shape=jax.ShapeDtypeStruct((length, width), jnp.bfloat16),
        scratch_shapes=[pltpu.VMEM((2, QB, 3 * QB), jnp.float32)],
        compiler_params=pltpu.CompilerParams(vmem_limit_bytes=48 << 20),
        name="attend",
    )(lines, q, k, v)

def bwd_kernel(lines_ref, q_ref, k_ref, v_ref, g_ref, dq_ref, dk_ref, dv_ref, diag_ref, far_ref, band_ref, acc_ref, far_acc, dk_acc, dv_acc):
    n = q_ref.shape[0] // QB
    lane = lax.broadcasted_iota(jnp.int32, (QB, 128), 1)
    for h in range(2):
        for t in range(3):
            start = 2 * QB - (t - 1) * QB - QB
            line = lines_ref[h, 1:2, start:start + 2 * QB]
            spread = pltpu.roll(jnp.broadcast_to(line, (QB, 2 * QB)), QB, 1, stride=1, stride_axis=0)
            band_ref[h, t * QB:(t + 1) * QB, :] = spread[:, :QB]
    acc_ref[...] = jnp.zeros_like(acc_ref)
    far_acc[...] = jnp.zeros_like(far_acc)
    for i in range(n):
        rows = slice(i * QB, (i + 1) * QB)
        grads = []
        for h in range(2):
            keep = (lane < 64) == (h == 0)
            low_bias = lines_ref[h, 0:1, 0:1]
            high_bias = lines_ref[h, 0:1, 4 * QB - 1:]
            q = jnp.where(keep, q_ref[rows, :], 0)
            g = jnp.where(keep, g_ref[rows, :], 0)
            s = lax.dot_general(k_ref[...], q, (((1,), (1,)), ((), ())), preferred_element_type=jnp.float32)
            parts = []
            for j in range(n):
                d = j - i
                b = band_ref[h, (d + 1) * QB:(d + 2) * QB, :] if abs(d) <= 1 else (low_bias if d < 0 else high_bias)
                parts.append(s[j * QB:(j + 1) * QB, :] + b)
            s = jnp.concatenate(parts, axis=0)
            m = jnp.max(s, axis=0, keepdims=True)
            p = jnp.exp(s - m)
            w = p * (1.0 / jnp.sum(p, axis=0, keepdims=True))
            dp = lax.dot_general(v_ref[...], g, (((1,), (1,)), ((), ())), preferred_element_type=jnp.float32)
            delta = jnp.sum(w * dp, axis=0, keepdims=True)
            ds = w * (dp - delta)
            for j in range(n):
                d = j - i
                tile = ds[j * QB:(j + 1) * QB, :]
                if abs(d) <= 1:
                    acc_ref[h, (d + 1) * QB:(d + 2) * QB, :] += tile
                else:
                    far_acc[h, 0 if d < 0 else 1] += jnp.sum(tile.reshape(QB // 8, 8, QB), axis=0)
            low = ds.astype(jnp.bfloat16)
            dv = jnp.dot(w.astype(jnp.bfloat16), g, preferred_element_type=jnp.float32)
            dk = jnp.dot(low, q, preferred_element_type=jnp.float32)
            if i == 0 and h == 0:
                dv_acc[...] = dv
                dk_acc[...] = dk
            else:
                dv_acc[...] += dv
                dk_acc[...] += dk
            grads.append(lax.dot_general(low, k_ref[...], (((0,), (0,)), ((), ())), preferred_element_type=jnp.float32))
        dq_ref[rows, :] = jnp.where(lane < 64, grads[0], grads[1]).astype(jnp.bfloat16)
    dk_ref[...] = dk_acc[...].astype(jnp.bfloat16)
    dv_ref[...] = dv_acc[...].astype(jnp.bfloat16)
    row = lax.broadcasted_iota(jnp.int32, (8, 2 * QB), 0)
    for h in range(2):
        for t in range(3):
            tile = acc_ref[h, t * QB:(t + 1) * QB, :]
            wide = jnp.concatenate([tile, jnp.zeros_like(tile)], axis=1)
            groups = sum(pltpu.roll(wide[8 * e:8 * e + 8], QB - 8 * e, 1) for e in range(QB // 8))
            turned = groups * (row == 0).astype(jnp.float32)
            for e in range(1, 8):
                turned = turned + pltpu.roll(jnp.where(row == e, groups, 0.0), 2 * QB - e, 1)
            diag_ref[h, t:t + 1, :] = jnp.sum(turned, axis=0, keepdims=True)
        far_ref[h, 0:1] = jnp.sum(far_acc[h, 0], axis=0, keepdims=True)
        far_ref[h, 1:2] = jnp.sum(far_acc[h, 1], axis=0, keepdims=True)

def attend_back(q, k, v, g, lines):
    length, width = q.shape
    heads = width // 64
    col = pl.BlockSpec((length, 128), lambda h: (0, h))
    out = jax.ShapeDtypeStruct((length, width), jnp.bfloat16)
    dq, dk, dv, diag, far = pl.pallas_call(
        bwd_kernel,
        grid=(width // 128,),
        in_specs=[pl.BlockSpec((2, 2, 4 * QB), lambda h: (h, 0, 0)), col, col, col, col],
        out_specs=[col, col, col, pl.BlockSpec((2, 3, 2 * QB), lambda h: (h, 0, 0)), pl.BlockSpec((2, 2, QB), lambda h: (h, 0, 0))],
        out_shape=[out, out, out, jax.ShapeDtypeStruct((heads, 3, 2 * QB), jnp.float32), jax.ShapeDtypeStruct((heads, 2, QB), jnp.float32)],
        scratch_shapes=[
            pltpu.VMEM((2, 3 * QB, QB), jnp.float32),
            pltpu.VMEM((2, 3 * QB, QB), jnp.float32),
            pltpu.VMEM((2, 2, 8, QB), jnp.float32),
            pltpu.VMEM((length, 128), jnp.float32),
            pltpu.VMEM((length, 128), jnp.float32),
        ],
        compiler_params=pltpu.CompilerParams(vmem_limit_bytes=48 << 20),
        name="attend_back",
    )(lines, q, k, v, g)
    r = (np.arange(3)[:, None] - 1) * QB - (np.arange(2 * QB)[None] - QB)
    onehot = (bucket_np(r)[..., None] == np.arange(32)).astype(np.float32)
    dbias = jnp.einsum("htx,txb->bh", diag, jnp.asarray(onehot), precision=lax.Precision.HIGHEST)
    far = jnp.sum(far, axis=2)
    dbias = dbias.at[15].add(far[:, 0]).at[31].add(far[:, 1])
    return dq, dk, dv, dbias


def expert_kernel(label_ref, x_ref, u_ref, router_ref, win_ref, wout_ref, rows_ref, back_ref, dw_ref, drouter_ref,
                  xt_ref, g_ref, gt_ref, prob_ref, out_acc, back_acc, hid_ref, pre_ref):
    step = pl.program_id(0)
    count = x_ref.shape[0]
    tile = min(512, count)
    lane = lax.broadcasted_iota(jnp.int32, (tile, 128), 1)
    own = lane == label_ref[0]
    spans = [slice(r * tile, (r + 1) * tile) for r in range(count // tile)]

    @pl.when(step == 0)
    def _():
        for rows in spans:
            logits = jnp.dot(x_ref[rows, :], router_ref[...], preferred_element_type=jnp.float32)
            logits = jnp.where(lane < 4, logits, -jnp.inf)
            raised = jnp.exp(logits - jnp.max(logits, axis=1, keepdims=True))
            prob = raised / jnp.sum(raised, axis=1, keepdims=True)
            prob_ref[rows, :] = prob
            gate = jnp.sum(jnp.where(own, prob, 0.0), axis=1, keepdims=True)
            grad = (gate * u_ref[rows, :].astype(jnp.float32)).astype(jnp.bfloat16)
            g_ref[rows, :] = grad
            gt_ref[:, rows] = grad.T
            xt_ref[:, rows] = x_ref[rows, :].T
        out_acc[...] = jnp.zeros_like(out_acc)
        back_acc[...] = jnp.zeros_like(back_acc)

    for rows in spans:
        pre = jnp.dot(x_ref[rows, :], win_ref[...], preferred_element_type=jnp.float32)
        square = pre * pre
        turn = jnp.tanh(0.7978845608028654 * pre * (1.0 + 0.044715 * square))
        half = 0.5 * (1.0 + turn)
        hidden = (pre * half).astype(jnp.bfloat16)
        slope = half + pre * (0.5 * (1.0 - turn * turn)) * (0.7978845608028654 + 0.1070322243 * square)
        hid_ref[rows, :] = hidden
        out_acc[rows, :] += jnp.dot(hidden, wout_ref[...], preferred_element_type=jnp.float32)
        hidden_grad = lax.dot_general(g_ref[rows, :], wout_ref[...], (((1,), (1,)), ((), ())), preferred_element_type=jnp.float32)
        pre_grad = (hidden_grad * slope).astype(jnp.bfloat16)
        pre_ref[rows, :] = pre_grad
        back_acc[rows, :] += lax.dot_general(pre_grad, win_ref[...], (((1,), (1,)), ((), ())), preferred_element_type=jnp.float32)
    dw_ref[0] = jnp.dot(xt_ref[...], pre_ref[...], preferred_element_type=jnp.float32).astype(dw_ref.dtype)
    dw_ref[1] = jnp.dot(gt_ref[...], hid_ref[...], preferred_element_type=jnp.float32).astype(dw_ref.dtype)

    @pl.when(step == pl.num_programs(0) - 1)
    def _():
        total = jnp.zeros(drouter_ref.shape, jnp.float32)
        for rows in spans:
            prob = prob_ref[rows, :]
            gate = jnp.sum(jnp.where(own, prob, 0.0), axis=1, keepdims=True)
            out = out_acc[rows, :].astype(jnp.bfloat16).astype(jnp.float32)
            rows_ref[rows, :] = (gate * out).astype(jnp.bfloat16)
            gate_grad = jnp.sum(u_ref[rows, :].astype(jnp.float32) * out, axis=1, keepdims=True)
            logit_grad = prob * (jnp.where(own, gate_grad, 0.0) - gate * gate_grad)
            high = logit_grad.astype(jnp.bfloat16)
            low = (logit_grad - high.astype(jnp.float32)).astype(jnp.bfloat16)
            back = back_acc[rows, :].astype(jnp.bfloat16).astype(jnp.float32)
            for part in (high, low):
                back += lax.dot_general(part, router_ref[...], (((1,), (1,)), ((), ())), preferred_element_type=jnp.float32)
                total += jnp.dot(xt_ref[:, rows], part, preferred_element_type=jnp.float32)
            back_ref[rows, :] = back.astype(jnp.bfloat16)
        drouter_ref[...] = total


def run_expert(label, rows_in, upstream_rows, router_weight, w_in, w_out):
    count, width = rows_in.shape
    inner = w_in.shape[1]
    chunk = 256
    once = pl.Buffered(1)
    whole = lambda f, lab: (0, 0)
    router_wide = jnp.pad(router_weight, ((0, 0), (0, 128 - router_weight.shape[1])))
    return pl.pallas_call(
        expert_kernel,
        grid_spec=pltpu.PrefetchScalarGridSpec(
            num_scalar_prefetch=1,
            grid=(inner // chunk,),
            in_specs=[
                pl.BlockSpec((count, width), whole, pipeline_mode=once),
                pl.BlockSpec((count, width), whole, pipeline_mode=once),
                pl.BlockSpec((width, 128), whole, pipeline_mode=once),
                pl.BlockSpec((width, chunk), lambda f, lab: (0, f)),
                pl.BlockSpec((chunk, width), lambda f, lab: (f, 0)),
            ],
            out_specs=[
                pl.BlockSpec((count, width), whole, pipeline_mode=once),
                pl.BlockSpec((count, width), whole, pipeline_mode=once),
                pl.BlockSpec((2, width, chunk), lambda f, lab: (0, 0, f)),
                pl.BlockSpec((width, 128), whole, pipeline_mode=once),
            ],
            scratch_shapes=[
                pltpu.VMEM((width, count), jnp.bfloat16),
                pltpu.VMEM((count, width), jnp.bfloat16),
                pltpu.VMEM((width, count), jnp.bfloat16),
                pltpu.VMEM((count, 128), jnp.float32),
                pltpu.VMEM((count, width), jnp.float32),
                pltpu.VMEM((count, width), jnp.float32),
                pltpu.VMEM((count, chunk), jnp.bfloat16),
                pltpu.VMEM((count, chunk), jnp.bfloat16),
            ],
        ),
        out_shape=[
            jax.ShapeDtypeStruct((count, width), jnp.bfloat16),
            jax.ShapeDtypeStruct((count, width), jnp.bfloat16),
            jax.ShapeDtypeStruct((2, width, inner), jnp.bfloat16),
            jax.ShapeDtypeStruct((width, 128), jnp.float32),
        ],
        compiler_params=pltpu.CompilerParams(vmem_limit_bytes=60 << 20),
        name="experts",
    )(label, rows_in, upstream_rows, router_wide, w_in, w_out)


def make_dispatch(routes, labels, capacity):
    hits = (routes[..., None] == labels).astype(jnp.int32)
    places = jnp.sum((jnp.cumsum(hits, axis=1) - 1) * hits, axis=-1)
    expert_match = routes[None, :, None, :] == labels[:, None, None, None]
    slot_match = places[:, None, :] == jnp.arange(capacity, dtype=jnp.int32)[None, :, None]
    return (expert_match & slot_match[None]).astype(jnp.bfloat16)


def exchange(pieces, axis, sign):
    size = lax.axis_size(axis)
    return [pieces[0]] + [
        lax.ppermute(pieces[turn], axis, [(at, (at + sign * turn) % size) for at in range(size)])
        for turn in range(1, size)
    ]


def trade(blocks):
    at = lax.axis_index("ctx")
    mine = lax.dynamic_index_in_dim(blocks, at, 0, keepdims=False)
    other = lax.dynamic_index_in_dim(blocks, 1 - at, 0, keepdims=False)
    arrived = lax.ppermute(other, "ctx", [(0, 1), (1, 0)])
    return jnp.stack([jnp.where(at == 0, mine, arrived), jnp.where(at == 0, arrived, mine)])


def norm_scale(value_rows):
    return lax.rsqrt(jnp.mean(value_rows * value_rows, axis=-1, keepdims=True) + norm_eps)


def norm_back(value_rows, scale, gain_vector, grad_rows):
    scaled = grad_rows * gain_vector
    shrink = jnp.mean(scaled * value_rows, axis=-1, keepdims=True) * scale * scale * scale
    return scale * scaled - value_rows * shrink, jnp.sum(grad_rows * value_rows * scale, axis=(0, 1))


def wide_dot(rows, weight):
    return jnp.einsum("sxd,de->sxe", rows, weight, preferred_element_type=jnp.float32)


def wide_dot_back(rows, weight):
    return jnp.einsum("sxe,de->sxd", rows, weight, preferred_element_type=jnp.float32)


def weight_dot(left, right):
    return jnp.einsum("sxd,sxe->de", left, right, preferred_element_type=jnp.float32)


def split_rows(flat):
    high = flat.astype(jnp.bfloat16)
    return high, (flat - high.astype(jnp.float32)).astype(jnp.bfloat16)


def sum_all(matrices, smalls):
    width = matrices[0].shape[1]
    flat = jnp.concatenate([jnp.ravel(small) for small in smalls])
    fill = -flat.shape[0] % (8 * width)
    flat = jnp.pad(flat, (0, fill)).reshape(-1, width)
    packed = jnp.concatenate([matrix.astype(jnp.bfloat16) for matrix in matrices] + list(split_rows(flat)))
    packed = lax.psum(packed, ("dp", "ctx", "expert")).astype(jnp.float32)
    outs, at = [], 0
    for matrix in matrices:
        outs.append(packed[at : at + matrix.shape[0]])
        at += matrix.shape[0]
    rows = flat.shape[0]
    flat = (packed[at : at + rows] + packed[at + rows : at + 2 * rows]).reshape(-1)
    at = 0
    for small in smalls:
        outs.append(flat[at : at + small.size].reshape(small.shape))
        at += small.size
    return outs


def per_device(
    tokens,
    cotangent,
    routes,
    norm1_gain,
    query_weight,
    key_weight,
    value_weight,
    output_weight,
    bias_table,
    norm2_gain,
    router_weight,
    w_in,
    w_out,
):
    seq_count, local_len, model_width = tokens.shape
    owners = lax.axis_size("expert")
    capacity = local_len // 2
    whole_seq = seq_count == 2 and lax.axis_size("ctx") == 2 and local_len % QB == 0
    if whole_seq:
        tokens, cotangent, routes = trade(tokens), trade(cotangent), trade(routes)
    label = lax.axis_index("expert")
    labels = (label + jnp.arange(owners, dtype=jnp.int32)) % owners
    dispatch = make_dispatch(routes, labels, capacity)

    def to_owners(rows):
        sent = jnp.einsum("escx,sxd->escd", dispatch, rows, preferred_element_type=jnp.float32)
        sent = sent.astype(jnp.bfloat16)
        return jnp.concatenate(exchange(list(sent), "expert", 1)).reshape(-1, model_width)

    def to_tokens(rows):
        pieces = list(rows.reshape(owners, seq_count, capacity, model_width))
        pieces = jnp.stack(exchange(pieces, "expert", -1))
        return jnp.einsum("escx,escd->sxd", dispatch, pieces, preferred_element_type=jnp.float32)

    upstream_rows = to_owners(cotangent)
    inputs = tokens.astype(jnp.float32)
    scale1 = norm_scale(inputs)
    attn_in = (inputs * scale1 * norm1_gain).astype(jnp.bfloat16)
    queries = wide_dot(attn_in, query_weight).astype(jnp.bfloat16)
    keys = wide_dot(attn_in, key_weight).astype(jnp.bfloat16)
    values = wide_dot(attn_in, value_weight).astype(jnp.bfloat16)
    if whole_seq:
        lines = bias_lines(bias_table)
        flat = (seq_count * local_len, model_width)
        qkv = [rows.reshape(flat) for rows in (queries, keys, values)]
        attended = attend(*qkv, lines).reshape(tokens.shape)
    else:
        first_pos = lax.axis_index("ctx") * local_len
        keys = lax.all_gather(keys, "ctx", axis=1, tiled=True)
        values = lax.all_gather(values, "ctx", axis=1, tiled=True)
        buckets = bucket_grid(first_pos, local_len, keys.shape[1])
        attended, log_totals = attend_rows(queries, keys, values, buckets, bias_table, DH)
        attended = attended.astype(jnp.bfloat16)
    residual1 = inputs + wide_dot(attended, output_weight)
    scale2 = norm_scale(residual1)
    router_in = (residual1 * scale2 * norm2_gain).astype(jnp.bfloat16)
    rows_in = to_owners(router_in)
    rows_out, rows_back, grad_experts, grad_router = run_expert(
        label.astype(jnp.int32).reshape(1), rows_in, upstream_rows, router_weight, w_in[0], w_out[0]
    )
    grad_router = grad_router[:, : router_weight.shape[1]]
    router_in_grad = to_tokens(rows_back)
    block_out = (residual1 + to_tokens(rows_out)).astype(jnp.bfloat16)
    grad_experts = lax.psum_scatter(grad_experts, ("dp", "ctx"), scatter_dimension=2, tiled=True)
    norm2_back, grad_norm2 = norm_back(residual1, scale2, norm2_gain, router_in_grad)
    residual_grad = cotangent.astype(jnp.float32) + norm2_back
    attn_grad = residual_grad.astype(jnp.bfloat16)
    grad_w_output = weight_dot(attended, attn_grad)
    mixed_grad = wide_dot_back(attn_grad, output_weight).astype(jnp.bfloat16)
    grad_w_output, grad_norm2, grad_router = sum_all([grad_w_output], [grad_norm2, grad_router])
    if whole_seq:
        *grads, grad_bias = attend_back(*qkv, mixed_grad.reshape(flat), lines)
        query_low, key_low, value_low = (rows.reshape(tokens.shape) for rows in grads)
    else:
        query_grad, _, diag_grad, key_part, value_part = attend_back_rows(
            queries, keys, values, mixed_grad, log_totals, buckets, bias_table, DH
        )
        grad_bias = diag_grad.T
        query_low = query_grad.astype(jnp.bfloat16)
        key_low = lax.psum_scatter(key_part, "ctx", scatter_dimension=1, tiled=True).astype(jnp.bfloat16)
        value_low = lax.psum_scatter(value_part, "ctx", scatter_dimension=1, tiled=True).astype(jnp.bfloat16)
    norm_in_grad = wide_dot_back(query_low, query_weight)
    norm_in_grad = norm_in_grad + wide_dot_back(key_low, key_weight)
    norm_in_grad = norm_in_grad + wide_dot_back(value_low, value_weight)
    norm1_back, grad_norm1 = norm_back(inputs, scale1, norm1_gain, norm_in_grad)
    d_tokens = residual_grad + norm1_back
    grad_w_query, grad_w_key, grad_w_value, grad_bias, grad_norm1 = sum_all(
        [weight_dot(attn_in, rows) for rows in (query_low, key_low, value_low)], [grad_bias, grad_norm1]
    )
    if whole_seq:
        block_out, d_tokens = trade(block_out), trade(d_tokens)
    grad_experts = grad_experts.astype(jnp.float32)
    return (
        block_out,
        d_tokens,
        grad_norm1,
        grad_w_query,
        grad_w_key,
        grad_w_value,
        grad_w_output,
        grad_bias,
        grad_norm2,
        grad_router,
        grad_experts[0][None],
        grad_experts[1].T[None],
    )


def solution(mesh):
    rows = P(("dp", "expert"), "ctx", None)
    in_specs = (rows, rows, P(("dp", "expert"), "ctx")) + (P(),) * 8 + (P("expert", None, None),) * 2
    out_specs = (rows, rows) + (P(),) * 8 + (P("expert", None, ("dp", "ctx")), P("expert", ("dp", "ctx"), None))
    return jax.shard_map(per_device, mesh=mesh, in_specs=in_specs, out_specs=out_specs, check_vma=False)
```

time: 2310 us -> 660 us (0.29)
  other arithmetic: 912 us -> 27.7 us
  matrix products: 377 us -> 45.3 us
  local copies, waits for them, and re-layouts: 359 us -> 69.1 us
  blocking collectives: 189 us -> 0 us
  Pallas kernels: 0 us -> 171 us
  waiting for transfers between devices: 430 us -> 276 us
  starting transfers between devices: 10.1 us -> 47.3 us
    add x27 -> x6, other arithmetic: 730 us -> 6.3 us  [the longest x1 4.59 us: per_device(): d_tokens = residual_grad + norm1_back]
    dot_general x108 -> x18, matrix products: 376 us -> 45.3 us  [the longest x4 12.6 us: weight_dot(): jnp.einsum('sxd,sxe->de', left, right, preferred_element_type=jnp.float32)]
    another operation x17 -> x4, local copies, waits for them, and re-layouts: 259 us -> 8.22 us  [the longest x1 5.1 us: to_tokens(): pieces = list(rows.reshape(owners, seq_count, capacity, model_width))]
    ppermute x0 -> x17, waiting for transfers between devices: none -> 201 us  [the longest x12 199 us: exchange(): lax.ppermute(pieces[turn], axis, [(at, (at + sign * turn) % size) for at...]
    reduce_sum x39 -> x3, other arithmetic: 172 us -> 0.62 us  [the longest x1 0.38 us: norm_scale(): jnp.mean(value_rows * value_rows, axis=-1, keepdims=True) + norm_eps]
    pallas_call x0 -> x3, Pallas kernels: none -> 171 us  [the longest x1 83.4 us: run_expert(): pl.pallas_call(expert_kernel, grid_spec=pltpu.PrefetchScalarGridSpec(num_...]
    all_to_all x2 -> x0, blocking collectives: 149 us -> none  [the longest x1 75.9 us: per_device(): lax.all_to_all(outgoing, 'expert', split_axis=0, concat_axis=0, tiled=True)]
    all_to_all x2 -> x0, waiting for transfers between devices: 139 us -> none  [the longest x1 69.8 us: per_device(): lax.all_to_all(from_rows(expert_out, owners, seq_count, capacity), 'exper...]
  transfers between devices with their start and end apart: 9 -> 19, of which waited for: 6 -> 8; matrix products, arithmetic and copies ran while one was open for 4% -> 13% of each run, Pallas kernels for 0% -> 4%
where the time goes in v1:
time: 660 us; the launch traced here: 653 us
  waiting for transfers between devices  276 us (42%)
  Pallas kernels  171 us (26%)
  local copies, waits for them, and re-layouts  69.1 us (10%)
  starting transfers between devices  47.3 us (7%)
  matrix products  45.3 us (7%)
  other arithmetic  27.7 us (4%)
  between operations  16.8 us (3%)
    ppermute x12, waiting for transfers between devices, exchange(): lax.ppermute(pieces[turn], axis, [(at, (at + sign * turn) % size) for at...  199 us
    pallas_call x1, Pallas kernels, run_expert(): pl.pallas_call(expert_kernel, grid_spec=pltpu.PrefetchScalarGridSpec(num_...  83.4 us
    psum x1, waiting for transfers between devices, sum_all(): packed = lax.psum(packed, ('dp', 'ctx', 'expert')).astype(jnp.float32)  74.8 us
    pallas_call x1, Pallas kernels, attend_back(): pl.pallas_call(bwd_kernel, grid=(width // 128,), in_specs=[pl.BlockSpec((...  60 us
    ppermute x12, starting transfers between devices, exchange(): lax.ppermute(pieces[turn], axis, [(at, (at + sign * turn) % size) for at...  46.1 us
    unnamed x106, local copies, waits for them, and re-layouts  43.2 us
    pallas_call x1, Pallas kernels, attend(): pl.pallas_call(fwd_kernel, grid=(width // 128,), in_specs=[pl.BlockSpec((...  27.2 us
  transfers between devices with their start and end apart: 19, of which 8 were waited for; matrix products, arithmetic and copies ran while one was open for 13% of the time, Pallas kernels for 4%

profile of v1, /device:TPU:0, one launch (start us, length us, event | category | flops | bytes accessed | tf_op | source)
XLA Modules:
  0.0 653.1 jit_solution(1660154529661262590)
XLA Ops:
  9.4 2.1 dynamic-slice_bitcast_fusion.2
  11.6 2.1 dynamic-slice_bitcast_fusion.3
  14.6 2.4 reduce-window.6
  21.5 2.6 convolution_convert_fusion.1
  25.5 1.8 fusion.71
  27.4 3.0 convert_bitcast_fusion
  31.8 2.6 collective-permute-start.6
  34.4 2.2 collective-permute-start.8
  37.6 27.2 %attend.1 = bf16[1024,768]{1,0:T(8,128)(2,1)S(1)} custom-call(f32[12,2,1024]{2,1,0:T(2,128)S(1)} %bitcast.235, bf16[1024,768]{1,0:T(8,128)(2,1)S(1)} %bitcast.229, bf16[1024,768]{1,0:T(8,128)(2,1)S(1)} %bitcast.227, bf16[1024,768]{1,0:T(8,128)(2,1)} %bitcast.245), custom_call_target="tpu_custom_call" | custom-call | tf_op jit(solution)/shard_map/attend/pallas_call | solution.py:195
  66.4 3.1 convert_bitcast_fusion.1
  72.6 2.2 collective-permute-start.4
  74.8 14.7 %collective-permute-start.3 = (bf16[2,256,768]{2,1,0:T(8,128)(2,1)}, bf16[2,256,768]{2,1,0:T(8,128)(2,1)}, u32[]{:S(2)}, u32[]{:S(2)}) collective-permute-start(bf16[2,256,768]{2,1,0:T(8,128)(2,1)} %get-tuple-element.118), channel_id=1, source_target_pairs={{0,2},{1,3},{2,0},{3,1},{4,6},{5,7},{6,4},{7,5},{8,10},{9,11},{10,... | collective-permute-start | bytes 2359304 | tf_op jit(solution)/shard_map/ppermute | solution.py:420
  90.5 32.0 %collective-permute-done.7 = bf16[2,256,768]{2,1,0:T(8,128)(2,1)} collective-permute-done((bf16[2,256,768]{2,1,0:T(8,128)(2,1)}, bf16[2,256,768]{2,1,0:T(8,128)(2,1)}, u32[]{:S(2)}, u32[]{:S(2)}) %collective-permute-start.7) | collective-permute-done | bytes 786464 | tf_op jit(solution)/shard_map/ppermute | solution.py:420
  122.5 3.2 pad_maximum_fusion.1
  125.7 47.1 %collective-permute-done.3 = bf16[2,256,768]{2,1,0:T(8,128)(2,1)} collective-permute-done((bf16[2,256,768]{2,1,0:T(8,128)(2,1)}, bf16[2,256,768]{2,1,0:T(8,128)(2,1)}, u32[]{:S(2)}, u32[]{:S(2)}) %collective-permute-start.3) | collective-permute-done | bytes 786464 | tf_op jit(solution)/shard_map/ppermute | solution.py:420
  172.7 3.1 pad_maximum_fusion
  175.8 83.4 %experts.1 = (bf16[2048,768]{1,0:T(8,128)(2,1)}, bf16[2048,768]{1,0:T(8,128)(2,1)}, bf16[2,768,3072]{2,1,0:T(8,128)(2,1)}, f32[768,128]{1,0:T(8,128)}) custom-call(s32[1]{0:T(128)} %bitcast.21.label_ref, bf16[2048,768]{1,0:T(8,128)(2,1)} %bitcast.244, bf16[2048,768]{1,0:T(8,128)(2,1)} %bitcast.243, bf16[768,128]{1,0:T(8,128)(2,1)} %pad.16.router_ref, ...), custom_call_target="tpu_custom_call" | custom-call | tf_op jit(solution)/shard_map/experts/pallas_call | solution.py:369
  259.2 5.1 fusion.96
  264.3 2.2 collective-permute-start.14
  266.5 1.6 collective-permute-start.13
  268.3 18.6 %collective-permute-done.15 = bf16[2,256,768]{2,1,0:T(8,128)(2,1)} collective-permute-done((bf16[2,256,768]{2,1,0:T(8,128)(2,1)}, bf16[2,256,768]{2,1,0:T(8,128)(2,1)}, u32[]{:S(2)}, u32[]{:S(2)}) %collective-permute-start.15) | collective-permute-done | bytes 786464 | tf_op jit(solution)/shard_map/ppermute | solution.py:420
  287.0 32.7 %collective-permute-done.14 = bf16[2,256,768]{2,1,0:T(8,128)(2,1)} collective-permute-done((bf16[2,256,768]{2,1,0:T(8,128)(2,1)}, bf16[2,256,768]{2,1,0:T(8,128)(2,1)}, u32[]{:S(2)}, u32[]{:S(2)}) %collective-permute-start.14) | collective-permute-done | bytes 786464 | tf_op jit(solution)/shard_map/ppermute | solution.py:420
  319.7 4.5 fusion.31
  325.6 2.5 bitcast_convert_fusion
  328.2 2.6 convolution_convert_fusion
  330.8 60.0 %attend_back.1 = (bf16[1024,768]{1,0:T(8,128)(2,1)S(1)}, bf16[1024,768]{1,0:T(8,128)(2,1)S(1)}, bf16[1024,768]{1,0:T(8,128)(2,1)S(1)}, f32[12,3,512]{2,1,0:T(4,128)S(1)}, f32[12,2,256]{2,1,0:T(2,128)S(1)}) custom-call(f32[12,2,1024]{2,1,0:T(2,128)S(1)} %bitcast.236, bf16[1024,768]{1,0:T(8,128)(2,1)} %bitcast.230, bf16[1024,768]{1,0:T(8,128)(2,1)} %bitcast.228, ...), custom_call_target="tpu_custom_call" | custom-call | tf_op jit(solution)/shard_map/attend_back/pallas_call | solution.py:277
  390.8 3.2 fusion.66
  394.0 2.6 fusion.56
  397.6 3.3 fusion.63
  401.0 3.4 fusion.15
  404.5 4.7 fusion.57
  409.2 2.7 fusion.58
  414.3 23.9 %copy.105 = bf16[2,768,3072]{1,0,2:T(2,128)(2,1)} copy(bf16[2,768,3072]{2,1,0:T(8,128)(2,1)} %get-tuple-element.53) | data formatting | bytes 18874368
  438.2 9.2 %copy.113 = bf16[384,8,2,768]{3,1,2,0:T(8,128)(2,1)} copy(bf16[384,8,2,768]{3,2,1,0:T(2,128)(2,1)} %bitcast.242) | data formatting | bytes 18874368
  447.5 15.4 %collective-permute-start.9 = (bf16[2,256,768]{2,1,0:T(8,128)(2,1)}, bf16[2,256,768]{2,1,0:T(8,128)(2,1)S(1)}, u32[]{:S(2)}, u32[]{:S(2)}) collective-permute-start(bf16[2,256,768]{2,1,0:T(8,128)(2,1)} %bitcast.254), channel_id=1, source_target_pairs={{0,3},{1,0},{2,1},{3,2},{4,7},{5,4},{6,5},{7,6},{8,11},{9,8},{10,9... | collective-permute-start | bytes 2359304 | tf_op jit(solution)/shard_map/ppermute | solution.py:420
  462.9 2.5 collective-permute-start.10
  465.4 4.6 fusion.13
  470.3 16.1 %collective-permute-done.9 = bf16[2,256,768]{2,1,0:T(8,128)(2,1)S(1)} collective-permute-done((bf16[2,256,768]{2,1,0:T(8,128)(2,1)}, bf16[2,256,768]{2,1,0:T(8,128)(2,1)S(1)}, u32[]{:S(2)}, u32[]{:S(2)}) %collective-permute-start.9) | collective-permute-done | bytes 786464 | tf_op jit(solution)/shard_map/ppermute | solution.py:420
  486.3 52.7 %collective-permute-done.10 = bf16[2,256,768]{2,1,0:T(8,128)(2,1)S(1)} collective-permute-done((bf16[2,256,768]{2,1,0:T(8,128)(2,1)S(1)}, bf16[2,256,768]{2,1,0:T(8,128)(2,1)S(1)}, u32[]{:S(2)}, u32[]{:S(2)}) %collective-permute-start.10) | collective-permute-done | bytes 786464 | tf_op jit(solution)/shard_map/ppermute | solution.py:420
  539.1 2.2 fusion.32
  541.4 2.3 collective-permute-done.12
  545.3 1.9 pad_maximum_fusion.2
  547.1 74.8 %all-reduce.6.cloned.1.call-done = (bf16[2320,768]{1,0:T(8,128)(2,1)}, bf16[784,768]{1,0:T(8,128)(2,1)}) async-done(((bf16[2320,768]{1,0:T(8,128)(2,1)}, bf16[784,768]{1,0:T(8,128)(2,1)}), (bf16[2320,768]{1,0:T(8,128)(2,1)}, bf16[784,768]{1,0:T(8,128)(2,1)})) %all-reduce.6.cloned.1.call-update) | async-done | bytes 4767760 | tf_op jit(solution)/shard_map/psum | solution.py:466
  622.0 2.9 slice.141
  624.9 1.6 convert_element_type.119
  632.5 5.1 fusion.95
  637.6 2.9 reshape.298
  640.5 2.0 copy.106
  (189 shorter events, 31.7 us)
Async XLA Ops:
  8.0 13.4 %copy-start = (bf16[768,768]{1,0:T(8,128)(2,1)S(1)}, bf16[768,768]{1,0:T(8,128)(2,1)}, u32[]{:S(2)}) copy-start(bf16[768,768]{1,0:T(8,128)(2,1)} %param.25) | copy-start | bytes 3538948
  8.0 6.0 copy-start.36
  8.0 10.2 %copy-start.27 = (bf16[2,512,768]{2,1,0:T(8,128)(2,1)S(1)}, bf16[2,512,768]{2,1,0:T(8,128)(2,1)}, u32[]{:S(2)}) copy-start(bf16[2,512,768]{2,1,0:T(8,128)(2,1)} %param.19) | copy-start | bytes 4718596
  8.1 6.0 copy-start.39
  8.1 613.9 %all-reduce.6.cloned.1.call-start = ((), (), s32[]{:S(2)}) async-start(), calls=%async_computation.2 | async-start | bytes 9535488 | tf_op jit(solution)/shard_map/psum | solution.py:466
  9.0 5.5 collective-permute-start.1
  11.5 14.0 %collective-permute-start.5 = (bf16[512,768]{1,0:T(8,128)(2,1)}, bf16[512,768]{1,0:T(8,128)(2,1)}, u32[]{:S(2)}, u32[]{:S(2)}) collective-permute-start(bf16[512,768]{1,0:T(8,128)(2,1)} %dynamic-slice_bitcast_fusion.2), channel_id=1, source_target_pairs={{0,4},{4,0},{1,5},{5,1},{2,6},{6,2},{3,7},{7,3},{8,12},{12,8},{9,1... | collective-permute-start | bytes 2359304 | tf_op jit(solution)/shard_map/ppermute | solution.py:429
  13.6 4.6 collective-permute-start
  17.9 301.7 %copy-start.42 = (pred[4,2,512]{2,0,1:T(4,128)(4,1)}, pred[4,2,512]{2,0,1:T(4,128)(4,1)S(1)}, u32[]{:S(2)}) copy-start(pred[4,2,512]{2,0,1:T(4,128)(4,1)S(1)} %broadcast_compare_fusion) | copy-start | bytes 12292
  18.1 301.5 %copy-start.34 = (pred[2,256,512]{1,2,0:T(8,128)(4,1)}, pred[2,256,512]{1,2,0:T(8,128)(4,1)S(1)}, u32[]{:S(2)}) copy-start(pred[2,256,512]{1,2,0:T(8,128)(4,1)S(1)} %iota_compare_fusion) | copy-start | bytes 786436
  19.6 45.3 %copy-start.8 = (bf16[1,512,768]{2,1,0:T(8,128)(2,1)}, bf16[1,512,768]{2,1,0:T(8,128)(2,1)S(1)}, u32[]{:S(2)}) copy-start(bf16[1,512,768]{2,1,0:T(8,128)(2,1)S(1)} %get-tuple-element.123) | copy-start | bytes 2359300
  19.6 45.3 %copy-start.12 = (bf16[1,512,768]{2,1,0:T(8,128)(2,1)}, bf16[1,512,768]{2,1,0:T(8,128)(2,1)S(1)}, u32[]{:S(2)}) copy-start(bf16[1,512,768]{2,1,0:T(8,128)(2,1)S(1)} %get-tuple-element.124) | copy-start | bytes 2359300
  21.5 16.2 %copy-start.2 = (bf16[2,512,768]{2,1,0:T(8,128)(2,1)}, bf16[2,512,768]{2,1,0:T(8,128)(2,1)S(1)}, u32[]{:S(2)}) copy-start(bf16[2,512,768]{2,1,0:T(8,128)(2,1)S(1)} %convolution_convert_fusion.2) | copy-start | bytes 4718596
  25.5 12.1 %copy-start.3 = (bf16[2,512,768]{2,1,0:T(8,128)(2,1)}, bf16[2,512,768]{2,1,0:T(8,128)(2,1)S(1)}, u32[]{:S(2)}) copy-start(bf16[2,512,768]{2,1,0:T(8,128)(2,1)S(1)} %convolution_convert_fusion.3) | copy-start | bytes 4718596
  31.8 43.0 %collective-permute-start.6 = (bf16[2,256,768]{2,1,0:T(8,128)(2,1)S(1)}, bf16[2,256,768]{2,1,0:T(8,128)(2,1)}, u32[]{:S(2)}, u32[]{:S(2)}) collective-permute-start(bf16[2,256,768]{2,1,0:T(8,128)(2,1)S(1)} %get-tuple-element.112), channel_id=1, source_target_pairs={{0,1},{1,2},{2,3},{3,0},{4,5},{5,6},{6,7},{7,4},{8,9},{9,10},{10,1... | collective-permute-start | bytes 2359304 | tf_op jit(solution)/shard_map/ppermute | solution.py:420
  34.4 56.1 %collective-permute-start.8 = (bf16[2,256,768]{2,1,0:T(8,128)(2,1)}, bf16[2,256,768]{2,1,0:T(8,128)(2,1)}, u32[]{:S(2)}, u32[]{:S(2)}) collective-permute-start(bf16[2,256,768]{2,1,0:T(8,128)(2,1)} %get-tuple-element.113), channel_id=1, source_target_pairs={{0,3},{1,0},{2,1},{3,2},{4,7},{5,4},{6,5},{7,6},{8,11},{9,8},{10,9... | collective-permute-start | bytes 2359304 | tf_op jit(solution)/shard_map/ppermute | solution.py:420
  36.6 85.9 %collective-permute-start.7 = (bf16[2,256,768]{2,1,0:T(8,128)(2,1)}, bf16[2,256,768]{2,1,0:T(8,128)(2,1)}, u32[]{:S(2)}, u32[]{:S(2)}) collective-permute-start(bf16[2,256,768]{2,1,0:T(8,128)(2,1)} %get-tuple-element.114), channel_id=1, source_target_pairs={{0,2},{1,3},{2,0},{3,1},{4,6},{5,7},{6,4},{7,5},{8,10},{9,11},{10,... | collective-permute-start | bytes 2359304 | tf_op jit(solution)/shard_map/ppermute | solution.py:420
  37.6 27.2 %copy-start.44 = (bf16[768,768]{1,0:T(8,128)(2,1)S(1)}, bf16[768,768]{1,0:T(8,128)(2,1)}, u32[]{:S(2)}) copy-start(bf16[768,768]{1,0:T(8,128)(2,1)} %param.26) | copy-start | bytes 3538948
  69.6 20.0 %copy-start.40 = (bf16[768,4]{0,1:T(4,128)(2,1)S(1)}, bf16[768,4]{0,1:T(4,128)(2,1)}, u32[]{:S(2)}) copy-start(bf16[768,4]{0,1:T(4,128)(2,1)} %param.29) | copy-start | bytes 18436
  71.0 54.6 %collective-permute-start.2 = (bf16[2,256,768]{2,1,0:T(8,128)(2,1)}, bf16[2,256,768]{2,1,0:T(8,128)(2,1)}, u32[]{:S(2)}, u32[]{:S(2)}) collective-permute-start(bf16[2,256,768]{2,1,0:T(8,128)(2,1)} %get-tuple-element.116), channel_id=1, source_target_pairs={{0,1},{1,2},{2,3},{3,0},{4,5},{5,6},{6,7},{7,4},{8,9},{9,10},{10,1... | collective-permute-start | bytes 2359304 | tf_op jit(solution)/shard_map/ppermute | solution.py:420
  72.6 53.1 %collective-permute-start.4 = (bf16[2,256,768]{2,1,0:T(8,128)(2,1)}, bf16[2,256,768]{2,1,0:T(8,128)(2,1)}, u32[]{:S(2)}, u32[]{:S(2)}) collective-permute-start(bf16[2,256,768]{2,1,0:T(8,128)(2,1)} %get-tuple-element.117), channel_id=1, source_target_pairs={{0,3},{1,0},{2,1},{3,2},{4,7},{5,4},{6,5},{7,6},{8,11},{9,8},{10,9... | collective-permute-start | bytes 2359304 | tf_op jit(solution)/shard_map/ppermute | solution.py:420
  74.8 97.9 %collective-permute-start.3 = (bf16[2,256,768]{2,1,0:T(8,128)(2,1)}, bf16[2,256,768]{2,1,0:T(8,128)(2,1)}, u32[]{:S(2)}, u32[]{:S(2)}) collective-permute-start(bf16[2,256,768]{2,1,0:T(8,128)(2,1)} %get-tuple-element.118), channel_id=1, source_target_pairs={{0,2},{1,3},{2,0},{3,1},{4,6},{5,7},{6,4},{7,5},{8,10},{9,11},{10,... | collective-permute-start | bytes 2359304 | tf_op jit(solution)/shard_map/ppermute | solution.py:420
  259.2 8.9 %copy-start.33 = (f32[768,128]{1,0:T(8,128)S(1)}, f32[768,128]{1,0:T(8,128)}, u32[]{:S(2)}) copy-start(f32[768,128]{1,0:T(8,128)} %get-tuple-element.52) | copy-start | bytes 1179652
  264.3 22.7 %collective-permute-start.15 = (bf16[2,256,768]{2,1,0:T(8,128)(2,1)}, bf16[2,256,768]{2,1,0:T(8,128)(2,1)}, u32[]{:S(2)}, u32[]{:S(2)}) collective-permute-start(bf16[2,256,768]{2,1,0:T(8,128)(2,1)} %bitcast.64), channel_id=1, source_target_pairs={{0,1},{1,2},{2,3},{3,0},{4,5},{5,6},{6,7},{7,4},{8,9},{9,10},{10,1... | collective-permute-start | bytes 2359304 | tf_op jit(solution)/shard_map/ppermute | solution.py:420
  264.3 55.4 %collective-permute-start.14 = (bf16[2,256,768]{2,1,0:T(8,128)(2,1)}, bf16[2,256,768]{2,1,0:T(8,128)(2,1)}, u32[]{:S(2)}, u32[]{:S(2)}) collective-permute-start(bf16[2,256,768]{2,1,0:T(8,128)(2,1)} %bitcast.62), channel_id=1, source_target_pairs={{0,2},{1,3},{2,0},{3,1},{4,6},{5,7},{6,4},{7,5},{8,10},{9,11},{10,... | collective-permute-start | bytes 2359304 | tf_op jit(solution)/shard_map/ppermute | solution.py:420
  266.5 53.2 %collective-permute-start.13 = (bf16[2,256,768]{2,1,0:T(8,128)(2,1)S(1)}, bf16[2,256,768]{2,1,0:T(8,128)(2,1)}, u32[]{:S(2)}, u32[]{:S(2)}) collective-permute-start(bf16[2,256,768]{2,1,0:T(8,128)(2,1)S(1)} %bitcast.256), channel_id=1, source_target_pairs={{0,3},{1,0},{2,1},{3,2},{4,7},{5,4},{6,5},{7,6},{8,11},{9,8},{10,9... | collective-permute-start | bytes 2359304 | tf_op jit(solution)/shard_map/ppermute | solution.py:420
  319.7 4.5 copy-start.20
  319.7 4.5 copy-start.22
  319.7 4.5 copy-start.24
  330.8 60.1 %copy-start.47 = (bf16[768,768]{1,0:T(8,128)(2,1)S(1)}, bf16[768,768]{1,0:T(8,128)(2,1)}, u32[]{:S(2)}) copy-start(bf16[768,768]{1,0:T(8,128)(2,1)} %param.23) | copy-start | bytes 3538948
  397.6 3.3 copy-start.10
  397.6 3.3 copy-start.14
  404.4 4.7 copy-start.11
  404.4 4.7 copy-start.15
  409.2 3.9 copy-start.29
  414.2 223.3 %reduce-scatter.4.cloned.1.call-start = ((), (), s32[]{:S(2)}) async-start(), calls=%async_computation.1 | async-start | bytes 10616832
  447.4 15.5 %copy-start.32 = (bf16[512,768]{1,0:T(8,128)(2,1)S(1)}, bf16[512,768]{1,0:T(8,128)(2,1)}, u32[]{:S(2)}) copy-start(bf16[512,768]{1,0:T(8,128)(2,1)} %get-tuple-element.134) | copy-start | bytes 2359300
  447.5 17.9 %copy-start.31 = (bf16[512,768]{1,0:T(8,128)(2,1)S(1)}, bf16[512,768]{1,0:T(8,128)(2,1)}, u32[]{:S(2)}) copy-start(bf16[512,768]{1,0:T(8,128)(2,1)} %get-tuple-element.135) | copy-start | bytes 2359300
  447.5 18.0 %copy-start.16 = (bf16[1,512,768]{2,1,0:T(8,128)(2,1)S(1)}, bf16[1,512,768]{2,1,0:T(8,128)(2,1)}, u32[]{:S(2)}) copy-start(bf16[1,512,768]{2,1,0:T(8,128)(2,1)} %copy-done.12) | copy-start | bytes 2359300
  447.5 38.9 %collective-permute-start.9 = (bf16[2,256,768]{2,1,0:T(8,128)(2,1)}, bf16[2,256,768]{2,1,0:T(8,128)(2,1)S(1)}, u32[]{:S(2)}, u32[]{:S(2)}) collective-permute-start(bf16[2,256,768]{2,1,0:T(8,128)(2,1)} %bitcast.254), channel_id=1, source_target_pairs={{0,3},{1,0},{2,1},{3,2},{4,7},{5,4},{6,5},{7,6},{8,11},{9,8},{10,9... | collective-permute-start | bytes 2359304 | tf_op jit(solution)/shard_map/ppermute | solution.py:420
  462.9 76.1 %collective-permute-start.10 = (bf16[2,256,768]{2,1,0:T(8,128)(2,1)S(1)}, bf16[2,256,768]{2,1,0:T(8,128)(2,1)S(1)}, u32[]{:S(2)}, u32[]{:S(2)}) collective-permute-start(bf16[2,256,768]{2,1,0:T(8,128)(2,1)S(1)} %bitcast.253), channel_id=1, source_target_pairs={{0,2},{1,3},{2,0},{3,1},{4,6},{5,7},{6,4},{7,5},{8,10},{9,11},{10,... | collective-permute-start | bytes 2359304 | tf_op jit(solution)/shard_map/ppermute | solution.py:420
  465.4 73.6 %collective-permute-start.11 = (bf16[2,256,768]{2,1,0:T(8,128)(2,1)S(1)}, bf16[2,256,768]{2,1,0:T(8,128)(2,1)S(1)}, u32[]{:S(2)}, u32[]{:S(2)}) collective-permute-start(bf16[2,256,768]{2,1,0:T(8,128)(2,1)S(1)} %bitcast.252), channel_id=1, source_target_pairs={{0,1},{1,2},{2,3},{3,0},{4,5},{5,6},{6,7},{7,4},{8,9},{9,10},{10,1... | collective-permute-start | bytes 2359304 | tf_op jit(solution)/shard_map/ppermute | solution.py:420
  465.4 73.6 %copy-start.30 = (bf16[512,768]{1,0:T(8,128)(2,1)S(1)}, bf16[512,768]{1,0:T(8,128)(2,1)}, u32[]{:S(2)}) copy-start(bf16[512,768]{1,0:T(8,128)(2,1)} %get-tuple-element.136) | copy-start | bytes 2359300
  465.4 73.6 %copy-start.35 = (pred[2,256,512]{1,2,0:T(8,128)(4,1)S(1)}, pred[2,256,512]{1,2,0:T(8,128)(4,1)}, u32[]{:S(2)}) copy-start(pred[2,256,512]{1,2,0:T(8,128)(4,1)} %copy-done.34) | copy-start | bytes 786436
  470.0 69.0 %copy-start.25 = (f32[2,512,768]{2,1,0:T(8,128)S(1)}, f32[2,512,768]{2,1,0:T(8,128)}, u32[]{:S(2)}) copy-start(f32[2,512,768]{2,1,0:T(8,128)} %copy-done.23) | copy-start | bytes 9437188
  470.1 69.0 %copy-start.43 = (pred[4,2,512]{2,0,1:T(4,128)(4,1)S(1)}, pred[4,2,512]{2,0,1:T(4,128)(4,1)}, u32[]{:S(2)}) copy-start(pred[4,2,512]{2,0,1:T(4,128)(4,1)} %copy-done.42) | copy-start | bytes 12292
  470.2 74.9 %collective-permute-start.16 = (f32[512,768]{1,0:T(8,128)S(1)}, f32[512,768]{1,0:T(8,128)S(1)}, u32[]{:S(2)}, u32[]{:S(2)}) collective-permute-start(f32[512,768]{1,0:T(8,128)S(1)} %dynamic-slice_bitcast_fusion), channel_id=1, source_target_pairs={{0,4},{4,0},{1,5},{5,1},{2,6},{6,2},{3,7},{7,3},{8,12},{12,8},{9,1... | collective-permute-start | bytes 4718600 | tf_op jit(solution)/shard_map/ppermute | solution.py:429
  541.3 2.4 collective-permute-start.12
  (20 other events, 49.6 us)
Sparse Core Ops, SparseCore 0:
  414.4 207.5 all-reduce.5
Sparse Core Ops, SparseCore 1:
  447.6 92.3 reduce-scatter.3

commit v2 on v1

--- a/solution.py
+++ b/solution.py
@@ -161,15 +161,15 @@
     onehot = (bucket_np(both)[..., None] == np.arange(32)).astype(np.float32)
     return jnp.einsum("lcb,bh->hlc", jnp.asarray(onehot), bias_table, precision=lax.Precision.HIGHEST)
 
-def fwd_kernel(lines_ref, q_ref, k_ref, v_ref, o_ref, band_ref):
-    n = q_ref.shape[0] // QB
+def fwd_kernel(first, lines_ref, q_ref, k_ref, v_ref, o_ref, band_ref):
+    n = k_ref.shape[0] // QB
     lane = lax.broadcasted_iota(jnp.int32, (QB, 128), 1)
     for h in range(2):
         line = lines_ref[h, 0:1, :]
         spread = pltpu.roll(jnp.broadcast_to(line, (QB, 4 * QB)), 0, 1, stride=1, stride_axis=0)
         band_ref[h] = spread[:, QB:]
-    for i in range(n):
-        rows = slice(i * QB, (i + 1) * QB)
+    for i in range(first, first + q_ref.shape[0] // QB):
+        rows = slice((i - first) * QB, (i - first + 1) * QB)
         outs = []
         for h in range(2):
             low_bias = lines_ref[h, 0:1, 0:1]
@@ -189,17 +189,19 @@
             outs.append(o * (1.0 / l))
         o_ref[rows, :] = jnp.where(lane < 64, outs[0], outs[1]).astype(jnp.bfloat16)
 
-def attend(q, k, v, lines):
+def attend(q, k, v, lines, first, count):
     length, width = q.shape
     col = pl.BlockSpec((length, 128), lambda h: (0, h))
+    span = pl.BlockSpec((count, 128), lambda h: (first // count, h))
     return pl.pallas_call(
-        fwd_kernel,
+        lambda *refs: fwd_kernel(first // QB, *refs),
         grid=(width // 128,),
-        in_specs=[pl.BlockSpec((2, 2, 4 * QB), lambda h: (h, 0, 0)), col, col, col],
-        out_specs=col,
-        out_shape=jax.ShapeDtypeStruct((length, width), jnp.bfloat16),
+        in_specs=[pl.BlockSpec((2, 2, 4 * QB), lambda h: (h, 0, 0)), span, col, col],
+        out_specs=pl.BlockSpec((count, 128), lambda h: (0, h)),
+        out_shape=jax.ShapeDtypeStruct((count, width), jnp.bfloat16),
         scratch_shapes=[pltpu.VMEM((2, QB, 3 * QB), jnp.float32)],
         compiler_params=pltpu.CompilerParams(vmem_limit_bytes=48 << 20),
+        cost_estimate=pl.CostEstimate(flops=40 * count * length * width, bytes_accessed=6 * length * width, transcendentals=count * length * width // 64),
         name="attend",
     )(lines, q, k, v)
 
@@ -288,6 +290,7 @@
             pltpu.VMEM((length, 128), jnp.float32),
         ],
         compiler_params=pltpu.CompilerParams(vmem_limit_bytes=48 << 20),
+        cost_estimate=pl.CostEstimate(flops=84 * length * length * width, bytes_accessed=14 * length * width, transcendentals=length * length * width // 64),
         name="attend_back",
     )(lines, q, k, v, g)
     r = (np.arange(3)[:, None] - 1) * QB - (np.arange(2 * QB)[None] - QB)
@@ -298,112 +301,146 @@
     return dq, dk, dv, dbias
 
 
-def expert_kernel(label_ref, x_ref, u_ref, router_ref, win_ref, wout_ref, rows_ref, back_ref, dw_ref, drouter_ref,
-                  xt_ref, g_ref, gt_ref, prob_ref, out_acc, back_acc, hid_ref, pre_ref):
+def expert_kernel(label_ref, *refs):
+    count = (len(refs) - 10) // 4
+    x_refs, u_refs = refs[:count], refs[count : 2 * count]
+    router_ref, win_ref, wout_ref = refs[2 * count : 2 * count + 3]
+    rest = refs[2 * count + 3 :]
+    rows_refs, back_refs = rest[:count], rest[count : 2 * count]
+    g_ref, hid_ref, pre_ref, drouter_ref, prob_ref, out_acc, back_acc = rest[2 * count :]
     step = pl.program_id(0)
-    count = x_ref.shape[0]
-    tile = min(512, count)
+    tile = x_refs[0].shape[0]
     lane = lax.broadcasted_iota(jnp.int32, (tile, 128), 1)
     own = lane == label_ref[0]
-    spans = [slice(r * tile, (r + 1) * tile) for r in range(count // tile)]
+    spans = [slice(r * tile, (r + 1) * tile) for r in range(count)]
 
     @pl.when(step == 0)
     def _():
-        for rows in spans:
-            logits = jnp.dot(x_ref[rows, :], router_ref[...], preferred_element_type=jnp.float32)
+        for piece, rows in enumerate(spans):
+            logits = jnp.dot(x_refs[piece][...], router_ref[...], preferred_element_type=jnp.float32)
             logits = jnp.where(lane < 4, logits, -jnp.inf)
             raised = jnp.exp(logits - jnp.max(logits, axis=1, keepdims=True))
             prob = raised / jnp.sum(raised, axis=1, keepdims=True)
             prob_ref[rows, :] = prob
             gate = jnp.sum(jnp.where(own, prob, 0.0), axis=1, keepdims=True)
-            grad = (gate * u_ref[rows, :].astype(jnp.float32)).astype(jnp.bfloat16)
-            g_ref[rows, :] = grad
-            gt_ref[:, rows] = grad.T
-            xt_ref[:, rows] = x_ref[rows, :].T
+            g_ref[rows, :] = (gate * u_refs[piece][...].astype(jnp.float32)).astype(jnp.bfloat16)
         out_acc[...] = jnp.zeros_like(out_acc)
         back_acc[...] = jnp.zeros_like(back_acc)
 
-    for rows in spans:
-        pre = jnp.dot(x_ref[rows, :], win_ref[...], preferred_element_type=jnp.float32)
+    for piece, rows in enumerate(spans):
+        pre = jnp.dot(x_refs[piece][...], win_ref[...], preferred_element_type=jnp.float32)
         square = pre * pre
-        turn = jnp.tanh(0.7978845608028654 * pre * (1.0 + 0.044715 * square))
-        half = 0.5 * (1.0 + turn)
+        turn = jnp.tanh(pre * (0.7978845608028654 + 0.035677408136300125 * square))
+        half = 0.5 + 0.5 * turn
         hidden = (pre * half).astype(jnp.bfloat16)
-        slope = half + pre * (0.5 * (1.0 - turn * turn)) * (0.7978845608028654 + 0.1070322243 * square)
+        slope = half + pre * (half - half * half) * (1.5957691216057308 + 0.21406444881780074 * square)
         hid_ref[rows, :] = hidden
         out_acc[rows, :] += jnp.dot(hidden, wout_ref[...], preferred_element_type=jnp.float32)
         hidden_grad = lax.dot_general(g_ref[rows, :], wout_ref[...], (((1,), (1,)), ((), ())), preferred_element_type=jnp.float32)
         pre_grad = (hidden_grad * slope).astype(jnp.bfloat16)
         pre_ref[rows, :] = pre_grad
         back_acc[rows, :] += lax.dot_general(pre_grad, win_ref[...], (((1,), (1,)), ((), ())), preferred_element_type=jnp.float32)
-    dw_ref[0] = jnp.dot(xt_ref[...], pre_ref[...], preferred_element_type=jnp.float32).astype(dw_ref.dtype)
-    dw_ref[1] = jnp.dot(gt_ref[...], hid_ref[...], preferred_element_type=jnp.float32).astype(dw_ref.dtype)
 
     @pl.when(step == pl.num_programs(0) - 1)
     def _():
         total = jnp.zeros(drouter_ref.shape, jnp.float32)
-        for rows in spans:
+        for piece, rows in enumerate(spans):
             prob = prob_ref[rows, :]
             gate = jnp.sum(jnp.where(own, prob, 0.0), axis=1, keepdims=True)
             out = out_acc[rows, :].astype(jnp.bfloat16).astype(jnp.float32)
-            rows_ref[rows, :] = (gate * out).astype(jnp.bfloat16)
-            gate_grad = jnp.sum(u_ref[rows, :].astype(jnp.float32) * out, axis=1, keepdims=True)
+            rows_refs[piece][...] = (gate * out).astype(jnp.bfloat16)
+            gate_grad = jnp.sum(u_refs[piece][...].astype(jnp.float32) * out, axis=1, keepdims=True)
             logit_grad = prob * (jnp.where(own, gate_grad, 0.0) - gate * gate_grad)
             high = logit_grad.astype(jnp.bfloat16)
             low = (logit_grad - high.astype(jnp.float32)).astype(jnp.bfloat16)
             back = back_acc[rows, :].astype(jnp.bfloat16).astype(jnp.float32)
             for part in (high, low):
                 back += lax.dot_general(part, router_ref[...], (((1,), (1,)), ((), ())), preferred_element_type=jnp.float32)
-                total += jnp.dot(xt_ref[:, rows], part, preferred_element_type=jnp.float32)
-            back_ref[rows, :] = back.astype(jnp.bfloat16)
+                total += lax.dot_general(x_refs[piece][...], part, (((0,), (0,)), ((), ())), preferred_element_type=jnp.float32)
+            back_refs[piece][...] = back.astype(jnp.bfloat16)
         drouter_ref[...] = total
 
 
-def run_expert(label, rows_in, upstream_rows, router_weight, w_in, w_out):
-    count, width = rows_in.shape
-    inner = w_in.shape[1]
-    chunk = 256
+def run_expert(label, pieces, upstream_pieces, router_wide, w_in, w_out, chunk=768):
+    count, (tile, width) = len(pieces), pieces[0].shape
+    rows, inner = count * tile, w_in.shape[1]
     once = pl.Buffered(1)
-    whole = lambda f, lab: (0, 0)
-    router_wide = jnp.pad(router_weight, ((0, 0), (0, 128 - router_weight.shape[1])))
-    return pl.pallas_call(
+    piece = pl.BlockSpec((tile, width), lambda f, lab: (0, 0), pipeline_mode=once)
+    inner_block = pl.BlockSpec((rows, chunk), lambda f, lab: (0, f))
+    low = lambda *shape: jax.ShapeDtypeStruct(shape, jnp.bfloat16)
+    outs = pl.pallas_call(
         expert_kernel,
         grid_spec=pltpu.PrefetchScalarGridSpec(
             num_scalar_prefetch=1,
             grid=(inner // chunk,),
-            in_specs=[
-                pl.BlockSpec((count, width), whole, pipeline_mode=once),
-                pl.BlockSpec((count, width), whole, pipeline_mode=once),
-                pl.BlockSpec((width, 128), whole, pipeline_mode=once),
+            in_specs=[piece] * (2 * count) + [
+                pl.BlockSpec((width, 128), lambda f, lab: (0, 0), pipeline_mode=once),
                 pl.BlockSpec((width, chunk), lambda f, lab: (0, f)),
                 pl.BlockSpec((chunk, width), lambda f, lab: (f, 0)),
             ],
-            out_specs=[
-                pl.BlockSpec((count, width), whole, pipeline_mode=once),
-                pl.BlockSpec((count, width), whole, pipeline_mode=once),
-                pl.BlockSpec((2, width, chunk), lambda f, lab: (0, 0, f)),
-                pl.BlockSpec((width, 128), whole, pipeline_mode=once),
+            out_specs=[piece] * (2 * count) + [
+                pl.BlockSpec((rows, width), lambda f, lab: (0, 0), pipeline_mode=once),
+                inner_block,
+                inner_block,
+                pl.BlockSpec((width, 128), lambda f, lab: (0, 0), pipeline_mode=once),
             ],
             scratch_shapes=[
-                pltpu.VMEM((width, count), jnp.bfloat16),
-                pltpu.VMEM((count, width), jnp.bfloat16),
-                pltpu.VMEM((width, count), jnp.bfloat16),
-                pltpu.VMEM((count, 128), jnp.float32),
-                pltpu.VMEM((count, width), jnp.float32),
-                pltpu.VMEM((count, width), jnp.float32),
-                pltpu.VMEM((count, chunk), jnp.bfloat16),
-                pltpu.VMEM((count, chunk), jnp.bfloat16),
+                pltpu.VMEM((rows, 128), jnp.float32),
+                pltpu.VMEM((rows, width), jnp.float32),
+                pltpu.VMEM((rows, width), jnp.float32),
             ],
         ),
-        out_shape=[
-            jax.ShapeDtypeStruct((count, width), jnp.bfloat16),
-            jax.ShapeDtypeStruct((count, width), jnp.bfloat16),
-            jax.ShapeDtypeStruct((2, width, inner), jnp.bfloat16),
-            jax.ShapeDtypeStruct((width, 128), jnp.float32),
-        ],
-        compiler_params=pltpu.CompilerParams(vmem_limit_bytes=60 << 20),
+        out_shape=[low(tile, width)] * (2 * count)
+        + [low(rows, width), low(rows, inner), low(rows, inner), jax.ShapeDtypeStruct((width, 128), jnp.float32)],
+        compiler_params=pltpu.CompilerParams(vmem_limit_bytes=48 << 20),
+        cost_estimate=pl.CostEstimate(flops=16 * rows * width * inner, bytes_accessed=8 * width * inner, transcendentals=rows * inner),
         name="experts",
-    )(label, rows_in, upstream_rows, router_wide, w_in, w_out)
+    )(label, *pieces, *upstream_pieces, router_wide, w_in, w_out)
+    return outs[:count], outs[count : 2 * count], outs[2 * count :]
+
+
+def expert_grads_kernel(groups, count, *refs):
+    x_refs, refs = refs[: groups * count], refs[groups * count :]
+    g_refs, hid_refs, pre_refs = refs[:groups], refs[groups : 2 * groups], refs[2 * groups : 3 * groups]
+    dw_ref, xt_ref, gt_ref = refs[3 * groups :]
+    width = xt_ref.shape[0]
+    tile = x_refs[0].shape[0]
+    rows = g_refs[0].shape[0]
+
+    @pl.when(pl.program_id(0) == 0)
+    def _():
+        for at in range(groups):
+            gt_ref[:, at * rows : (at + 1) * rows] = g_refs[at][...].T
+            for piece in range(count):
+                start = at * rows + piece * tile
+                xt_ref[:, start : start + tile] = x_refs[at * count + piece][...].T
+
+    for side, (left, right) in enumerate(((xt_ref, pre_refs), (gt_ref, hid_refs))):
+        total = sum(
+            jnp.dot(left[:, at * rows : (at + 1) * rows], right[at][...], preferred_element_type=jnp.float32)
+            for at in range(groups)
+        )
+        dw_ref[:, side * width : (side + 1) * width] = total.astype(jnp.bfloat16).T
+
+
+def expert_grads(pieces, grads, hiddens, pre_grads, chunk=512):
+    groups, count = len(grads), len(pieces) // len(grads)
+    (tile, width), (rows, inner) = pieces[0].shape, hiddens[0].shape
+    once = pl.Buffered(1)
+    inner_block = pl.BlockSpec((rows, chunk), lambda f: (0, f))
+    return pl.pallas_call(
+        lambda *refs: expert_grads_kernel(groups, count, *refs),
+        grid=(inner // chunk,),
+        in_specs=[pl.BlockSpec((tile, width), lambda f: (0, 0), pipeline_mode=once)] * (groups * count)
+        + [pl.BlockSpec((rows, width), lambda f: (0, 0), pipeline_mode=once)] * groups
+        + [inner_block] * (2 * groups),
+        out_specs=pl.BlockSpec((chunk, 2 * width), lambda f: (f, 0)),
+        out_shape=jax.ShapeDtypeStruct((inner, 2 * width), jnp.bfloat16),
+        scratch_shapes=[pltpu.VMEM((width, groups * rows), jnp.bfloat16)] * 2,
+        compiler_params=pltpu.CompilerParams(vmem_limit_bytes=48 << 20),
+        cost_estimate=pl.CostEstimate(flops=6 * groups * rows * width * inner, bytes_accessed=4 * (groups * rows + width) * inner, transcendentals=0),
+        name="expert_grads",
+    )(*pieces, *grads, *hiddens, *pre_grads)
 
 
 def make_dispatch(routes, labels, capacity):
@@ -497,57 +534,90 @@
     capacity = local_len // 2
     whole_seq = seq_count == 2 and lax.axis_size("ctx") == 2 and local_len % QB == 0
     if whole_seq:
-        tokens, cotangent, routes = trade(tokens), trade(cotangent), trade(routes)
+        routes, cotangent, tokens = trade(routes), trade(cotangent), trade(tokens)
+    groups = [slice(0, 1), slice(1, 2)] if whole_seq else [slice(0, seq_count)]
     label = lax.axis_index("expert")
     labels = (label + jnp.arange(owners, dtype=jnp.int32)) % owners
     dispatch = make_dispatch(routes, labels, capacity)
 
-    def to_owners(rows):
-        sent = jnp.einsum("escx,sxd->escd", dispatch, rows, preferred_element_type=jnp.float32)
-        sent = sent.astype(jnp.bfloat16)
-        return jnp.concatenate(exchange(list(sent), "expert", 1)).reshape(-1, model_width)
-
-    def to_tokens(rows):
-        pieces = list(rows.reshape(owners, seq_count, capacity, model_width))
-        pieces = jnp.stack(exchange(pieces, "expert", -1))
-        return jnp.einsum("escx,escd->sxd", dispatch, pieces, preferred_element_type=jnp.float32)
-
-    upstream_rows = to_owners(cotangent)
+    together = lax.optimization_barrier
+
+    def sort_rows(group, rows):
+        sent = [
+            jnp.einsum("scx,sxd->scd", dispatch[turn, group], rows, preferred_element_type=jnp.float32)
+            for turn in range(owners)
+        ]
+        return [piece.astype(jnp.bfloat16).reshape(-1, model_width) for piece in sent]
+
+    def place_rows(group, pieces):
+        pieces = jnp.stack(pieces).reshape(owners, -1, capacity, model_width)
+        return jnp.einsum("escx,escd->sxd", dispatch[:, group], pieces, preferred_element_type=jnp.float32)
+
     inputs = tokens.astype(jnp.float32)
     scale1 = norm_scale(inputs)
     attn_in = (inputs * scale1 * norm1_gain).astype(jnp.bfloat16)
     queries = wide_dot(attn_in, query_weight).astype(jnp.bfloat16)
     keys = wide_dot(attn_in, key_weight).astype(jnp.bfloat16)
     values = wide_dot(attn_in, value_weight).astype(jnp.bfloat16)
+    sorted_upstream = [sort_rows(group, cotangent[group]) for group in groups]
+    sorted_upstream, queries = together((sorted_upstream, queries))
+    upstream = [exchange(rows, "expert", 1) for rows in sorted_upstream]
     if whole_seq:
         lines = bias_lines(bias_table)
         flat = (seq_count * local_len, model_width)
         qkv = [rows.reshape(flat) for rows in (queries, keys, values)]
-        attended = attend(*qkv, lines).reshape(tokens.shape)
     else:
         first_pos = lax.axis_index("ctx") * local_len
         keys = lax.all_gather(keys, "ctx", axis=1, tiled=True)
         values = lax.all_gather(values, "ctx", axis=1, tiled=True)
         buckets = bucket_grid(first_pos, local_len, keys.shape[1])
         attended, log_totals = attend_rows(queries, keys, values, buckets, bias_table, DH)
-        attended = attended.astype(jnp.bfloat16)
-    residual1 = inputs + wide_dot(attended, output_weight)
-    scale2 = norm_scale(residual1)
-    router_in = (residual1 * scale2 * norm2_gain).astype(jnp.bfloat16)
-    rows_in = to_owners(router_in)
-    rows_out, rows_back, grad_experts, grad_router = run_expert(
-        label.astype(jnp.int32).reshape(1), rows_in, upstream_rows, router_weight, w_in[0], w_out[0]
-    )
-    grad_router = grad_router[:, : router_weight.shape[1]]
-    router_in_grad = to_tokens(rows_back)
-    block_out = (residual1 + to_tokens(rows_out)).astype(jnp.bfloat16)
-    grad_experts = lax.psum_scatter(grad_experts, ("dp", "ctx"), scatter_dimension=2, tiled=True)
-    norm2_back, grad_norm2 = norm_back(residual1, scale2, norm2_gain, router_in_grad)
-    residual_grad = cotangent.astype(jnp.float32) + norm2_back
-    attn_grad = residual_grad.astype(jnp.bfloat16)
-    grad_w_output = weight_dot(attended, attn_grad)
-    mixed_grad = wide_dot_back(attn_grad, output_weight).astype(jnp.bfloat16)
-    grad_w_output, grad_norm2, grad_router = sum_all([grad_w_output], [grad_norm2, grad_router])
+    attended_groups, residual1, scale2, arrived = [], [], [], []
+    in_flight, fed = upstream[0], queries.reshape(-1, model_width)
+    for at, group in enumerate(groups):
+        if whole_seq:
+            rows = attend(fed, *qkv[1:], lines, at * local_len, local_len)[None]
+        else:
+            rows = attended.astype(jnp.bfloat16)
+        rows, in_flight = together((rows, in_flight))
+        if at == 0:
+            upstream[0] = in_flight
+        else:
+            arrived[-1] = in_flight
+        attended_groups.append(rows)
+        residual1.append(inputs[group] + wide_dot(rows, output_weight))
+        scale2.append(norm_scale(residual1[-1]))
+        router_in = (residual1[-1] * scale2[-1] * norm2_gain).astype(jnp.bfloat16)
+        sorted_rows, fed = together((sort_rows(group, router_in), fed))
+        in_flight = exchange(sorted_rows, "expert", 1)
+        arrived.append(in_flight)
+    attended = attended_groups
+    router_wide = jnp.pad(router_weight, ((0, 0), (0, 128 - router_weight.shape[1])))
+    label = label.astype(jnp.int32).reshape(1)
+    done, back = [], []
+    for rows, grads in zip(arrived, upstream):
+        result = run_expert(label, rows, grads, router_wide, w_in[0], w_out[0])
+        if back:
+            result, back[-1] = together((result, back[-1]))
+        done.append(result)
+        back.append(exchange(result[1], "expert", -1))
+    rows_out = [item[0] for item in done]
+    grad_rows, hiddens, pre_grads, grad_router = zip(*[item[2] for item in done])
+    grad_router = sum(grad_router)[:, : router_weight.shape[1]]
+    grad_experts = expert_grads(sum(arrived, []), grad_rows, hiddens, pre_grads)
+    grad_experts, back[-1], rows_out = together((grad_experts, back[-1], rows_out))
+    grad_experts = lax.psum_scatter(grad_experts, ("dp", "ctx"), scatter_dimension=0, tiled=True)
+    returned = [exchange(list(rows), "expert", -1) for rows in rows_out]
+    residual_grad, attn_grad, mixed_grad, grad_norm2 = [], [], [], 0.0
+    for group, rows, scale, pieces in zip(groups, residual1, scale2, back):
+        norm2_back, gain_part = norm_back(rows, scale, norm2_gain, place_rows(group, pieces))
+        grad_norm2 = grad_norm2 + gain_part
+        residual_grad.append(cotangent[group].astype(jnp.float32) + norm2_back)
+        attn_grad.append(residual_grad[-1].astype(jnp.bfloat16))
+        mixed_grad.append(wide_dot_back(attn_grad[-1], output_weight).astype(jnp.bfloat16))
+    grad_w_output = sum(weight_dot(left, right) for left, right in zip(attended, attn_grad))
+    residual_grad, mixed_grad = jnp.concatenate(residual_grad), jnp.concatenate(mixed_grad)
+    early_sums = sum_all([grad_w_output], [grad_norm2, grad_router])
     if whole_seq:
         *grads, grad_bias = attend_back(*qkv, mixed_grad.reshape(flat), lines)
         query_low, key_low, value_low = (rows.reshape(tokens.shape) for rows in grads)
@@ -559,14 +629,20 @@
         query_low = query_grad.astype(jnp.bfloat16)
         key_low = lax.psum_scatter(key_part, "ctx", scatter_dimension=1, tiled=True).astype(jnp.bfloat16)
         value_low = lax.psum_scatter(value_part, "ctx", scatter_dimension=1, tiled=True).astype(jnp.bfloat16)
+    early_sums, returned, query_low, key_low, value_low = together(
+        (early_sums, returned, query_low, key_low, value_low)
+    )
+    block_out = [rows + place_rows(group, pieces) for group, rows, pieces in zip(groups, residual1, returned)]
+    block_out = jnp.concatenate(block_out).astype(jnp.bfloat16)
+    grad_w_output, grad_norm2, grad_router = early_sums
     norm_in_grad = wide_dot_back(query_low, query_weight)
     norm_in_grad = norm_in_grad + wide_dot_back(key_low, key_weight)
     norm_in_grad = norm_in_grad + wide_dot_back(value_low, value_weight)
     norm1_back, grad_norm1 = norm_back(inputs, scale1, norm1_gain, norm_in_grad)
     d_tokens = residual_grad + norm1_back
-    grad_w_query, grad_w_key, grad_w_value, grad_bias, grad_norm1 = sum_all(
-        [weight_dot(attn_in, rows) for rows in (query_low, key_low, value_low)], [grad_bias, grad_norm1]
-    )
+    grad_qkv = [weight_dot(attn_in, rows) for rows in (query_low, key_low, value_low)]
+    grad_qkv, grad_experts = together((grad_qkv, grad_experts))
+    grad_w_query, grad_w_key, grad_w_value, grad_bias, grad_norm1 = sum_all(grad_qkv, [grad_bias, grad_norm1])
     if whole_seq:
         block_out, d_tokens = trade(block_out), trade(d_tokens)
     grad_experts = grad_experts.astype(jnp.float32)
@@ -581,8 +657,8 @@
         grad_bias,
         grad_norm2,
         grad_router,
-        grad_experts[0][None],
-        grad_experts[1].T[None],
+        grad_experts[:, :model_width].T[None],
+        grad_experts[:, model_width:][None],
     )
 
 

time: 660 us -> 644 us (0.976)
  waiting for transfers between devices: 276 us -> 229 us
  starting transfers between devices: 47.3 us -> 83.4 us
  local copies, waits for them, and re-layouts: 69.1 us -> 49.6 us
  other arithmetic: 27.7 us -> 34.4 us
    ppermute x12 -> x24, waiting for transfers between devices: 199 us -> 18.3 us  [exchange(): lax.ppermute(pieces[turn], axis, [(at, (at + sign * turn) % size) for at...]
    psum x1 -> x2, waiting for transfers between devices: 74.8 us -> 210 us  [sum_all(): packed = lax.psum(packed, ('dp', 'ctx', 'expert')).astype(jnp.float32)]
    ppermute x12 -> x24, starting transfers between devices: 46.1 us -> 82 us  [exchange(): lax.ppermute(pieces[turn], axis, [(at, (at + sign * turn) % size) for at...]
    pallas_call x1 -> x3, Pallas kernels: 27.2 us -> 56.2 us  [the longest x2 29.1 us: attend(): pl.pallas_call(lambda *refs: fwd_kernel(first // QB, *refs), grid=(width...]
    pallas_call x1 -> x2, Pallas kernels: 83.4 us -> 59.5 us  [run_expert(): pl.pallas_call(expert_kernel, grid_spec=pltpu.PrefetchScalarGridSpec(num_...]
    unnamed x106 -> x195, local copies, waits for them, and re-layouts: 43.2 us -> 27.1 us
    another operation x4 -> x1, local copies, waits for them, and re-layouts: 8.22 us -> 0.29 us  [the longest x1 5.1 us: to_tokens(): pieces = list(rows.reshape(owners, seq_count, capacity, model_width))]
    dot_general x4 -> x20, matrix products: 12.8 us -> 20.3 us  [the longest x4 11.1 us: place_rows(): jnp.einsum('escx,escd->sxd', dispatch[:, group], pieces, preferred_elemen...]
  transfers between devices with their start and end apart: 19 -> 32, of which waited for: 8 -> 6; matrix products, arithmetic and copies ran while one was open for 13% -> 13% of each run, Pallas kernels for 4% -> 28%
where the time goes in v2:
time: 644 us; the launch traced here: 636 us
  waiting for transfers between devices  229 us (36%)
  Pallas kernels  176 us (27%)
  starting transfers between devices  83.4 us (13%)
  local copies, waits for them, and re-layouts  49.6 us (8%)
  matrix products  47.1 us (7%)
  other arithmetic  34.4 us (5%)
  between operations  17.1 us (3%)
    psum x2, waiting for transfers between devices, sum_all(): packed = lax.psum(packed, ('dp', 'ctx', 'expert')).astype(jnp.float32)  210 us
    ppermute x24, starting transfers between devices, exchange(): lax.ppermute(pieces[turn], axis, [(at, (at + sign * turn) % size) for at...  82 us
    pallas_call x1, Pallas kernels, attend_back(): pl.pallas_call(bwd_kernel, grid=(width // 128,), in_specs=[pl.BlockSpec((...  60.1 us
    pallas_call x2, Pallas kernels, run_expert(): pl.pallas_call(expert_kernel, grid_spec=pltpu.PrefetchScalarGridSpec(num_...  59.5 us
    pallas_call x2, Pallas kernels, attend(): pl.pallas_call(lambda *refs: fwd_kernel(first // QB, *refs), grid=(width...  29.1 us
    pallas_call x1, Pallas kernels, expert_grads(): pl.pallas_call(lambda *refs: expert_grads_kernel(groups, count, *refs), g...  27.1 us
    unnamed x195, local copies, waits for them, and re-layouts  27.1 us
    ppermute x24, waiting for transfers between devices, exchange(): lax.ppermute(pieces[turn], axis, [(at, (at + sign * turn) % size) for at...  18.3 us
  transfers between devices with their start and end apart: 32, of which 6 were waited for; matrix products, arithmetic and copies ran while one was open for 13% of the time, Pallas kernels for 28%

profile of v2, /device:TPU:0, one launch (start us, length us, event | category | flops | bytes accessed | tf_op | source)
XLA Modules:
  0.0 636.3 jit_solution(17576995367125250171)
XLA Ops:
  9.5 2.1 dynamic-slice_bitcast_fusion.1
  13.8 2.4 reduce-window.6
  18.1 1.9 bitcast_select_fusion.2
  29.4 1.5 convolution_convert_fusion.1
  34.2 2.7 collective-permute-start.3
  36.9 2.6 collective-permute-start.4
  42.0 14.7 %attend.2 = bf16[512,768]{1,0:T(8,128)(2,1)S(1)} custom-call(f32[12,2,1024]{2,1,0:T(2,128)S(1)} %bitcast.300, bf16[1024,768]{1,0:T(8,128)(2,1)S(1)} %bitcast.309, bf16[1024,768]{1,0:T(8,128)(2,1)S(1)} %bitcast.303, bf16[1024,768]{1,0:T(8,128)(2,1)S(1)} %bitcast.306), custom_call_target="tpu_custom_call" | custom-call | flops 16106127360 | bytes 4718592 | tf_op jit(solution)/shard_map/attend/pallas_call | solution.py:196
  57.0 8.8 %collective-permute-done.4.refs_6_ = bf16[256,768]{1,0:T(8,128)(2,1)S(1)} collective-permute-done((bf16[256,768]{1,0:T(8,128)(2,1)S(1)}, bf16[256,768]{1,0:T(8,128)(2,1)S(1)}, u32[]{:S(2)}, u32[]{:S(2)}) %collective-permute-start.4) | collective-permute-done | bytes 393248 | tf_op jit(solution)/shard_map/ppermute | solution.py:457
  69.2 34.1 %collective-permute-start.6 = (bf16[256,768]{1,0:T(8,128)(2,1)S(1)}, bf16[256,768]{1,0:T(8,128)(2,1)S(1)}, u32[]{:S(2)}, u32[]{:S(2)}) collective-permute-start(bf16[256,768]{1,0:T(8,128)(2,1)S(1)} %convolution_convert_fusion.11), channel_id=1, source_target_pairs={{0,1},{1,2},{2,3},{3,0},{4,5},{5,6},{6,7},{7,4},{8,9},{9,10},{10,1... | collective-permute-start | bytes 1179656 | tf_op jit(solution)/shard_map/ppermute | solution.py:457
  103.4 2.4 collective-permute-start.8
  105.8 14.3 %attend.3 = bf16[512,768]{1,0:T(8,128)(2,1)S(1)} custom-call(f32[12,2,1024]{2,1,0:T(2,128)S(1)} %bitcast.301, bf16[1024,768]{1,0:T(8,128)(2,1)S(1)} %bitcast.310, bf16[1024,768]{1,0:T(8,128)(2,1)S(1)} %bitcast.304, bf16[1024,768]{1,0:T(8,128)(2,1)S(1)} %bitcast.307), custom_call_target="tpu_custom_call" | custom-call | flops 16106127360 | bytes 4718592 | tf_op jit(solution)/shard_map/attend/pallas_call | solution.py:196
  120.2 2.0 collective-permute-start.14
  122.2 2.5 collective-permute-done.7.refs_2_
  124.7 5.1 collective-permute-done.8.refs_3_
  129.8 2.3 multiply_reduce_fusion
  134.5 16.1 %collective-permute-start.9 = (bf16[256,768]{1,0:T(8,128)(2,1)S(1)}, bf16[256,768]{1,0:T(8,128)(2,1)S(1)}, u32[]{:S(2)}, u32[]{:S(2)}) collective-permute-start(bf16[256,768]{1,0:T(8,128)(2,1)S(1)} %convolution_convert_fusion.7), channel_id=1, source_target_pairs={{0,1},{1,2},{2,3},{3,0},{4,5},{5,6},{6,7},{7,4},{8,9},{9,10},{10,1... | collective-permute-start | bytes 1179656 | tf_op jit(solution)/shard_map/ppermute | solution.py:457
  150.7 3.4 collective-permute-start.10
  154.5 29.5 %experts.3 = (bf16[256,768]{1,0:T(8,128)(2,1)S(1)}, bf16[256,768]{1,0:T(8,128)(2,1)}, bf16[256,768]{1,0:T(8,128)(2,1)}, bf16[256,768]{1,0:T(8,128)(2,1)S(1)}, bf...) custom-call(s32[1]{0:T(128)} %bitcast.34.label_ref, ...), custom_call_target="tpu_custom_call" | custom-call | flops 38654705664 | bytes 18874368 | tf_op jit(solution)/shard_map/experts/pallas_call | solution.py:371
  188.4 2.0 collective-permute-start.16
  191.6 30.0 %experts.2 = (bf16[256,768]{1,0:T(8,128)(2,1)S(1)}, bf16[256,768]{1,0:T(8,128)(2,1)}, bf16[256,768]{1,0:T(8,128)(2,1)}, bf16[256,768]{1,0:T(8,128)(2,1)S(1)}, bf...) custom-call(s32[1]{0:T(128)} %bitcast.34.label_ref, ...), custom_call_target="tpu_custom_call" | custom-call | flops 38654705664 | bytes 18874368 | tf_op jit(solution)/shard_map/experts/pallas_call | solution.py:371
  224.6 3.7 collective-permute-start.18
  229.1 27.1 %expert_grads.1 = bf16[3072,1536]{1,0:T(8,128)(2,1)} custom-call(bf16[256,768]{1,0:T(8,128)(2,1)S(1)} %convolution_convert_fusion.12.refs_0_, bf16[256,768]{1,0:T(8,128)(2,1)S(1)} %collective-permute-done.6.refs_1_, bf16[256,768]{1,0:T(8,128)(2,1)S(1)} %collective-permute-done.7.refs_2_, bf16[256,768]{1,0:T(8,128)(2,1)S(1)} %collective-permute-done.8.refs_3_, ...), custom_call_target="tpu_custom_call" | custom-call | flops 28991029248 | bytes 34603008 | tf_op jit(solution)/shard_map/expert_grads/pallas_call | solution.py:431
  258.2 1.8 collective-permute-done.19
  260.1 2.7 fusion.11
  263.4 3.3 fusion.49
  270.2 3.8 convert_add_fusion.1
  278.4 1.5 collective-permute-start.21
  281.2 1.9 collective-permute-start.23
  283.1 2.3 collective-permute-start.24
  285.4 2.1 fusion.54
  289.7 60.1 %attend_back.1 = (bf16[1024,768]{1,0:T(8,128)(2,1)S(1)}, bf16[1024,768]{1,0:T(8,128)(2,1)S(1)}, bf16[1024,768]{1,0:T(8,128)(2,1)S(1)}, f32[12,3,512]{2,1,0:T(4,128)S(1)}, f32[12,2,256]{2,1,0:T(2,128)S(1)}) custom-call(f32[12,2,1024]{2,1,0:T(2,128)S(1)} %bitcast.302, bf16[1024,768]{1,0:T(8,128)(2,1)} %bitcast.311, bf16[1024,768]{1,0:T(8,128)(2,1)} %bitcast.305, ...), custom_call_target="tpu_custom_call" | custom-call | flops 67645734912 | bytes 11010048 | tf_op jit(solution)/shard_map/attend_back/pallas_call | solution.py:279
  354.2 82.9 %all-reduce.6.cloned.1.call-done = bf16[784,768]{1,0:T(8,128)(2,1)} async-done(((bf16[784,768]{1,0:T(8,128)(2,1)}), bf16[784,768]{1,0:T(8,128)(2,1)}) %all-reduce.6.cloned.1.call-update) | async-done | bytes 1204240 | tf_op jit(solution)/shard_map/psum | solution.py:503
  437.0 1.4 convert_element_type.201
  439.7 3.0 slice.195
  443.4 2.5 fusion.42
  446.0 2.5 fusion.43
  453.5 3.5 fusion.7
  458.9 3.4 fusion.5
  465.7 2.6 convolution_bitcast_fusion.2
  468.3 2.6 convolution_bitcast_fusion.1
  470.9 2.6 convolution_bitcast_fusion
  473.6 2.5 convert_dynamic-update-slice_fusion.2
  481.9 1.5 select_bitcast_fusion.1
  485.8 1.7 fusion.40
  487.5 1.9 pad_maximum_fusion
  492.2 127.2 %all-reduce.8.cloned.1.call-done = bf16[2320,768]{1,0:T(8,128)(2,1)} async-done(((bf16[2320,768]{1,0:T(8,128)(2,1)}), bf16[2320,768]{1,0:T(8,128)(2,1)}) %all-reduce.8.cloned.1.call-update) | async-done | bytes 3563536 | tf_op jit(solution)/shard_map/psum | solution.py:503
  619.4 2.6 convert_element_type.212
  623.6 5.1 fusion.108
  (329 shorter events, 78.9 us)
Async XLA Ops:
  8.0 22.9 %copy-start = (bf16[768,768]{1,0:T(8,128)(2,1)S(1)}, bf16[768,768]{1,0:T(8,128)(2,1)}, u32[]{:S(2)}) copy-start(bf16[768,768]{1,0:T(8,128)(2,1)} %param.25) | copy-start | bytes 3538948
  8.0 429.0 %all-reduce.6.cloned.1.call-start = ((), (), s32[]{:S(2)}) async-start(), calls=%async_computation.1 | async-start | bytes 2408448 | tf_op jit(solution)/shard_map/psum | solution.py:503
  9.0 4.7 collective-permute-start.1
  11.6 6.5 %collective-permute-start.2 = (bf16[512,768]{1,0:T(8,128)(2,1)}, bf16[512,768]{1,0:T(8,128)(2,1)}, u32[]{:S(2)}, u32[]{:S(2)}) collective-permute-start(bf16[512,768]{1,0:T(8,128)(2,1)} %dynamic-slice_bitcast_fusion.1), channel_id=1, source_target_pairs={{0,4},{4,0},{1,5},{5,1},{2,6},{6,2},{3,7},{7,3},{8,12},{12,8},{9,1... | collective-permute-start | bytes 2359304 | tf_op jit(solution)/shard_map/ppermute | solution.py:466
  12.6 13.2 %collective-permute-start = (bf16[512,768]{1,0:T(8,128)(2,1)}, bf16[512,768]{1,0:T(8,128)(2,1)}, u32[]{:S(2)}, u32[]{:S(2)}) collective-permute-start(bf16[512,768]{1,0:T(8,128)(2,1)} %dynamic-slice_bitcast_fusion.2), channel_id=1, source_target_pairs={{0,4},{4,0},{1,5},{5,1},{2,6},{6,2},{3,7},{7,3},{8,12},{12,8},{9,1... | collective-permute-start | bytes 2359304 | tf_op jit(solution)/shard_map/ppermute | solution.py:466
  13.4 92.4 %copy-start.3 = (f32[2,1024,12]{1,0,2:T(2,128)}, f32[2,1024,12]{1,0,2:T(2,128)S(1)}, u32[]{:S(2)}) copy-start(f32[2,1024,12]{1,0,2:T(2,128)S(1)} %copy.56) | copy-start | bytes 294916
  13.7 140.8 %copy-start.1 = (bf16[768,128]{1,0:T(8,128)(2,1)}, bf16[768,128]{1,0:T(8,128)(2,1)S(1)}, u32[]{:S(2)}) copy-start(bf16[768,128]{1,0:T(8,128)(2,1)S(1)} %pad.16.refs_8_) | copy-start | bytes 589828
  18.1 116.0 %copy-start.59 = (pred[4,2,256,512]{2,3,0,1:T(32,128)(4,1)}, pred[4,2,256,512]{2,3,0,1:T(32,128)(4,1)S(1)}, u32[]{:S(2)}) copy-start(pred[4,2,256,512]{2,3,0,1:T(32,128)(4,1)S(1)} %broadcast_and_fusion) | copy-start | bytes 3145732
  27.6 29.2 %copy-start.25 = (bf16[1,512,768]{2,1,0:T(8,128)(2,1)}, bf16[1,512,768]{2,1,0:T(8,128)(2,1)S(1)}, u32[]{:S(2)}) copy-start(bf16[1,512,768]{2,1,0:T(8,128)(2,1)S(1)} %get-tuple-element.289) | copy-start | bytes 2359300
  27.6 29.2 %copy-start.27 = (bf16[1,512,768]{2,1,0:T(8,128)(2,1)}, bf16[1,512,768]{2,1,0:T(8,128)(2,1)S(1)}, u32[]{:S(2)}) copy-start(bf16[1,512,768]{2,1,0:T(8,128)(2,1)S(1)} %get-tuple-element.290) | copy-start | bytes 2359300
  30.9 74.9 %copy-start.8 = (bf16[2,512,768]{2,1,0:T(8,128)(2,1)}, bf16[2,512,768]{2,1,0:T(8,128)(2,1)S(1)}, u32[]{:S(2)}) copy-start(bf16[2,512,768]{2,1,0:T(8,128)(2,1)S(1)} %convolution_convert_fusion.1) | copy-start | bytes 4718596
  32.8 73.1 %copy-start.9 = (bf16[2,512,768]{2,1,0:T(8,128)(2,1)}, bf16[2,512,768]{2,1,0:T(8,128)(2,1)S(1)}, u32[]{:S(2)}) copy-start(bf16[2,512,768]{2,1,0:T(8,128)(2,1)S(1)} %convolution_convert_fusion) | copy-start | bytes 4718596
  34.2 71.6 %copy-start.10 = (bf16[2,512,768]{2,1,0:T(8,128)(2,1)}, bf16[2,512,768]{2,1,0:T(8,128)(2,1)S(1)}, u32[]{:S(2)}) copy-start(bf16[2,512,768]{2,1,0:T(8,128)(2,1)S(1)} %convolution_convert_fusion.2) | copy-start | bytes 4718596
  34.2 22.8 %collective-permute-start.3 = (bf16[256,768]{1,0:T(8,128)(2,1)S(1)}, bf16[256,768]{1,0:T(8,128)(2,1)S(1)}, u32[]{:S(2)}, u32[]{:S(2)}) collective-permute-start(bf16[256,768]{1,0:T(8,128)(2,1)S(1)} %convolution_convert_fusion.19), channel_id=1, source_target_pairs={{0,1},{1,2},{2,3},{3,0},{4,5},{5,6},{6,7},{7,4},{8,9},{9,10},{10,1... | collective-permute-start | bytes 1179656 | tf_op jit(solution)/shard_map/ppermute | solution.py:457
  36.9 29.0 %collective-permute-start.4 = (bf16[256,768]{1,0:T(8,128)(2,1)S(1)}, bf16[256,768]{1,0:T(8,128)(2,1)S(1)}, u32[]{:S(2)}, u32[]{:S(2)}) collective-permute-start(bf16[256,768]{1,0:T(8,128)(2,1)S(1)} %convolution_convert_fusion.18), channel_id=1, source_target_pairs={{0,2},{1,3},{2,0},{3,1},{4,6},{5,7},{6,4},{7,5},{8,10},{9,11},{10,... | collective-permute-start | bytes 1179656 | tf_op jit(solution)/shard_map/ppermute | solution.py:457
  39.5 26.4 %collective-permute-start.5 = (bf16[256,768]{1,0:T(8,128)(2,1)S(1)}, bf16[256,768]{1,0:T(8,128)(2,1)S(1)}, u32[]{:S(2)}, u32[]{:S(2)}) collective-permute-start(bf16[256,768]{1,0:T(8,128)(2,1)S(1)} %convolution_convert_fusion.17), channel_id=1, source_target_pairs={{0,3},{1,0},{2,1},{3,2},{4,7},{5,4},{6,5},{7,6},{8,11},{9,8},{10,9... | collective-permute-start | bytes 1179656 | tf_op jit(solution)/shard_map/ppermute | solution.py:457
  40.8 113.2 %collective-permute-start.12 = (bf16[256,768]{1,0:T(8,128)(2,1)}, bf16[256,768]{1,0:T(8,128)(2,1)S(1)}, u32[]{:S(2)}, u32[]{:S(2)}) collective-permute-start(bf16[256,768]{1,0:T(8,128)(2,1)} %convolution_convert_fusion.15), channel_id=1, source_target_pairs={{0,1},{1,2},{2,3},{3,0},{4,5},{5,6},{6,7},{7,4},{8,9},{9,10},{10,1... | collective-permute-start | bytes 1179656 | tf_op jit(solution)/shard_map/ppermute | solution.py:457
  41.7 144.5 %collective-permute-start.13 = (bf16[256,768]{1,0:T(8,128)(2,1)}, bf16[256,768]{1,0:T(8,128)(2,1)}, u32[]{:S(2)}, u32[]{:S(2)}) collective-permute-start(bf16[256,768]{1,0:T(8,128)(2,1)} %convolution_convert_fusion.14), channel_id=1, source_target_pairs={{0,2},{1,3},{2,0},{3,1},{4,6},{5,7},{6,4},{7,5},{8,10},{9,11},{10,... | collective-permute-start | bytes 1179656 | tf_op jit(solution)/shard_map/ppermute | solution.py:457
  56.8 9.1 %copy-start.43 = (bf16[768,768]{1,0:T(8,128)(2,1)S(1)}, bf16[768,768]{1,0:T(8,128)(2,1)}, u32[]{:S(2)}) copy-start(bf16[768,768]{1,0:T(8,128)(2,1)} %param.26) | copy-start | bytes 3538948
  57.0 9.8 %copy-start.40 = (f32[2,512,768]{2,1,0:T(8,128)}, f32[2,512,768]{2,1,0:T(8,128)S(1)}, u32[]{:S(2)}) copy-start(f32[2,512,768]{2,1,0:T(8,128)S(1)} %fusion.107) | copy-start | bytes 9437188
  69.2 50.9 %collective-permute-start.6 = (bf16[256,768]{1,0:T(8,128)(2,1)S(1)}, bf16[256,768]{1,0:T(8,128)(2,1)S(1)}, u32[]{:S(2)}, u32[]{:S(2)}) collective-permute-start(bf16[256,768]{1,0:T(8,128)(2,1)S(1)} %convolution_convert_fusion.11), channel_id=1, source_target_pairs={{0,1},{1,2},{2,3},{3,0},{4,5},{5,6},{6,7},{7,4},{8,9},{9,10},{10,1... | collective-permute-start | bytes 1179656 | tf_op jit(solution)/shard_map/ppermute | solution.py:457
  103.4 21.3 %collective-permute-start.7 = (bf16[256,768]{1,0:T(8,128)(2,1)S(1)}, bf16[256,768]{1,0:T(8,128)(2,1)S(1)}, u32[]{:S(2)}, u32[]{:S(2)}) collective-permute-start(bf16[256,768]{1,0:T(8,128)(2,1)S(1)} %convolution_convert_fusion.10), channel_id=1, source_target_pairs={{0,2},{1,3},{2,0},{3,1},{4,6},{5,7},{6,4},{7,5},{8,10},{9,11},{10,... | collective-permute-start | bytes 1179656 | tf_op jit(solution)/shard_map/ppermute | solution.py:457
  103.4 26.4 %collective-permute-start.8 = (bf16[256,768]{1,0:T(8,128)(2,1)S(1)}, bf16[256,768]{1,0:T(8,128)(2,1)S(1)}, u32[]{:S(2)}, u32[]{:S(2)}) collective-permute-start(bf16[256,768]{1,0:T(8,128)(2,1)S(1)} %convolution_convert_fusion.9), channel_id=1, source_target_pairs={{0,3},{1,0},{2,1},{3,2},{4,7},{5,4},{6,5},{7,6},{8,11},{9,8},{10,9... | collective-permute-start | bytes 1179656 | tf_op jit(solution)/shard_map/ppermute | solution.py:457
  120.2 67.4 %collective-permute-start.14 = (bf16[256,768]{1,0:T(8,128)(2,1)}, bf16[256,768]{1,0:T(8,128)(2,1)S(1)}, u32[]{:S(2)}, u32[]{:S(2)}) collective-permute-start(bf16[256,768]{1,0:T(8,128)(2,1)} %convolution_convert_fusion.13), channel_id=1, source_target_pairs={{0,3},{1,0},{2,1},{3,2},{4,7},{5,4},{6,5},{7,6},{8,11},{9,8},{10,9... | collective-permute-start | bytes 1179656 | tf_op jit(solution)/shard_map/ppermute | solution.py:457
  134.5 55.9 %collective-permute-start.9 = (bf16[256,768]{1,0:T(8,128)(2,1)S(1)}, bf16[256,768]{1,0:T(8,128)(2,1)S(1)}, u32[]{:S(2)}, u32[]{:S(2)}) collective-permute-start(bf16[256,768]{1,0:T(8,128)(2,1)S(1)} %convolution_convert_fusion.7), channel_id=1, source_target_pairs={{0,1},{1,2},{2,3},{3,0},{4,5},{5,6},{6,7},{7,4},{8,9},{9,10},{10,1... | collective-permute-start | bytes 1179656 | tf_op jit(solution)/shard_map/ppermute | solution.py:457
  150.7 40.0 %collective-permute-start.10 = (bf16[256,768]{1,0:T(8,128)(2,1)S(1)}, bf16[256,768]{1,0:T(8,128)(2,1)S(1)}, u32[]{:S(2)}, u32[]{:S(2)}) collective-permute-start(bf16[256,768]{1,0:T(8,128)(2,1)S(1)} %convolution_convert_fusion.6), channel_id=1, source_target_pairs={{0,2},{1,3},{2,0},{3,1},{4,6},{5,7},{6,4},{7,5},{8,10},{9,11},{10,... | collective-permute-start | bytes 1179656 | tf_op jit(solution)/shard_map/ppermute | solution.py:457
  154.0 36.6 %collective-permute-start.11 = (bf16[256,768]{1,0:T(8,128)(2,1)S(1)}, bf16[256,768]{1,0:T(8,128)(2,1)S(1)}, u32[]{:S(2)}, u32[]{:S(2)}) collective-permute-start(bf16[256,768]{1,0:T(8,128)(2,1)S(1)} %convolution_convert_fusion.5), channel_id=1, source_target_pairs={{0,3},{1,0},{2,1},{3,2},{4,7},{5,4},{6,5},{7,6},{8,11},{9,8},{10,9... | collective-permute-start | bytes 1179656 | tf_op jit(solution)/shard_map/ppermute | solution.py:457
  186.2 36.9 %collective-permute-start.15 = (bf16[256,768]{1,0:T(8,128)(2,1)S(1)}, bf16[256,768]{1,0:T(8,128)(2,1)S(1)}, u32[]{:S(2)}, u32[]{:S(2)}) collective-permute-start(bf16[256,768]{1,0:T(8,128)(2,1)S(1)} %get-tuple-element.181), channel_id=1, source_target_pairs={{0,3},{1,0},{2,1},{3,2},{4,7},{5,4},{6,5},{7,6},{8,11},{9,8},{10,9... | collective-permute-start | bytes 1179656 | tf_op jit(solution)/shard_map/ppermute | solution.py:457
  188.4 34.7 %collective-permute-start.16 = (bf16[256,768]{1,0:T(8,128)(2,1)S(1)}, bf16[256,768]{1,0:T(8,128)(2,1)S(1)}, u32[]{:S(2)}, u32[]{:S(2)}) collective-permute-start(bf16[256,768]{1,0:T(8,128)(2,1)S(1)} %get-tuple-element.182), channel_id=1, source_target_pairs={{0,2},{1,3},{2,0},{3,1},{4,6},{5,7},{6,4},{7,5},{8,10},{9,11},{10,... | collective-permute-start | bytes 1179656 | tf_op jit(solution)/shard_map/ppermute | solution.py:457
  190.4 32.7 %collective-permute-start.17 = (bf16[256,768]{1,0:T(8,128)(2,1)S(1)}, bf16[256,768]{1,0:T(8,128)(2,1)S(1)}, u32[]{:S(2)}, u32[]{:S(2)}) collective-permute-start(bf16[256,768]{1,0:T(8,128)(2,1)S(1)} %get-tuple-element.183), channel_id=1, source_target_pairs={{0,1},{1,2},{2,3},{3,0},{4,5},{5,6},{6,7},{7,4},{8,9},{9,10},{10,1... | collective-permute-start | bytes 1179656 | tf_op jit(solution)/shard_map/ppermute | solution.py:457
  191.6 37.5 %copy-start.24 = (bf16[1024,768]{1,0:T(8,128)(2,1)S(1)}, bf16[1024,768]{1,0:T(8,128)(2,1)}, u32[]{:S(2)}) copy-start(bf16[1024,768]{1,0:T(8,128)(2,1)} %get-tuple-element.188.refs_8_) | copy-start | bytes 4718596
  224.6 33.6 %collective-permute-start.18 = (bf16[256,768]{1,0:T(8,128)(2,1)}, bf16[256,768]{1,0:T(8,128)(2,1)}, u32[]{:S(2)}, u32[]{:S(2)}) collective-permute-start(bf16[256,768]{1,0:T(8,128)(2,1)} %get-tuple-element.195), channel_id=1, source_target_pairs={{0,3},{1,0},{2,1},{3,2},{4,7},{5,4},{6,5},{7,6},{8,11},{9,8},{10,9... | collective-permute-start | bytes 1179656 | tf_op jit(solution)/shard_map/ppermute | solution.py:457
  228.3 31.7 %collective-permute-start.19 = (bf16[256,768]{1,0:T(8,128)(2,1)}, bf16[256,768]{1,0:T(8,128)(2,1)}, u32[]{:S(2)}, u32[]{:S(2)}) collective-permute-start(bf16[256,768]{1,0:T(8,128)(2,1)} %get-tuple-element.196), channel_id=1, source_target_pairs={{0,2},{1,3},{2,0},{3,1},{4,6},{5,7},{6,4},{7,5},{8,10},{9,11},{10,... | collective-permute-start | bytes 1179656 | tf_op jit(solution)/shard_map/ppermute | solution.py:457
  228.3 31.7 %collective-permute-start.20 = (bf16[256,768]{1,0:T(8,128)(2,1)}, bf16[256,768]{1,0:T(8,128)(2,1)}, u32[]{:S(2)}, u32[]{:S(2)}) collective-permute-start(bf16[256,768]{1,0:T(8,128)(2,1)} %get-tuple-element.197), channel_id=1, source_target_pairs={{0,1},{1,2},{2,3},{3,0},{4,5},{5,6},{6,7},{7,4},{8,9},{9,10},{10,1... | collective-permute-start | bytes 1179656 | tf_op jit(solution)/shard_map/ppermute | solution.py:457
  277.7 7.7 %copy-start.37 = (f32[1,512,768]{2,1,0:T(8,128)S(1)}, f32[1,512,768]{2,1,0:T(8,128)}, u32[]{:S(2)}) copy-start(f32[1,512,768]{2,1,0:T(8,128)} %copy-done.36) | copy-start | bytes 4718596
  277.7 195.9 %reduce-scatter.2.cloned.1.call-start = ((), (), s32[]{:S(2)}) async-start(), calls=%async_computation.2 | async-start | bytes 10616832 | tf_op jit(solution)/shard_map/reduce_scatter | solution.py:609
  278.3 341.2 %all-reduce.8.cloned.1.call-start = ((), (), s32[]{:S(2)}) async-start(), calls=%async_computation.3 | async-start | bytes 7127040 | tf_op jit(solution)/shard_map/psum | solution.py:503
  278.3 9.2 %copy-start.39 = (f32[1,512,768]{2,1,0:T(8,128)S(1)}, f32[1,512,768]{2,1,0:T(8,128)}, u32[]{:S(2)}) copy-start(f32[1,512,768]{2,1,0:T(8,128)} %copy-done.38) | copy-start | bytes 4718596
  278.3 9.2 %copy-start.44 = (bf16[768,768]{1,0:T(8,128)(2,1)S(1)}, bf16[768,768]{1,0:T(8,128)(2,1)}, u32[]{:S(2)}) copy-start(bf16[768,768]{1,0:T(8,128)(2,1)} %param.26) | copy-start | bytes 3538948
  278.4 74.3 %collective-permute-start.21 = (bf16[256,768]{1,0:T(8,128)(2,1)}, bf16[256,768]{1,0:T(8,128)(2,1)}, u32[]{:S(2)}, u32[]{:S(2)}) collective-permute-start(bf16[256,768]{1,0:T(8,128)(2,1)} %get-tuple-element.213), channel_id=1, source_target_pairs={{0,3},{1,0},{2,1},{3,2},{4,7},{5,4},{6,5},{7,6},{8,11},{9,8},{10,9... | collective-permute-start | bytes 1179656 | tf_op jit(solution)/shard_map/ppermute | solution.py:457
  279.9 163.4 %collective-permute-start.22 = (bf16[256,768]{1,0:T(8,128)(2,1)}, bf16[256,768]{1,0:T(8,128)(2,1)}, u32[]{:S(2)}, u32[]{:S(2)}) collective-permute-start(bf16[256,768]{1,0:T(8,128)(2,1)} %get-tuple-element.214), channel_id=1, source_target_pairs={{0,2},{1,3},{2,0},{3,1},{4,6},{5,7},{6,4},{7,5},{8,10},{9,11},{10,... | collective-permute-start | bytes 1179656 | tf_op jit(solution)/shard_map/ppermute | solution.py:457
  281.2 162.1 %collective-permute-start.23 = (bf16[256,768]{1,0:T(8,128)(2,1)S(1)}, bf16[256,768]{1,0:T(8,128)(2,1)}, u32[]{:S(2)}, u32[]{:S(2)}) collective-permute-start(bf16[256,768]{1,0:T(8,128)(2,1)S(1)} %copy-done.6), channel_id=1, source_target_pairs={{0,1},{1,2},{2,3},{3,0},{4,5},{5,6},{6,7},{7,4},{8,9},{9,10},{10,1... | collective-permute-start | bytes 1179656 | tf_op jit(solution)/shard_map/ppermute | solution.py:457
  283.1 160.2 %collective-permute-start.24 = (bf16[256,768]{1,0:T(8,128)(2,1)}, bf16[256,768]{1,0:T(8,128)(2,1)}, u32[]{:S(2)}, u32[]{:S(2)}) collective-permute-start(bf16[256,768]{1,0:T(8,128)(2,1)} %get-tuple-element.217), channel_id=1, source_target_pairs={{0,3},{1,0},{2,1},{3,2},{4,7},{5,4},{6,5},{7,6},{8,11},{9,8},{10,9... | collective-permute-start | bytes 1179656 | tf_op jit(solution)/shard_map/ppermute | solution.py:457
  285.4 157.9 %collective-permute-start.25 = (bf16[256,768]{1,0:T(8,128)(2,1)}, bf16[256,768]{1,0:T(8,128)(2,1)}, u32[]{:S(2)}, u32[]{:S(2)}) collective-permute-start(bf16[256,768]{1,0:T(8,128)(2,1)} %get-tuple-element.218), channel_id=1, source_target_pairs={{0,2},{1,3},{2,0},{3,1},{4,6},{5,7},{6,4},{7,5},{8,10},{9,11},{10,... | collective-permute-start | bytes 1179656 | tf_op jit(solution)/shard_map/ppermute | solution.py:457
  289.7 62.5 %copy-start.64 = (f32[3,512,32]{1,2,0:T(8,128)S(1)}, f32[3,512,32]{1,2,0:T(8,128)}, u32[]{:S(2)}) copy-start(f32[3,512,32]{1,2,0:T(8,128)} %constant.142.clone) | copy-start | bytes 589828
  352.6 90.7 %collective-permute-start.26 = (bf16[256,768]{1,0:T(8,128)(2,1)}, bf16[256,768]{1,0:T(8,128)(2,1)}, u32[]{:S(2)}, u32[]{:S(2)}) collective-permute-start(bf16[256,768]{1,0:T(8,128)(2,1)} %copy-done.7), channel_id=1, source_target_pairs={{0,1},{1,2},{2,3},{3,0},{4,5},{5,6},{6,7},{7,4},{8,9},{9,10},{10,1... | collective-permute-start | bytes 1179656 | tf_op jit(solution)/shard_map/ppermute | solution.py:457
  449.7 32.1 %collective-permute-start.27 = (bf16[512,768]{1,0:T(8,128)(2,1)}, bf16[512,768]{1,0:T(8,128)(2,1)}, u32[]{:S(2)}, u32[]{:S(2)}) collective-permute-start(bf16[512,768]{1,0:T(8,128)(2,1)} %fusion.70), channel_id=1, source_target_pairs={{0,4},{4,0},{1,5},{5,1},{2,6},{6,2},{3,7},{7,3},{8,12},{12,8},{9,1... | collective-permute-start | bytes 2359304 | tf_op jit(solution)/shard_map/ppermute | solution.py:466
  464.7 19.9 %collective-permute-start.28 = (f32[512,768]{1,0:T(8,128)}, f32[512,768]{1,0:T(8,128)}, u32[]{:S(2)}, u32[]{:S(2)}) collective-permute-start(f32[512,768]{1,0:T(8,128)} %dynamic-slice_bitcast_fusion), channel_id=1, source_target_pairs={{0,4},{4,0},{1,5},{5,1},{2,6},{6,2},{3,7},{7,3},{8,12},{12,8},{9,1... | collective-permute-start | bytes 4718600 | tf_op jit(solution)/shard_map/ppermute | solution.py:466
  (78 other events, 176.4 us)
Sparse Core Ops, SparseCore 0:
  277.8 159.1 all-reduce.5
  480.2 139.1 all-reduce.7
Sparse Core Ops, SparseCore 1:
  282.1 76.6 reduce-scatter.1

commit v3 on v2

--- a/solution.py
+++ b/solution.py
@@ -205,7 +205,7 @@
         name="attend",
     )(lines, q, k, v)
 
-def bwd_kernel(lines_ref, q_ref, k_ref, v_ref, g_ref, dq_ref, dk_ref, dv_ref, diag_ref, far_ref, band_ref, acc_ref, far_acc, dk_acc, dv_acc):
+def bwd_kernel(lines_ref, fold_ref, q_ref, k_ref, v_ref, g_ref, grad_ref, bias_ref, band_ref, acc_ref, far_acc, dk_acc, dv_acc):
     n = q_ref.shape[0] // QB
     lane = lax.broadcasted_iota(jnp.int32, (QB, 128), 1)
     for h in range(2):
@@ -255,33 +255,48 @@
                 dv_acc[...] += dv
                 dk_acc[...] += dk
             grads.append(lax.dot_general(low, k_ref[...], (((0,), (0,)), ((), ())), preferred_element_type=jnp.float32))
-        dq_ref[rows, :] = jnp.where(lane < 64, grads[0], grads[1]).astype(jnp.bfloat16)
-    dk_ref[...] = dk_acc[...].astype(jnp.bfloat16)
-    dv_ref[...] = dv_acc[...].astype(jnp.bfloat16)
+        grad_ref[0, rows, :] = jnp.where(lane < 64, grads[0], grads[1]).astype(jnp.bfloat16)
+    grad_ref[1] = dk_acc[...].astype(jnp.bfloat16)
+    grad_ref[2] = dv_acc[...].astype(jnp.bfloat16)
     row = lax.broadcasted_iota(jnp.int32, (8, 2 * QB), 0)
     for h in range(2):
+        total = jnp.zeros((8, 128), jnp.float32)
         for t in range(3):
             tile = acc_ref[h, t * QB:(t + 1) * QB, :]
             wide = jnp.concatenate([tile, jnp.zeros_like(tile)], axis=1)
-            groups = sum(pltpu.roll(wide[8 * e:8 * e + 8], QB - 8 * e, 1) for e in range(QB // 8))
-            turned = groups * (row == 0).astype(jnp.float32)
+            moved = sum(pltpu.roll(wide[8 * e:8 * e + 8], QB - 8 * e, 1) for e in range(QB // 8))
+            turned = jnp.where(row == 0, moved, 0.0)
             for e in range(1, 8):
-                turned = turned + pltpu.roll(jnp.where(row == e, groups, 0.0), 2 * QB - e, 1)
-            diag_ref[h, t:t + 1, :] = jnp.sum(turned, axis=0, keepdims=True)
-        far_ref[h, 0:1] = jnp.sum(far_acc[h, 0], axis=0, keepdims=True)
-        far_ref[h, 1:2] = jnp.sum(far_acc[h, 1], axis=0, keepdims=True)
-
-def attend_back(q, k, v, g, lines):
-    length, width = q.shape
-    heads = width // 64
-    col = pl.BlockSpec((length, 128), lambda h: (0, h))
-    out = jax.ShapeDtypeStruct((length, width), jnp.bfloat16)
-    dq, dk, dv, diag, far = pl.pallas_call(
-        bwd_kernel,
-        grid=(width // 128,),
-        in_specs=[pl.BlockSpec((2, 2, 4 * QB), lambda h: (h, 0, 0)), col, col, col, col],
-        out_specs=[col, col, col, pl.BlockSpec((2, 3, 2 * QB), lambda h: (h, 0, 0)), pl.BlockSpec((2, 2, QB), lambda h: (h, 0, 0))],
-        out_shape=[out, out, out, jax.ShapeDtypeStruct((heads, 3, 2 * QB), jnp.float32), jax.ShapeDtypeStruct((heads, 2, QB), jnp.float32)],
+                turned = turned + pltpu.roll(jnp.where(row == e, moved, 0.0), 2 * QB - e, 1)
+            total = total + jnp.dot(turned, fold_ref[t], precision=lax.Precision.HIGHEST, preferred_element_type=jnp.float32)
+        total = jnp.sum(total, axis=0, keepdims=True)
+        ends = [jnp.sum(jnp.sum(far_acc[h, side], axis=0, keepdims=True), axis=1, keepdims=True) for side in range(2)]
+        column = lax.broadcasted_iota(jnp.int32, (1, 128), 1)
+        total = total + jnp.where(column == 15, ends[0], 0.0) + jnp.where(column == 31, ends[1], 0.0)
+        bias_ref[0, h:h + 1, :] = total
+
+
+def attend_back(q, k, v, g, lines, first_pair, pairs, total_pairs=None, earlier=None):
+    length = q.shape[0]
+    r = (np.arange(3)[:, None] - 1) * QB - (np.arange(2 * QB)[None] - QB)
+    fold = (bucket_np(r)[..., None] == np.arange(128)).astype(np.float32)
+    col = pl.BlockSpec((length, 128), lambda h: (0, h + first_pair))
+    offset = first_pair % total_pairs if total_pairs else 0
+    kept = [] if earlier is None else [earlier]
+    grads, bias = pl.pallas_call(
+        lambda *refs: bwd_kernel(*refs[:6], *refs[6 + len(kept):]),
+        grid=(pairs,),
+        in_specs=[
+            pl.BlockSpec((2, 2, 4 * QB), lambda h: (h + first_pair, 0, 0)),
+            pl.BlockSpec((3, 2 * QB, 128), lambda h: (0, 0, 0)),
+            col, col, col, col,
+        ]
+        + [pl.BlockSpec(memory_space=pl.ANY)] * len(kept),
+        out_specs=[pl.BlockSpec((3, length, 128), lambda h: (0, 0, h + offset)), pl.BlockSpec((1, 2, 128), lambda h: (h, 0, 0))],
+        out_shape=[
+            jax.ShapeDtypeStruct((3, length, 128 * (total_pairs or pairs)), jnp.bfloat16),
+            jax.ShapeDtypeStruct((pairs, 2, 128), jnp.float32),
+        ],
         scratch_shapes=[
             pltpu.VMEM((2, 3 * QB, QB), jnp.float32),
             pltpu.VMEM((2, 3 * QB, QB), jnp.float32),
@@ -290,22 +305,19 @@
             pltpu.VMEM((length, 128), jnp.float32),
         ],
         compiler_params=pltpu.CompilerParams(vmem_limit_bytes=48 << 20),
-        cost_estimate=pl.CostEstimate(flops=84 * length * length * width, bytes_accessed=14 * length * width, transcendentals=length * length * width // 64),
+        cost_estimate=pl.CostEstimate(
+            flops=84 * length * length * 128 * pairs, bytes_accessed=14 * length * 128 * pairs, transcendentals=2 * length * length * pairs
+        ),
+        input_output_aliases={6: 0} if kept else {},
         name="attend_back",
-    )(lines, q, k, v, g)
-    r = (np.arange(3)[:, None] - 1) * QB - (np.arange(2 * QB)[None] - QB)
-    onehot = (bucket_np(r)[..., None] == np.arange(32)).astype(np.float32)
-    dbias = jnp.einsum("htx,txb->bh", diag, jnp.asarray(onehot), precision=lax.Precision.HIGHEST)
-    far = jnp.sum(far, axis=2)
-    dbias = dbias.at[15].add(far[:, 0]).at[31].add(far[:, 1])
-    return dq, dk, dv, dbias
-
-
-def expert_kernel(label_ref, *refs):
-    count = (len(refs) - 10) // 4
+    )(lines, jnp.asarray(fold), q, k, v, g, *kept)
+    return grads, bias.reshape(2 * pairs, 128)
+
+
+def expert_kernel(count, label_ref, *refs):
     x_refs, u_refs = refs[:count], refs[count : 2 * count]
     router_ref, win_ref, wout_ref = refs[2 * count : 2 * count + 3]
-    rest = refs[2 * count + 3 :]
+    rest = refs[len(refs) - 7 - 2 * count :]
     rows_refs, back_refs = rest[:count], rest[count : 2 * count]
     g_ref, hid_ref, pre_ref, drouter_ref, prob_ref, out_acc, back_acc = rest[2 * count :]
     step = pl.program_id(0)
@@ -361,7 +373,7 @@
         drouter_ref[...] = total
 
 
-def run_expert(label, pieces, upstream_pieces, router_wide, w_in, w_out, chunk=768):
+def run_expert(label, pieces, upstream_pieces, router_wide, w_in, w_out, group, group_count, earlier, chunk=768):
     count, (tile, width) = len(pieces), pieces[0].shape
     rows, inner = count * tile, w_in.shape[1]
     once = pl.Buffered(1)
@@ -369,7 +381,7 @@
     inner_block = pl.BlockSpec((rows, chunk), lambda f, lab: (0, f))
     low = lambda *shape: jax.ShapeDtypeStruct(shape, jnp.bfloat16)
     outs = pl.pallas_call(
-        expert_kernel,
+        lambda *refs: expert_kernel(count, *refs),
         grid_spec=pltpu.PrefetchScalarGridSpec(
             num_scalar_prefetch=1,
             grid=(inner // chunk,),
@@ -377,8 +389,11 @@
                 pl.BlockSpec((width, 128), lambda f, lab: (0, 0), pipeline_mode=once),
                 pl.BlockSpec((width, chunk), lambda f, lab: (0, f)),
                 pl.BlockSpec((chunk, width), lambda f, lab: (f, 0)),
-            ],
-            out_specs=[piece] * (2 * count) + [
+            ]
+            + [pl.BlockSpec(memory_space=pl.ANY)] * len(earlier),
+            out_specs=[pl.BlockSpec((tile, width), lambda f, lab: (group, 0), pipeline_mode=once)] * count
+            + [piece] * count
+            + [
                 pl.BlockSpec((rows, width), lambda f, lab: (0, 0), pipeline_mode=once),
                 inner_block,
                 inner_block,
@@ -390,12 +405,14 @@
                 pltpu.VMEM((rows, width), jnp.float32),
             ],
         ),
-        out_shape=[low(tile, width)] * (2 * count)
+        out_shape=[low(group_count * tile, width)] * count
+        + [low(tile, width)] * count
         + [low(rows, width), low(rows, inner), low(rows, inner), jax.ShapeDtypeStruct((width, 128), jnp.float32)],
         compiler_params=pltpu.CompilerParams(vmem_limit_bytes=48 << 20),
         cost_estimate=pl.CostEstimate(flops=16 * rows * width * inner, bytes_accessed=8 * width * inner, transcendentals=rows * inner),
+        input_output_aliases={2 * count + 4 + at: at for at in range(len(earlier))},
         name="experts",
-    )(label, *pieces, *upstream_pieces, router_wide, w_in, w_out)
+    )(label, *pieces, *upstream_pieces, router_wide, w_in, w_out, *earlier)
     return outs[:count], outs[count : 2 * count], outs[2 * count :]
 
 
@@ -438,7 +455,9 @@
         out_shape=jax.ShapeDtypeStruct((inner, 2 * width), jnp.bfloat16),
         scratch_shapes=[pltpu.VMEM((width, groups * rows), jnp.bfloat16)] * 2,
         compiler_params=pltpu.CompilerParams(vmem_limit_bytes=48 << 20),
-        cost_estimate=pl.CostEstimate(flops=6 * groups * rows * width * inner, bytes_accessed=4 * (groups * rows + width) * inner, transcendentals=0),
+        cost_estimate=pl.CostEstimate(
+            flops=6 * groups * rows * width * inner, bytes_accessed=4 * (groups * rows + width) * inner, transcendentals=0
+        ),
         name="expert_grads",
     )(*pieces, *grads, *hiddens, *pre_grads)
 
@@ -489,29 +508,65 @@
     return jnp.einsum("sxd,sxe->de", left, right, preferred_element_type=jnp.float32)
 
 
-def split_rows(flat):
-    high = flat.astype(jnp.bfloat16)
-    return high, (flat - high.astype(jnp.float32)).astype(jnp.bfloat16)
-
-
-def sum_all(matrices, smalls):
-    width = matrices[0].shape[1]
-    flat = jnp.concatenate([jnp.ravel(small) for small in smalls])
-    fill = -flat.shape[0] % (8 * width)
-    flat = jnp.pad(flat, (0, fill)).reshape(-1, width)
-    packed = jnp.concatenate([matrix.astype(jnp.bfloat16) for matrix in matrices] + list(split_rows(flat)))
-    packed = lax.psum(packed, ("dp", "ctx", "expert")).astype(jnp.float32)
-    outs, at = [], 0
-    for matrix in matrices:
-        outs.append(packed[at : at + matrix.shape[0]])
-        at += matrix.shape[0]
-    rows = flat.shape[0]
-    flat = (packed[at : at + rows] + packed[at + rows : at + 2 * rows]).reshape(-1)
-    at = 0
-    for small in smalls:
-        outs.append(flat[at : at + small.size].reshape(small.shape))
-        at += small.size
-    return outs
+def pack_sums(matrices, small=None):
+    parts = [matrix.astype(jnp.bfloat16) for matrix in matrices]
+    if small is not None:
+        small = jnp.pad(small, ((0, -small.shape[0] % 64), (0, parts[0].shape[1] - small.shape[1])))
+        high = small.astype(jnp.bfloat16)
+        parts += [high, (small - high.astype(jnp.float32)).astype(jnp.bfloat16)]
+    return jnp.concatenate(parts)
+
+
+def add_low(*parts):
+    return sum(part.astype(jnp.float32) for part in parts).astype(jnp.bfloat16)
+
+
+def swap(part, axis, turn):
+    return lax.ppermute(part, axis, [(to, to ^ turn) for to in range(lax.axis_size(axis))])
+
+
+class Summing:
+    steps = 4
+
+    def __init__(self, packed):
+        self.core, self.plane = lax.axis_index("ctx"), lax.axis_index("dp")
+        self.planes = lax.axis_size("dp")
+        self.part = packed.reshape(self.planes, 2, -1, packed.shape[1])
+        self.step = 0
+
+    def sends(self):
+        if self.step == 0:
+            return [lax.dynamic_index_in_dim(self.part, 1 - self.core, 1, keepdims=False)]
+        if self.step == 1:
+            return [
+                lax.dynamic_index_in_dim(self.part, self.plane ^ turn, 0, keepdims=False)
+                for turn in range(1, self.planes)
+            ]
+        return [self.part]
+
+    def move(self, sent):
+        axis, first = (("ctx", 1), ("dp", 1), ("expert", 1), ("expert", 2))[self.step]
+        return [swap(part, axis, first + at) for at, part in enumerate(sent)]
+
+    def take(self, arrived):
+        if self.step == 0:
+            self.part = lax.dynamic_index_in_dim(self.part, self.core, 1, keepdims=False)
+        elif self.step == 1:
+            self.part = lax.dynamic_index_in_dim(self.part, self.plane, 0, keepdims=False)
+        self.part = add_low(self.part, *arrived)
+        self.step += 1
+
+    def finish(self):
+        return lax.all_gather(self.part, ("dp", "ctx"), axis=0, tiled=True)
+
+
+def matrix_of(sums, index, rows):
+    return sums[index * rows : (index + 1) * rows]
+
+
+def small_of(sums, start):
+    high, low = jnp.split(sums[start:].astype(jnp.float32), 2)
+    return high + low
 
 
 def per_device(
@@ -561,7 +616,7 @@
     values = wide_dot(attn_in, value_weight).astype(jnp.bfloat16)
     sorted_upstream = [sort_rows(group, cotangent[group]) for group in groups]
     sorted_upstream, queries = together((sorted_upstream, queries))
-    upstream = [exchange(rows, "expert", 1) for rows in sorted_upstream]
+    upstream = [exchange(sorted_upstream[0], "expert", 1)]
     if whole_seq:
         lines = bias_lines(bias_table)
         flat = (seq_count * local_len, model_width)
@@ -583,7 +638,8 @@
         if at == 0:
             upstream[0] = in_flight
         else:
-            arrived[-1] = in_flight
+            arrived[-1], sorted_upstream[at] = together((in_flight, sorted_upstream[at]))
+            upstream.append(exchange(sorted_upstream[at], "expert", 1))
         attended_groups.append(rows)
         residual1.append(inputs[group] + wide_dot(rows, output_weight))
         scale2.append(norm_scale(residual1[-1]))
@@ -595,19 +651,20 @@
     router_wide = jnp.pad(router_weight, ((0, 0), (0, 128 - router_weight.shape[1])))
     label = label.astype(jnp.int32).reshape(1)
     done, back = [], []
-    for rows, grads in zip(arrived, upstream):
-        result = run_expert(label, rows, grads, router_wide, w_in[0], w_out[0])
+    for at, (rows, grads) in enumerate(zip(arrived, upstream)):
+        earlier = done[-1][0] if done else []
+        result = run_expert(label, rows, grads, router_wide, w_in[0], w_out[0], at, len(groups), earlier)
         if back:
             result, back[-1] = together((result, back[-1]))
         done.append(result)
         back.append(exchange(result[1], "expert", -1))
-    rows_out = [item[0] for item in done]
+    rows_out = done[-1][0]
     grad_rows, hiddens, pre_grads, grad_router = zip(*[item[2] for item in done])
-    grad_router = sum(grad_router)[:, : router_weight.shape[1]]
+    grad_router = sum(grad_router)[:, : router_weight.shape[1]].T
     grad_experts = expert_grads(sum(arrived, []), grad_rows, hiddens, pre_grads)
     grad_experts, back[-1], rows_out = together((grad_experts, back[-1], rows_out))
     grad_experts = lax.psum_scatter(grad_experts, ("dp", "ctx"), scatter_dimension=0, tiled=True)
-    returned = [exchange(list(rows), "expert", -1) for rows in rows_out]
+    returned = exchange(list(rows_out), "expert", -1)
     residual_grad, attn_grad, mixed_grad, grad_norm2 = [], [], [], 0.0
     for group, rows, scale, pieces in zip(groups, residual1, scale2, back):
         norm2_back, gain_part = norm_back(rows, scale, norm2_gain, place_rows(group, pieces))
@@ -617,32 +674,85 @@
         mixed_grad.append(wide_dot_back(attn_grad[-1], output_weight).astype(jnp.bfloat16))
     grad_w_output = sum(weight_dot(left, right) for left, right in zip(attended, attn_grad))
     residual_grad, mixed_grad = jnp.concatenate(residual_grad), jnp.concatenate(mixed_grad)
-    early_sums = sum_all([grad_w_output], [grad_norm2, grad_router])
+    early_small = jnp.concatenate([grad_router, grad_norm2[None]])
+    projections = (query_weight, key_weight, value_weight)
     if whole_seq:
-        *grads, grad_bias = attend_back(*qkv, mixed_grad.reshape(flat), lines)
-        query_low, key_low, value_low = (rows.reshape(tokens.shape) for rows in grads)
+        rows_in = attn_in.reshape(flat)
+        half = model_width // 2
+        pairs = half // 128
+        mixed_grad = mixed_grad.reshape(flat)
+
+        def weight_grads(grads):
+            return [jnp.dot(rows_in.T, part, preferred_element_type=jnp.float32) for part in grads]
+
+        first_grads, first_bias = attend_back(*qkv, mixed_grad, lines, 0, pairs)
+        matrices = [grad_w_output[:, :half], grad_w_output[:, half:]] + weight_grads(first_grads)
+        early = Summing(pack_sums(matrices, early_small.reshape(-1, half)))
+        second_grads, biases = None, [first_bias]
+        for at in range(pairs, 2 * pairs):
+            sent, mixed_grad = together((early.sends(), mixed_grad))
+            moved = early.move(sent)
+            second_grads, bias = attend_back(*qkv, mixed_grad, lines, at, 1, pairs, second_grads)
+            second_grads, moved = together((second_grads, moved))
+            early.take(moved)
+            biases.append(bias)
+        second_grads, returned, grad_experts = together((second_grads, returned, grad_experts))
+        late = Summing(pack_sums(weight_grads(second_grads), jnp.concatenate(biases)))
+        early.take(early.move(early.sends()))
+        early_sums = early.finish()
+        for step in range(late.steps):
+            late.take(late.move(late.sends()))
+        late.part, early_sums = together((late.part, early_sums))
+        sums = [early_sums, late.finish()]
+        norm_in_grad = 0.0
+        low_parts = (first_grads, second_grads)
+        for at, grads in enumerate(low_parts):
+            span = slice(at * 128 * pairs, (at + 1) * 128 * pairs)
+            for kind in range(3):
+                norm_in_grad += jnp.einsum(
+                    "xe,de->xd", grads[kind], projections[kind][:, span], preferred_element_type=jnp.float32
+                )
+        norm_in_grad = norm_in_grad.reshape(tokens.shape)
+        grad_qkv = [
+            jnp.concatenate(
+                [matrix_of(sums[0], 2 + kind, model_width), matrix_of(sums[1], kind, model_width)], axis=1
+            ).astype(jnp.float32)
+            for kind in range(3)
+        ]
+        grad_w_output = jnp.concatenate([matrix_of(sums[0], side, model_width) for side in range(2)], axis=1)
+        small = small_of(sums[0], 5 * model_width).reshape(-1, model_width)
+        grad_bias = small_of(sums[1], 3 * model_width)
     else:
         query_grad, _, diag_grad, key_part, value_part = attend_back_rows(
             queries, keys, values, mixed_grad, log_totals, buckets, bias_table, DH
         )
-        grad_bias = diag_grad.T
-        query_low = query_grad.astype(jnp.bfloat16)
-        key_low = lax.psum_scatter(key_part, "ctx", scatter_dimension=1, tiled=True).astype(jnp.bfloat16)
-        value_low = lax.psum_scatter(value_part, "ctx", scatter_dimension=1, tiled=True).astype(jnp.bfloat16)
-    early_sums, returned, query_low, key_low, value_low = together(
-        (early_sums, returned, query_low, key_low, value_low)
-    )
-    block_out = [rows + place_rows(group, pieces) for group, rows, pieces in zip(groups, residual1, returned)]
+        low_parts = [query_grad.astype(jnp.bfloat16)] + [
+            lax.psum_scatter(part, "ctx", scatter_dimension=1, tiled=True).astype(jnp.bfloat16)
+            for part in (key_part, value_part)
+        ]
+        norm_in_grad = sum(wide_dot_back(*pair) for pair in zip(low_parts, projections))
+        sums = lax.psum(
+            pack_sums([grad_w_output] + [weight_dot(attn_in, rows) for rows in low_parts], early_small),
+            ("dp", "ctx", "expert"),
+        )
+        grad_bias = lax.psum(diag_grad, ("dp", "ctx", "expert"))
+        grad_w_output, *grad_qkv = (matrix_of(sums, kind, model_width).astype(jnp.float32) for kind in range(4))
+        small = small_of(sums, 4 * model_width)
+    grad_bias = grad_bias[: bias_table.shape[1], : bias_table.shape[0]].T
+    grad_norm1 = sum(jnp.sum(grad * weight.astype(jnp.float32), axis=1) for grad, weight in zip(grad_qkv, projections))
+    grad_norm1 = grad_norm1 / norm1_gain
+    grad_w_query, grad_w_key, grad_w_value = grad_qkv
+    grad_w_output = grad_w_output.astype(jnp.float32)
+    experts = router_weight.shape[1]
+    grad_router, grad_norm2 = small[:experts, :].T, small[experts]
+    returned = [piece.reshape(len(groups), -1, model_width) for piece in returned]
+    block_out = [
+        rows + place_rows(group, [piece[at] for piece in returned])
+        for at, (group, rows) in enumerate(zip(groups, residual1))
+    ]
     block_out = jnp.concatenate(block_out).astype(jnp.bfloat16)
-    grad_w_output, grad_norm2, grad_router = early_sums
-    norm_in_grad = wide_dot_back(query_low, query_weight)
-    norm_in_grad = norm_in_grad + wide_dot_back(key_low, key_weight)
-    norm_in_grad = norm_in_grad + wide_dot_back(value_low, value_weight)
-    norm1_back, grad_norm1 = norm_back(inputs, scale1, norm1_gain, norm_in_grad)
+    norm1_back, _ = norm_back(inputs, scale1, norm1_gain, norm_in_grad)
     d_tokens = residual_grad + norm1_back
-    grad_qkv = [weight_dot(attn_in, rows) for rows in (query_low, key_low, value_low)]
-    grad_qkv, grad_experts = together((grad_qkv, grad_experts))
-    grad_w_query, grad_w_key, grad_w_value, grad_bias, grad_norm1 = sum_all(grad_qkv, [grad_bias, grad_norm1])
     if whole_seq:
         block_out, d_tokens = trade(block_out), trade(d_tokens)
     grad_experts = grad_experts.astype(jnp.float32)

time: 644 us -> 537 us (0.83)
  waiting for transfers between devices: 229 us -> 100 us
  matrix products: 47.1 us -> 62.5 us
  starting transfers between devices: 83.4 us -> 72.2 us
  Pallas kernels: 176 us -> 185 us
  other arithmetic: 34.4 us -> 41.5 us
    psum x2 -> x0, waiting for transfers between devices: 210 us -> none  [sum_all(): packed = lax.psum(packed, ('dp', 'ctx', 'expert')).astype(jnp.float32)]
    ppermute x0 -> x12, waiting for transfers between devices: none -> 61 us  [swap(): lax.ppermute(part, axis, [(to, to ^ turn) for to in range(lax.axis_size(a...]
    dot_general x1 -> x12, matrix products: 0.22 us -> 28.2 us  [the longest x6 17.2 us: per_device(): jnp.einsum('xe,de->xd', grads[kind], projections[kind][:, span], preferre...]
    ppermute x24 -> x21, starting transfers between devices: 82 us -> 57.3 us  [exchange(): lax.ppermute(pieces[turn], axis, [(at, (at + sign * turn) % size) for at...]
    ppermute x24 -> x21, waiting for transfers between devices: 18.3 us -> 34 us  [exchange(): lax.ppermute(pieces[turn], axis, [(at, (at + sign * turn) % size) for at...]
    ppermute x0 -> x12, starting transfers between devices: none -> 13.4 us  [swap(): lax.ppermute(part, axis, [(to, to ^ turn) for to in range(lax.axis_size(a...]
    pallas_call x3 -> x6, Pallas kernels: 120 us -> 129 us  [the longest x4 69.7 us: attend_back(): pl.pallas_call(lambda *refs: bwd_kernel(*refs[:6], *refs[6 + len(kept):])...]
    dot_general x5 -> x2, matrix products: 9.61 us -> 1.65 us  [weight_dot(): jnp.einsum('sxd,sxe->de', left, right, preferred_element_type=jnp.float32)]
  transfers between devices with their start and end apart: 32 -> 41, of which waited for: 6 -> 12; matrix products, arithmetic and copies ran while one was open for 13% -> 20% of each run, Pallas kernels for 28% -> 35%
where the time goes in v3:
time: 537 us; the launch traced here: 529 us
  Pallas kernels  185 us (34%)
  waiting for transfers between devices  100 us (19%)
  starting transfers between devices  72.2 us (13%)
  matrix products  62.5 us (12%)
  local copies, waits for them, and re-layouts  52.2 us (10%)
  other arithmetic  41.5 us (8%)
  between operations  15.4 us (3%)
    pallas_call x4, Pallas kernels, attend_back(): pl.pallas_call(lambda *refs: bwd_kernel(*refs[:6], *refs[6 + len(kept):])...  69.7 us
    ppermute x12, waiting for transfers between devices, swap(): lax.ppermute(part, axis, [(to, to ^ turn) for to in range(lax.axis_size(a...  61 us
    pallas_call x2, Pallas kernels, run_expert(): pl.pallas_call(lambda *refs: expert_kernel(count, *refs), grid_spec=pltpu...  59.3 us
    ppermute x21, starting transfers between devices, exchange(): lax.ppermute(pieces[turn], axis, [(at, (at + sign * turn) % size) for at...  57.3 us
    ppermute x21, waiting for transfers between devices, exchange(): lax.ppermute(pieces[turn], axis, [(at, (at + sign * turn) % size) for at...  34 us
    pallas_call x2, Pallas kernels, attend(): pl.pallas_call(lambda *refs: fwd_kernel(first // QB, *refs), grid=(width...  29 us
    unnamed x235, local copies, waits for them, and re-layouts  27.4 us
    pallas_call x1, Pallas kernels, expert_grads(): pl.pallas_call(lambda *refs: expert_grads_kernel(groups, count, *refs), g...  27.1 us
  transfers between devices with their start and end apart: 41, of which 12 were waited for; matrix products, arithmetic and copies ran while one was open for 20% of the time, Pallas kernels for 35%

profile of v3, /device:TPU:0, one launch (start us, length us, event | category | flops | bytes accessed | tf_op | source)
XLA Modules:
  0.0 529.1 jit_solution(9526550813417803252)
XLA Ops:
  8.7 2.1 dynamic-slice_bitcast_fusion.3
  12.7 2.4 reduce-window.6
  35.0 2.6 collective-permute-start.3
  37.7 2.6 collective-permute-start.4
  42.1 14.7 %attend.2 = bf16[512,768]{1,0:T(8,128)(2,1)S(1)} custom-call(f32[12,2,1024]{2,1,0:T(2,128)S(1)} %bitcast.360, bf16[1024,768]{1,0:T(8,128)(2,1)S(1)} %bitcast.372, bf16[1024,768]{1,0:T(8,128)(2,1)S(1)} %bitcast.378, bf16[1024,768]{1,0:T(8,128)(2,1)S(1)} %bitcast.384), custom_call_target="tpu_custom_call" | custom-call | flops 16106127360 | bytes 4718592 | tf_op jit(solution)/shard_map/attend/pallas_call | solution.py:196
  57.0 9.6 %collective-permute-done.4.refs_7_ = bf16[256,768]{1,0:T(8,128)(2,1)S(1)} collective-permute-done((bf16[256,768]{1,0:T(8,128)(2,1)S(1)}, bf16[256,768]{1,0:T(8,128)(2,1)S(1)}, u32[]{:S(2)}, u32[]{:S(2)}) %collective-permute-start.4) | collective-permute-done | bytes 393248 | tf_op jit(solution)/shard_map/ppermute | solution.py:476
  70.8 8.9 %collective-permute-start.6 = (bf16[256,768]{1,0:T(8,128)(2,1)S(1)}, bf16[256,768]{1,0:T(8,128)(2,1)S(1)}, u32[]{:S(2)}, u32[]{:S(2)}) collective-permute-start(bf16[256,768]{1,0:T(8,128)(2,1)S(1)} %convolution_convert_fusion.17), channel_id=1, source_target_pairs={{0,1},{1,2},{2,3},{3,0},{4,5},{5,6},{6,7},{7,4},{8,9},{9,10},{10,1... | collective-permute-start | bytes 1179656 | tf_op jit(solution)/shard_map/ppermute | solution.py:476
  82.0 14.3 %attend.3 = bf16[512,768]{1,0:T(8,128)(2,1)S(1)} custom-call(f32[12,2,1024]{2,1,0:T(2,128)S(1)} %bitcast.361, bf16[1024,768]{1,0:T(8,128)(2,1)S(1)} %bitcast.373, bf16[1024,768]{1,0:T(8,128)(2,1)S(1)} %bitcast.379, bf16[1024,768]{1,0:T(8,128)(2,1)S(1)} %bitcast.385), custom_call_target="tpu_custom_call" | custom-call | flops 16106127360 | bytes 4718592 | tf_op jit(solution)/shard_map/attend/pallas_call | solution.py:196
  96.4 10.3 %collective-permute-done.7.refs_3_.refs_2_ = bf16[256,768]{1,0:T(8,128)(2,1)S(1)} collective-permute-done((bf16[256,768]{1,0:T(8,128)(2,1)S(1)}, bf16[256,768]{1,0:T(8,128)(2,1)S(1)}, u32[]{:S(2)}, u32[]{:S(2)}) %collective-permute-start.7) | collective-permute-done | bytes 393248 | tf_op jit(solution)/shard_map/ppermute | solution.py:476
  112.5 7.9 %collective-permute-start.10 = (bf16[256,768]{1,0:T(8,128)(2,1)}, bf16[256,768]{1,0:T(8,128)(2,1)S(1)}, u32[]{:S(2)}, u32[]{:S(2)}) collective-permute-start(bf16[256,768]{1,0:T(8,128)(2,1)} %convolution_convert_fusion.12), channel_id=1, source_target_pairs={{0,2},{1,3},{2,0},{3,1},{4,6},{5,7},{6,4},{7,5},{8,10},{9,11},{10,... | collective-permute-start | bytes 1179656 | tf_op jit(solution)/shard_map/ppermute | solution.py:476
  122.2 3.4 collective-permute-start.11
  126.9 3.1 collective-permute-start.13
  130.0 9.0 %collective-permute-done.10.refs_3_.refs_6_ = bf16[256,768]{1,0:T(8,128)(2,1)S(1)} collective-permute-done((bf16[256,768]{1,0:T(8,128)(2,1)}, bf16[256,768]{1,0:T(8,128)(2,1)S(1)}, u32[]{:S(2)}, u32[]{:S(2)}) %collective-permute-start.10) | collective-permute-done | bytes 393248 | tf_op jit(solution)/shard_map/ppermute | solution.py:476
  139.8 11.6 %collective-permute-start.14 = (bf16[256,768]{1,0:T(8,128)(2,1)}, bf16[256,768]{1,0:T(8,128)(2,1)S(1)}, u32[]{:S(2)}, u32[]{:S(2)}) collective-permute-start(bf16[256,768]{1,0:T(8,128)(2,1)} %convolution_convert_fusion.19), channel_id=1, source_target_pairs={{0,3},{1,0},{2,1},{3,2},{4,7},{5,4},{6,5},{7,6},{8,11},{9,8},{10,9... | collective-permute-start | bytes 1179656 | tf_op jit(solution)/shard_map/ppermute | solution.py:476
  158.3 29.3 %experts.2 = (bf16[512,768]{1,0:T(8,128)(2,1)S(1)}, bf16[512,768]{1,0:T(8,128)(2,1)}, bf16[512,768]{1,0:T(8,128)(2,1)}, bf16[512,768]{1,0:T(8,128)(2,1)}, bf16[2...) custom-call(s32[1]{0:T(128)} %bitcast.34.refs_0_, ...), custom_call_target="tpu_custom_call" | custom-call | flops 38654705664 | bytes 18874368 | tf_op jit(solution)/shard_map/experts/pallas_call | solution.py:383
  188.5 2.4 collective-permute-start.17
  191.0 30.0 %experts.3 = (bf16[512,768]{1,0:T(8,128)(2,1)S(1)}, bf16[512,768]{1,0:T(8,128)(2,1)}, bf16[512,768]{1,0:T(8,128)(2,1)}, bf16[512,768]{1,0:T(8,128)(2,1)}, bf16[2...) custom-call(s32[1]{0:T(128)} %bitcast.34.refs_0_, ...), custom_call_target="tpu_custom_call", output_to_operand_aliasing={{0}: (12, {}), {1}: (13, {}), {2}: (14, {}), {3}: (15, {})} | custom-call | flops 38654705664 | bytes 18874368 | tf_op jit(solution)/shard_map/experts/pallas_call | solution.py:383
  224.1 2.3 collective-permute-start.18
  229.0 27.1 %expert_grads.1 = bf16[3072,1536]{1,0:T(8,128)(2,1)} custom-call(bf16[256,768]{1,0:T(8,128)(2,1)S(1)} %copy-done.36, bf16[256,768]{1,0:T(8,128)(2,1)S(1)} %copy-done.7, bf16[256,768]{1,0:T(8,128)(2,1)S(1)} %copy-done.10, bf16[256,768]{1,0:T(8,128)(2,1)S(1)} %copy-done.13, bf16[256,768]{1,0:T(8,128)(2,1)S(1)} %copy-done.37, ...), custom_call_target="tpu_custom_call" | custom-call | flops 28991029248 | bytes 34603008 | tf_op jit(solution)/shard_map/expert_grads/pallas_call | solution.py:448
  256.2 5.1 collective-permute-done.19
  263.6 2.7 fusion.6
  267.4 3.2 fusion.42
  273.3 5.1 convert_add_fusion.3
  285.2 33.2 %attend_back.4 = (bf16[3,1024,384]{2,1,0:T(8,128)(2,1)}, f32[3,2,128]{2,1,0:T(2,128)S(1)}) custom-call(f32[12,2,1024]{2,1,0:T(2,128)S(1)} %bitcast.362, f32[3,512,128]{2,1,0:T(8,128)S(1)} %copy-done.30, bf16[1024,768]{1,0:T(8,128)(2,1)S(1)} %bitcast.374, bf16[1024,768]{1,0:T(8,128)(2,1)S(1)} %bitcast.380, bf16[1024,768]{1,0:T(8,128)(2,1)S(1)} %bitcast.386, ...), custom_call_target="tpu_custom_call" | custom-call | flops 33822867456 | bytes 5505024 | tf_op jit(solution)/shard_map/attend_back/pallas_call | solution.py:286
  318.3 2.4 fusion.54
  328.0 4.0 fusion.74
  332.0 12.2 %attend_back.5 = (bf16[3,1024,384]{2,1,0:T(8,128)(2,1)}, f32[1,2,128]{2,1,0:T(2,128)S(1)}) custom-call(f32[12,2,1024]{2,1,0:T(2,128)S(1)} %bitcast.363, f32[3,512,128]{2,1,0:T(8,128)S(1)} %copy-done.30, bf16[1024,768]{1,0:T(8,128)(2,1)S(1)} %bitcast.375, bf16[1024,768]{1,0:T(8,128)(2,1)S(1)} %bitcast.381, bf16[1024,768]{1,0:T(8,128)(2,1)S(1)} %bitcast.387, ...), custom_call_target="tpu_custom_call" | custom-call | flops 11274289152 | bytes 1835008 | tf_op jit(solution)/shard_map/attend_back/pallas_call | solution.py:286
  349.7 12.2 %attend_back.6 = (bf16[3,1024,384]{2,1,0:T(8,128)(2,1)}, f32[1,2,128]{2,1,0:T(2,128)S(1)}) custom-call(f32[12,2,1024]{2,1,0:T(2,128)S(1)} %bitcast.364, f32[3,512,128]{2,1,0:T(8,128)S(1)} %copy-done.30, bf16[1024,768]{1,0:T(8,128)(2,1)S(1)} %bitcast.376, bf16[1024,768]{1,0:T(8,128)(2,1)S(1)} %bitcast.382, ...), custom_call_target="tpu_custom_call", output_to_operand_aliasing={{0}: (6, {})} | custom-call | flops 11274289152 | bytes 1835008 | tf_op jit(solution)/shard_map/attend_back/pallas_call | solution.py:286
  361.9 2.3 collective-permute-start.28
  364.3 2.3 collective-permute-done.23
  368.5 12.1 %attend_back.7 = (bf16[3,1024,384]{2,1,0:T(8,128)(2,1)}, f32[1,2,128]{2,1,0:T(2,128)S(1)}) custom-call(f32[12,2,1024]{2,1,0:T(2,128)S(1)} %bitcast.365, f32[3,512,128]{2,1,0:T(8,128)S(1)} %copy-done.30, bf16[1024,768]{1,0:T(8,128)(2,1)S(1)} %bitcast.377, bf16[1024,768]{1,0:T(8,128)(2,1)S(1)} %bitcast.383, ...), custom_call_target="tpu_custom_call", output_to_operand_aliasing={{0}: (6, {})} | custom-call | flops 11274289152 | bytes 1835008 | tf_op jit(solution)/shard_map/attend_back/pallas_call | solution.py:286
  380.6 24.4 %collective-permute-done.25 = bf16[496,384]{1,0:T(8,128)(2,1)S(1)} collective-permute-done((bf16[496,384]{1,0:T(8,128)(2,1)S(1)}, bf16[496,384]{1,0:T(8,128)(2,1)S(1)}, u32[]{:S(2)}, u32[]{:S(2)}) %collective-permute-start.25) | collective-permute-done | bytes 380960 | tf_op jit(solution)/shard_map/ppermute | solution.py:525
  405.6 3.9 fusion.77
  409.4 3.9 fusion.80
  413.4 11.3 %collective-permute-done.37 = bf16[496,384]{1,0:T(8,128)(2,1)S(1)} collective-permute-done((bf16[496,384]{1,0:T(8,128)(2,1)S(1)}, bf16[496,384]{1,0:T(8,128)(2,1)S(1)}, u32[]{:S(2)}, u32[]{:S(2)}) %collective-permute-start.37) | collective-permute-done | bytes 380960 | tf_op jit(solution)/shard_map/ppermute | solution.py:525
  425.7 2.6 fusion.51
  428.3 2.8 fusion.50
  438.1 3.4 fusion
  441.5 2.8 maximum_add_fusion
  453.0 2.1 slice_bitcast_fusion.38
  455.0 5.3 %collective-permute-done.32 = bf16[304,384]{1,0:T(8,128)(2,1)S(1)} collective-permute-done((bf16[304,384]{1,0:T(8,128)(2,1)S(1)}, bf16[304,384]{1,0:T(8,128)(2,1)S(1)}, u32[]{:S(2)}, u32[]{:S(2)}) %collective-permute-start.32) | collective-permute-done | bytes 233504 | tf_op jit(solution)/shard_map/ppermute | solution.py:525
  460.4 5.7 %collective-permute-done.34 = bf16[304,384]{1,0:T(8,128)(2,1)S(1)} collective-permute-done((bf16[304,384]{1,0:T(8,128)(2,1)S(1)}, bf16[304,384]{1,0:T(8,128)(2,1)S(1)}, u32[]{:S(2)}, u32[]{:S(2)}) %collective-permute-start.34) | collective-permute-done | bytes 233504 | tf_op jit(solution)/shard_map/ppermute | solution.py:525
  469.8 3.9 collective-permute-done.35
  473.8 2.5 collective-permute-start.36
  478.3 8.1 %collective-permute-done.36 = bf16[304,384]{1,0:T(8,128)(2,1)S(1)} collective-permute-done((bf16[304,384]{1,0:T(8,128)(2,1)S(1)}, bf16[304,384]{1,0:T(8,128)(2,1)S(1)}, u32[]{:S(2)}, u32[]{:S(2)}) %collective-permute-start.36) | collective-permute-done | bytes 233504 | tf_op jit(solution)/shard_map/ppermute | solution.py:525
  487.3 2.5 fusion.37
  504.8 2.1 fusion.138
  508.4 4.9 all-gather.5.cloned.1.call-done
  (409 shorter events, 131.1 us)
Async XLA Ops:
  7.2 59.5 %copy-start = (bf16[768,768]{1,0:T(8,128)(2,1)S(1)}, bf16[768,768]{1,0:T(8,128)(2,1)}, u32[]{:S(2)}) copy-start(bf16[768,768]{1,0:T(8,128)(2,1)} %param.25) | copy-start | bytes 3538948
  7.2 418.5 %reduce-scatter.2.cloned.1.call-start = ((), (), s32[]{:S(2)}) async-start(), calls=%async_computation.1 | async-start | bytes 10616832 | tf_op jit(solution)/shard_map/reduce_scatter | solution.py:666
  8.1 4.4 collective-permute-start.1
  10.7 6.3 %collective-permute-start.2 = (bf16[512,768]{1,0:T(8,128)(2,1)}, bf16[512,768]{1,0:T(8,128)(2,1)}, u32[]{:S(2)}, u32[]{:S(2)}) collective-permute-start(bf16[512,768]{1,0:T(8,128)(2,1)} %dynamic-slice_bitcast_fusion.3), channel_id=1, source_target_pairs={{0,4},{4,0},{1,5},{5,1},{2,6},{6,2},{3,7},{7,3},{8,12},{12,8},{9,1... | collective-permute-start | bytes 2359304 | tf_op jit(solution)/shard_map/ppermute | solution.py:485
  11.7 15.0 %collective-permute-start = (bf16[512,768]{1,0:T(8,128)(2,1)}, bf16[512,768]{1,0:T(8,128)(2,1)}, u32[]{:S(2)}, u32[]{:S(2)}) collective-permute-start(bf16[512,768]{1,0:T(8,128)(2,1)} %dynamic-slice_bitcast_fusion.4), channel_id=1, source_target_pairs={{0,4},{4,0},{1,5},{5,1},{2,6},{6,2},{3,7},{7,3},{8,12},{12,8},{9,1... | collective-permute-start | bytes 2359304 | tf_op jit(solution)/shard_map/ppermute | solution.py:485
  12.6 69.4 %copy-start.4 = (f32[2,1024,12]{1,0,2:T(2,128)}, f32[2,1024,12]{1,0,2:T(2,128)S(1)}, u32[]{:S(2)}) copy-start(f32[2,1024,12]{1,0,2:T(2,128)S(1)} %copy.57) | copy-start | bytes 294916
  17.0 94.4 %copy-start.85 = (pred[4,2,256,512]{2,3,0,1:T(32,128)(4,1)}, pred[4,2,256,512]{2,3,0,1:T(32,128)(4,1)S(1)}, u32[]{:S(2)}) copy-start(pred[4,2,256,512]{2,3,0,1:T(32,128)(4,1)S(1)} %broadcast_and_fusion) | copy-start | bytes 3145732
  31.8 50.2 %copy-start.22 = (bf16[2,512,768]{2,1,0:T(8,128)(2,1)}, bf16[2,512,768]{2,1,0:T(8,128)(2,1)S(1)}, u32[]{:S(2)}) copy-start(bf16[2,512,768]{2,1,0:T(8,128)(2,1)S(1)} %convolution_convert_fusion.2) | copy-start | bytes 4718596
  33.6 48.4 %copy-start.24 = (bf16[2,512,768]{2,1,0:T(8,128)(2,1)}, bf16[2,512,768]{2,1,0:T(8,128)(2,1)S(1)}, u32[]{:S(2)}) copy-start(bf16[2,512,768]{2,1,0:T(8,128)(2,1)S(1)} %convolution_convert_fusion.1) | copy-start | bytes 4718596
  35.0 47.0 %copy-start.27 = (bf16[2,512,768]{2,1,0:T(8,128)(2,1)}, bf16[2,512,768]{2,1,0:T(8,128)(2,1)S(1)}, u32[]{:S(2)}) copy-start(bf16[2,512,768]{2,1,0:T(8,128)(2,1)S(1)} %convolution_convert_fusion) | copy-start | bytes 4718596
  35.0 22.0 %collective-permute-start.3 = (bf16[256,768]{1,0:T(8,128)(2,1)}, bf16[256,768]{1,0:T(8,128)(2,1)S(1)}, u32[]{:S(2)}, u32[]{:S(2)}) collective-permute-start(bf16[256,768]{1,0:T(8,128)(2,1)} %convolution_convert_fusion.25), channel_id=1, source_target_pairs={{0,1},{1,2},{2,3},{3,0},{4,5},{5,6},{6,7},{7,4},{8,9},{9,10},{10,1... | collective-permute-start | bytes 1179656 | tf_op jit(solution)/shard_map/ppermute | solution.py:476
  37.7 29.0 %collective-permute-start.4 = (bf16[256,768]{1,0:T(8,128)(2,1)S(1)}, bf16[256,768]{1,0:T(8,128)(2,1)S(1)}, u32[]{:S(2)}, u32[]{:S(2)}) collective-permute-start(bf16[256,768]{1,0:T(8,128)(2,1)S(1)} %convolution_convert_fusion.24), channel_id=1, source_target_pairs={{0,2},{1,3},{2,0},{3,1},{4,6},{5,7},{6,4},{7,5},{8,10},{9,11},{10,... | collective-permute-start | bytes 1179656 | tf_op jit(solution)/shard_map/ppermute | solution.py:476
  40.3 26.4 %collective-permute-start.5 = (bf16[256,768]{1,0:T(8,128)(2,1)S(1)}, bf16[256,768]{1,0:T(8,128)(2,1)S(1)}, u32[]{:S(2)}, u32[]{:S(2)}) collective-permute-start(bf16[256,768]{1,0:T(8,128)(2,1)S(1)} %convolution_convert_fusion.23), channel_id=1, source_target_pairs={{0,3},{1,0},{2,1},{3,2},{4,7},{5,4},{6,5},{7,6},{8,11},{9,8},{10,9... | collective-permute-start | bytes 1179656 | tf_op jit(solution)/shard_map/ppermute | solution.py:476
  70.8 25.6 %collective-permute-start.6 = (bf16[256,768]{1,0:T(8,128)(2,1)S(1)}, bf16[256,768]{1,0:T(8,128)(2,1)S(1)}, u32[]{:S(2)}, u32[]{:S(2)}) collective-permute-start(bf16[256,768]{1,0:T(8,128)(2,1)S(1)} %convolution_convert_fusion.17), channel_id=1, source_target_pairs={{0,1},{1,2},{2,3},{3,0},{4,5},{5,6},{6,7},{7,4},{8,9},{9,10},{10,1... | collective-permute-start | bytes 1179656 | tf_op jit(solution)/shard_map/ppermute | solution.py:476
  79.6 27.0 %collective-permute-start.7 = (bf16[256,768]{1,0:T(8,128)(2,1)S(1)}, bf16[256,768]{1,0:T(8,128)(2,1)S(1)}, u32[]{:S(2)}, u32[]{:S(2)}) collective-permute-start(bf16[256,768]{1,0:T(8,128)(2,1)S(1)} %convolution_convert_fusion.16), channel_id=1, source_target_pairs={{0,2},{1,3},{2,0},{3,1},{4,6},{5,7},{6,4},{7,5},{8,10},{9,11},{10,... | collective-permute-start | bytes 1179656 | tf_op jit(solution)/shard_map/ppermute | solution.py:476
  81.3 25.4 %collective-permute-start.8 = (bf16[256,768]{1,0:T(8,128)(2,1)S(1)}, bf16[256,768]{1,0:T(8,128)(2,1)S(1)}, u32[]{:S(2)}, u32[]{:S(2)}) collective-permute-start(bf16[256,768]{1,0:T(8,128)(2,1)S(1)} %convolution_convert_fusion.15), channel_id=1, source_target_pairs={{0,3},{1,0},{2,1},{3,2},{4,7},{5,4},{6,5},{7,6},{8,11},{9,8},{10,9... | collective-permute-start | bytes 1179656 | tf_op jit(solution)/shard_map/ppermute | solution.py:476
  96.4 55.0 %copy-start.6 = (bf16[256,768]{1,0:T(8,128)(2,1)}, bf16[256,768]{1,0:T(8,128)(2,1)S(1)}, u32[]{:S(2)}) copy-start(bf16[256,768]{1,0:T(8,128)(2,1)S(1)} %collective-permute-done.6.refs_2_.refs_1_) | copy-start | bytes 1179652
  112.5 26.5 %collective-permute-start.10 = (bf16[256,768]{1,0:T(8,128)(2,1)}, bf16[256,768]{1,0:T(8,128)(2,1)S(1)}, u32[]{:S(2)}, u32[]{:S(2)}) collective-permute-start(bf16[256,768]{1,0:T(8,128)(2,1)} %convolution_convert_fusion.12), channel_id=1, source_target_pairs={{0,2},{1,3},{2,0},{3,1},{4,6},{5,7},{6,4},{7,5},{8,10},{9,11},{10,... | collective-permute-start | bytes 1179656 | tf_op jit(solution)/shard_map/ppermute | solution.py:476
  122.2 66.2 %collective-permute-start.11 = (bf16[256,768]{1,0:T(8,128)(2,1)}, bf16[256,768]{1,0:T(8,128)(2,1)S(1)}, u32[]{:S(2)}, u32[]{:S(2)}) collective-permute-start(bf16[256,768]{1,0:T(8,128)(2,1)} %convolution_convert_fusion.11), channel_id=1, source_target_pairs={{0,3},{1,0},{2,1},{3,2},{4,7},{5,4},{6,5},{7,6},{8,11},{9,8},{10,9... | collective-permute-start | bytes 1179656 | tf_op jit(solution)/shard_map/ppermute | solution.py:476
  125.6 62.8 %collective-permute-start.9 = (bf16[256,768]{1,0:T(8,128)(2,1)}, bf16[256,768]{1,0:T(8,128)(2,1)S(1)}, u32[]{:S(2)}, u32[]{:S(2)}) collective-permute-start(bf16[256,768]{1,0:T(8,128)(2,1)} %convolution_convert_fusion.13), channel_id=1, source_target_pairs={{0,1},{1,2},{2,3},{3,0},{4,5},{5,6},{6,7},{7,4},{8,9},{9,10},{10,1... | collective-permute-start | bytes 1179656 | tf_op jit(solution)/shard_map/ppermute | solution.py:476
  125.7 62.9 %collective-permute-start.12 = (bf16[256,768]{1,0:T(8,128)(2,1)}, bf16[256,768]{1,0:T(8,128)(2,1)S(1)}, u32[]{:S(2)}, u32[]{:S(2)}) collective-permute-start(bf16[256,768]{1,0:T(8,128)(2,1)} %convolution_convert_fusion.21), channel_id=1, source_target_pairs={{0,1},{1,2},{2,3},{3,0},{4,5},{5,6},{6,7},{7,4},{8,9},{9,10},{10,1... | collective-permute-start | bytes 1179656 | tf_op jit(solution)/shard_map/ppermute | solution.py:476
  126.9 64.0 %collective-permute-start.13 = (bf16[256,768]{1,0:T(8,128)(2,1)}, bf16[256,768]{1,0:T(8,128)(2,1)S(1)}, u32[]{:S(2)}, u32[]{:S(2)}) collective-permute-start(bf16[256,768]{1,0:T(8,128)(2,1)} %convolution_convert_fusion.20), channel_id=1, source_target_pairs={{0,2},{1,3},{2,0},{3,1},{4,6},{5,7},{6,4},{7,5},{8,10},{9,11},{10,... | collective-permute-start | bytes 1179656 | tf_op jit(solution)/shard_map/ppermute | solution.py:476
  139.8 51.2 %collective-permute-start.14 = (bf16[256,768]{1,0:T(8,128)(2,1)}, bf16[256,768]{1,0:T(8,128)(2,1)S(1)}, u32[]{:S(2)}, u32[]{:S(2)}) collective-permute-start(bf16[256,768]{1,0:T(8,128)(2,1)} %convolution_convert_fusion.19), channel_id=1, source_target_pairs={{0,3},{1,0},{2,1},{3,2},{4,7},{5,4},{6,5},{7,6},{8,11},{9,8},{10,9... | collective-permute-start | bytes 1179656 | tf_op jit(solution)/shard_map/ppermute | solution.py:476
  188.4 34.2 %collective-permute-start.15 = (bf16[256,768]{1,0:T(8,128)(2,1)S(1)}, bf16[256,768]{1,0:T(8,128)(2,1)S(1)}, u32[]{:S(2)}, u32[]{:S(2)}) collective-permute-start(bf16[256,768]{1,0:T(8,128)(2,1)S(1)} %get-tuple-element.182), channel_id=1, source_target_pairs={{0,3},{1,0},{2,1},{3,2},{4,7},{5,4},{6,5},{7,6},{8,11},{9,8},{10,9... | collective-permute-start | bytes 1179656 | tf_op jit(solution)/shard_map/ppermute | solution.py:476
  188.5 34.2 %collective-permute-start.16 = (bf16[256,768]{1,0:T(8,128)(2,1)S(1)}, bf16[256,768]{1,0:T(8,128)(2,1)S(1)}, u32[]{:S(2)}, u32[]{:S(2)}) collective-permute-start(bf16[256,768]{1,0:T(8,128)(2,1)S(1)} %get-tuple-element.183), channel_id=1, source_target_pairs={{0,2},{1,3},{2,0},{3,1},{4,6},{5,7},{6,4},{7,5},{8,10},{9,11},{10,... | collective-permute-start | bytes 1179656 | tf_op jit(solution)/shard_map/ppermute | solution.py:476
  188.5 34.1 %collective-permute-start.17 = (bf16[256,768]{1,0:T(8,128)(2,1)S(1)}, bf16[256,768]{1,0:T(8,128)(2,1)S(1)}, u32[]{:S(2)}, u32[]{:S(2)}) collective-permute-start(bf16[256,768]{1,0:T(8,128)(2,1)S(1)} %get-tuple-element.184), channel_id=1, source_target_pairs={{0,1},{1,2},{2,3},{3,0},{4,5},{5,6},{6,7},{7,4},{8,9},{9,10},{10,1... | collective-permute-start | bytes 1179656 | tf_op jit(solution)/shard_map/ppermute | solution.py:476
  224.1 32.0 %collective-permute-start.18 = (bf16[256,768]{1,0:T(8,128)(2,1)}, bf16[256,768]{1,0:T(8,128)(2,1)}, u32[]{:S(2)}, u32[]{:S(2)}) collective-permute-start(bf16[256,768]{1,0:T(8,128)(2,1)} %get-tuple-element.196), channel_id=1, source_target_pairs={{0,3},{1,0},{2,1},{3,2},{4,7},{5,4},{6,5},{7,6},{8,11},{9,8},{10,9... | collective-permute-start | bytes 1179656 | tf_op jit(solution)/shard_map/ppermute | solution.py:476
  226.5 34.8 %collective-permute-start.19 = (bf16[256,768]{1,0:T(8,128)(2,1)}, bf16[256,768]{1,0:T(8,128)(2,1)}, u32[]{:S(2)}, u32[]{:S(2)}) collective-permute-start(bf16[256,768]{1,0:T(8,128)(2,1)} %get-tuple-element.197), channel_id=1, source_target_pairs={{0,2},{1,3},{2,0},{3,1},{4,6},{5,7},{6,4},{7,5},{8,10},{9,11},{10,... | collective-permute-start | bytes 1179656 | tf_op jit(solution)/shard_map/ppermute | solution.py:476
  227.1 34.2 %collective-permute-start.20 = (bf16[256,768]{1,0:T(8,128)(2,1)}, bf16[256,768]{1,0:T(8,128)(2,1)}, u32[]{:S(2)}, u32[]{:S(2)}) collective-permute-start(bf16[256,768]{1,0:T(8,128)(2,1)} %get-tuple-element.198), channel_id=1, source_target_pairs={{0,1},{1,2},{2,3},{3,0},{4,5},{5,6},{6,7},{7,4},{8,9},{9,10},{10,1... | collective-permute-start | bytes 1179656 | tf_op jit(solution)/shard_map/ppermute | solution.py:476
  261.3 225.9 %all-gather.3.cloned.1.call-start = ((), (), s32[]{:S(2)}) async-start(), calls=%async_computation.2 | async-start | bytes 3428352 | tf_op jit(solution)/shard_map/all_gather | solution.py:560
  325.9 18.3 %collective-permute-start.21 = (bf16[4,496,384]{2,1,0:T(8,128)(2,1)}, bf16[4,496,384]{2,1,0:T(8,128)(2,1)}, u32[]{:S(2)}, u32[]{:S(2)}) collective-permute-start(bf16[4,496,384]{2,1,0:T(8,128)(2,1)} %dynamic-slice_bitcast_fusion.1), channel_id=1, source_target_pairs={{0,4},{4,0},{1,5},{5,1},{2,6},{6,2},{3,7},{7,3},{8,12},{12,8},{9,1... | collective-permute-start | bytes 4571144 | tf_op jit(solution)/shard_map/ppermute | solution.py:525
  325.9 99.7 %collective-permute-start.26 = (bf16[512,768]{1,0:T(8,128)(2,1)}, bf16[512,768]{1,0:T(8,128)(2,1)}, u32[]{:S(2)}, u32[]{:S(2)}) collective-permute-start(bf16[512,768]{1,0:T(8,128)(2,1)} %get-tuple-element.229), channel_id=1, source_target_pairs={{0,3},{1,0},{2,1},{3,2},{4,7},{5,4},{6,5},{7,6},{8,11},{9,8},{10,9... | collective-permute-start | bytes 2359304 | tf_op jit(solution)/shard_map/ppermute | solution.py:476
  326.3 99.3 %collective-permute-start.27 = (bf16[512,768]{1,0:T(8,128)(2,1)}, bf16[512,768]{1,0:T(8,128)(2,1)}, u32[]{:S(2)}, u32[]{:S(2)}) collective-permute-start(bf16[512,768]{1,0:T(8,128)(2,1)} %get-tuple-element.230), channel_id=1, source_target_pairs={{0,2},{1,3},{2,0},{3,1},{4,6},{5,7},{6,4},{7,5},{8,10},{9,11},{10,... | collective-permute-start | bytes 2359304 | tf_op jit(solution)/shard_map/ppermute | solution.py:476
  346.1 15.8 %collective-permute-start.22 = (bf16[496,384]{1,0:T(8,128)(2,1)S(1)}, bf16[496,384]{1,0:T(8,128)(2,1)S(1)}, u32[]{:S(2)}, u32[]{:S(2)}) collective-permute-start(bf16[496,384]{1,0:T(8,128)(2,1)S(1)} %get-tuple-element.217), channel_id=1, source_target_pairs={{0,8},{8,0},{16,24},{24,16},{1,9},{9,1},{17,25},{25,17},{2,10},{10... | collective-permute-start | bytes 1142792 | tf_op jit(solution)/shard_map/ppermute | solution.py:525
  347.7 18.9 %collective-permute-start.23 = (bf16[496,384]{1,0:T(8,128)(2,1)S(1)}, bf16[496,384]{1,0:T(8,128)(2,1)S(1)}, u32[]{:S(2)}, u32[]{:S(2)}) collective-permute-start(bf16[496,384]{1,0:T(8,128)(2,1)S(1)} %get-tuple-element.218), channel_id=1, source_target_pairs={{0,16},{8,24},{16,0},{24,8},{1,17},{9,25},{17,1},{25,9},{2,18},{10... | collective-permute-start | bytes 1142792 | tf_op jit(solution)/shard_map/ppermute | solution.py:525
  349.2 17.3 %collective-permute-start.24 = (bf16[496,384]{1,0:T(8,128)(2,1)S(1)}, bf16[496,384]{1,0:T(8,128)(2,1)S(1)}, u32[]{:S(2)}, u32[]{:S(2)}) collective-permute-start(bf16[496,384]{1,0:T(8,128)(2,1)S(1)} %get-tuple-element.219), channel_id=1, source_target_pairs={{0,24},{8,16},{16,8},{24,0},{1,25},{9,17},{17,9},{25,1},{2,26},{10... | collective-permute-start | bytes 1142792 | tf_op jit(solution)/shard_map/ppermute | solution.py:525
  361.9 63.7 %collective-permute-start.28 = (bf16[512,768]{1,0:T(8,128)(2,1)}, bf16[512,768]{1,0:T(8,128)(2,1)}, u32[]{:S(2)}, u32[]{:S(2)}) collective-permute-start(bf16[512,768]{1,0:T(8,128)(2,1)} %get-tuple-element.231), channel_id=1, source_target_pairs={{0,1},{1,2},{2,3},{3,0},{4,5},{5,6},{6,7},{7,4},{8,9},{9,10},{10,1... | collective-permute-start | bytes 2359304 | tf_op jit(solution)/shard_map/ppermute | solution.py:476
  366.8 38.2 %collective-permute-start.25 = (bf16[496,384]{1,0:T(8,128)(2,1)S(1)}, bf16[496,384]{1,0:T(8,128)(2,1)S(1)}, u32[]{:S(2)}, u32[]{:S(2)}) collective-permute-start(bf16[496,384]{1,0:T(8,128)(2,1)S(1)} %fusion.96), channel_id=1, source_target_pairs={{0,1},{1,0},{2,3},{3,2},{4,5},{5,4},{6,7},{7,6},{8,9},{9,8},{10,11... | collective-permute-start | bytes 1142792 | tf_op jit(solution)/shard_map/ppermute | solution.py:525
  405.1 19.6 %collective-permute-start.37 = (bf16[496,384]{1,0:T(8,128)(2,1)S(1)}, bf16[496,384]{1,0:T(8,128)(2,1)S(1)}, u32[]{:S(2)}, u32[]{:S(2)}) collective-permute-start(bf16[496,384]{1,0:T(8,128)(2,1)S(1)} %add_convert_fusion.2), channel_id=1, source_target_pairs={{0,2},{1,3},{2,0},{3,1},{4,6},{5,7},{6,4},{7,5},{8,10},{9,11},{10,... | collective-permute-start | bytes 1142792 | tf_op jit(solution)/shard_map/ppermute | solution.py:525
  425.6 87.8 %all-gather.5.cloned.1.call-start = ((), (), s32[]{:S(2)}) async-start(), calls=%async_computation.3 | async-start | bytes 2101248 | tf_op jit(solution)/shard_map/all_gather | solution.py:560
  433.9 14.0 %collective-permute-start.31 = (bf16[4,304,384]{2,1,0:T(8,128)(2,1)}, bf16[4,304,384]{2,1,0:T(8,128)(2,1)}, u32[]{:S(2)}, u32[]{:S(2)}) collective-permute-start(bf16[4,304,384]{2,1,0:T(8,128)(2,1)} %dynamic-slice_bitcast_fusion.2), channel_id=1, source_target_pairs={{0,4},{4,0},{1,5},{5,1},{2,6},{6,2},{3,7},{7,3},{8,12},{12,8},{9,1... | collective-permute-start | bytes 2801672 | tf_op jit(solution)/shard_map/ppermute | solution.py:525
  446.8 51.2 %collective-permute-start.30 = (f32[512,768]{1,0:T(8,128)}, f32[512,768]{1,0:T(8,128)}, u32[]{:S(2)}, u32[]{:S(2)}) collective-permute-start(f32[512,768]{1,0:T(8,128)} %dynamic-slice_bitcast_fusion), channel_id=1, source_target_pairs={{0,4},{4,0},{1,5},{5,1},{2,6},{6,2},{3,7},{7,3},{8,12},{12,8},{9,1... | collective-permute-start | bytes 4718600 | tf_op jit(solution)/shard_map/ppermute | solution.py:485
  449.4 11.0 %collective-permute-start.32 = (bf16[304,384]{1,0:T(8,128)(2,1)S(1)}, bf16[304,384]{1,0:T(8,128)(2,1)S(1)}, u32[]{:S(2)}, u32[]{:S(2)}) collective-permute-start(bf16[304,384]{1,0:T(8,128)(2,1)S(1)} %get-tuple-element.313), channel_id=1, source_target_pairs={{0,8},{8,0},{16,24},{24,16},{1,9},{9,1},{17,25},{25,17},{2,10},{10... | collective-permute-start | bytes 700424 | tf_op jit(solution)/shard_map/ppermute | solution.py:525
  450.8 9.6 %collective-permute-start.33 = (bf16[304,384]{1,0:T(8,128)(2,1)S(1)}, bf16[304,384]{1,0:T(8,128)(2,1)S(1)}, u32[]{:S(2)}, u32[]{:S(2)}) collective-permute-start(bf16[304,384]{1,0:T(8,128)(2,1)S(1)} %get-tuple-element.315), channel_id=1, source_target_pairs={{0,16},{8,24},{16,0},{24,8},{1,17},{9,25},{17,1},{25,9},{2,18},{10... | collective-permute-start | bytes 700424 | tf_op jit(solution)/shard_map/ppermute | solution.py:525
  452.4 13.6 %collective-permute-start.34 = (bf16[304,384]{1,0:T(8,128)(2,1)S(1)}, bf16[304,384]{1,0:T(8,128)(2,1)S(1)}, u32[]{:S(2)}, u32[]{:S(2)}) collective-permute-start(bf16[304,384]{1,0:T(8,128)(2,1)S(1)} %get-tuple-element.314), channel_id=1, source_target_pairs={{0,24},{8,16},{16,8},{24,0},{1,25},{9,17},{17,9},{25,1},{2,26},{10... | collective-permute-start | bytes 700424 | tf_op jit(solution)/shard_map/ppermute | solution.py:525
  466.2 7.6 %collective-permute-start.35 = (bf16[304,384]{1,0:T(8,128)(2,1)S(1)}, bf16[304,384]{1,0:T(8,128)(2,1)S(1)}, u32[]{:S(2)}, u32[]{:S(2)}) collective-permute-start(bf16[304,384]{1,0:T(8,128)(2,1)S(1)} %fusion.117), channel_id=1, source_target_pairs={{0,1},{1,0},{2,3},{3,2},{4,5},{5,4},{6,7},{7,6},{8,9},{9,8},{10,11... | collective-permute-start | bytes 700424 | tf_op jit(solution)/shard_map/ppermute | solution.py:525
  473.8 12.6 %collective-permute-start.36 = (bf16[304,384]{1,0:T(8,128)(2,1)S(1)}, bf16[304,384]{1,0:T(8,128)(2,1)S(1)}, u32[]{:S(2)}, u32[]{:S(2)}) collective-permute-start(bf16[304,384]{1,0:T(8,128)(2,1)S(1)} %add_convert_fusion.4), channel_id=1, source_target_pairs={{0,2},{1,3},{2,0},{3,1},{4,6},{5,7},{6,4},{7,5},{8,10},{9,11},{10,... | collective-permute-start | bytes 700424 | tf_op jit(solution)/shard_map/ppermute | solution.py:525
  491.4 3.8 collective-permute-start.29
  (108 other events, 700.2 us)
Sparse Core Ops, SparseCore 0:
  261.4 76.0 reduce-scatter.1
  425.7 33.7 all-gather.2
  487.3 25.9 all-gather.4

commit v4 on v3

--- a/solution.py
+++ b/solution.py
@@ -201,7 +201,7 @@
         out_shape=jax.ShapeDtypeStruct((count, width), jnp.bfloat16),
         scratch_shapes=[pltpu.VMEM((2, QB, 3 * QB), jnp.float32)],
         compiler_params=pltpu.CompilerParams(vmem_limit_bytes=48 << 20),
-        cost_estimate=pl.CostEstimate(flops=40 * count * length * width, bytes_accessed=6 * length * width, transcendentals=count * length * width // 64),
+        cost_estimate=pl.CostEstimate(flops=count * length * width, bytes_accessed=2 * length * width, transcendentals=0),
         name="attend",
     )(lines, q, k, v)
 
@@ -462,12 +462,123 @@
     )(*pieces, *grads, *hiddens, *pre_grads)
 
 
-def make_dispatch(routes, labels, capacity):
-    hits = (routes[..., None] == labels).astype(jnp.int32)
-    places = jnp.sum((jnp.cumsum(hits, axis=1) - 1) * hits, axis=-1)
-    expert_match = routes[None, :, None, :] == labels[:, None, None, None]
-    slot_match = places[:, None, :] == jnp.arange(capacity, dtype=jnp.int32)[None, :, None]
-    return (expert_match & slot_match[None]).astype(jnp.bfloat16)
+def sort_matrix(slot, slots):
+    row = lax.broadcasted_iota(jnp.int32, (slots, slot.shape[1]), 0)
+    return (row == slot).astype(jnp.float32).astype(jnp.bfloat16)
+
+
+def sort_into(piece_refs, block, slot, rows):
+    capacity = slot.shape[1] // 2
+    matrix = sort_matrix(slot, len(piece_refs) * capacity)
+    moved = jnp.dot(matrix, rows, preferred_element_type=jnp.float32).astype(jnp.bfloat16)
+    for turn, piece_ref in enumerate(piece_refs):
+        piece_ref[block * capacity : (block + 1) * capacity, :] = moved[turn * capacity : (turn + 1) * capacity]
+
+
+def norm_scale_rows(rows):
+    return lax.rsqrt(jnp.mean(rows * rows, axis=-1, keepdims=True) + norm_eps)
+
+
+def sort_kernel(owners, label_ref, routes_ref, rows_ref, *refs):
+    piece_refs, slot_ref = refs[:owners], refs[owners]
+    blocks, _, length = routes_ref.shape
+    first = lax.broadcasted_iota(jnp.int32, (length, length), 0)
+    second = lax.broadcasted_iota(jnp.int32, (length, length), 1)
+    upto = (first <= second).astype(jnp.float32).astype(jnp.bfloat16)
+    for block in range(blocks):
+        routes = routes_ref[block]
+        hits = (lax.broadcasted_iota(jnp.int32, (8, length), 0) == routes).astype(jnp.float32)
+        counts = jnp.dot(hits.astype(jnp.bfloat16), upto, preferred_element_type=jnp.float32)
+        place = jnp.sum(hits * counts, axis=0, keepdims=True).astype(jnp.int32) - 1
+        turn = routes - label_ref[0]
+        turn = jnp.where(turn < 0, turn + owners, turn)
+        slot = turn * (length // 2) + place
+        slot_ref[block] = slot
+        sort_into(piece_refs, block, slot, rows_ref[block])
+
+
+def sort_upstream(label, routes, rows, owners):
+    blocks, length, width = rows.shape
+    vmem = pl.BlockSpec(memory_space=pltpu.VMEM)
+    piece = jax.ShapeDtypeStruct((blocks * length // 2, width), jnp.bfloat16)
+    *pieces, slots = pl.pallas_call(
+        lambda *refs: sort_kernel(owners, *refs),
+        in_specs=[pl.BlockSpec(memory_space=pltpu.SMEM), vmem, vmem],
+        out_specs=[vmem] * (owners + 1),
+        out_shape=[piece] * owners + [jax.ShapeDtypeStruct((blocks, 1, length), jnp.int32)],
+        compiler_params=pltpu.CompilerParams(vmem_limit_bytes=48 << 20),
+        name="sort_upstream",
+    )(label, routes.reshape(blocks, 1, length), rows)
+    return pieces, slots
+
+
+def after_attention_kernel(slot_ref, attended_ref, tokens_ref, weight_ref, gain_ref, residual_ref, *piece_refs):
+    for block in range(slot_ref.shape[0]):
+        mixed = jnp.dot(attended_ref[block], weight_ref[...], preferred_element_type=jnp.float32)
+        residual = tokens_ref[block].astype(jnp.float32) + mixed
+        residual_ref[block] = residual
+        router_in = (residual * norm_scale_rows(residual) * gain_ref[...]).astype(jnp.bfloat16)
+        sort_into(piece_refs, block, slot_ref[block], router_in)
+
+
+def after_attention(slots, attended, tokens, weight, gain, owners):
+    blocks, length, width = tokens.shape
+    vmem = pl.BlockSpec(memory_space=pltpu.VMEM)
+    piece = jax.ShapeDtypeStruct((blocks * length // 2, width), jnp.bfloat16)
+    residual, *pieces = pl.pallas_call(
+        after_attention_kernel,
+        in_specs=[vmem] * 5,
+        out_specs=[vmem] * (owners + 1),
+        out_shape=[jax.ShapeDtypeStruct(tokens.shape, jnp.float32)] + [piece] * owners,
+        compiler_params=pltpu.CompilerParams(vmem_limit_bytes=48 << 20),
+        name="after_attention",
+    )(slots, attended, tokens, weight, gain[None])
+    return residual, pieces
+
+
+def before_attention_kernel(owners, slot_ref, *refs):
+    piece_refs = refs[:owners]
+    residual_ref, upstream_ref, attended_ref, weight_ref, gain_ref = refs[owners : owners + 5]
+    residual_grad_ref, mixed_grad_ref, weight_grad_ref, gain_grad_ref = refs[owners + 5 :]
+    blocks, _, length = slot_ref.shape
+    capacity = length // 2
+    weight_grad, gain_grad = 0.0, 0.0
+    for block in range(blocks):
+        matrix = sort_matrix(slot_ref[block], owners * capacity)
+        rows = jnp.concatenate([ref[block * capacity : (block + 1) * capacity, :] for ref in piece_refs])
+        grad = lax.dot_general(matrix, rows, (((0,), (0,)), ((), ())), preferred_element_type=jnp.float32)
+        residual = residual_ref[block]
+        scale = norm_scale_rows(residual)
+        normed = residual * scale
+        scaled = grad * gain_ref[...]
+        shrink = jnp.mean(scaled * normed, axis=-1, keepdims=True)
+        gain_grad += jnp.sum(grad * normed, axis=0, keepdims=True)
+        residual_grad = upstream_ref[block].astype(jnp.float32) + scale * (scaled - normed * shrink)
+        residual_grad_ref[block] = residual_grad
+        low = residual_grad.astype(jnp.bfloat16)
+        mixed_grad = lax.dot_general(low, weight_ref[...], (((1,), (1,)), ((), ())), preferred_element_type=jnp.float32)
+        mixed_grad_ref[block] = mixed_grad.astype(jnp.bfloat16)
+        weight_grad += lax.dot_general(attended_ref[block], low, (((0,), (0,)), ((), ())), preferred_element_type=jnp.float32)
+    weight_grad_ref[...] = weight_grad
+    gain_grad_ref[...] = gain_grad
+
+
+def before_attention(slots, pieces, residual, upstream, attended, weight, gain):
+    width = residual.shape[2]
+    vmem = pl.BlockSpec(memory_space=pltpu.VMEM)
+    return pl.pallas_call(
+        lambda *refs: before_attention_kernel(len(pieces), *refs),
+        in_specs=[vmem] * (len(pieces) + 6),
+        out_specs=[vmem] * 4,
+        out_shape=[
+            jax.ShapeDtypeStruct(residual.shape, jnp.float32),
+            jax.ShapeDtypeStruct(residual.shape, jnp.bfloat16),
+            jax.ShapeDtypeStruct((width, width), jnp.float32),
+            jax.ShapeDtypeStruct((1, width), jnp.float32),
+        ],
+        compiler_params=pltpu.CompilerParams(vmem_limit_bytes=56 << 20),
+        name="before_attention",
+    )(slots, *pieces, residual, upstream, attended, weight, gain[None])
 
 
 def exchange(pieces, axis, sign):
@@ -484,6 +595,15 @@
     other = lax.dynamic_index_in_dim(blocks, 1 - at, 0, keepdims=False)
     arrived = lax.ppermute(other, "ctx", [(0, 1), (1, 0)])
     return jnp.stack([jnp.where(at == 0, mine, arrived), jnp.where(at == 0, arrived, mine)])
+
+
+def place_rows(slots, pieces):
+    blocks, _, length = slots.shape
+    width = pieces[0].shape[-1]
+    rows = jnp.stack(pieces).reshape(len(pieces), blocks, -1, width).swapaxes(0, 1).reshape(blocks, -1, width)
+    places = jnp.arange(rows.shape[1], dtype=jnp.int32)
+    matrix = (slots == places[None, :, None]).astype(jnp.bfloat16)
+    return jnp.einsum("bsx,bsd->bxd", matrix, rows, preferred_element_type=jnp.float32)
 
 
 def norm_scale(value_rows):
@@ -591,32 +711,19 @@
     if whole_seq:
         routes, cotangent, tokens = trade(routes), trade(cotangent), trade(tokens)
     groups = [slice(0, 1), slice(1, 2)] if whole_seq else [slice(0, seq_count)]
-    label = lax.axis_index("expert")
-    labels = (label + jnp.arange(owners, dtype=jnp.int32)) % owners
-    dispatch = make_dispatch(routes, labels, capacity)
-
+    label = lax.axis_index("expert").astype(jnp.int32).reshape(1)
     together = lax.optimization_barrier
 
-    def sort_rows(group, rows):
-        sent = [
-            jnp.einsum("scx,sxd->scd", dispatch[turn, group], rows, preferred_element_type=jnp.float32)
-            for turn in range(owners)
-        ]
-        return [piece.astype(jnp.bfloat16).reshape(-1, model_width) for piece in sent]
-
-    def place_rows(group, pieces):
-        pieces = jnp.stack(pieces).reshape(owners, -1, capacity, model_width)
-        return jnp.einsum("escx,escd->sxd", dispatch[:, group], pieces, preferred_element_type=jnp.float32)
-
+    sorted_upstream, slots = zip(*[sort_upstream(label, routes[group], cotangent[group], owners) for group in groups])
+    sorted_upstream = list(sorted_upstream)
+    sorted_upstream[0], tokens = together((sorted_upstream[0], tokens))
+    upstream = [exchange(sorted_upstream[0], "expert", 1)]
     inputs = tokens.astype(jnp.float32)
     scale1 = norm_scale(inputs)
     attn_in = (inputs * scale1 * norm1_gain).astype(jnp.bfloat16)
     queries = wide_dot(attn_in, query_weight).astype(jnp.bfloat16)
     keys = wide_dot(attn_in, key_weight).astype(jnp.bfloat16)
     values = wide_dot(attn_in, value_weight).astype(jnp.bfloat16)
-    sorted_upstream = [sort_rows(group, cotangent[group]) for group in groups]
-    sorted_upstream, queries = together((sorted_upstream, queries))
-    upstream = [exchange(sorted_upstream[0], "expert", 1)]
     if whole_seq:
         lines = bias_lines(bias_table)
         flat = (seq_count * local_len, model_width)
@@ -627,7 +734,7 @@
         values = lax.all_gather(values, "ctx", axis=1, tiled=True)
         buckets = bucket_grid(first_pos, local_len, keys.shape[1])
         attended, log_totals = attend_rows(queries, keys, values, buckets, bias_table, DH)
-    attended_groups, residual1, scale2, arrived = [], [], [], []
+    attended_groups, residual1, arrived = [], [], []
     in_flight, fed = upstream[0], queries.reshape(-1, model_width)
     for at, group in enumerate(groups):
         if whole_seq:
@@ -641,15 +748,12 @@
             arrived[-1], sorted_upstream[at] = together((in_flight, sorted_upstream[at]))
             upstream.append(exchange(sorted_upstream[at], "expert", 1))
         attended_groups.append(rows)
-        residual1.append(inputs[group] + wide_dot(rows, output_weight))
-        scale2.append(norm_scale(residual1[-1]))
-        router_in = (residual1[-1] * scale2[-1] * norm2_gain).astype(jnp.bfloat16)
-        sorted_rows, fed = together((sort_rows(group, router_in), fed))
+        residual, sorted_rows = after_attention(slots[at], rows, tokens[group], output_weight, norm2_gain, owners)
+        residual1.append(residual)
+        sorted_rows, fed = together((sorted_rows, fed))
         in_flight = exchange(sorted_rows, "expert", 1)
         arrived.append(in_flight)
-    attended = attended_groups
     router_wide = jnp.pad(router_weight, ((0, 0), (0, 128 - router_weight.shape[1])))
-    label = label.astype(jnp.int32).reshape(1)
     done, back = [], []
     for at, (rows, grads) in enumerate(zip(arrived, upstream)):
         earlier = done[-1][0] if done else []
@@ -665,16 +769,15 @@
     grad_experts, back[-1], rows_out = together((grad_experts, back[-1], rows_out))
     grad_experts = lax.psum_scatter(grad_experts, ("dp", "ctx"), scatter_dimension=0, tiled=True)
     returned = exchange(list(rows_out), "expert", -1)
-    residual_grad, attn_grad, mixed_grad, grad_norm2 = [], [], [], 0.0
-    for group, rows, scale, pieces in zip(groups, residual1, scale2, back):
-        norm2_back, gain_part = norm_back(rows, scale, norm2_gain, place_rows(group, pieces))
-        grad_norm2 = grad_norm2 + gain_part
-        residual_grad.append(cotangent[group].astype(jnp.float32) + norm2_back)
-        attn_grad.append(residual_grad[-1].astype(jnp.bfloat16))
-        mixed_grad.append(wide_dot_back(attn_grad[-1], output_weight).astype(jnp.bfloat16))
-    grad_w_output = sum(weight_dot(left, right) for left, right in zip(attended, attn_grad))
+    residual_grad, mixed_grad, grad_w_output, grad_norm2 = zip(
+        *[
+            before_attention(slot, pieces, residual, cotangent[group], rows, output_weight, norm2_gain)
+            for slot, pieces, residual, group, rows in zip(slots, back, residual1, groups, attended_groups)
+        ]
+    )
     residual_grad, mixed_grad = jnp.concatenate(residual_grad), jnp.concatenate(mixed_grad)
-    early_small = jnp.concatenate([grad_router, grad_norm2[None]])
+    grad_w_output, grad_norm2 = sum(grad_w_output), sum(grad_norm2)
+    early_small = jnp.concatenate([grad_router, grad_norm2])
     projections = (query_weight, key_weight, value_weight)
     if whole_seq:
         rows_in = attn_in.reshape(flat)
@@ -747,8 +850,8 @@
     grad_router, grad_norm2 = small[:experts, :].T, small[experts]
     returned = [piece.reshape(len(groups), -1, model_width) for piece in returned]
     block_out = [
-        rows + place_rows(group, [piece[at] for piece in returned])
-        for at, (group, rows) in enumerate(zip(groups, residual1))
+        rows + place_rows(slot, [piece[at] for piece in returned])
+        for at, (slot, rows) in enumerate(zip(slots, residual1))
     ]
     block_out = jnp.concatenate(block_out).astype(jnp.bfloat16)
     norm1_back, _ = norm_back(inputs, scale1, norm1_gain, norm_in_grad)

time: 537 us -> 527 us (0.981)
  matrix products: 62.5 us -> 30.6 us
  Pallas kernels: 185 us -> 210 us
  starting transfers between devices: 72.2 us -> 87.9 us
  local copies, waits for them, and re-layouts: 52.2 us -> 41.4 us
  other arithmetic: 41.5 us -> 34.8 us
    dot_general x24 -> x2, matrix products: 28.1 us -> 2.5 us  [place_rows(): jnp.einsum('bsx,bsd->bxd', matrix, rows, preferred_element_type=jnp.float32)]
    pallas_call x0 -> x6, Pallas kernels: none -> 24.1 us  [the longest x2 16.5 us: before_attention(): pl.pallas_call(lambda *refs: before_attention_kernel(len(pieces), *refs),...]
    ppermute x21, starting transfers between devices: 57.3 us -> 73.1 us  [exchange(): lax.ppermute(pieces[turn], axis, [(at, (at + sign * turn) % size) for at...]
    ppermute x21, waiting for transfers between devices: 34 us -> 27.2 us  [exchange(): lax.ppermute(pieces[turn], axis, [(at, (at + sign * turn) % size) for at...]
    unnamed x235 -> x199, local copies, waits for them, and re-layouts: 27.4 us -> 23.6 us
  transfers between devices with their start and end apart: 41 -> 41, of which waited for: 12 -> 13; matrix products, arithmetic and copies ran while one was open for 20% -> 14% of each run, Pallas kernels for 35% -> 40%
where the time goes in v4:
time: 527 us; the launch traced here: 518 us
  Pallas kernels  210 us (40%)
  waiting for transfers between devices  98.4 us (19%)
  starting transfers between devices  87.9 us (17%)
  local copies, waits for them, and re-layouts  41.4 us (8%)
  other arithmetic  34.8 us (7%)
  matrix products  30.6 us (6%)
  between operations  15.2 us (3%)
    ppermute x21, starting transfers between devices, exchange(): lax.ppermute(pieces[turn], axis, [(at, (at + sign * turn) % size) for at...  73.1 us
    pallas_call x4, Pallas kernels, attend_back(): pl.pallas_call(lambda *refs: bwd_kernel(*refs[:6], *refs[6 + len(kept):])...  70 us
    ppermute x12, waiting for transfers between devices, swap(): lax.ppermute(part, axis, [(to, to ^ turn) for to in range(lax.axis_size(a...  63.2 us
    pallas_call x2, Pallas kernels, run_expert(): pl.pallas_call(lambda *refs: expert_kernel(count, *refs), grid_spec=pltpu...  59.4 us
    pallas_call x2, Pallas kernels, attend(): pl.pallas_call(lambda *refs: fwd_kernel(first // QB, *refs), grid=(width...  29 us
    ppermute x21, waiting for transfers between devices, exchange(): lax.ppermute(pieces[turn], axis, [(at, (at + sign * turn) % size) for at...  27.2 us
    pallas_call x1, Pallas kernels, expert_grads(): pl.pallas_call(lambda *refs: expert_grads_kernel(groups, count, *refs), g...  27.1 us
    unnamed x199, local copies, waits for them, and re-layouts  23.6 us
  transfers between devices with their start and end apart: 41, of which 13 were waited for; matrix products, arithmetic and copies ran while one was open for 14% of the time, Pallas kernels for 40%

profile of v4, /device:TPU:0, one launch (start us, length us, event | category | flops | bytes accessed | tf_op | source)
XLA Modules:
  0.0 517.9 jit_solution(1607867334953477673)
XLA Ops:
  7.3 2.2 dynamic-slice_bitcast_fusion.3
  23.4 2.6 collective-permute-start.3
  26.1 2.6 collective-permute-start.4
  31.4 14.7 %attend.2 = bf16[512,768]{1,0:T(8,128)(2,1)S(1)} custom-call(f32[12,2,1024]{2,1,0:T(2,128)S(1)} %bitcast.222, bf16[1024,768]{1,0:T(8,128)(2,1)S(1)} %bitcast.204, bf16[1024,768]{1,0:T(8,128)(2,1)S(1)} %bitcast.210, bf16[1024,768]{1,0:T(8,128)(2,1)S(1)} %bitcast.216), custom_call_target="tpu_custom_call" | custom-call | flops 402653184 | bytes 1572864 | tf_op jit(solution)/shard_map/attend/pallas_call | solution.py:196
  46.3 8.5 %collective-permute-done.4.refs_7_ = bf16[256,768]{1,0:T(8,128)(2,1)S(1)} collective-permute-done((bf16[256,768]{1,0:T(8,128)(2,1)S(1)}, bf16[256,768]{1,0:T(8,128)(2,1)S(1)}, u32[]{:S(2)}, u32[]{:S(2)}) %collective-permute-start.4) | collective-permute-done | bytes 393248 | tf_op jit(solution)/shard_map/ppermute | solution.py:587
  54.9 2.3 after_attention.2
  57.2 9.0 %collective-permute-start.6 = (bf16[256,768]{1,0:T(8,128)(2,1)S(1)}, bf16[256,768]{1,0:T(8,128)(2,1)S(1)}, u32[]{:S(2)}, u32[]{:S(2)}) collective-permute-start(bf16[256,768]{1,0:T(8,128)(2,1)S(1)} %get-tuple-element.172), channel_id=1, source_target_pairs={{0,1},{1,2},{2,3},{3,0},{4,5},{5,6},{6,7},{7,4},{8,9},{9,10},{10,1... | collective-permute-start | bytes 1179656 | tf_op jit(solution)/shard_map/ppermute | solution.py:587
  71.3 14.3 %attend.3 = bf16[512,768]{1,0:T(8,128)(2,1)S(1)} custom-call(f32[12,2,1024]{2,1,0:T(2,128)S(1)} %bitcast.223, bf16[1024,768]{1,0:T(8,128)(2,1)S(1)} %bitcast.205, bf16[1024,768]{1,0:T(8,128)(2,1)S(1)} %bitcast.211, bf16[1024,768]{1,0:T(8,128)(2,1)S(1)} %bitcast.217), custom_call_target="tpu_custom_call" | custom-call | flops 402653184 | bytes 1572864 | tf_op jit(solution)/shard_map/attend/pallas_call | solution.py:196
  86.6 6.7 %collective-permute-done.7.refs_3_.refs_2_ = bf16[256,768]{1,0:T(8,128)(2,1)S(1)} collective-permute-done((bf16[256,768]{1,0:T(8,128)(2,1)S(1)}, bf16[256,768]{1,0:T(8,128)(2,1)S(1)}, u32[]{:S(2)}, u32[]{:S(2)}) %collective-permute-start.7) | collective-permute-done | bytes 393248 | tf_op jit(solution)/shard_map/ppermute | solution.py:587
  94.7 8.1 %collective-permute-start.12 = (bf16[256,768]{1,0:T(8,128)(2,1)}, bf16[256,768]{1,0:T(8,128)(2,1)}, u32[]{:S(2)}, u32[]{:S(2)}) collective-permute-start(bf16[256,768]{1,0:T(8,128)(2,1)} %get-tuple-element.193), channel_id=1, source_target_pairs={{0,1},{1,2},{2,3},{3,0},{4,5},{5,6},{6,7},{7,4},{8,9},{9,10},{10,1... | collective-permute-start | bytes 1179656 | tf_op jit(solution)/shard_map/ppermute | solution.py:587
  105.6 2.4 collective-permute-start.13
  108.0 2.3 after_attention.3
  112.9 2.9 collective-permute-start.11
  116.9 29.7 %experts.2 = (bf16[512,768]{1,0:T(8,128)(2,1)S(1)}, bf16[512,768]{1,0:T(8,128)(2,1)}, bf16[512,768]{1,0:T(8,128)(2,1)}, bf16[512,768]{1,0:T(8,128)(2,1)}, bf16[2...) custom-call(s32[1]{0:T(128)} %bitcast.refs_0_, ...), custom_call_target="tpu_custom_call" | custom-call | flops 38654705664 | bytes 18874368 | tf_op jit(solution)/shard_map/experts/pallas_call | solution.py:383
  147.4 10.2 %collective-permute-start.15 = (bf16[256,768]{1,0:T(8,128)(2,1)S(1)}, bf16[256,768]{1,0:T(8,128)(2,1)S(1)}, u32[]{:S(2)}, u32[]{:S(2)}) collective-permute-start(bf16[256,768]{1,0:T(8,128)(2,1)S(1)} %get-tuple-element.221), channel_id=1, source_target_pairs={{0,3},{1,0},{2,1},{3,2},{4,7},{5,4},{6,5},{7,6},{8,11},{9,8},{10,9... | collective-permute-start | bytes 1179656 | tf_op jit(solution)/shard_map/ppermute | solution.py:587
  157.5 7.6 %collective-permute-done.10.refs_3_.refs_6_ = bf16[256,768]{1,0:T(8,128)(2,1)S(1)} collective-permute-done((bf16[256,768]{1,0:T(8,128)(2,1)S(1)}, bf16[256,768]{1,0:T(8,128)(2,1)S(1)}, u32[]{:S(2)}, u32[]{:S(2)}) %collective-permute-start.10) | collective-permute-done | bytes 393248 | tf_op jit(solution)/shard_map/ppermute | solution.py:587
  165.1 15.3 %collective-permute-start.17 = (bf16[256,768]{1,0:T(8,128)(2,1)S(1)}, bf16[256,768]{1,0:T(8,128)(2,1)S(1)}, u32[]{:S(2)}, u32[]{:S(2)}) collective-permute-start(bf16[256,768]{1,0:T(8,128)(2,1)S(1)} %get-tuple-element.223), channel_id=1, source_target_pairs={{0,1},{1,2},{2,3},{3,0},{4,5},{5,6},{6,7},{7,4},{8,9},{9,10},{10,1... | collective-permute-start | bytes 1179656 | tf_op jit(solution)/shard_map/ppermute | solution.py:587
  180.4 29.7 %experts.3 = (bf16[512,768]{1,0:T(8,128)(2,1)S(1)}, bf16[512,768]{1,0:T(8,128)(2,1)}, bf16[512,768]{1,0:T(8,128)(2,1)}, bf16[512,768]{1,0:T(8,128)(2,1)}, bf16[2...) custom-call(s32[1]{0:T(128)} %bitcast.refs_0_, ...), custom_call_target="tpu_custom_call", output_to_operand_aliasing={{0}: (12, {}), {1}: (13, {}), {2}: (14, {}), {3}: (15, {})} | custom-call | flops 38654705664 | bytes 18874368 | tf_op jit(solution)/shard_map/experts/pallas_call | solution.py:383
  211.9 2.9 collective-permute-start.18
  214.8 7.2 %collective-permute-start.19 = (bf16[256,768]{1,0:T(8,128)(2,1)S(1)}, bf16[256,768]{1,0:T(8,128)(2,1)}, u32[]{:S(2)}, u32[]{:S(2)}) collective-permute-start(bf16[256,768]{1,0:T(8,128)(2,1)S(1)} %get-tuple-element.237), channel_id=1, source_target_pairs={{0,2},{1,3},{2,0},{3,1},{4,6},{5,7},{6,4},{7,5},{8,10},{9,11},{10,... | collective-permute-start | bytes 1179656 | tf_op jit(solution)/shard_map/ppermute | solution.py:587
  223.9 27.1 %expert_grads.1 = bf16[3072,1536]{1,0:T(8,128)(2,1)} custom-call(bf16[256,768]{1,0:T(8,128)(2,1)S(1)} %copy-done.30, bf16[256,768]{1,0:T(8,128)(2,1)S(1)} %copy-done.32, bf16[256,768]{1,0:T(8,128)(2,1)S(1)} %copy-done.34, bf16[256,768]{1,0:T(8,128)(2,1)S(1)} %copy-done.36, bf16[256,768]{1,0:T(8,128)(2,1)S(1)} %get-tuple-element.180.refs_1_.refs_4_, ...), custom_call_target="tpu_custom_call" | custom-call | flops 28991029248 | bytes 34603008 | tf_op jit(solution)/shard_map/expert_grads/pallas_call | solution.py:448
  251.0 4.4 collective-permute-done.19.refs_3_
  255.8 7.6 %before_attention.2 = (f32[1,512,768]{2,1,0:T(8,128)}, bf16[1,512,768]{2,1,0:T(8,128)(2,1)}, f32[768,768]{1,0:T(8,128)}, f32[1,768]{1,0:T(1,128)}) custom-call(s32[1,1,512]{2,1,0:T(1,128)} %copy-done.25, bf16[256,768]{1,0:T(8,128)(2,1)} %copy-done.22, bf16[256,768]{1,0:T(8,128)(2,1)} %copy-done.85, bf16[256,768]{1,0:T(8,128)(2,1)} %copy-done.86, ...), custom_call_target="tpu_custom_call" | custom-call | tf_op jit(solution)/shard_map/before_attention/pallas_call | solution.py:569
  263.4 8.9 %before_attention.3 = (f32[1,512,768]{2,1,0:T(8,128)}, bf16[1,512,768]{2,1,0:T(8,128)(2,1)}, f32[768,768]{1,0:T(8,128)}, f32[1,768]{1,0:T(1,128)}) custom-call(s32[1,1,512]{2,1,0:T(1,128)} %copy-done.27, bf16[256,768]{1,0:T(8,128)(2,1)} %copy-done.23, bf16[256,768]{1,0:T(8,128)(2,1)} %collective-permute-done.18.refs_2_, ...), custom_call_target="tpu_custom_call" | custom-call | tf_op jit(solution)/shard_map/before_attention/pallas_call | solution.py:569
  273.0 2.6 pad_maximum_fusion.2
  275.6 2.2 add_convert_fusion
  279.4 33.4 %attend_back.4 = (bf16[3,1024,384]{2,1,0:T(8,128)(2,1)}, f32[3,2,128]{2,1,0:T(2,128)S(1)}) custom-call(f32[12,2,1024]{2,1,0:T(2,128)S(1)} %bitcast.224, f32[3,512,128]{2,1,0:T(8,128)S(1)} %copy-done.48, bf16[1024,768]{1,0:T(8,128)(2,1)S(1)} %bitcast.206, bf16[1024,768]{1,0:T(8,128)(2,1)S(1)} %bitcast.212, bf16[1024,768]{1,0:T(8,128)(2,1)S(1)} %bitcast.218, ...), custom_call_target="tpu_custom_call" | custom-call | flops 33822867456 | bytes 5505024 | tf_op jit(solution)/shard_map/attend_back/pallas_call | solution.py:286
  312.8 2.6 fusion.19
  321.2 4.2 fusion.37
  325.4 12.2 %attend_back.5 = (bf16[3,1024,384]{2,1,0:T(8,128)(2,1)}, f32[1,2,128]{2,1,0:T(2,128)S(1)}) custom-call(f32[12,2,1024]{2,1,0:T(2,128)S(1)} %bitcast.225, f32[3,512,128]{2,1,0:T(8,128)S(1)} %copy-done.49, bf16[1024,768]{1,0:T(8,128)(2,1)S(1)} %bitcast.207, bf16[1024,768]{1,0:T(8,128)(2,1)S(1)} %bitcast.213, bf16[1024,768]{1,0:T(8,128)(2,1)S(1)} %bitcast.219, ...), custom_call_target="tpu_custom_call" | custom-call | flops 11274289152 | bytes 1835008 | tf_op jit(solution)/shard_map/attend_back/pallas_call | solution.py:286
  343.1 12.3 %attend_back.6 = (bf16[3,1024,384]{2,1,0:T(8,128)(2,1)}, f32[1,2,128]{2,1,0:T(2,128)S(1)}) custom-call(f32[12,2,1024]{2,1,0:T(2,128)S(1)} %bitcast.226, f32[3,512,128]{2,1,0:T(8,128)S(1)} %copy-done.49, bf16[1024,768]{1,0:T(8,128)(2,1)S(1)} %bitcast.208, bf16[1024,768]{1,0:T(8,128)(2,1)S(1)} %bitcast.214, ...), custom_call_target="tpu_custom_call", output_to_operand_aliasing={{0}: (6, {})} | custom-call | flops 11274289152 | bytes 1835008 | tf_op jit(solution)/shard_map/attend_back/pallas_call | solution.py:286
  355.4 2.1 collective-permute-start.28
  357.5 2.7 collective-permute-done.23
  361.9 12.1 %attend_back.7 = (bf16[3,1024,384]{2,1,0:T(8,128)(2,1)}, f32[1,2,128]{2,1,0:T(2,128)S(1)}) custom-call(f32[12,2,1024]{2,1,0:T(2,128)S(1)} %bitcast.227, f32[3,512,128]{2,1,0:T(8,128)S(1)} %copy-done.49, bf16[1024,768]{1,0:T(8,128)(2,1)S(1)} %bitcast.209, bf16[1024,768]{1,0:T(8,128)(2,1)S(1)} %bitcast.215, ...), custom_call_target="tpu_custom_call", output_to_operand_aliasing={{0}: (6, {})} | custom-call | flops 11274289152 | bytes 1835008 | tf_op jit(solution)/shard_map/attend_back/pallas_call | solution.py:286
  373.9 23.2 %collective-permute-done.25 = bf16[496,384]{1,0:T(8,128)(2,1)S(1)} collective-permute-done((bf16[496,384]{1,0:T(8,128)(2,1)S(1)}, bf16[496,384]{1,0:T(8,128)(2,1)S(1)}, u32[]{:S(2)}, u32[]{:S(2)}) %collective-permute-start.25) | collective-permute-done | bytes 380960 | tf_op jit(solution)/shard_map/ppermute | solution.py:645
  398.0 3.0 collective-permute-start.37
  401.0 2.1 fusion.40
  403.2 4.2 fusion.43
  407.4 11.2 %collective-permute-done.37 = bf16[496,384]{1,0:T(8,128)(2,1)} collective-permute-done((bf16[496,384]{1,0:T(8,128)(2,1)}, bf16[496,384]{1,0:T(8,128)(2,1)}, u32[]{:S(2)}, u32[]{:S(2)}) %collective-permute-start.37) | collective-permute-done | bytes 380960 | tf_op jit(solution)/shard_map/ppermute | solution.py:645
  420.6 2.8 fusion.16
  441.8 5.6 %collective-permute-done.32 = bf16[304,384]{1,0:T(8,128)(2,1)S(1)} collective-permute-done((bf16[304,384]{1,0:T(8,128)(2,1)S(1)}, bf16[304,384]{1,0:T(8,128)(2,1)S(1)}, u32[]{:S(2)}, u32[]{:S(2)}) %collective-permute-start.32) | collective-permute-done | bytes 233504 | tf_op jit(solution)/shard_map/ppermute | solution.py:645
  447.4 5.5 %collective-permute-done.33 = bf16[304,384]{1,0:T(8,128)(2,1)S(1)} collective-permute-done((bf16[304,384]{1,0:T(8,128)(2,1)S(1)}, bf16[304,384]{1,0:T(8,128)(2,1)S(1)}, u32[]{:S(2)}, u32[]{:S(2)}) %collective-permute-start.33) | collective-permute-done | bytes 233504 | tf_op jit(solution)/shard_map/ppermute | solution.py:645
  452.9 4.1 collective-permute-done.34
  457.2 2.2 slice_bitcast_fusion.2
  459.6 5.0 collective-permute-done.35
  467.7 6.0 %collective-permute-done.36 = bf16[304,384]{1,0:T(8,128)(2,1)S(1)} collective-permute-done((bf16[304,384]{1,0:T(8,128)(2,1)S(1)}, bf16[304,384]{1,0:T(8,128)(2,1)S(1)}, u32[]{:S(2)}, u32[]{:S(2)}) %collective-permute-start.36) | collective-permute-done | bytes 233504 | tf_op jit(solution)/shard_map/ppermute | solution.py:645
  494.2 7.9 %all-gather.5.cloned.1.call-done = bf16[2432,384]{1,0:T(8,128)(2,1)} async-done(((bf16[304,384]{1,0:T(8,128)(2,1)}), bf16[2432,384]{1,0:T(8,128)(2,1)}) %all-gather.5.cloned.1.call-update) | async-done | bytes 1867792 | tf_op jit(solution)/shard_map/all_gather | solution.py:680
  508.1 2.5 multiply_reduce_fusion
  (336 shorter events, 101.9 us)
Async XLA Ops:
  7.2 413.4 %reduce-scatter.2.cloned.1.call-start = ((), (), s32[]{:S(2)}) async-start(), calls=%async_computation.1 | async-start | bytes 10616832 | tf_op jit(solution)/shard_map/reduce_scatter | solution.py:770
  9.5 4.4 collective-permute-start.2
  11.3 1.9 collective-permute-start
  12.3 3.1 collective-permute-start.1
  13.1 57.4 %copy-start.18 = (f32[2,1024,12]{1,0,2:T(2,128)}, f32[2,1024,12]{1,0,2:T(2,128)S(1)}, u32[]{:S(2)}) copy-start(f32[2,1024,12]{1,0,2:T(2,128)S(1)} %copy.52) | copy-start | bytes 294916
  13.2 94.8 %copy-start.24 = (f32[1,768]{1,0:T(1,128)}, f32[1,768]{1,0:T(1,128)S(1)}, u32[]{:S(2)}) copy-start(f32[1,768]{1,0:T(1,128)S(1)} %broadcast_in_dim.11.gain_ref.refs_9_) | copy-start | bytes 9220
  17.3 51.5 %copy-start.3 = (bf16[1,512,768]{2,1,0:T(8,128)(2,1)}, bf16[1,512,768]{2,1,0:T(8,128)(2,1)S(1)}, u32[]{:S(2)}) copy-start(bf16[1,512,768]{2,1,0:T(8,128)(2,1)S(1)} %get-tuple-element.335.refs_2_.refs_6_) | copy-start | bytes 2359300
  22.0 48.5 %copy-start.7 = (bf16[2,512,768]{2,1,0:T(8,128)(2,1)}, bf16[2,512,768]{2,1,0:T(8,128)(2,1)S(1)}, u32[]{:S(2)}) copy-start(bf16[2,512,768]{2,1,0:T(8,128)(2,1)S(1)} %convolution_convert_fusion.2) | copy-start | bytes 4718596
  23.4 47.1 %copy-start.9 = (bf16[2,512,768]{2,1,0:T(8,128)(2,1)}, bf16[2,512,768]{2,1,0:T(8,128)(2,1)S(1)}, u32[]{:S(2)}) copy-start(bf16[2,512,768]{2,1,0:T(8,128)(2,1)S(1)} %convolution_convert_fusion.1) | copy-start | bytes 4718596
  23.4 22.8 %collective-permute-start.3 = (bf16[256,768]{1,0:T(8,128)(2,1)S(1)}, bf16[256,768]{1,0:T(8,128)(2,1)S(1)}, u32[]{:S(2)}, u32[]{:S(2)}) collective-permute-start(bf16[256,768]{1,0:T(8,128)(2,1)S(1)} %get-tuple-element.160), channel_id=1, source_target_pairs={{0,1},{1,2},{2,3},{3,0},{4,5},{5,6},{6,7},{7,4},{8,9},{9,10},{10,1... | collective-permute-start | bytes 1179656 | tf_op jit(solution)/shard_map/ppermute | solution.py:587
  26.1 28.8 %collective-permute-start.4 = (bf16[256,768]{1,0:T(8,128)(2,1)S(1)}, bf16[256,768]{1,0:T(8,128)(2,1)S(1)}, u32[]{:S(2)}, u32[]{:S(2)}) collective-permute-start(bf16[256,768]{1,0:T(8,128)(2,1)S(1)} %get-tuple-element.161), channel_id=1, source_target_pairs={{0,2},{1,3},{2,0},{3,1},{4,6},{5,7},{6,4},{7,5},{8,10},{9,11},{10,... | collective-permute-start | bytes 1179656 | tf_op jit(solution)/shard_map/ppermute | solution.py:587
  28.7 26.2 %collective-permute-start.5 = (bf16[256,768]{1,0:T(8,128)(2,1)S(1)}, bf16[256,768]{1,0:T(8,128)(2,1)S(1)}, u32[]{:S(2)}, u32[]{:S(2)}) collective-permute-start(bf16[256,768]{1,0:T(8,128)(2,1)S(1)} %get-tuple-element.162), channel_id=1, source_target_pairs={{0,3},{1,0},{2,1},{3,2},{4,7},{5,4},{6,5},{7,6},{8,11},{9,8},{10,9... | collective-permute-start | bytes 1179656 | tf_op jit(solution)/shard_map/ppermute | solution.py:587
  57.2 28.5 %collective-permute-start.6 = (bf16[256,768]{1,0:T(8,128)(2,1)S(1)}, bf16[256,768]{1,0:T(8,128)(2,1)S(1)}, u32[]{:S(2)}, u32[]{:S(2)}) collective-permute-start(bf16[256,768]{1,0:T(8,128)(2,1)S(1)} %get-tuple-element.172), channel_id=1, source_target_pairs={{0,1},{1,2},{2,3},{3,0},{4,5},{5,6},{6,7},{7,4},{8,9},{9,10},{10,1... | collective-permute-start | bytes 1179656 | tf_op jit(solution)/shard_map/ppermute | solution.py:587
  66.2 27.0 %collective-permute-start.7 = (bf16[256,768]{1,0:T(8,128)(2,1)S(1)}, bf16[256,768]{1,0:T(8,128)(2,1)S(1)}, u32[]{:S(2)}, u32[]{:S(2)}) collective-permute-start(bf16[256,768]{1,0:T(8,128)(2,1)S(1)} %get-tuple-element.173), channel_id=1, source_target_pairs={{0,2},{1,3},{2,0},{3,1},{4,6},{5,7},{6,4},{7,5},{8,10},{9,11},{10,... | collective-permute-start | bytes 1179656 | tf_op jit(solution)/shard_map/ppermute | solution.py:587
  67.8 26.2 %collective-permute-start.8 = (bf16[256,768]{1,0:T(8,128)(2,1)S(1)}, bf16[256,768]{1,0:T(8,128)(2,1)S(1)}, u32[]{:S(2)}, u32[]{:S(2)}) collective-permute-start(bf16[256,768]{1,0:T(8,128)(2,1)S(1)} %get-tuple-element.174), channel_id=1, source_target_pairs={{0,3},{1,0},{2,1},{3,2},{4,7},{5,4},{6,5},{7,6},{8,11},{9,8},{10,9... | collective-permute-start | bytes 1179656 | tf_op jit(solution)/shard_map/ppermute | solution.py:587
  85.7 60.9 %copy-start.6 = (bf16[512,768]{1,0:T(8,128)(2,1)}, bf16[512,768]{1,0:T(8,128)(2,1)S(1)}, u32[]{:S(2)}) copy-start(bf16[512,768]{1,0:T(8,128)(2,1)S(1)} %attend.3) | copy-start | bytes 2359300
  94.7 21.1 %collective-permute-start.12 = (bf16[256,768]{1,0:T(8,128)(2,1)}, bf16[256,768]{1,0:T(8,128)(2,1)}, u32[]{:S(2)}, u32[]{:S(2)}) collective-permute-start(bf16[256,768]{1,0:T(8,128)(2,1)} %get-tuple-element.193), channel_id=1, source_target_pairs={{0,1},{1,2},{2,3},{3,0},{4,5},{5,6},{6,7},{7,4},{8,9},{9,10},{10,1... | collective-permute-start | bytes 1179656 | tf_op jit(solution)/shard_map/ppermute | solution.py:587
  105.6 41.8 %collective-permute-start.13 = (bf16[256,768]{1,0:T(8,128)(2,1)}, bf16[256,768]{1,0:T(8,128)(2,1)S(1)}, u32[]{:S(2)}, u32[]{:S(2)}) collective-permute-start(bf16[256,768]{1,0:T(8,128)(2,1)} %copy-done.47), channel_id=1, source_target_pairs={{0,2},{1,3},{2,0},{3,1},{4,6},{5,7},{6,4},{7,5},{8,10},{9,11},{10,... | collective-permute-start | bytes 1179656 | tf_op jit(solution)/shard_map/ppermute | solution.py:587
  108.0 49.5 %collective-permute-start.14 = (bf16[256,768]{1,0:T(8,128)(2,1)S(1)}, bf16[256,768]{1,0:T(8,128)(2,1)S(1)}, u32[]{:S(2)}, u32[]{:S(2)}) collective-permute-start(bf16[256,768]{1,0:T(8,128)(2,1)S(1)} %get-tuple-element.195), channel_id=1, source_target_pairs={{0,3},{1,0},{2,1},{3,2},{4,7},{5,4},{6,5},{7,6},{8,11},{9,8},{10,9... | collective-permute-start | bytes 1179656 | tf_op jit(solution)/shard_map/ppermute | solution.py:587
  111.5 53.6 %collective-permute-start.10 = (bf16[256,768]{1,0:T(8,128)(2,1)S(1)}, bf16[256,768]{1,0:T(8,128)(2,1)S(1)}, u32[]{:S(2)}, u32[]{:S(2)}) collective-permute-start(bf16[256,768]{1,0:T(8,128)(2,1)S(1)} %get-tuple-element.182), channel_id=1, source_target_pairs={{0,2},{1,3},{2,0},{3,1},{4,6},{5,7},{6,4},{7,5},{8,10},{9,11},{10,... | collective-permute-start | bytes 1179656 | tf_op jit(solution)/shard_map/ppermute | solution.py:587
  112.9 67.4 %collective-permute-start.11 = (bf16[256,768]{1,0:T(8,128)(2,1)S(1)}, bf16[256,768]{1,0:T(8,128)(2,1)S(1)}, u32[]{:S(2)}, u32[]{:S(2)}) collective-permute-start(bf16[256,768]{1,0:T(8,128)(2,1)S(1)} %get-tuple-element.183), channel_id=1, source_target_pairs={{0,3},{1,0},{2,1},{3,2},{4,7},{5,4},{6,5},{7,6},{8,11},{9,8},{10,9... | collective-permute-start | bytes 1179656 | tf_op jit(solution)/shard_map/ppermute | solution.py:587
  115.9 64.5 %collective-permute-start.9 = (bf16[256,768]{1,0:T(8,128)(2,1)S(1)}, bf16[256,768]{1,0:T(8,128)(2,1)S(1)}, u32[]{:S(2)}, u32[]{:S(2)}) collective-permute-start(bf16[256,768]{1,0:T(8,128)(2,1)S(1)} %get-tuple-element.181), channel_id=1, source_target_pairs={{0,1},{1,2},{2,3},{3,0},{4,5},{5,6},{6,7},{7,4},{8,9},{9,10},{10,1... | collective-permute-start | bytes 1179656 | tf_op jit(solution)/shard_map/ppermute | solution.py:587
  116.9 63.5 %copy-start.44 = (bf16[256,768]{1,0:T(8,128)(2,1)S(1)}, bf16[256,768]{1,0:T(8,128)(2,1)}, u32[]{:S(2)}) copy-start(bf16[256,768]{1,0:T(8,128)(2,1)} %copy-done.43) | copy-start | bytes 1179652
  147.4 64.4 %collective-permute-start.15 = (bf16[256,768]{1,0:T(8,128)(2,1)S(1)}, bf16[256,768]{1,0:T(8,128)(2,1)S(1)}, u32[]{:S(2)}, u32[]{:S(2)}) collective-permute-start(bf16[256,768]{1,0:T(8,128)(2,1)S(1)} %get-tuple-element.221), channel_id=1, source_target_pairs={{0,3},{1,0},{2,1},{3,2},{4,7},{5,4},{6,5},{7,6},{8,11},{9,8},{10,9... | collective-permute-start | bytes 1179656 | tf_op jit(solution)/shard_map/ppermute | solution.py:587
  157.5 54.3 %collective-permute-start.16 = (bf16[256,768]{1,0:T(8,128)(2,1)S(1)}, bf16[256,768]{1,0:T(8,128)(2,1)S(1)}, u32[]{:S(2)}, u32[]{:S(2)}) collective-permute-start(bf16[256,768]{1,0:T(8,128)(2,1)S(1)} %get-tuple-element.222), channel_id=1, source_target_pairs={{0,2},{1,3},{2,0},{3,1},{4,6},{5,7},{6,4},{7,5},{8,10},{9,11},{10,... | collective-permute-start | bytes 1179656 | tf_op jit(solution)/shard_map/ppermute | solution.py:587
  165.1 46.7 %collective-permute-start.17 = (bf16[256,768]{1,0:T(8,128)(2,1)S(1)}, bf16[256,768]{1,0:T(8,128)(2,1)S(1)}, u32[]{:S(2)}, u32[]{:S(2)}) collective-permute-start(bf16[256,768]{1,0:T(8,128)(2,1)S(1)} %get-tuple-element.223), channel_id=1, source_target_pairs={{0,1},{1,2},{2,3},{3,0},{4,5},{5,6},{6,7},{7,4},{8,9},{9,10},{10,1... | collective-permute-start | bytes 1179656 | tf_op jit(solution)/shard_map/ppermute | solution.py:587
  211.9 39.1 %collective-permute-start.18 = (bf16[256,768]{1,0:T(8,128)(2,1)S(1)}, bf16[256,768]{1,0:T(8,128)(2,1)}, u32[]{:S(2)}, u32[]{:S(2)}) collective-permute-start(bf16[256,768]{1,0:T(8,128)(2,1)S(1)} %get-tuple-element.236), channel_id=1, source_target_pairs={{0,3},{1,0},{2,1},{3,2},{4,7},{5,4},{6,5},{7,6},{8,11},{9,8},{10,9... | collective-permute-start | bytes 1179656 | tf_op jit(solution)/shard_map/ppermute | solution.py:587
  214.8 40.6 %collective-permute-start.19 = (bf16[256,768]{1,0:T(8,128)(2,1)S(1)}, bf16[256,768]{1,0:T(8,128)(2,1)}, u32[]{:S(2)}, u32[]{:S(2)}) collective-permute-start(bf16[256,768]{1,0:T(8,128)(2,1)S(1)} %get-tuple-element.237), channel_id=1, source_target_pairs={{0,2},{1,3},{2,0},{3,1},{4,6},{5,7},{6,4},{7,5},{8,10},{9,11},{10,... | collective-permute-start | bytes 1179656 | tf_op jit(solution)/shard_map/ppermute | solution.py:587
  221.9 33.5 %collective-permute-start.20 = (bf16[256,768]{1,0:T(8,128)(2,1)S(1)}, bf16[256,768]{1,0:T(8,128)(2,1)}, u32[]{:S(2)}, u32[]{:S(2)}) collective-permute-start(bf16[256,768]{1,0:T(8,128)(2,1)S(1)} %get-tuple-element.238), channel_id=1, source_target_pairs={{0,1},{1,2},{2,3},{3,0},{4,5},{5,6},{6,7},{7,4},{8,9},{9,10},{10,1... | collective-permute-start | bytes 1179656 | tf_op jit(solution)/shard_map/ppermute | solution.py:587
  255.4 219.1 %all-gather.3.cloned.1.call-start = ((), (), s32[]{:S(2)}) async-start(), calls=%async_computation.2 | async-start | bytes 3428352 | tf_op jit(solution)/shard_map/all_gather | solution.py:680
  320.7 16.9 %collective-permute-start.21 = (bf16[4,496,384]{2,1,0:T(8,128)(2,1)}, bf16[4,496,384]{2,1,0:T(8,128)(2,1)}, u32[]{:S(2)}, u32[]{:S(2)}) collective-permute-start(bf16[4,496,384]{2,1,0:T(8,128)(2,1)} %dynamic-slice_bitcast_fusion.1), channel_id=1, source_target_pairs={{0,4},{4,0},{1,5},{5,1},{2,6},{6,2},{3,7},{7,3},{8,12},{12,8},{9,1... | collective-permute-start | bytes 4571144 | tf_op jit(solution)/shard_map/ppermute | solution.py:645
  320.7 99.8 %collective-permute-start.26 = (bf16[512,768]{1,0:T(8,128)(2,1)}, bf16[512,768]{1,0:T(8,128)(2,1)}, u32[]{:S(2)}, u32[]{:S(2)}) collective-permute-start(bf16[512,768]{1,0:T(8,128)(2,1)} %get-tuple-element.275), channel_id=1, source_target_pairs={{0,3},{1,0},{2,1},{3,2},{4,7},{5,4},{6,5},{7,6},{8,11},{9,8},{10,9... | collective-permute-start | bytes 2359304 | tf_op jit(solution)/shard_map/ppermute | solution.py:587
  321.1 99.4 %collective-permute-start.27 = (bf16[512,768]{1,0:T(8,128)(2,1)}, bf16[512,768]{1,0:T(8,128)(2,1)}, u32[]{:S(2)}, u32[]{:S(2)}) collective-permute-start(bf16[512,768]{1,0:T(8,128)(2,1)} %get-tuple-element.276), channel_id=1, source_target_pairs={{0,2},{1,3},{2,0},{3,1},{4,6},{5,7},{6,4},{7,5},{8,10},{9,11},{10,... | collective-permute-start | bytes 2359304 | tf_op jit(solution)/shard_map/ppermute | solution.py:587
  339.6 15.8 %collective-permute-start.22 = (bf16[496,384]{1,0:T(8,128)(2,1)S(1)}, bf16[496,384]{1,0:T(8,128)(2,1)S(1)}, u32[]{:S(2)}, u32[]{:S(2)}) collective-permute-start(bf16[496,384]{1,0:T(8,128)(2,1)S(1)} %get-tuple-element.263), channel_id=1, source_target_pairs={{0,8},{8,0},{16,24},{24,16},{1,9},{9,1},{17,25},{25,17},{2,10},{10... | collective-permute-start | bytes 1142792 | tf_op jit(solution)/shard_map/ppermute | solution.py:645
  341.0 19.2 %collective-permute-start.23 = (bf16[496,384]{1,0:T(8,128)(2,1)S(1)}, bf16[496,384]{1,0:T(8,128)(2,1)S(1)}, u32[]{:S(2)}, u32[]{:S(2)}) collective-permute-start(bf16[496,384]{1,0:T(8,128)(2,1)S(1)} %get-tuple-element.264), channel_id=1, source_target_pairs={{0,16},{8,24},{16,0},{24,8},{1,17},{9,25},{17,1},{25,9},{2,18},{10... | collective-permute-start | bytes 1142792 | tf_op jit(solution)/shard_map/ppermute | solution.py:645
  342.5 17.6 %collective-permute-start.24 = (bf16[496,384]{1,0:T(8,128)(2,1)S(1)}, bf16[496,384]{1,0:T(8,128)(2,1)S(1)}, u32[]{:S(2)}, u32[]{:S(2)}) collective-permute-start(bf16[496,384]{1,0:T(8,128)(2,1)S(1)} %get-tuple-element.265), channel_id=1, source_target_pairs={{0,24},{8,16},{16,8},{24,0},{1,25},{9,17},{17,9},{25,1},{2,26},{10... | collective-permute-start | bytes 1142792 | tf_op jit(solution)/shard_map/ppermute | solution.py:645
  355.4 65.2 %collective-permute-start.28 = (bf16[512,768]{1,0:T(8,128)(2,1)}, bf16[512,768]{1,0:T(8,128)(2,1)}, u32[]{:S(2)}, u32[]{:S(2)}) collective-permute-start(bf16[512,768]{1,0:T(8,128)(2,1)} %get-tuple-element.277), channel_id=1, source_target_pairs={{0,1},{1,2},{2,3},{3,0},{4,5},{5,6},{6,7},{7,4},{8,9},{9,10},{10,1... | collective-permute-start | bytes 2359304 | tf_op jit(solution)/shard_map/ppermute | solution.py:587
  360.4 36.8 %collective-permute-start.25 = (bf16[496,384]{1,0:T(8,128)(2,1)S(1)}, bf16[496,384]{1,0:T(8,128)(2,1)S(1)}, u32[]{:S(2)}, u32[]{:S(2)}) collective-permute-start(bf16[496,384]{1,0:T(8,128)(2,1)S(1)} %fusion.52), channel_id=1, source_target_pairs={{0,1},{1,0},{2,3},{3,2},{4,5},{5,4},{6,7},{7,6},{8,9},{9,8},{10,11... | collective-permute-start | bytes 1142792 | tf_op jit(solution)/shard_map/ppermute | solution.py:645
  398.0 20.5 %collective-permute-start.37 = (bf16[496,384]{1,0:T(8,128)(2,1)}, bf16[496,384]{1,0:T(8,128)(2,1)}, u32[]{:S(2)}, u32[]{:S(2)}) collective-permute-start(bf16[496,384]{1,0:T(8,128)(2,1)} %add_convert_fusion.2), channel_id=1, source_target_pairs={{0,2},{1,3},{2,0},{3,1},{4,6},{5,7},{6,4},{7,5},{8,10},{9,11},{10,... | collective-permute-start | bytes 1142792 | tf_op jit(solution)/shard_map/ppermute | solution.py:645
  420.5 81.6 %all-gather.5.cloned.1.call-start = ((), (), s32[]{:S(2)}) async-start(), calls=%async_computation.3 | async-start | bytes 2101248 | tf_op jit(solution)/shard_map/all_gather | solution.py:680
  425.8 10.3 %collective-permute-start.31 = (bf16[4,304,384]{2,1,0:T(8,128)(2,1)S(1)}, bf16[4,304,384]{2,1,0:T(8,128)(2,1)S(1)}, u32[]{:S(2)}, u32[]{:S(2)}) collective-permute-start(bf16[4,304,384]{2,1,0:T(8,128)(2,1)S(1)} %dynamic-slice_bitcast_fusion.2), channel_id=1, source_target_pairs={{0,4},{4,0},{1,5},{5,1},{2,6},{6,2},{3,7},{7,3},{8,12},{12,8},{9,1... | collective-permute-start | bytes 2801672 | tf_op jit(solution)/shard_map/ppermute | solution.py:645
  436.2 48.1 %collective-permute-start.30 = (f32[512,768]{1,0:T(8,128)}, f32[512,768]{1,0:T(8,128)}, u32[]{:S(2)}, u32[]{:S(2)}) collective-permute-start(f32[512,768]{1,0:T(8,128)} %dynamic-slice_bitcast_fusion), channel_id=1, source_target_pairs={{0,4},{4,0},{1,5},{5,1},{2,6},{6,2},{3,7},{7,3},{8,12},{12,8},{9,1... | collective-permute-start | bytes 4718600 | tf_op jit(solution)/shard_map/ppermute | solution.py:596
  437.0 10.4 %collective-permute-start.32 = (bf16[304,384]{1,0:T(8,128)(2,1)S(1)}, bf16[304,384]{1,0:T(8,128)(2,1)S(1)}, u32[]{:S(2)}, u32[]{:S(2)}) collective-permute-start(bf16[304,384]{1,0:T(8,128)(2,1)S(1)} %get-tuple-element.347), channel_id=1, source_target_pairs={{0,8},{8,0},{16,24},{24,16},{1,9},{9,1},{17,25},{25,17},{2,10},{10... | collective-permute-start | bytes 700424 | tf_op jit(solution)/shard_map/ppermute | solution.py:645
  438.3 14.6 %collective-permute-start.33 = (bf16[304,384]{1,0:T(8,128)(2,1)S(1)}, bf16[304,384]{1,0:T(8,128)(2,1)S(1)}, u32[]{:S(2)}, u32[]{:S(2)}) collective-permute-start(bf16[304,384]{1,0:T(8,128)(2,1)S(1)} %get-tuple-element.349), channel_id=1, source_target_pairs={{0,16},{8,24},{16,0},{24,8},{1,17},{9,25},{17,1},{25,9},{2,18},{10... | collective-permute-start | bytes 700424 | tf_op jit(solution)/shard_map/ppermute | solution.py:645
  439.9 17.1 %collective-permute-start.34 = (bf16[304,384]{1,0:T(8,128)(2,1)S(1)}, bf16[304,384]{1,0:T(8,128)(2,1)S(1)}, u32[]{:S(2)}, u32[]{:S(2)}) collective-permute-start(bf16[304,384]{1,0:T(8,128)(2,1)S(1)} %get-tuple-element.348), channel_id=1, source_target_pairs={{0,24},{8,16},{16,8},{24,0},{1,25},{9,17},{17,9},{25,1},{2,26},{10... | collective-permute-start | bytes 700424 | tf_op jit(solution)/shard_map/ppermute | solution.py:645
  457.1 7.5 %collective-permute-start.35 = (bf16[304,384]{1,0:T(8,128)(2,1)S(1)}, bf16[304,384]{1,0:T(8,128)(2,1)S(1)}, u32[]{:S(2)}, u32[]{:S(2)}) collective-permute-start(bf16[304,384]{1,0:T(8,128)(2,1)S(1)} %fusion.73), channel_id=1, source_target_pairs={{0,1},{1,0},{2,3},{3,2},{4,5},{5,4},{6,7},{7,6},{8,9},{9,8},{10,11... | collective-permute-start | bytes 700424 | tf_op jit(solution)/shard_map/ppermute | solution.py:645
  464.7 9.0 %collective-permute-start.36 = (bf16[304,384]{1,0:T(8,128)(2,1)S(1)}, bf16[304,384]{1,0:T(8,128)(2,1)S(1)}, u32[]{:S(2)}, u32[]{:S(2)}) collective-permute-start(bf16[304,384]{1,0:T(8,128)(2,1)S(1)} %add_convert_fusion.4), channel_id=1, source_target_pairs={{0,2},{1,3},{2,0},{3,1},{4,6},{5,7},{6,4},{7,5},{8,10},{9,11},{10,... | collective-permute-start | bytes 700424 | tf_op jit(solution)/shard_map/ppermute | solution.py:645
  478.4 3.0 collective-permute-start.29
  (90 other events, 865.2 us)
Sparse Core Ops, SparseCore 0:
  255.5 74.6 reduce-scatter.1
  420.6 39.8 all-gather.2
  474.6 27.4 all-gather.4

commit v5 on v4

--- a/solution.py
+++ b/solution.py
@@ -205,7 +205,7 @@
         name="attend",
     )(lines, q, k, v)
 
-def bwd_kernel(lines_ref, fold_ref, q_ref, k_ref, v_ref, g_ref, grad_ref, bias_ref, band_ref, acc_ref, far_acc, dk_acc, dv_acc):
+def bwd_kernel(lines_ref, fold_ref, q_ref, k_ref, v_ref, g_ref, xt_ref, grad_ref, sums_ref, band_ref, acc_ref, far_acc, dk_acc, dv_acc):
     n = q_ref.shape[0] // QB
     lane = lax.broadcasted_iota(jnp.int32, (QB, 128), 1)
     for h in range(2):
@@ -259,6 +259,7 @@
     grad_ref[1] = dk_acc[...].astype(jnp.bfloat16)
     grad_ref[2] = dv_acc[...].astype(jnp.bfloat16)
     row = lax.broadcasted_iota(jnp.int32, (8, 2 * QB), 0)
+    totals = []
     for h in range(2):
         total = jnp.zeros((8, 128), jnp.float32)
         for t in range(3):
@@ -273,29 +274,41 @@
         ends = [jnp.sum(jnp.sum(far_acc[h, side], axis=0, keepdims=True), axis=1, keepdims=True) for side in range(2)]
         column = lax.broadcasted_iota(jnp.int32, (1, 128), 1)
         total = total + jnp.where(column == 15, ends[0], 0.0) + jnp.where(column == 31, ends[1], 0.0)
-        bias_ref[0, h:h + 1, :] = total
-
-
-def attend_back(q, k, v, g, lines, first_pair, pairs, total_pairs=None, earlier=None):
-    length = q.shape[0]
+        totals.append(total)
+    width = xt_ref.shape[0]
+    for kind in range(3):
+        weight = jnp.dot(xt_ref[...], grad_ref[kind], preferred_element_type=jnp.float32)
+        sums_ref[kind * width:(kind + 1) * width, :] = weight.astype(jnp.bfloat16)
+    high = [total.astype(jnp.bfloat16).astype(jnp.float32) for total in totals]
+    rows = high + [total - part for total, part in zip(totals, high)]
+    small = jnp.concatenate(rows + [jnp.zeros((124, 128), jnp.float32)], axis=0)
+    sums_ref[3 * width:, :] = small.astype(jnp.bfloat16)
+
+
+def attend_back(q, k, v, g, xt, lines, first_pair, pairs, total_pairs, earlier=()):
+    length, width = q.shape
+    rows = 3 * width + 128
     r = (np.arange(3)[:, None] - 1) * QB - (np.arange(2 * QB)[None] - QB)
     fold = (bucket_np(r)[..., None] == np.arange(128)).astype(np.float32)
     col = pl.BlockSpec((length, 128), lambda h: (0, h + first_pair))
-    offset = first_pair % total_pairs if total_pairs else 0
-    kept = [] if earlier is None else [earlier]
-    grads, bias = pl.pallas_call(
-        lambda *refs: bwd_kernel(*refs[:6], *refs[6 + len(kept):]),
+    offset = first_pair % total_pairs
+    return pl.pallas_call(
+        lambda *refs: bwd_kernel(*refs[:7], *refs[7 + len(earlier):]),
         grid=(pairs,),
         in_specs=[
             pl.BlockSpec((2, 2, 4 * QB), lambda h: (h + first_pair, 0, 0)),
             pl.BlockSpec((3, 2 * QB, 128), lambda h: (0, 0, 0)),
             col, col, col, col,
+            pl.BlockSpec((width, length), lambda h: (0, 0), pipeline_mode=pl.Buffered(1)),
         ]
-        + [pl.BlockSpec(memory_space=pl.ANY)] * len(kept),
-        out_specs=[pl.BlockSpec((3, length, 128), lambda h: (0, 0, h + offset)), pl.BlockSpec((1, 2, 128), lambda h: (h, 0, 0))],
+        + [pl.BlockSpec(memory_space=pl.ANY)] * len(earlier),
+        out_specs=[
+            pl.BlockSpec((3, length, 128), lambda h: (0, 0, h + offset)),
+            pl.BlockSpec((rows, 128), lambda h: (0, h + offset)),
+        ],
         out_shape=[
-            jax.ShapeDtypeStruct((3, length, 128 * (total_pairs or pairs)), jnp.bfloat16),
-            jax.ShapeDtypeStruct((pairs, 2, 128), jnp.float32),
+            jax.ShapeDtypeStruct((3, length, 128 * total_pairs), jnp.bfloat16),
+            jax.ShapeDtypeStruct((rows, 128 * total_pairs), jnp.bfloat16),
         ],
         scratch_shapes=[
             pltpu.VMEM((2, 3 * QB, QB), jnp.float32),
@@ -308,10 +321,9 @@
         cost_estimate=pl.CostEstimate(
             flops=84 * length * length * 128 * pairs, bytes_accessed=14 * length * 128 * pairs, transcendentals=2 * length * length * pairs
         ),
-        input_output_aliases={6: 0} if kept else {},
+        input_output_aliases={7: 0, 8: 1} if earlier else {},
         name="attend_back",
-    )(lines, jnp.asarray(fold), q, k, v, g, *kept)
-    return grads, bias.reshape(2 * pairs, 128)
+    )(lines, jnp.asarray(fold), q, k, v, g, xt, *earlier)
 
 
 def expert_kernel(count, label_ref, *refs):
@@ -373,8 +385,8 @@
         drouter_ref[...] = total
 
 
-def run_expert(label, pieces, upstream_pieces, router_wide, w_in, w_out, group, group_count, earlier, chunk=768):
-    count, (tile, width) = len(pieces), pieces[0].shape
+def run_expert(label, pieces, upstream_pieces, tile, upstream_part, router_wide, w_in, w_out, group, group_count, earlier, chunk=768):
+    count, width = len(pieces), pieces[0].shape[1]
     rows, inner = count * tile, w_in.shape[1]
     once = pl.Buffered(1)
     piece = pl.BlockSpec((tile, width), lambda f, lab: (0, 0), pipeline_mode=once)
@@ -385,7 +397,9 @@
         grid_spec=pltpu.PrefetchScalarGridSpec(
             num_scalar_prefetch=1,
             grid=(inner // chunk,),
-            in_specs=[piece] * (2 * count) + [
+            in_specs=[piece] * count
+            + [pl.BlockSpec((tile, width), lambda f, lab: (upstream_part, 0), pipeline_mode=once)] * count
+            + [
                 pl.BlockSpec((width, 128), lambda f, lab: (0, 0), pipeline_mode=once),
                 pl.BlockSpec((width, chunk), lambda f, lab: (0, f)),
                 pl.BlockSpec((chunk, width), lambda f, lab: (f, 0)),
@@ -421,8 +435,8 @@
     g_refs, hid_refs, pre_refs = refs[:groups], refs[groups : 2 * groups], refs[2 * groups : 3 * groups]
     dw_ref, xt_ref, gt_ref = refs[3 * groups :]
     width = xt_ref.shape[0]
-    tile = x_refs[0].shape[0]
     rows = g_refs[0].shape[0]
+    tile = rows // count
 
     @pl.when(pl.program_id(0) == 0)
     def _():
@@ -442,7 +456,8 @@
 
 def expert_grads(pieces, grads, hiddens, pre_grads, chunk=512):
     groups, count = len(grads), len(pieces) // len(grads)
-    (tile, width), (rows, inner) = pieces[0].shape, hiddens[0].shape
+    width, (rows, inner) = pieces[0].shape[1], hiddens[0].shape
+    tile = rows // count
     once = pl.Buffered(1)
     inner_block = pl.BlockSpec((rows, chunk), lambda f: (0, f))
     return pl.pallas_call(
@@ -497,15 +512,21 @@
         sort_into(piece_refs, block, slot, rows_ref[block])
 
 
-def sort_upstream(label, routes, rows, owners):
+def one_step(shape):
+    return pl.BlockSpec(shape, lambda step: (0,) * len(shape), pipeline_mode=pl.Buffered(1))
+
+
+def sort_upstream(label, routes, rows, owners, part, parts):
     blocks, length, width = rows.shape
-    vmem = pl.BlockSpec(memory_space=pltpu.VMEM)
-    piece = jax.ShapeDtypeStruct((blocks * length // 2, width), jnp.bfloat16)
+    count = blocks * length // 2
     *pieces, slots = pl.pallas_call(
         lambda *refs: sort_kernel(owners, *refs),
-        in_specs=[pl.BlockSpec(memory_space=pltpu.SMEM), vmem, vmem],
-        out_specs=[vmem] * (owners + 1),
-        out_shape=[piece] * owners + [jax.ShapeDtypeStruct((blocks, 1, length), jnp.int32)],
+        grid=(1,),
+        in_specs=[pl.BlockSpec(memory_space=pltpu.SMEM), one_step((blocks, 1, length)), one_step(rows.shape)],
+        out_specs=[pl.BlockSpec((count, width), lambda step: (part, 0), pipeline_mode=pl.Buffered(1))] * owners
+        + [one_step((blocks, 1, length))],
+        out_shape=[jax.ShapeDtypeStruct((parts * count, width), jnp.bfloat16)] * owners
+        + [jax.ShapeDtypeStruct((blocks, 1, length), jnp.int32)],
         compiler_params=pltpu.CompilerParams(vmem_limit_bytes=48 << 20),
         name="sort_upstream",
     )(label, routes.reshape(blocks, 1, length), rows)
@@ -521,18 +542,24 @@
         sort_into(piece_refs, block, slot_ref[block], router_in)
 
 
-def after_attention(slots, attended, tokens, weight, gain, owners):
+def after_attention(slots, attended, tokens, weight, gain, owners, earlier):
     blocks, length, width = tokens.shape
-    vmem = pl.BlockSpec(memory_space=pltpu.VMEM)
-    piece = jax.ShapeDtypeStruct((blocks * length // 2, width), jnp.bfloat16)
+    count = blocks * length // 2
+    parts = 2 if earlier else 1
     residual, *pieces = pl.pallas_call(
-        after_attention_kernel,
-        in_specs=[vmem] * 5,
-        out_specs=[vmem] * (owners + 1),
-        out_shape=[jax.ShapeDtypeStruct(tokens.shape, jnp.float32)] + [piece] * owners,
+        lambda *refs: after_attention_kernel(*refs[:5], *refs[5 + len(earlier) :]),
+        grid=(1,),
+        in_specs=[
+            one_step(slots.shape), one_step(tokens.shape), one_step(tokens.shape), one_step(weight.shape), one_step((1, width))
+        ]
+        + [pl.BlockSpec(memory_space=pl.ANY)] * len(earlier),
+        out_specs=[one_step(tokens.shape)] + [one_step((count, width))] * owners,
+        out_shape=[jax.ShapeDtypeStruct(tokens.shape, jnp.float32)]
+        + [jax.ShapeDtypeStruct((parts * count, width), jnp.bfloat16)] * owners,
+        input_output_aliases={5 + at: 1 + at for at in range(len(earlier))},
         compiler_params=pltpu.CompilerParams(vmem_limit_bytes=48 << 20),
         name="after_attention",
-    )(slots, attended, tokens, weight, gain[None])
+    )(slots, attended, tokens, weight, gain[None], *earlier)
     return residual, pieces
 
 
@@ -581,11 +608,11 @@
     )(slots, *pieces, residual, upstream, attended, weight, gain[None])
 
 
-def exchange(pieces, axis, sign):
-    size = lax.axis_size(axis)
+def exchange(pieces, axis, sign, size=None, skipped=0):
+    size = size or lax.axis_size(axis)
     return [pieces[0]] + [
-        lax.ppermute(pieces[turn], axis, [(at, (at + sign * turn) % size) for at in range(size)])
-        for turn in range(1, size)
+        lax.ppermute(piece, axis, [(at, (at + sign * turn) % size) for at in range(size)])
+        for turn, piece in enumerate(pieces[1:], 1 + skipped)
     ]
 
 
@@ -595,6 +622,121 @@
     other = lax.dynamic_index_in_dim(blocks, 1 - at, 0, keepdims=False)
     arrived = lax.ppermute(other, "ctx", [(0, 1), (1, 0)])
     return jnp.stack([jnp.where(at == 0, mine, arrived), jnp.where(at == 0, arrived, mine)])
+
+
+def token_grads_kernel(first_ref, second_ref, *refs):
+    weight_refs, (tokens_ref, residual_grad_ref, gain_ref, out_ref) = refs[:3], refs[3:]
+    grad = 0.0
+    for kind in range(3):
+        low = jnp.concatenate([first_ref[kind], second_ref[kind]], axis=1)
+        grad += lax.dot_general(low, weight_refs[kind][...], (((1,), (1,)), ((), ())), preferred_element_type=jnp.float32)
+    rows = tokens_ref[...].astype(jnp.float32)
+    scale = norm_scale_rows(rows)
+    normed = rows * scale
+    scaled = grad * gain_ref[...]
+    shrink = jnp.mean(scaled * normed, axis=-1, keepdims=True)
+    out_ref[...] = residual_grad_ref[...] + scale * (scaled - normed * shrink)
+
+
+def token_grads(first, second, weights, tokens, residual_grad, gain):
+    length, width = tokens.shape
+    half = pl.BlockSpec((3, QB, width // 2), lambda step: (0, step, 0))
+    rows = pl.BlockSpec((QB, width), lambda step: (step, 0))
+    return pl.pallas_call(
+        token_grads_kernel,
+        grid=(length // QB,),
+        in_specs=[half, half] + [one_step((width, width))] * 3 + [rows, rows, one_step((1, width))],
+        out_specs=rows,
+        out_shape=jax.ShapeDtypeStruct((length, width), jnp.float32),
+        compiler_params=pltpu.CompilerParams(vmem_limit_bytes=48 << 20),
+        cost_estimate=pl.CostEstimate(flops=6 * length * width * width, bytes_accessed=14 * length * width, transcendentals=0),
+        name="token_grads",
+    )(first, second, *weights, tokens, residual_grad, gain[None])
+
+
+def layer_output_kernel(groups, owners, *refs):
+    slot_refs, residual_refs = refs[:groups], refs[groups : 2 * groups]
+    piece_refs, out_ref = refs[2 * groups : 2 * groups + owners], refs[-1]
+    blocks, _, length = slot_refs[0].shape
+    capacity = length // 2
+    for group in range(groups):
+        for block in range(blocks):
+            at = group * blocks + block
+            matrix = sort_matrix(slot_refs[group][block], owners * capacity)
+            rows = jnp.concatenate([ref[at * capacity : (at + 1) * capacity, :] for ref in piece_refs])
+            moved = lax.dot_general(matrix, rows, (((0,), (0,)), ((), ())), preferred_element_type=jnp.float32)
+            out_ref[at] = (residual_refs[group][block] + moved).astype(jnp.bfloat16)
+
+
+def layer_output(slots, residuals, pieces):
+    blocks, length, width = residuals[0].shape
+    vmem = pl.BlockSpec(memory_space=pltpu.VMEM)
+    return pl.pallas_call(
+        lambda *refs: layer_output_kernel(len(slots), len(pieces), *refs),
+        in_specs=[vmem] * (2 * len(slots) + len(pieces)),
+        out_specs=vmem,
+        out_shape=jax.ShapeDtypeStruct((len(slots) * blocks, length, width), jnp.bfloat16),
+        compiler_params=pltpu.CompilerParams(vmem_limit_bytes=48 << 20),
+        name="layer_output",
+    )(*slots, *residuals, *pieces)
+
+
+def weight_outputs_kernel(first_ref, second_ref, *refs):
+    weight_refs, gain_ref, out_refs, gain_grad_ref = refs[:3], refs[3], refs[4:7], refs[7]
+    width = gain_ref.shape[1]
+    half = width // 2
+    total = 0.0
+    for kind in range(3):
+        for side, ref in enumerate((first_ref, second_ref)):
+            columns = slice(side * half, (side + 1) * half)
+            grad = ref[kind * width : (kind + 1) * width, :].astype(jnp.float32)
+            out_refs[kind][:, columns] = grad
+            total += jnp.sum(grad * weight_refs[kind][:, columns].astype(jnp.float32), axis=1, keepdims=True)
+    total = jnp.broadcast_to(total, (width, 128)).T
+    gain_grad_ref[...] = total[:1] / gain_ref[...]
+
+
+def weight_outputs(first, second, weights, gain):
+    width = gain.shape[0]
+    vmem = pl.BlockSpec(memory_space=pltpu.VMEM)
+    return pl.pallas_call(
+        weight_outputs_kernel,
+        in_specs=[vmem] * 6,
+        out_specs=[vmem] * 4,
+        out_shape=[jax.ShapeDtypeStruct((width, width), jnp.float32)] * 3 + [jax.ShapeDtypeStruct((1, width), jnp.float32)],
+        compiler_params=pltpu.CompilerParams(vmem_limit_bytes=48 << 20),
+        name="weight_outputs",
+    )(first, second, *weights, gain[None])
+
+
+def token_grads_kernel(first_ref, second_ref, *refs):
+    weight_refs, (tokens_ref, residual_grad_ref, gain_ref, out_ref) = refs[:3], refs[3:]
+    grad = 0.0
+    for kind in range(3):
+        low = jnp.concatenate([first_ref[kind], second_ref[kind]], axis=1)
+        grad += lax.dot_general(low, weight_refs[kind][...], (((1,), (1,)), ((), ())), preferred_element_type=jnp.float32)
+    rows = tokens_ref[...].astype(jnp.float32)
+    scale = norm_scale_rows(rows)
+    normed = rows * scale
+    scaled = grad * gain_ref[...]
+    shrink = jnp.mean(scaled * normed, axis=-1, keepdims=True)
+    out_ref[...] = residual_grad_ref[...] + scale * (scaled - normed * shrink)
+
+
+def token_grads(first, second, weights, tokens, residual_grad, gain):
+    length, width = tokens.shape
+    half = pl.BlockSpec((3, QB, width // 2), lambda step: (0, step, 0))
+    rows = pl.BlockSpec((QB, width), lambda step: (step, 0))
+    return pl.pallas_call(
+        token_grads_kernel,
+        grid=(length // QB,),
+        in_specs=[half, half] + [one_step((width, width))] * 3 + [rows, rows, one_step((1, width))],
+        out_specs=rows,
+        out_shape=jax.ShapeDtypeStruct((length, width), jnp.float32),
+        compiler_params=pltpu.CompilerParams(vmem_limit_bytes=48 << 20),
+        cost_estimate=pl.CostEstimate(flops=6 * length * width * width, bytes_accessed=14 * length * width, transcendentals=0),
+        name="token_grads",
+    )(first, second, *weights, tokens, residual_grad, gain[None])
 
 
 def place_rows(slots, pieces):
@@ -714,10 +856,14 @@
     label = lax.axis_index("expert").astype(jnp.int32).reshape(1)
     together = lax.optimization_barrier
 
-    sorted_upstream, slots = zip(*[sort_upstream(label, routes[group], cotangent[group], owners) for group in groups])
-    sorted_upstream = list(sorted_upstream)
-    sorted_upstream[0], tokens = together((sorted_upstream[0], tokens))
-    upstream = [exchange(sorted_upstream[0], "expert", 1)]
+    sorted_upstream, slots = zip(
+        *[
+            sort_upstream(label, routes[group], cotangent[group], owners, at, 1 + at)
+            for at, group in enumerate(groups)
+        ]
+    )
+    sorted_first, tokens = together((sorted_upstream[0], tokens))
+    upstream = [exchange(sorted_first, "expert", 1)]
     inputs = tokens.astype(jnp.float32)
     scale1 = norm_scale(inputs)
     attn_in = (inputs * scale1 * norm1_gain).astype(jnp.bfloat16)
@@ -745,19 +891,25 @@
         if at == 0:
             upstream[0] = in_flight
         else:
-            arrived[-1], sorted_upstream[at] = together((in_flight, sorted_upstream[at]))
-            upstream.append(exchange(sorted_upstream[at], "expert", 1))
+            arrived[-1] = in_flight
         attended_groups.append(rows)
-        residual, sorted_rows = after_attention(slots[at], rows, tokens[group], output_weight, norm2_gain, owners)
+        earlier = sorted_upstream[at] if at else []
+        residual, sorted_rows = after_attention(
+            slots[at], rows, tokens[group], output_weight, norm2_gain, owners, earlier
+        )
         residual1.append(residual)
         sorted_rows, fed = together((sorted_rows, fed))
         in_flight = exchange(sorted_rows, "expert", 1)
         arrived.append(in_flight)
     router_wide = jnp.pad(router_weight, ((0, 0), (0, 128 - router_weight.shape[1])))
     done, back = [], []
+    upstream += arrived[1:]
+    tile = seq_count // len(groups) * local_len // 2
     for at, (rows, grads) in enumerate(zip(arrived, upstream)):
         earlier = done[-1][0] if done else []
-        result = run_expert(label, rows, grads, router_wide, w_in[0], w_out[0], at, len(groups), earlier)
+        result = run_expert(
+            label, rows, grads, tile, min(at, 1), router_wide, w_in[0], w_out[0], at, len(groups), earlier
+        )
         if back:
             result, back[-1] = together((result, back[-1]))
         done.append(result)
@@ -768,7 +920,8 @@
     grad_experts = expert_grads(sum(arrived, []), grad_rows, hiddens, pre_grads)
     grad_experts, back[-1], rows_out = together((grad_experts, back[-1], rows_out))
     grad_experts = lax.psum_scatter(grad_experts, ("dp", "ctx"), scatter_dimension=0, tiled=True)
-    returned = exchange(list(rows_out), "expert", -1)
+    if not whole_seq:
+        returned = exchange(list(rows_out), "expert", -1)
     residual_grad, mixed_grad, grad_w_output, grad_norm2 = zip(
         *[
             before_attention(slot, pieces, residual, cotangent[group], rows, output_weight, norm2_gain)
@@ -780,51 +933,56 @@
     early_small = jnp.concatenate([grad_router, grad_norm2])
     projections = (query_weight, key_weight, value_weight)
     if whole_seq:
-        rows_in = attn_in.reshape(flat)
         half = model_width // 2
         pairs = half // 128
         mixed_grad = mixed_grad.reshape(flat)
-
-        def weight_grads(grads):
-            return [jnp.dot(rows_in.T, part, preferred_element_type=jnp.float32) for part in grads]
-
-        first_grads, first_bias = attend_back(*qkv, mixed_grad, lines, 0, pairs)
-        matrices = [grad_w_output[:, :half], grad_w_output[:, half:]] + weight_grads(first_grads)
+        turned = attn_in.reshape(flat).T
+        returned = exchange(list(rows_out[:-1]), "expert", -1, owners)
+        first = attend_back(*qkv, mixed_grad, turned, lines, 0, pairs, pairs)
+        first, returned, last_rows = together((first, returned, rows_out[-1]))
+        returned.append(exchange([None, last_rows], "expert", -1, owners, owners - 2)[1])
+        first_grads, first_sums = first
+        matrices = [first_sums, grad_w_output[:, :half], grad_w_output[:, half:]]
         early = Summing(pack_sums(matrices, early_small.reshape(-1, half)))
-        second_grads, biases = None, [first_bias]
+        second = ()
         for at in range(pairs, 2 * pairs):
             sent, mixed_grad = together((early.sends(), mixed_grad))
             moved = early.move(sent)
-            second_grads, bias = attend_back(*qkv, mixed_grad, lines, at, 1, pairs, second_grads)
-            second_grads, moved = together((second_grads, moved))
+            second = attend_back(*qkv, mixed_grad, turned, lines, at, 1, pairs, second)
+            if at == pairs + 1:
+                second, moved, returned = together((second, moved, returned))
+            else:
+                second, moved = together((second, moved))
             early.take(moved)
-            biases.append(bias)
-        second_grads, returned, grad_experts = together((second_grads, returned, grad_experts))
-        late = Summing(pack_sums(weight_grads(second_grads), jnp.concatenate(biases)))
-        early.take(early.move(early.sends()))
+        (second_grads, second_sums), grad_experts = together((second, grad_experts))
+        late = Summing(second_sums)
+        sent, sent_late, returned = together((early.sends(), late.sends(), returned))
+        moved, moved_late = early.move(sent), late.move(sent_late)
+        block_out = layer_output(slots, residual1, returned)
+        moved, moved_late, block_out = together((moved, moved_late, block_out))
+        early.take(moved)
+        late.take(moved_late)
         early_sums = early.finish()
-        for step in range(late.steps):
+        sent_late, second_grads = together((late.sends(), second_grads))
+        moved_late = late.move(sent_late)
+        d_tokens = token_grads(
+            first_grads, second_grads, projections, tokens.reshape(flat), residual_grad.reshape(flat), norm1_gain
+        ).reshape(tokens.shape)
+        moved_late, d_tokens = together((moved_late, d_tokens))
+        late.take(moved_late)
+        for step in range(2):
             late.take(late.move(late.sends()))
         late.part, early_sums = together((late.part, early_sums))
         sums = [early_sums, late.finish()]
-        norm_in_grad = 0.0
-        low_parts = (first_grads, second_grads)
-        for at, grads in enumerate(low_parts):
-            span = slice(at * 128 * pairs, (at + 1) * 128 * pairs)
-            for kind in range(3):
-                norm_in_grad += jnp.einsum(
-                    "xe,de->xd", grads[kind], projections[kind][:, span], preferred_element_type=jnp.float32
-                )
-        norm_in_grad = norm_in_grad.reshape(tokens.shape)
-        grad_qkv = [
-            jnp.concatenate(
-                [matrix_of(sums[0], 2 + kind, model_width), matrix_of(sums[1], kind, model_width)], axis=1
-            ).astype(jnp.float32)
-            for kind in range(3)
-        ]
-        grad_w_output = jnp.concatenate([matrix_of(sums[0], side, model_width) for side in range(2)], axis=1)
-        small = small_of(sums[0], 5 * model_width).reshape(-1, model_width)
-        grad_bias = small_of(sums[1], 3 * model_width)
+        *grad_qkv, grad_norm1 = weight_outputs(*sums, projections, norm1_gain)
+        grad_norm1 = grad_norm1[0]
+        start = 3 * model_width + 128
+        grad_w_output = jnp.concatenate(
+            [matrix_of(sums[0][start:], side, model_width) for side in range(2)], axis=1
+        )
+        small = small_of(sums[0], start + 2 * model_width).reshape(-1, model_width)
+        grad_bias = jnp.concatenate([part[start - 128 : start - 124] for part in sums], axis=1).astype(jnp.float32)
+        grad_bias = (grad_bias[:2] + grad_bias[2:]).reshape(2, -1, 128).swapaxes(0, 1).reshape(-1, 128)
     else:
         query_grad, _, diag_grad, key_part, value_part = attend_back_rows(
             queries, keys, values, mixed_grad, log_totals, buckets, bias_table, DH
@@ -841,21 +999,16 @@
         grad_bias = lax.psum(diag_grad, ("dp", "ctx", "expert"))
         grad_w_output, *grad_qkv = (matrix_of(sums, kind, model_width).astype(jnp.float32) for kind in range(4))
         small = small_of(sums, 4 * model_width)
+        norm1_back, grad_norm1 = norm_back(inputs, scale1, norm1_gain, norm_in_grad)
+        grad_norm1 = lax.psum(grad_norm1, ("dp", "ctx", "expert"))
     grad_bias = grad_bias[: bias_table.shape[1], : bias_table.shape[0]].T
-    grad_norm1 = sum(jnp.sum(grad * weight.astype(jnp.float32), axis=1) for grad, weight in zip(grad_qkv, projections))
-    grad_norm1 = grad_norm1 / norm1_gain
     grad_w_query, grad_w_key, grad_w_value = grad_qkv
     grad_w_output = grad_w_output.astype(jnp.float32)
     experts = router_weight.shape[1]
     grad_router, grad_norm2 = small[:experts, :].T, small[experts]
-    returned = [piece.reshape(len(groups), -1, model_width) for piece in returned]
-    block_out = [
-        rows + place_rows(slot, [piece[at] for piece in returned])
-        for at, (slot, rows) in enumerate(zip(slots, residual1))
-    ]
-    block_out = jnp.concatenate(block_out).astype(jnp.bfloat16)
-    norm1_back, _ = norm_back(inputs, scale1, norm1_gain, norm_in_grad)
-    d_tokens = residual_grad + norm1_back
+    if not whole_seq:
+        block_out = layer_output(slots, residual1, returned)
+        d_tokens = residual_grad + norm1_back
     if whole_seq:
         block_out, d_tokens = trade(block_out), trade(d_tokens)
     grad_experts = grad_experts.astype(jnp.float32)

time: 527 us -> 504 us (0.956)
  Pallas kernels: 210 us -> 242 us
  matrix products: 30.6 us -> 4.47 us
  starting transfers between devices: 87.9 us -> 69.7 us
  waiting for transfers between devices: 98.4 us -> 89.9 us
  other arithmetic: 34.8 us -> 27.6 us
    pallas_call x8 -> x11, Pallas kernels: 77.6 us -> 108 us  [the longest x4 82 us: attend_back(): pl.pallas_call(lambda *refs: bwd_kernel(*refs[:7], *refs[7 + len(earlier)...]
    dot_general x14 -> x0, matrix products: 26.1 us -> none  [the longest x6 14 us: per_device(): jnp.einsum('xe,de->xd', grads[kind], projections[kind][:, span], preferre...]
    ppermute x12, waiting for transfers between devices: 63.2 us -> 42.5 us  [swap(): lax.ppermute(part, axis, [(to, to ^ turn) for to in range(lax.axis_size(a...]
    ppermute x21 -> x18, starting transfers between devices: 73.1 us -> 55.8 us  [exchange(): lax.ppermute(piece, axis, [(at, (at + sign * turn) % size) for at in rang...]
    ppermute x21 -> x18, waiting for transfers between devices: 27.2 us -> 43.2 us  [exchange(): lax.ppermute(piece, axis, [(at, (at + sign * turn) % size) for at in rang...]
    unnamed x199 -> x174, local copies, waits for them, and re-layouts: 23.6 us -> 29.6 us
  transfers between devices with their start and end apart: 41 -> 38, of which waited for: 13 -> 14; matrix products, arithmetic and copies ran while one was open for 14% -> 9% of each run, Pallas kernels for 40% -> 46%
where the time goes in v5:
time: 504 us; the launch traced here: 495 us
  Pallas kernels  242 us (48%)
  waiting for transfers between devices  89.9 us (18%)
  starting transfers between devices  69.7 us (14%)
  local copies, waits for them, and re-layouts  46.2 us (9%)
  other arithmetic  27.6 us (5%)
  between operations  15 us (3%)
    pallas_call x4, Pallas kernels, attend_back(): pl.pallas_call(lambda *refs: bwd_kernel(*refs[:7], *refs[7 + len(earlier)...  82 us
    pallas_call x2, Pallas kernels, run_expert(): pl.pallas_call(lambda *refs: expert_kernel(count, *refs), grid_spec=pltpu...  60 us
    ppermute x18, starting transfers between devices, exchange(): lax.ppermute(piece, axis, [(at, (at + sign * turn) % size) for at in rang...  55.8 us
    ppermute x18, waiting for transfers between devices, exchange(): lax.ppermute(piece, axis, [(at, (at + sign * turn) % size) for at in rang...  43.2 us
    ppermute x12, waiting for transfers between devices, swap(): lax.ppermute(part, axis, [(to, to ^ turn) for to in range(lax.axis_size(a...  42.5 us
    unnamed x174, local copies, waits for them, and re-layouts  29.6 us
    pallas_call x2, Pallas kernels, attend(): pl.pallas_call(lambda *refs: fwd_kernel(first // QB, *refs), grid=(width...  29 us
    pallas_call x1, Pallas kernels, expert_grads(): pl.pallas_call(lambda *refs: expert_grads_kernel(groups, count, *refs), g...  27.9 us
  transfers between devices with their start and end apart: 38, of which 14 were waited for; matrix products, arithmetic and copies ran while one was open for 9% of the time, Pallas kernels for 46%

profile of v5, /device:TPU:0, one launch (start us, length us, event | category | flops | bytes accessed | tf_op | source)
XLA Modules:
  0.0 494.9 jit_solution(13600721487928964879)
XLA Ops:
  7.3 2.2 dynamic-slice_bitcast_fusion.4
  13.8 1.8 copy-done.70
  18.5 3.0 collective-permute-start.3
  21.5 2.6 collective-permute-start.4
  31.0 14.7 %attend.2 = bf16[512,768]{1,0:T(8,128)(2,1)S(1)} custom-call(f32[12,2,1024]{2,1,0:T(2,128)S(1)} %bitcast.158, bf16[1024,768]{1,0:T(8,128)(2,1)S(1)} %bitcast.152, bf16[1024,768]{1,0:T(8,128)(2,1)S(1)} %bitcast.146, bf16[1024,768]{1,0:T(8,128)(2,1)S(1)} %bitcast.140), custom_call_target="tpu_custom_call" | custom-call | flops 402653184 | bytes 1572864 | tf_op jit(solution)/shard_map/attend/pallas_call | solution.py:196
  45.9 4.0 collective-permute-done.4.refs_7_
  50.0 3.2 after_attention.2
  55.1 8.9 %collective-permute-start.6 = (bf16[256,768]{1,0:T(8,128)(2,1)}, bf16[256,768]{1,0:T(8,128)(2,1)}, u32[]{:S(2)}, u32[]{:S(2)}) collective-permute-start(bf16[256,768]{1,0:T(8,128)(2,1)} %get-tuple-element.194), channel_id=1, source_target_pairs={{0,1},{1,2},{2,3},{3,0},{4,5},{5,6},{6,7},{7,4},{8,9},{9,10},{10,1... | collective-permute-start | bytes 1179656 | tf_op jit(solution)/shard_map/ppermute | solution.py:614
  72.5 14.3 %attend.3 = bf16[512,768]{1,0:T(8,128)(2,1)S(1)} custom-call(f32[12,2,1024]{2,1,0:T(2,128)S(1)} %bitcast.159, bf16[1024,768]{1,0:T(8,128)(2,1)S(1)} %bitcast.153, bf16[1024,768]{1,0:T(8,128)(2,1)S(1)} %bitcast.147, bf16[1024,768]{1,0:T(8,128)(2,1)S(1)} %bitcast.141), custom_call_target="tpu_custom_call" | custom-call | flops 402653184 | bytes 1572864 | tf_op jit(solution)/shard_map/attend/pallas_call | solution.py:196
  86.8 4.0 collective-permute-done.7.refs_3_.refs_2_
  90.9 2.8 after_attention.3
  93.7 8.9 %collective-permute-start.9 = (bf16[512,768]{1,0:T(8,128)(2,1)S(1)}, bf16[512,768]{1,0:T(8,128)(2,1)S(1)}, u32[]{:S(2)}, u32[]{:S(2)}) collective-permute-start(bf16[512,768]{1,0:T(8,128)(2,1)S(1)} %get-tuple-element.207), channel_id=1, source_target_pairs={{0,1},{1,2},{2,3},{3,0},{4,5},{5,6},{6,7},{7,4},{8,9},{9,10},{10,1... | collective-permute-start | bytes 2359304 | tf_op jit(solution)/shard_map/ppermute | solution.py:614
  102.6 2.0 collective-permute-start.10
  105.0 29.8 %experts.2 = (bf16[512,768]{1,0:T(8,128)(2,1)S(1)}, bf16[512,768]{1,0:T(8,128)(2,1)}, bf16[512,768]{1,0:T(8,128)(2,1)}, bf16[512,768]{1,0:T(8,128)(2,1)}, bf16[2...) custom-call(s32[1]{0:T(128)} %bitcast.2.refs_0_, ...), custom_call_target="tpu_custom_call" | custom-call | flops 38654705664 | bytes 18874368 | tf_op jit(solution)/shard_map/experts/pallas_call | solution.py:395
  135.5 2.0 collective-permute-start.12
  138.8 16.3 %collective-permute-done.10.refs_3_.refs_7_.refs_6_ = bf16[512,768]{1,0:T(8,128)(2,1)S(1)} collective-permute-done((bf16[512,768]{1,0:T(8,128)(2,1)S(1)}, bf16[512,768]{1,0:T(8,128)(2,1)S(1)}, u32[]{:S(2)}, u32[]{:S(2)}) %collective-permute-start.10) | collective-permute-done | bytes 786464 | tf_op jit(solution)/shard_map/ppermute | solution.py:614
  157.4 30.2 %experts.3 = (bf16[512,768]{1,0:T(8,128)(2,1)S(1)}, bf16[512,768]{1,0:T(8,128)(2,1)}, bf16[512,768]{1,0:T(8,128)(2,1)}, bf16[512,768]{1,0:T(8,128)(2,1)S(1)}, bf...) custom-call(s32[1]{0:T(128)} %bitcast.2.refs_0_, ...), custom_call_target="tpu_custom_call", output_to_operand_aliasing={{0}: (12, {}), {1}: (13, {}), {2}: (14, {}), {3}: (15, {})} | custom-call | flops 38654705664 | bytes 18874368 | tf_op jit(solution)/shard_map/experts/pallas_call | solution.py:395
  189.3 16.3 %collective-permute-done.13.refs_3_ = bf16[256,768]{1,0:T(8,128)(2,1)S(1)} collective-permute-done((bf16[256,768]{1,0:T(8,128)(2,1)S(1)}, bf16[256,768]{1,0:T(8,128)(2,1)S(1)}, u32[]{:S(2)}, u32[]{:S(2)}) %collective-permute-start.13) | collective-permute-done | bytes 393248 | tf_op jit(solution)/shard_map/ppermute | solution.py:614
  205.6 19.4 %collective-permute-start.15 = (bf16[256,768]{1,0:T(8,128)(2,1)}, bf16[256,768]{1,0:T(8,128)(2,1)}, u32[]{:S(2)}, u32[]{:S(2)}) collective-permute-start(bf16[256,768]{1,0:T(8,128)(2,1)} %get-tuple-element.251), channel_id=1, source_target_pairs={{0,3},{1,0},{2,1},{3,2},{4,7},{5,4},{6,5},{7,6},{8,11},{9,8},{10,9... | collective-permute-start | bytes 1179656 | tf_op jit(solution)/shard_map/ppermute | solution.py:614
  229.1 27.9 %expert_grads.1 = bf16[3072,1536]{1,0:T(8,128)(2,1)} custom-call(bf16[256,768]{1,0:T(8,128)(2,1)S(1)} %copy-done.49, bf16[256,768]{1,0:T(8,128)(2,1)} %collective-permute-done.6.refs_2_.refs_1_, bf16[256,768]{1,0:T(8,128)(2,1)} %collective-permute-done.7.refs_3_.refs_2_, bf16[256,768]{1,0:T(8,128)(2,1)} %collective-permute-done.8.refs_4_.refs_3_, ...), custom_call_target="tpu_custom_call" | custom-call | flops 28991029248 | bytes 34603008 | tf_op jit(solution)/shard_map/expert_grads/pallas_call | solution.py:463
  257.0 2.4 collective-permute-done.16.refs_3_
  259.9 1.7 copy.74
  261.7 8.4 %before_attention.2 = (f32[1,512,768]{2,1,0:T(8,128)}, bf16[1,512,768]{2,1,0:T(8,128)(2,1)}, f32[768,768]{1,0:T(8,128)}, f32[1,768]{1,0:T(1,128)}) custom-call(s32[1,1,512]{2,1,0:T(1,128)} %copy-done.36, bf16[256,768]{1,0:T(8,128)(2,1)} %copy-done.33, bf16[256,768]{1,0:T(8,128)(2,1)} %copy-done.73, bf16[256,768]{1,0:T(8,128)(2,1)} %copy-done.74, ...), custom_call_target="tpu_custom_call" | custom-call | tf_op jit(solution)/shard_map/before_attention/pallas_call | solution.py:596
  272.4 8.4 %before_attention.3 = (f32[1,512,768]{2,1,0:T(8,128)}, bf16[1,512,768]{2,1,0:T(8,128)(2,1)}, f32[768,768]{1,0:T(8,128)}, f32[1,768]{1,0:T(1,128)}) custom-call(s32[1,1,512]{2,1,0:T(1,128)} %copy-done.38, bf16[256,768]{1,0:T(8,128)(2,1)} %copy-done.34, bf16[256,768]{1,0:T(8,128)(2,1)} %collective-permute-done.15.refs_2_, ...), custom_call_target="tpu_custom_call" | custom-call | tf_op jit(solution)/shard_map/before_attention/pallas_call | solution.py:596
  280.9 2.6 pad_maximum_fusion.3
  283.5 38.8 %attend_back.4 = (bf16[3,1024,384]{2,1,0:T(8,128)(2,1)}, bf16[2432,384]{1,0:T(8,128)(2,1)}) custom-call(f32[12,2,1024]{2,1,0:T(2,128)S(1)} %bitcast.160, f32[3,512,128]{2,1,0:T(8,128)S(1)} %copy-done.58, bf16[1024,768]{1,0:T(8,128)(2,1)S(1)} %bitcast.154, bf16[1024,768]{1,0:T(8,128)(2,1)S(1)} %bitcast.148, bf16[1024,768]{1,0:T(8,128)(2,1)S(1)} %bitcast.142, ...), custom_call_target="tpu_custom_call" | custom-call | flops 33822867456 | bytes 5505024 | tf_op jit(solution)/shard_map/attend_back/pallas_call | solution.py:295
  322.4 2.7 add_convert_fusion
  330.7 14.5 %attend_back.5 = (bf16[3,1024,384]{2,1,0:T(8,128)(2,1)}, bf16[2432,384]{1,0:T(8,128)(2,1)}) custom-call(f32[12,2,1024]{2,1,0:T(2,128)S(1)} %bitcast.161, f32[3,512,128]{2,1,0:T(8,128)S(1)} %copy-done.59, bf16[1024,768]{1,0:T(8,128)(2,1)S(1)} %bitcast.155, bf16[1024,768]{1,0:T(8,128)(2,1)S(1)} %bitcast.149, bf16[1024,768]{1,0:T(8,128)(2,1)S(1)} %bitcast.143, ...), custom_call_target="tpu_custom_call" | custom-call | flops 11274289152 | bytes 1835008 | tf_op jit(solution)/shard_map/attend_back/pallas_call | solution.py:295
  345.3 1.9 fusion.3
  347.5 1.6 collective-permute-start.21
  349.1 1.7 collective-permute-start.22
  351.1 14.3 %attend_back.6 = (bf16[3,1024,384]{2,1,0:T(8,128)(2,1)}, bf16[2432,384]{1,0:T(8,128)(2,1)}) custom-call(f32[12,2,1024]{2,1,0:T(2,128)S(1)} %bitcast.162, f32[3,512,128]{2,1,0:T(8,128)S(1)} %copy-done.59, bf16[1024,768]{1,0:T(8,128)(2,1)S(1)} %bitcast.156, bf16[1024,768]{1,0:T(8,128)(2,1)S(1)} %bitcast.150, ...), custom_call_target="tpu_custom_call", output_to_operand_aliasing={{0}: (7, {}), {1}: (8, {})} | custom-call | flops 11274289152 | bytes 1835008 | tf_op jit(solution)/shard_map/attend_back/pallas_call | solution.py:295
  365.4 3.4 collective-permute-done.22
  371.0 14.3 %attend_back.7 = (bf16[3,1024,384]{2,1,0:T(8,128)(2,1)}, bf16[2432,384]{1,0:T(8,128)(2,1)}) custom-call(f32[12,2,1024]{2,1,0:T(2,128)S(1)} %bitcast.163, f32[3,512,128]{2,1,0:T(8,128)S(1)} %copy-done.59, bf16[1024,768]{1,0:T(8,128)(2,1)S(1)} %bitcast.157, bf16[1024,768]{1,0:T(8,128)(2,1)S(1)} %bitcast.151, ...), custom_call_target="tpu_custom_call", output_to_operand_aliasing={{0}: (7, {}), {1}: (8, {})} | custom-call | flops 11274289152 | bytes 1835008 | tf_op jit(solution)/shard_map/attend_back/pallas_call | solution.py:295
  387.1 2.7 collective-permute-start.26
  389.8 4.2 layer_output.1
  394.0 14.0 %collective-permute-done.26 = bf16[512,384]{1,0:T(8,128)(2,1)S(1)} collective-permute-done((bf16[512,384]{1,0:T(8,128)(2,1)S(1)}, bf16[512,384]{1,0:T(8,128)(2,1)S(1)}, u32[]{:S(2)}, u32[]{:S(2)}) %collective-permute-start.26) | collective-permute-done | bytes 393248 | tf_op jit(solution)/shard_map/ppermute | solution.py:787
  408.9 3.9 pad_maximum_fusion
  418.1 8.5 %token_grads.1 = f32[1024,768]{1,0:T(8,128)} custom-call(bf16[3,1024,384]{2,1,0:T(8,128)(2,1)} %get-tuple-element.324.first_ref, bf16[3,1024,384]{2,1,0:T(8,128)(2,1)} %get-tuple-element.325.second_ref, bf16[768,768]{1,0:T(8,128)(2,1)S(1)} %copy-done.21, bf16[768,768]{1,0:T(8,128)(2,1)S(1)} %copy-done.23, bf16[768,768]{1,0:T(8,128)(2,1)S(1)} %copy-done.26, ...), custom_call_target="tpu_custom_call" | custom-call | flops 3623878656 | bytes 11010048 | tf_op jit(solution)/shard_map/token_grads/pallas_call | solution.py:730
  428.1 4.5 collective-permute-done.31
  432.7 7.1 %collective-permute-done.33 = bf16[304,384]{1,0:T(8,128)(2,1)S(1)} collective-permute-done((bf16[304,384]{1,0:T(8,128)(2,1)S(1)}, bf16[304,384]{1,0:T(8,128)(2,1)S(1)}, u32[]{:S(2)}, u32[]{:S(2)}) %collective-permute-start.33) | collective-permute-done | bytes 233504 | tf_op jit(solution)/shard_map/ppermute | solution.py:787
  439.9 12.1 %collective-permute-done.34 = bf16[304,384]{1,0:T(8,128)(2,1)S(1)} collective-permute-done((bf16[304,384]{1,0:T(8,128)(2,1)S(1)}, bf16[304,384]{1,0:T(8,128)(2,1)S(1)}, u32[]{:S(2)}, u32[]{:S(2)}) %collective-permute-start.34) | collective-permute-done | bytes 233504 | tf_op jit(solution)/shard_map/ppermute | solution.py:787
  452.8 2.7 dynamic-slice_bitcast_fusion
  458.6 2.7 copy.73
  465.0 1.6 fusion.5
  466.7 2.0 pad_maximum_fusion.1
  474.1 3.9 all-gather.5.cloned.1.call-done.second_ref
  482.1 5.4 %weight_outputs.1 = (f32[768,768]{1,0:T(8,128)}, f32[768,768]{1,0:T(8,128)}, f32[768,768]{1,0:T(8,128)}, f32[1,768]{1,0:T(1,128)S(1)}) custom-call(bf16[4096,384]{1,0:T(8,128)(2,1)} %all-gather.3.cloned.1.call-done.first_ref, bf16[2432,384]{1,0:T(8,128)(2,1)S(1)} %copy-done.28, bf16[768,768]{1,0:T(8,128)(2,1)S(1)} %copy-done.21, ...), custom_call_target="tpu_custom_call" | custom-call | tf_op jit(solution)/shard_map/weight_outputs/pallas_call | solution.py:702
  (290 shorter events, 73.7 us)
Async XLA Ops:
  7.2 378.2 %reduce-scatter.2.cloned.1.call-start = ((), (), s32[]{:S(2)}) async-start(), calls=%async_computation.1 | async-start | bytes 10616832 | tf_op jit(solution)/shard_map/reduce_scatter | solution.py:922
  9.5 2.7 collective-permute-start.2
  10.0 1.9 collective-permute-start
  11.0 2.7 collective-permute-start.1
  11.8 79.1 %copy-start.35 = (f32[1,768]{1,0:T(1,128)}, f32[1,768]{1,0:T(1,128)S(1)}, u32[]{:S(2)}) copy-start(f32[1,768]{1,0:T(1,128)S(1)} %broadcast_in_dim.25.refs_4_.refs_9_) | copy-start | bytes 9220
  13.7 32.0 %copy-start.2 = (bf16[2,512,768]{2,1,0:T(8,128)(2,1)}, bf16[2,512,768]{2,1,0:T(8,128)(2,1)S(1)}, u32[]{:S(2)}) copy-start(bf16[2,512,768]{2,1,0:T(8,128)(2,1)S(1)} %pad_maximum_fusion.2) | copy-start | bytes 4718596
  16.9 50.2 %copy-start.5 = (bf16[1,512,768]{2,1,0:T(8,128)(2,1)}, bf16[1,512,768]{2,1,0:T(8,128)(2,1)S(1)}, u32[]{:S(2)}) copy-start(bf16[1,512,768]{2,1,0:T(8,128)(2,1)S(1)} %get-tuple-element.396.refs_2_.refs_6_) | copy-start | bytes 2359300
  18.1 31.9 %copy-start.36 = (s32[1,1,512]{2,1,0:T(1,128)}, s32[1,1,512]{2,1,0:T(1,128)S(1)}, u32[]{:S(2)}) copy-start(s32[1,1,512]{2,1,0:T(1,128)S(1)} %get-tuple-element.181.refs_0_) | copy-start | bytes 6148
  18.5 27.4 %collective-permute-start.3 = (bf16[256,768]{1,0:T(8,128)(2,1)S(1)}, bf16[256,768]{1,0:T(8,128)(2,1)S(1)}, u32[]{:S(2)}, u32[]{:S(2)}) collective-permute-start(bf16[256,768]{1,0:T(8,128)(2,1)S(1)} %get-tuple-element.184), channel_id=1, source_target_pairs={{0,1},{1,2},{2,3},{3,0},{4,5},{5,6},{6,7},{7,4},{8,9},{9,10},{10,1... | collective-permute-start | bytes 1179656 | tf_op jit(solution)/shard_map/ppermute | solution.py:614
  21.5 28.4 %collective-permute-start.4 = (bf16[256,768]{1,0:T(8,128)(2,1)S(1)}, bf16[256,768]{1,0:T(8,128)(2,1)S(1)}, u32[]{:S(2)}, u32[]{:S(2)}) collective-permute-start(bf16[256,768]{1,0:T(8,128)(2,1)S(1)} %get-tuple-element.185), channel_id=1, source_target_pairs={{0,2},{1,3},{2,0},{3,1},{4,6},{5,7},{6,4},{7,5},{8,10},{9,11},{10,... | collective-permute-start | bytes 1179656 | tf_op jit(solution)/shard_map/ppermute | solution.py:614
  24.1 25.8 %collective-permute-start.5 = (bf16[256,768]{1,0:T(8,128)(2,1)S(1)}, bf16[256,768]{1,0:T(8,128)(2,1)S(1)}, u32[]{:S(2)}, u32[]{:S(2)}) collective-permute-start(bf16[256,768]{1,0:T(8,128)(2,1)S(1)} %get-tuple-element.186), channel_id=1, source_target_pairs={{0,3},{1,0},{2,1},{3,2},{4,7},{5,4},{6,5},{7,6},{8,11},{9,8},{10,9... | collective-permute-start | bytes 1179656 | tf_op jit(solution)/shard_map/ppermute | solution.py:614
  45.9 20.9 %copy-start.79 = (bf16[768,4]{0,1:T(4,128)(2,1)S(1)}, bf16[768,4]{0,1:T(4,128)(2,1)}, u32[]{:S(2)}) copy-start(bf16[768,4]{0,1:T(4,128)(2,1)} %param.28) | copy-start | bytes 18436
  55.1 31.7 %collective-permute-start.6 = (bf16[256,768]{1,0:T(8,128)(2,1)}, bf16[256,768]{1,0:T(8,128)(2,1)}, u32[]{:S(2)}, u32[]{:S(2)}) collective-permute-start(bf16[256,768]{1,0:T(8,128)(2,1)} %get-tuple-element.194), channel_id=1, source_target_pairs={{0,1},{1,2},{2,3},{3,0},{4,5},{5,6},{6,7},{7,4},{8,9},{9,10},{10,1... | collective-permute-start | bytes 1179656 | tf_op jit(solution)/shard_map/ppermute | solution.py:614
  63.9 26.9 %collective-permute-start.7 = (bf16[256,768]{1,0:T(8,128)(2,1)}, bf16[256,768]{1,0:T(8,128)(2,1)}, u32[]{:S(2)}, u32[]{:S(2)}) collective-permute-start(bf16[256,768]{1,0:T(8,128)(2,1)} %get-tuple-element.195), channel_id=1, source_target_pairs={{0,2},{1,3},{2,0},{3,1},{4,6},{5,7},{6,4},{7,5},{8,10},{9,11},{10,... | collective-permute-start | bytes 1179656 | tf_op jit(solution)/shard_map/ppermute | solution.py:614
  65.5 25.3 %collective-permute-start.8 = (bf16[256,768]{1,0:T(8,128)(2,1)}, bf16[256,768]{1,0:T(8,128)(2,1)}, u32[]{:S(2)}, u32[]{:S(2)}) collective-permute-start(bf16[256,768]{1,0:T(8,128)(2,1)} %get-tuple-element.196), channel_id=1, source_target_pairs={{0,3},{1,0},{2,1},{3,2},{4,7},{5,4},{6,5},{7,6},{8,11},{9,8},{10,9... | collective-permute-start | bytes 1179656 | tf_op jit(solution)/shard_map/ppermute | solution.py:614
  93.7 44.9 %collective-permute-start.9 = (bf16[512,768]{1,0:T(8,128)(2,1)S(1)}, bf16[512,768]{1,0:T(8,128)(2,1)S(1)}, u32[]{:S(2)}, u32[]{:S(2)}) collective-permute-start(bf16[512,768]{1,0:T(8,128)(2,1)S(1)} %get-tuple-element.207), channel_id=1, source_target_pairs={{0,1},{1,2},{2,3},{3,0},{4,5},{5,6},{6,7},{7,4},{8,9},{9,10},{10,1... | collective-permute-start | bytes 2359304 | tf_op jit(solution)/shard_map/ppermute | solution.py:614
  102.6 52.5 %collective-permute-start.10 = (bf16[512,768]{1,0:T(8,128)(2,1)S(1)}, bf16[512,768]{1,0:T(8,128)(2,1)S(1)}, u32[]{:S(2)}, u32[]{:S(2)}) collective-permute-start(bf16[512,768]{1,0:T(8,128)(2,1)S(1)} %get-tuple-element.208), channel_id=1, source_target_pairs={{0,2},{1,3},{2,0},{3,1},{4,6},{5,7},{6,4},{7,5},{8,10},{9,11},{10,... | collective-permute-start | bytes 2359304 | tf_op jit(solution)/shard_map/ppermute | solution.py:614
  104.6 50.5 %collective-permute-start.11 = (bf16[512,768]{1,0:T(8,128)(2,1)S(1)}, bf16[512,768]{1,0:T(8,128)(2,1)S(1)}, u32[]{:S(2)}, u32[]{:S(2)}) collective-permute-start(bf16[512,768]{1,0:T(8,128)(2,1)S(1)} %get-tuple-element.209), channel_id=1, source_target_pairs={{0,3},{1,0},{2,1},{3,2},{4,7},{5,4},{6,5},{7,6},{8,11},{9,8},{10,9... | collective-permute-start | bytes 2359304 | tf_op jit(solution)/shard_map/ppermute | solution.py:614
  135.5 53.8 %collective-permute-start.12 = (bf16[256,768]{1,0:T(8,128)(2,1)S(1)}, bf16[256,768]{1,0:T(8,128)(2,1)S(1)}, u32[]{:S(2)}, u32[]{:S(2)}) collective-permute-start(bf16[256,768]{1,0:T(8,128)(2,1)S(1)} %get-tuple-element.235), channel_id=1, source_target_pairs={{0,3},{1,0},{2,1},{3,2},{4,7},{5,4},{6,5},{7,6},{8,11},{9,8},{10,9... | collective-permute-start | bytes 1179656 | tf_op jit(solution)/shard_map/ppermute | solution.py:614
  137.5 68.1 %collective-permute-start.13 = (bf16[256,768]{1,0:T(8,128)(2,1)S(1)}, bf16[256,768]{1,0:T(8,128)(2,1)S(1)}, u32[]{:S(2)}, u32[]{:S(2)}) collective-permute-start(bf16[256,768]{1,0:T(8,128)(2,1)S(1)} %get-tuple-element.236), channel_id=1, source_target_pairs={{0,2},{1,3},{2,0},{3,1},{4,6},{5,7},{6,4},{7,5},{8,10},{9,11},{10,... | collective-permute-start | bytes 1179656 | tf_op jit(solution)/shard_map/ppermute | solution.py:614
  138.6 67.0 %collective-permute-start.14 = (bf16[256,768]{1,0:T(8,128)(2,1)S(1)}, bf16[256,768]{1,0:T(8,128)(2,1)S(1)}, u32[]{:S(2)}, u32[]{:S(2)}) collective-permute-start(bf16[256,768]{1,0:T(8,128)(2,1)S(1)} %get-tuple-element.237), channel_id=1, source_target_pairs={{0,1},{1,2},{2,3},{3,0},{4,5},{5,6},{6,7},{7,4},{8,9},{9,10},{10,1... | collective-permute-start | bytes 1179656 | tf_op jit(solution)/shard_map/ppermute | solution.py:614
  189.3 36.4 %copy-start.47 = (bf16[512,768]{1,0:T(8,128)(2,1)}, bf16[512,768]{1,0:T(8,128)(2,1)S(1)}, u32[]{:S(2)}) copy-start(bf16[512,768]{1,0:T(8,128)(2,1)S(1)} %get-tuple-element.293) | copy-start | bytes 2359300
  189.3 36.4 %copy-start.73 = (bf16[256,768]{1,0:T(8,128)(2,1)}, bf16[256,768]{1,0:T(8,128)(2,1)S(1)}, u32[]{:S(2)}) copy-start(bf16[256,768]{1,0:T(8,128)(2,1)S(1)} %collective-permute-done.12.refs_2_) | copy-start | bytes 1179652
  205.6 20.1 %copy-start.74 = (bf16[256,768]{1,0:T(8,128)(2,1)}, bf16[256,768]{1,0:T(8,128)(2,1)S(1)}, u32[]{:S(2)}) copy-start(bf16[256,768]{1,0:T(8,128)(2,1)S(1)} %collective-permute-done.13.refs_3_) | copy-start | bytes 1179652
  205.6 51.3 %collective-permute-start.15 = (bf16[256,768]{1,0:T(8,128)(2,1)}, bf16[256,768]{1,0:T(8,128)(2,1)}, u32[]{:S(2)}, u32[]{:S(2)}) collective-permute-start(bf16[256,768]{1,0:T(8,128)(2,1)} %get-tuple-element.251), channel_id=1, source_target_pairs={{0,3},{1,0},{2,1},{3,2},{4,7},{5,4},{6,5},{7,6},{8,11},{9,8},{10,9... | collective-permute-start | bytes 1179656 | tf_op jit(solution)/shard_map/ppermute | solution.py:614
  225.0 34.4 %collective-permute-start.16 = (bf16[256,768]{1,0:T(8,128)(2,1)S(1)}, bf16[256,768]{1,0:T(8,128)(2,1)}, u32[]{:S(2)}, u32[]{:S(2)}) collective-permute-start(bf16[256,768]{1,0:T(8,128)(2,1)S(1)} %get-tuple-element.252), channel_id=1, source_target_pairs={{0,2},{1,3},{2,0},{3,1},{4,6},{5,7},{6,4},{7,5},{8,10},{9,11},{10,... | collective-permute-start | bytes 1179656 | tf_op jit(solution)/shard_map/ppermute | solution.py:614
  225.0 34.4 %collective-permute-start.17 = (bf16[256,768]{1,0:T(8,128)(2,1)S(1)}, bf16[256,768]{1,0:T(8,128)(2,1)}, u32[]{:S(2)}, u32[]{:S(2)}) collective-permute-start(bf16[256,768]{1,0:T(8,128)(2,1)S(1)} %get-tuple-element.253), channel_id=1, source_target_pairs={{0,1},{1,2},{2,3},{3,0},{4,5},{5,6},{6,7},{7,4},{8,9},{9,10},{10,1... | collective-permute-start | bytes 1179656 | tf_op jit(solution)/shard_map/ppermute | solution.py:614
  259.4 193.3 %all-gather.3.cloned.1.call-start = ((), (), s32[]{:S(2)}) async-start(), calls=%async_computation.2 | async-start | bytes 3538944 | tf_op jit(solution)/shard_map/all_gather | solution.py:822
  270.1 55.0 %collective-permute-start.18 = (bf16[512,768]{1,0:T(8,128)(2,1)}, bf16[512,768]{1,0:T(8,128)(2,1)}, u32[]{:S(2)}, u32[]{:S(2)}) collective-permute-start(bf16[512,768]{1,0:T(8,128)(2,1)} %get-tuple-element.267), channel_id=1, source_target_pairs={{0,3},{1,0},{2,1},{3,2},{4,7},{5,4},{6,5},{7,6},{8,11},{9,8},{10,9... | collective-permute-start | bytes 2359304 | tf_op jit(solution)/shard_map/ppermute | solution.py:614
  271.0 54.2 %collective-permute-start.19 = (bf16[512,768]{1,0:T(8,128)(2,1)}, bf16[512,768]{1,0:T(8,128)(2,1)}, u32[]{:S(2)}, u32[]{:S(2)}) collective-permute-start(bf16[512,768]{1,0:T(8,128)(2,1)} %get-tuple-element.268), channel_id=1, source_target_pairs={{0,2},{1,3},{2,0},{3,1},{4,6},{5,7},{6,4},{7,5},{8,10},{9,11},{10,... | collective-permute-start | bytes 2359304 | tf_op jit(solution)/shard_map/ppermute | solution.py:614
  283.5 38.9 %copy-start.82 = (f32[1,768]{1,0:T(1,128)S(1)}, f32[1,768]{1,0:T(1,128)}, u32[]{:S(2)}) copy-start(f32[1,768]{1,0:T(1,128)} %get-tuple-element.275) | copy-start | bytes 9220
  283.5 38.9 %copy-start.83 = (f32[1,768]{1,0:T(1,128)S(1)}, f32[1,768]{1,0:T(1,128)}, u32[]{:S(2)}) copy-start(f32[1,768]{1,0:T(1,128)} %get-tuple-element.276) | copy-start | bytes 9220
  328.0 17.3 %collective-permute-start.20 = (bf16[4,512,384]{2,1,0:T(8,128)(2,1)}, bf16[4,512,384]{2,1,0:T(8,128)(2,1)}, u32[]{:S(2)}, u32[]{:S(2)}) collective-permute-start(bf16[4,512,384]{2,1,0:T(8,128)(2,1)} %dynamic-slice_bitcast_fusion.1), channel_id=1, source_target_pairs={{0,4},{4,0},{1,5},{5,1},{2,6},{6,2},{3,7},{7,3},{8,12},{12,8},{9,1... | collective-permute-start | bytes 4718600 | tf_op jit(solution)/shard_map/ppermute | solution.py:787
  328.0 37.4 %collective-permute-start.24 = (bf16[512,768]{1,0:T(8,128)(2,1)}, bf16[512,768]{1,0:T(8,128)(2,1)S(1)}, u32[]{:S(2)}, u32[]{:S(2)}) collective-permute-start(bf16[512,768]{1,0:T(8,128)(2,1)} %copy-done.47), channel_id=1, source_target_pairs={{0,1},{1,2},{2,3},{3,0},{4,5},{5,6},{6,7},{7,4},{8,9},{9,10},{10,1... | collective-permute-start | bytes 2359304 | tf_op jit(solution)/shard_map/ppermute | solution.py:614
  347.5 17.9 %collective-permute-start.21 = (bf16[512,384]{1,0:T(8,128)(2,1)S(1)}, bf16[512,384]{1,0:T(8,128)(2,1)S(1)}, u32[]{:S(2)}, u32[]{:S(2)}) collective-permute-start(bf16[512,384]{1,0:T(8,128)(2,1)S(1)} %get-tuple-element.287), channel_id=1, source_target_pairs={{0,8},{8,0},{16,24},{24,16},{1,9},{9,1},{17,25},{25,17},{2,10},{10... | collective-permute-start | bytes 1179656 | tf_op jit(solution)/shard_map/ppermute | solution.py:787
  349.1 19.7 %collective-permute-start.22 = (bf16[512,384]{1,0:T(8,128)(2,1)S(1)}, bf16[512,384]{1,0:T(8,128)(2,1)S(1)}, u32[]{:S(2)}, u32[]{:S(2)}) collective-permute-start(bf16[512,384]{1,0:T(8,128)(2,1)S(1)} %get-tuple-element.288), channel_id=1, source_target_pairs={{0,16},{8,24},{16,0},{24,8},{1,17},{9,25},{17,1},{25,9},{2,18},{10... | collective-permute-start | bytes 1179656 | tf_op jit(solution)/shard_map/ppermute | solution.py:787
  350.8 18.0 %collective-permute-start.23 = (bf16[512,384]{1,0:T(8,128)(2,1)S(1)}, bf16[512,384]{1,0:T(8,128)(2,1)S(1)}, u32[]{:S(2)}, u32[]{:S(2)}) collective-permute-start(bf16[512,384]{1,0:T(8,128)(2,1)S(1)} %get-tuple-element.289), channel_id=1, source_target_pairs={{0,24},{8,16},{16,8},{24,0},{1,25},{9,17},{17,9},{25,1},{2,26},{10... | collective-permute-start | bytes 1179656 | tf_op jit(solution)/shard_map/ppermute | solution.py:787
  369.4 15.9 %collective-permute-start.25 = (bf16[512,384]{1,0:T(8,128)(2,1)S(1)}, bf16[512,384]{1,0:T(8,128)(2,1)S(1)}, u32[]{:S(2)}, u32[]{:S(2)}) collective-permute-start(bf16[512,384]{1,0:T(8,128)(2,1)S(1)} %fusion.12), channel_id=1, source_target_pairs={{0,1},{1,0},{2,3},{3,2},{4,5},{5,4},{6,7},{7,6},{8,9},{9,8},{10,11... | collective-permute-start | bytes 1179656 | tf_op jit(solution)/shard_map/ppermute | solution.py:787
  386.9 21.1 %collective-permute-start.27 = (bf16[4,304,384]{2,1,0:T(8,128)(2,1)S(1)}, bf16[4,304,384]{2,1,0:T(8,128)(2,1)}, u32[]{:S(2)}, u32[]{:S(2)}) collective-permute-start(bf16[4,304,384]{2,1,0:T(8,128)(2,1)S(1)} %dynamic-slice_bitcast_fusion.2), channel_id=1, source_target_pairs={{0,4},{4,0},{1,5},{5,1},{2,6},{6,2},{3,7},{7,3},{8,12},{12,8},{9,1... | collective-permute-start | bytes 2801672 | tf_op jit(solution)/shard_map/ppermute | solution.py:787
  387.1 20.8 %collective-permute-start.26 = (bf16[512,384]{1,0:T(8,128)(2,1)S(1)}, bf16[512,384]{1,0:T(8,128)(2,1)S(1)}, u32[]{:S(2)}, u32[]{:S(2)}) collective-permute-start(bf16[512,384]{1,0:T(8,128)(2,1)S(1)} %add_convert_fusion.2), channel_id=1, source_target_pairs={{0,2},{1,3},{2,0},{3,1},{4,6},{5,7},{6,4},{7,5},{8,10},{9,11},{10,... | collective-permute-start | bytes 1179656 | tf_op jit(solution)/shard_map/ppermute | solution.py:787
  408.8 69.1 %all-gather.5.cloned.1.call-start = ((), (), s32[]{:S(2)}) async-start(), calls=%async_computation.3 | async-start | bytes 2101248 | tf_op jit(solution)/shard_map/all_gather | solution.py:822
  414.5 12.7 %collective-permute-start.29 = (bf16[304,384]{1,0:T(8,128)(2,1)S(1)}, bf16[304,384]{1,0:T(8,128)(2,1)S(1)}, u32[]{:S(2)}, u32[]{:S(2)}) collective-permute-start(bf16[304,384]{1,0:T(8,128)(2,1)S(1)} %get-tuple-element.321), channel_id=1, source_target_pairs={{0,8},{8,0},{16,24},{24,16},{1,9},{9,1},{17,25},{25,17},{2,10},{10... | collective-permute-start | bytes 700424 | tf_op jit(solution)/shard_map/ppermute | solution.py:787
  415.9 12.1 %collective-permute-start.30 = (bf16[304,384]{1,0:T(8,128)(2,1)S(1)}, bf16[304,384]{1,0:T(8,128)(2,1)S(1)}, u32[]{:S(2)}, u32[]{:S(2)}) collective-permute-start(bf16[304,384]{1,0:T(8,128)(2,1)S(1)} %get-tuple-element.322), channel_id=1, source_target_pairs={{0,16},{8,24},{16,0},{24,8},{1,17},{9,25},{17,1},{25,9},{2,18},{10... | collective-permute-start | bytes 700424 | tf_op jit(solution)/shard_map/ppermute | solution.py:787
  416.6 15.9 %collective-permute-start.31 = (bf16[304,384]{1,0:T(8,128)(2,1)S(1)}, bf16[304,384]{1,0:T(8,128)(2,1)S(1)}, u32[]{:S(2)}, u32[]{:S(2)}) collective-permute-start(bf16[304,384]{1,0:T(8,128)(2,1)S(1)} %get-tuple-element.323), channel_id=1, source_target_pairs={{0,24},{8,16},{16,8},{24,0},{1,25},{9,17},{17,9},{25,1},{2,26},{10... | collective-permute-start | bytes 700424 | tf_op jit(solution)/shard_map/ppermute | solution.py:787
  432.6 7.2 %collective-permute-start.33 = (bf16[304,384]{1,0:T(8,128)(2,1)S(1)}, bf16[304,384]{1,0:T(8,128)(2,1)S(1)}, u32[]{:S(2)}, u32[]{:S(2)}) collective-permute-start(bf16[304,384]{1,0:T(8,128)(2,1)S(1)} %fusion.21), channel_id=1, source_target_pairs={{0,1},{1,0},{2,3},{3,2},{4,5},{5,4},{6,7},{7,6},{8,9},{9,8},{10,11... | collective-permute-start | bytes 700424 | tf_op jit(solution)/shard_map/ppermute | solution.py:787
  439.9 12.1 %collective-permute-start.34 = (bf16[304,384]{1,0:T(8,128)(2,1)S(1)}, bf16[304,384]{1,0:T(8,128)(2,1)S(1)}, u32[]{:S(2)}, u32[]{:S(2)}) collective-permute-start(bf16[304,384]{1,0:T(8,128)(2,1)S(1)} %add_convert_fusion.4), channel_id=1, source_target_pairs={{0,2},{1,3},{2,0},{3,1},{4,6},{5,7},{6,4},{7,5},{8,10},{9,11},{10,... | collective-permute-start | bytes 700424 | tf_op jit(solution)/shard_map/ppermute | solution.py:787
  455.4 8.4 %collective-permute-start.32 = (f32[512,768]{1,0:T(8,128)}, f32[512,768]{1,0:T(8,128)}, u32[]{:S(2)}, u32[]{:S(2)}) collective-permute-start(f32[512,768]{1,0:T(8,128)} %dynamic-slice_bitcast_fusion), channel_id=1, source_target_pairs={{0,4},{4,0},{1,5},{5,1},{2,6},{6,2},{3,7},{7,3},{8,12},{12,8},{9,1... | collective-permute-start | bytes 4718600 | tf_op jit(solution)/shard_map/ppermute | solution.py:623
  455.5 5.7 %collective-permute-start.28 = (bf16[512,768]{1,0:T(8,128)(2,1)S(1)}, bf16[512,768]{1,0:T(8,128)(2,1)}, u32[]{:S(2)}, u32[]{:S(2)}) collective-permute-start(bf16[512,768]{1,0:T(8,128)(2,1)S(1)} %dynamic-slice_bitcast_fusion.3), channel_id=1, source_target_pairs={{0,4},{4,0},{1,5},{5,1},{2,6},{6,2},{3,7},{7,3},{8,12},{12,8},{9,1... | collective-permute-start | bytes 2359304 | tf_op jit(solution)/shard_map/ppermute | solution.py:623
  (75 other events, 429.0 us)
Sparse Core Ops, SparseCore 0:
  259.5 75.1 reduce-scatter.1
  408.9 39.5 all-gather.2
  452.9 24.9 all-gather.4

commit v6 on v5

--- a/solution.py
+++ b/solution.py
@@ -161,51 +161,62 @@
     onehot = (bucket_np(both)[..., None] == np.arange(32)).astype(np.float32)
     return jnp.einsum("lcb,bh->hlc", jnp.asarray(onehot), bias_table, precision=lax.Precision.HIGHEST)
 
-def fwd_kernel(first, lines_ref, q_ref, k_ref, v_ref, o_ref, band_ref):
+def tile_index(i, j, n, core):
+    half = n // 2
+    if i // half == j // half:
+        return max(-2, min(2, j - i)) + 2
+    return jnp.clip(j - i - n * core * (1 if i < j else -1), -2, 2) + 2
+
+
+def fwd_kernel(first, core_ref, lines_ref, q_ref, k_ref, v_ref, o_ref, total_ref, band_ref):
     n = k_ref.shape[0] // QB
     lane = lax.broadcasted_iota(jnp.int32, (QB, 128), 1)
     for h in range(2):
         line = lines_ref[h, 0:1, :]
         spread = pltpu.roll(jnp.broadcast_to(line, (QB, 4 * QB)), 0, 1, stride=1, stride_axis=0)
-        band_ref[h] = spread[:, QB:]
+        band_ref[h, 0] = jnp.broadcast_to(line[:, :1], (QB, QB))
+        for t in range(3):
+            band_ref[h, 1 + t] = spread[:, (1 + t) * QB:(2 + t) * QB]
+        band_ref[h, 4] = jnp.broadcast_to(line[:, 4 * QB - 1:], (QB, QB))
     for i in range(first, first + q_ref.shape[0] // QB):
         rows = slice((i - first) * QB, (i - first + 1) * QB)
         outs = []
         for h in range(2):
-            low_bias = lines_ref[h, 0:1, 0:1]
-            high_bias = lines_ref[h, 0:1, 4 * QB - 1:]
             q = jnp.where((lane < 64) == (h == 0), q_ref[rows, :], 0)
             s = lax.dot_general(q, k_ref[...], (((1,), (1,)), ((), ())), preferred_element_type=jnp.float32)
             parts = []
             for j in range(n):
-                d = j - i
-                b = band_ref[h, :, (d + 1) * QB:(d + 2) * QB] if abs(d) <= 1 else (low_bias if d < 0 else high_bias)
-                parts.append(s[:, j * QB:(j + 1) * QB] + b)
+                parts.append(s[:, j * QB:(j + 1) * QB] + band_ref[h, tile_index(i, j, n, core_ref[0])])
             s = jnp.concatenate(parts, axis=1)
             m = jnp.max(s, axis=1, keepdims=True)
             p = jnp.exp(s - m)
             l = jnp.sum(p, axis=1, keepdims=True)
             o = jnp.dot(p.astype(jnp.bfloat16), v_ref[...], preferred_element_type=jnp.float32)
             outs.append(o * (1.0 / l))
+            total = jnp.broadcast_to(m + jnp.log(l), (QB, 128)).T
+            total_ref[0, h:h + 1, rows] = total[:1]
         o_ref[rows, :] = jnp.where(lane < 64, outs[0], outs[1]).astype(jnp.bfloat16)
 
-def attend(q, k, v, lines, first, count):
+def attend(core, q, k, v, lines, first, count):
     length, width = q.shape
     col = pl.BlockSpec((length, 128), lambda h: (0, h))
     span = pl.BlockSpec((count, 128), lambda h: (first // count, h))
     return pl.pallas_call(
         lambda *refs: fwd_kernel(first // QB, *refs),
         grid=(width // 128,),
-        in_specs=[pl.BlockSpec((2, 2, 4 * QB), lambda h: (h, 0, 0)), span, col, col],
-        out_specs=pl.BlockSpec((count, 128), lambda h: (0, h)),
-        out_shape=jax.ShapeDtypeStruct((count, width), jnp.bfloat16),
-        scratch_shapes=[pltpu.VMEM((2, QB, 3 * QB), jnp.float32)],
+        in_specs=[pl.BlockSpec(memory_space=pltpu.SMEM), pl.BlockSpec((2, 2, 4 * QB), lambda h: (h, 0, 0)), span, col, col],
+        out_specs=[pl.BlockSpec((count, 128), lambda h: (0, h)), pl.BlockSpec((1, 2, count), lambda h: (h, 0, 0))],
+        out_shape=[
+            jax.ShapeDtypeStruct((count, width), jnp.bfloat16),
+            jax.ShapeDtypeStruct((width // 128, 2, count), jnp.float32),
+        ],
+        scratch_shapes=[pltpu.VMEM((2, 5, QB, QB), jnp.float32)],
         compiler_params=pltpu.CompilerParams(vmem_limit_bytes=48 << 20),
         cost_estimate=pl.CostEstimate(flops=count * length * width, bytes_accessed=2 * length * width, transcendentals=0),
         name="attend",
-    )(lines, q, k, v)
-
-def bwd_kernel(lines_ref, fold_ref, q_ref, k_ref, v_ref, g_ref, xt_ref, grad_ref, sums_ref, band_ref, acc_ref, far_acc, dk_acc, dv_acc):
+    )(core, lines, q, k, v)
+
+def bwd_kernel(core_ref, lines_ref, fold_ref, q_ref, k_ref, v_ref, g_ref, o_ref, total_ref, xt_ref, grad_ref, sums_ref, band_ref, acc_ref, dk_acc, dv_acc):
     n = q_ref.shape[0] // QB
     lane = lax.broadcasted_iota(jnp.int32, (QB, 128), 1)
     for h in range(2):
@@ -213,38 +224,28 @@
             start = 2 * QB - (t - 1) * QB - QB
             line = lines_ref[h, 1:2, start:start + 2 * QB]
             spread = pltpu.roll(jnp.broadcast_to(line, (QB, 2 * QB)), QB, 1, stride=1, stride_axis=0)
-            band_ref[h, t * QB:(t + 1) * QB, :] = spread[:, :QB]
+            band_ref[h, 1 + t] = spread[:, :QB]
+        band_ref[h, 0] = jnp.broadcast_to(lines_ref[h, 0:1, 0:1], (QB, QB))
+        band_ref[h, 4] = jnp.broadcast_to(lines_ref[h, 0:1, 4 * QB - 1:], (QB, QB))
     acc_ref[...] = jnp.zeros_like(acc_ref)
-    far_acc[...] = jnp.zeros_like(far_acc)
     for i in range(n):
         rows = slice(i * QB, (i + 1) * QB)
         grads = []
         for h in range(2):
             keep = (lane < 64) == (h == 0)
-            low_bias = lines_ref[h, 0:1, 0:1]
-            high_bias = lines_ref[h, 0:1, 4 * QB - 1:]
             q = jnp.where(keep, q_ref[rows, :], 0)
             g = jnp.where(keep, g_ref[rows, :], 0)
             s = lax.dot_general(k_ref[...], q, (((1,), (1,)), ((), ())), preferred_element_type=jnp.float32)
             parts = []
             for j in range(n):
-                d = j - i
-                b = band_ref[h, (d + 1) * QB:(d + 2) * QB, :] if abs(d) <= 1 else (low_bias if d < 0 else high_bias)
-                parts.append(s[j * QB:(j + 1) * QB, :] + b)
+                parts.append(s[j * QB:(j + 1) * QB, :] + band_ref[h, tile_index(i, j, n, core_ref[0])])
             s = jnp.concatenate(parts, axis=0)
-            m = jnp.max(s, axis=0, keepdims=True)
-            p = jnp.exp(s - m)
-            w = p * (1.0 / jnp.sum(p, axis=0, keepdims=True))
+            w = jnp.exp(s - total_ref[0, h:h + 1, rows])
             dp = lax.dot_general(v_ref[...], g, (((1,), (1,)), ((), ())), preferred_element_type=jnp.float32)
-            delta = jnp.sum(w * dp, axis=0, keepdims=True)
+            delta = jnp.sum((g.astype(jnp.float32) * o_ref[rows, :].astype(jnp.float32)).T, axis=0, keepdims=True)
             ds = w * (dp - delta)
             for j in range(n):
-                d = j - i
-                tile = ds[j * QB:(j + 1) * QB, :]
-                if abs(d) <= 1:
-                    acc_ref[h, (d + 1) * QB:(d + 2) * QB, :] += tile
-                else:
-                    far_acc[h, 0 if d < 0 else 1] += jnp.sum(tile.reshape(QB // 8, 8, QB), axis=0)
+                acc_ref[h, tile_index(i, j, n, core_ref[0])] += ds[j * QB:(j + 1) * QB, :]
             low = ds.astype(jnp.bfloat16)
             dv = jnp.dot(w.astype(jnp.bfloat16), g, preferred_element_type=jnp.float32)
             dk = jnp.dot(low, q, preferred_element_type=jnp.float32)
@@ -263,7 +264,7 @@
     for h in range(2):
         total = jnp.zeros((8, 128), jnp.float32)
         for t in range(3):
-            tile = acc_ref[h, t * QB:(t + 1) * QB, :]
+            tile = acc_ref[h, 1 + t]
             wide = jnp.concatenate([tile, jnp.zeros_like(tile)], axis=1)
             moved = sum(pltpu.roll(wide[8 * e:8 * e + 8], QB - 8 * e, 1) for e in range(QB // 8))
             turned = jnp.where(row == 0, moved, 0.0)
@@ -271,7 +272,7 @@
                 turned = turned + pltpu.roll(jnp.where(row == e, moved, 0.0), 2 * QB - e, 1)
             total = total + jnp.dot(turned, fold_ref[t], precision=lax.Precision.HIGHEST, preferred_element_type=jnp.float32)
         total = jnp.sum(total, axis=0, keepdims=True)
-        ends = [jnp.sum(jnp.sum(far_acc[h, side], axis=0, keepdims=True), axis=1, keepdims=True) for side in range(2)]
+        ends = [jnp.sum(jnp.sum(acc_ref[h, side], axis=0, keepdims=True), axis=1, keepdims=True) for side in (0, 4)]
         column = lax.broadcasted_iota(jnp.int32, (1, 128), 1)
         total = total + jnp.where(column == 15, ends[0], 0.0) + jnp.where(column == 31, ends[1], 0.0)
         totals.append(total)
@@ -285,7 +286,7 @@
     sums_ref[3 * width:, :] = small.astype(jnp.bfloat16)
 
 
-def attend_back(q, k, v, g, xt, lines, first_pair, pairs, total_pairs, earlier=()):
+def attend_back(core, q, k, v, g, o, totals, xt, lines, first_pair, pairs, total_pairs, earlier=()):
     length, width = q.shape
     rows = 3 * width + 128
     r = (np.arange(3)[:, None] - 1) * QB - (np.arange(2 * QB)[None] - QB)
@@ -293,12 +294,14 @@
     col = pl.BlockSpec((length, 128), lambda h: (0, h + first_pair))
     offset = first_pair % total_pairs
     return pl.pallas_call(
-        lambda *refs: bwd_kernel(*refs[:7], *refs[7 + len(earlier):]),
+        lambda *refs: bwd_kernel(*refs[:10], *refs[10 + len(earlier):]),
         grid=(pairs,),
         in_specs=[
+            pl.BlockSpec(memory_space=pltpu.SMEM),
             pl.BlockSpec((2, 2, 4 * QB), lambda h: (h + first_pair, 0, 0)),
             pl.BlockSpec((3, 2 * QB, 128), lambda h: (0, 0, 0)),
-            col, col, col, col,
+            col, col, col, col, col,
+            pl.BlockSpec((1, 2, length), lambda h: (h + first_pair, 0, 0)),
             pl.BlockSpec((width, length), lambda h: (0, 0), pipeline_mode=pl.Buffered(1)),
         ]
         + [pl.BlockSpec(memory_space=pl.ANY)] * len(earlier),
@@ -311,9 +314,8 @@
             jax.ShapeDtypeStruct((rows, 128 * total_pairs), jnp.bfloat16),
         ],
         scratch_shapes=[
-            pltpu.VMEM((2, 3 * QB, QB), jnp.float32),
-            pltpu.VMEM((2, 3 * QB, QB), jnp.float32),
-            pltpu.VMEM((2, 2, 8, QB), jnp.float32),
+            pltpu.VMEM((2, 5, QB, QB), jnp.float32),
+            pltpu.VMEM((2, 5, QB, QB), jnp.float32),
             pltpu.VMEM((length, 128), jnp.float32),
             pltpu.VMEM((length, 128), jnp.float32),
         ],
@@ -321,9 +323,9 @@
         cost_estimate=pl.CostEstimate(
             flops=84 * length * length * 128 * pairs, bytes_accessed=14 * length * 128 * pairs, transcendentals=2 * length * length * pairs
         ),
-        input_output_aliases={7: 0, 8: 1} if earlier else {},
+        input_output_aliases={10: 0, 11: 1} if earlier else {},
         name="attend_back",
-    )(lines, jnp.asarray(fold), q, k, v, g, xt, *earlier)
+    )(core, lines, jnp.asarray(fold), q, k, v, g, o, totals, xt, *earlier)
 
 
 def expert_kernel(count, label_ref, *refs):
@@ -563,17 +565,19 @@
     return residual, pieces
 
 
-def before_attention_kernel(owners, slot_ref, *refs):
+def before_attention_kernel(owners, earlier, slot_ref, *refs):
     piece_refs = refs[:owners]
     residual_ref, upstream_ref, attended_ref, weight_ref, gain_ref = refs[owners : owners + 5]
-    residual_grad_ref, mixed_grad_ref, weight_grad_ref, gain_grad_ref = refs[owners + 5 :]
+    residual_grad_ref, mixed_grad_ref, weight_grad_ref, gain_grad_ref = refs[-4:]
     blocks, _, length = slot_ref.shape
     capacity = length // 2
-    weight_grad, gain_grad = 0.0, 0.0
+    weight_grad, gain_grad = (refs[-6][...], refs[-5][...]) if earlier else (0.0, 0.0)
     for block in range(blocks):
-        matrix = sort_matrix(slot_ref[block], owners * capacity)
+        slot = jnp.broadcast_to(slot_ref[block].astype(jnp.float32), (128, length)).T[:, :1].astype(jnp.int32)
+        place = lax.broadcasted_iota(jnp.int32, (length, owners * capacity), 1)
+        matrix = (place == slot).astype(jnp.float32).astype(jnp.bfloat16)
         rows = jnp.concatenate([ref[block * capacity : (block + 1) * capacity, :] for ref in piece_refs])
-        grad = lax.dot_general(matrix, rows, (((0,), (0,)), ((), ())), preferred_element_type=jnp.float32)
+        grad = jnp.dot(matrix, rows, preferred_element_type=jnp.float32)
         residual = residual_ref[block]
         scale = norm_scale_rows(residual)
         normed = residual * scale
@@ -590,22 +594,30 @@
     gain_grad_ref[...] = gain_grad
 
 
-def before_attention(slots, pieces, residual, upstream, attended, weight, gain):
-    width = residual.shape[2]
-    vmem = pl.BlockSpec(memory_space=pltpu.VMEM)
+def before_attention(slots, pieces, residual, upstream, attended, weight, gain, group, group_count, earlier):
+    blocks, length, width = residual.shape
+    owners = len(pieces)
+    rows = one_step(residual.shape)
+    out_rows = pl.BlockSpec(residual.shape, lambda step: (group, 0, 0), pipeline_mode=pl.Buffered(1))
+    sums = [one_step((width, width)), one_step((1, width))]
+    shape = (group_count * blocks, length, width)
     return pl.pallas_call(
-        lambda *refs: before_attention_kernel(len(pieces), *refs),
-        in_specs=[vmem] * (len(pieces) + 6),
-        out_specs=[vmem] * 4,
+        lambda *refs: before_attention_kernel(owners, bool(earlier), *refs),
+        grid=(1,),
+        in_specs=[one_step(slots.shape)] + [one_step(pieces[0].shape)] * owners
+        + [rows, rows, rows, one_step((width, width)), one_step((1, width))]
+        + ([pl.BlockSpec(memory_space=pl.ANY)] * 2 + sums if earlier else []),
+        out_specs=[out_rows, out_rows] + sums,
         out_shape=[
-            jax.ShapeDtypeStruct(residual.shape, jnp.float32),
-            jax.ShapeDtypeStruct(residual.shape, jnp.bfloat16),
+            jax.ShapeDtypeStruct(shape, jnp.float32),
+            jax.ShapeDtypeStruct(shape, jnp.bfloat16),
             jax.ShapeDtypeStruct((width, width), jnp.float32),
             jax.ShapeDtypeStruct((1, width), jnp.float32),
         ],
+        input_output_aliases={owners + 6: 0, owners + 7: 1} if earlier else {},
         compiler_params=pltpu.CompilerParams(vmem_limit_bytes=56 << 20),
         name="before_attention",
-    )(slots, *pieces, residual, upstream, attended, weight, gain[None])
+    )(slots, *pieces, residual, upstream, attended, weight, gain[None], *earlier)
 
 
 def exchange(pieces, axis, sign, size=None, skipped=0):
@@ -616,47 +628,22 @@
     ]
 
 
-def trade(blocks):
+def own_and_other(blocks):
     at = lax.axis_index("ctx")
-    mine = lax.dynamic_index_in_dim(blocks, at, 0, keepdims=False)
-    other = lax.dynamic_index_in_dim(blocks, 1 - at, 0, keepdims=False)
+    own = lax.dynamic_index_in_dim(blocks, at, 0)
+    other = lax.dynamic_index_in_dim(blocks, 1 - at, 0)
+    return [own, lax.ppermute(other, "ctx", [(0, 1), (1, 0)])]
+
+
+def hand_back(own, other):
+    at = lax.axis_index("ctx")
     arrived = lax.ppermute(other, "ctx", [(0, 1), (1, 0)])
-    return jnp.stack([jnp.where(at == 0, mine, arrived), jnp.where(at == 0, arrived, mine)])
-
-
-def token_grads_kernel(first_ref, second_ref, *refs):
-    weight_refs, (tokens_ref, residual_grad_ref, gain_ref, out_ref) = refs[:3], refs[3:]
-    grad = 0.0
-    for kind in range(3):
-        low = jnp.concatenate([first_ref[kind], second_ref[kind]], axis=1)
-        grad += lax.dot_general(low, weight_refs[kind][...], (((1,), (1,)), ((), ())), preferred_element_type=jnp.float32)
-    rows = tokens_ref[...].astype(jnp.float32)
-    scale = norm_scale_rows(rows)
-    normed = rows * scale
-    scaled = grad * gain_ref[...]
-    shrink = jnp.mean(scaled * normed, axis=-1, keepdims=True)
-    out_ref[...] = residual_grad_ref[...] + scale * (scaled - normed * shrink)
-
-
-def token_grads(first, second, weights, tokens, residual_grad, gain):
-    length, width = tokens.shape
-    half = pl.BlockSpec((3, QB, width // 2), lambda step: (0, step, 0))
-    rows = pl.BlockSpec((QB, width), lambda step: (step, 0))
-    return pl.pallas_call(
-        token_grads_kernel,
-        grid=(length // QB,),
-        in_specs=[half, half] + [one_step((width, width))] * 3 + [rows, rows, one_step((1, width))],
-        out_specs=rows,
-        out_shape=jax.ShapeDtypeStruct((length, width), jnp.float32),
-        compiler_params=pltpu.CompilerParams(vmem_limit_bytes=48 << 20),
-        cost_estimate=pl.CostEstimate(flops=6 * length * width * width, bytes_accessed=14 * length * width, transcendentals=0),
-        name="token_grads",
-    )(first, second, *weights, tokens, residual_grad, gain[None])
+    return jnp.concatenate([jnp.where(at == 0, own, arrived), jnp.where(at == 0, arrived, own)])
 
 
 def layer_output_kernel(groups, owners, *refs):
     slot_refs, residual_refs = refs[:groups], refs[groups : 2 * groups]
-    piece_refs, out_ref = refs[2 * groups : 2 * groups + owners], refs[-1]
+    piece_refs = refs[2 * groups : 2 * groups + owners]
     blocks, _, length = slot_refs[0].shape
     capacity = length // 2
     for group in range(groups):
@@ -665,7 +652,7 @@
             matrix = sort_matrix(slot_refs[group][block], owners * capacity)
             rows = jnp.concatenate([ref[at * capacity : (at + 1) * capacity, :] for ref in piece_refs])
             moved = lax.dot_general(matrix, rows, (((0,), (0,)), ((), ())), preferred_element_type=jnp.float32)
-            out_ref[at] = (residual_refs[group][block] + moved).astype(jnp.bfloat16)
+            refs[len(refs) - groups + group][block] = (residual_refs[group][block] + moved).astype(jnp.bfloat16)
 
 
 def layer_output(slots, residuals, pieces):
@@ -674,8 +661,8 @@
     return pl.pallas_call(
         lambda *refs: layer_output_kernel(len(slots), len(pieces), *refs),
         in_specs=[vmem] * (2 * len(slots) + len(pieces)),
-        out_specs=vmem,
-        out_shape=jax.ShapeDtypeStruct((len(slots) * blocks, length, width), jnp.bfloat16),
+        out_specs=[vmem] * len(slots),
+        out_shape=[jax.ShapeDtypeStruct((blocks, length, width), jnp.bfloat16)] * len(slots),
         compiler_params=pltpu.CompilerParams(vmem_limit_bytes=48 << 20),
         name="layer_output",
     )(*slots, *residuals, *pieces)
@@ -850,19 +837,21 @@
     owners = lax.axis_size("expert")
     capacity = local_len // 2
     whole_seq = seq_count == 2 and lax.axis_size("ctx") == 2 and local_len % QB == 0
-    if whole_seq:
-        routes, cotangent, tokens = trade(routes), trade(cotangent), trade(tokens)
-    groups = [slice(0, 1), slice(1, 2)] if whole_seq else [slice(0, seq_count)]
+    split = own_and_other if whole_seq else lambda blocks: [blocks]
+    routes, cotangent, token_groups = split(routes), split(cotangent), split(tokens)
+    groups = range(len(routes))
+    core = lax.axis_index("ctx").astype(jnp.int32).reshape(1)
     label = lax.axis_index("expert").astype(jnp.int32).reshape(1)
     together = lax.optimization_barrier
 
     sorted_upstream, slots = zip(
         *[
-            sort_upstream(label, routes[group], cotangent[group], owners, at, 1 + at)
-            for at, group in enumerate(groups)
+            sort_upstream(label, routes[group], cotangent[group], owners, group, 1 + group)
+            for group in groups
         ]
     )
-    sorted_first, tokens = together((sorted_upstream[0], tokens))
+    sorted_first, token_groups = together((sorted_upstream[0], token_groups))
+    tokens = jnp.concatenate(token_groups)
     upstream = [exchange(sorted_first, "expert", 1)]
     inputs = tokens.astype(jnp.float32)
     scale1 = norm_scale(inputs)
@@ -881,10 +870,14 @@
         buckets = bucket_grid(first_pos, local_len, keys.shape[1])
         attended, log_totals = attend_rows(queries, keys, values, buckets, bias_table, DH)
     attended_groups, residual1, arrived = [], [], []
+    if whole_seq:
+        log_totals = []
     in_flight, fed = upstream[0], queries.reshape(-1, model_width)
     for at, group in enumerate(groups):
         if whole_seq:
-            rows = attend(fed, *qkv[1:], lines, at * local_len, local_len)[None]
+            rows, totals = attend(core, fed, *qkv[1:], lines, at * local_len, local_len)
+            rows = rows[None]
+            log_totals.append(totals)
         else:
             rows = attended.astype(jnp.bfloat16)
         rows, in_flight = together((rows, in_flight))
@@ -895,7 +888,7 @@
         attended_groups.append(rows)
         earlier = sorted_upstream[at] if at else []
         residual, sorted_rows = after_attention(
-            slots[at], rows, tokens[group], output_weight, norm2_gain, owners, earlier
+            slots[at], rows, token_groups[at], output_weight, norm2_gain, owners, earlier
         )
         residual1.append(residual)
         sorted_rows, fed = together((sorted_rows, fed))
@@ -903,15 +896,17 @@
         arrived.append(in_flight)
     router_wide = jnp.pad(router_weight, ((0, 0), (0, 128 - router_weight.shape[1])))
     done, back = [], []
-    upstream += arrived[1:]
     tile = seq_count // len(groups) * local_len // 2
-    for at, (rows, grads) in enumerate(zip(arrived, upstream)):
+    for at in groups:
+        rows, grads = arrived[at], upstream[0] if at == 0 else arrived[at]
         earlier = done[-1][0] if done else []
         result = run_expert(
             label, rows, grads, tile, min(at, 1), router_wide, w_in[0], w_out[0], at, len(groups), earlier
         )
         if back:
             result, back[-1] = together((result, back[-1]))
+        if at + 1 < len(arrived):
+            result, arrived[at + 1] = together((result, arrived[at + 1]))
         done.append(result)
         back.append(exchange(result[1], "expert", -1))
     rows_out = done[-1][0]
@@ -922,14 +917,13 @@
     grad_experts = lax.psum_scatter(grad_experts, ("dp", "ctx"), scatter_dimension=0, tiled=True)
     if not whole_seq:
         returned = exchange(list(rows_out), "expert", -1)
-    residual_grad, mixed_grad, grad_w_output, grad_norm2 = zip(
-        *[
-            before_attention(slot, pieces, residual, cotangent[group], rows, output_weight, norm2_gain)
-            for slot, pieces, residual, group, rows in zip(slots, back, residual1, groups, attended_groups)
-        ]
-    )
-    residual_grad, mixed_grad = jnp.concatenate(residual_grad), jnp.concatenate(mixed_grad)
-    grad_w_output, grad_norm2 = sum(grad_w_output), sum(grad_norm2)
+    backward = ()
+    for group in groups:
+        backward = before_attention(
+            slots[group], back[group], residual1[group], cotangent[group], attended_groups[group],
+            output_weight, norm2_gain, group, len(groups), backward,
+        )
+    residual_grad, mixed_grad, grad_w_output, grad_norm2 = backward
     early_small = jnp.concatenate([grad_router, grad_norm2])
     projections = (query_weight, key_weight, value_weight)
     if whole_seq:
@@ -937,8 +931,9 @@
         pairs = half // 128
         mixed_grad = mixed_grad.reshape(flat)
         turned = attn_in.reshape(flat).T
+        seen = (jnp.concatenate(attended_groups).reshape(flat), jnp.concatenate(log_totals, axis=2), turned)
         returned = exchange(list(rows_out[:-1]), "expert", -1, owners)
-        first = attend_back(*qkv, mixed_grad, turned, lines, 0, pairs, pairs)
+        first = attend_back(core, *qkv, mixed_grad, *seen, lines, 0, pairs, pairs)
         first, returned, last_rows = together((first, returned, rows_out[-1]))
         returned.append(exchange([None, last_rows], "expert", -1, owners, owners - 2)[1])
         first_grads, first_sums = first
@@ -948,7 +943,7 @@
         for at in range(pairs, 2 * pairs):
             sent, mixed_grad = together((early.sends(), mixed_grad))
             moved = early.move(sent)
-            second = attend_back(*qkv, mixed_grad, turned, lines, at, 1, pairs, second)
+            second = attend_back(core, *qkv, mixed_grad, *seen, lines, at, 1, pairs, second)
             if at == pairs + 1:
                 second, moved, returned = together((second, moved, returned))
             else:
@@ -1007,10 +1002,10 @@
     experts = router_weight.shape[1]
     grad_router, grad_norm2 = small[:experts, :].T, small[experts]
     if not whole_seq:
-        block_out = layer_output(slots, residual1, returned)
+        block_out = layer_output(slots, residual1, returned)[0]
         d_tokens = residual_grad + norm1_back
     if whole_seq:
-        block_out, d_tokens = trade(block_out), trade(d_tokens)
+        block_out, d_tokens = hand_back(*block_out), hand_back(d_tokens[:1], d_tokens[1:])
     grad_experts = grad_experts.astype(jnp.float32)
     return (
         block_out,

time: 504 us -> 493 us (0.978)
  Pallas kernels: 242 us -> 228 us
  local copies, waits for them, and re-layouts: 46.2 us -> 58 us
  other arithmetic: 27.6 us -> 21.9 us
    pallas_call x6, Pallas kernels: 98.8 us -> 82 us  [the longest x4 64.2 us: attend_back(): pl.pallas_call(lambda *refs: bwd_kernel(*refs[:10], *refs[10 + len(earlie...]
    another operation x8 -> x1, other arithmetic: 11.8 us -> 1.13 us  [the longest x7 9.04 us: trade(): jnp.stack([jnp.where(at == 0, mine, arrived), jnp.where(at == 0, arrived,...]
    unnamed x174 -> x185, local copies, waits for them, and re-layouts: 29.6 us -> 39.1 us
    squeeze x4 -> x0, local copies, waits for them, and re-layouts: 5.86 us -> none  [trade(): other = lax.dynamic_index_in_dim(blocks, 1 - at, 0, keepdims=False)]
  transfers between devices with their start and end apart: 38 -> 38, of which waited for: 14 -> 11; matrix products, arithmetic and copies ran while one was open for 9% -> 9% of each run, Pallas kernels for 46% -> 46%
where the time goes in v6:
time: 493 us; the launch traced here: 484 us
  Pallas kernels  228 us (46%)
  waiting for transfers between devices  85.3 us (17%)
  starting transfers between devices  70.5 us (14%)
  local copies, waits for them, and re-layouts  58 us (12%)
  other arithmetic  21.9 us (4%)
  between operations  15.1 us (3%)
    pallas_call x4, Pallas kernels, attend_back(): pl.pallas_call(lambda *refs: bwd_kernel(*refs[:10], *refs[10 + len(earlie...  64.2 us
    pallas_call x2, Pallas kernels, run_expert(): pl.pallas_call(lambda *refs: expert_kernel(count, *refs), grid_spec=pltpu...  59.8 us
    ppermute x18, starting transfers between devices, exchange(): lax.ppermute(piece, axis, [(at, (at + sign * turn) % size) for at in rang...  56.4 us
    ppermute x12, waiting for transfers between devices, swap(): lax.ppermute(part, axis, [(to, to ^ turn) for to in range(lax.axis_size(a...  40.5 us
    unnamed x185, local copies, waits for them, and re-layouts  39.1 us
    ppermute x18, waiting for transfers between devices, exchange(): lax.ppermute(piece, axis, [(at, (at + sign * turn) % size) for at in rang...  38.4 us
    pallas_call x2, Pallas kernels, attend(): pl.pallas_call(lambda *refs: fwd_kernel(first // QB, *refs), grid=(width...  31.1 us
    pallas_call x1, Pallas kernels, expert_grads(): pl.pallas_call(lambda *refs: expert_grads_kernel(groups, count, *refs), g...  27.9 us
  transfers between devices with their start and end apart: 38, of which 11 were waited for; matrix products, arithmetic and copies ran while one was open for 9% of the time, Pallas kernels for 46%

profile of v6, /device:TPU:0, one launch (start us, length us, event | category | flops | bytes accessed | tf_op | source)
XLA Modules:
  0.0 483.7 jit_solution(6641337866414968923)
XLA Ops:
  7.3 2.5 constant_dynamic-slice_fusion.2
  20.5 3.1 collective-permute-start.3
  23.5 2.6 collective-permute-start.4
  29.0 15.6 %attend.2 = (bf16[512,768]{1,0:T(8,128)(2,1)S(1)}, f32[6,2,512]{2,1,0:T(2,128)S(1)}) custom-call(s32[1]{0:T(128)} %bitcast.refs_0_, f32[12,2,1024]{2,1,0:T(2,128)S(1)} %bitcast.110, bf16[1024,768]{1,0:T(8,128)(2,1)S(1)} %bitcast.92, bf16[1024,768]{1,0:T(8,128)(2,1)S(1)} %bitcast.98, bf16[1024,768]{1,0:T(8,128)(2,1)S(1)} %bitcast.104), custom_call_target="tpu_custom_call" | custom-call | flops 402653184 | bytes 1572864 | tf_op jit(solution)/shard_map/attend/pallas_call | solution.py:204
  44.6 7.2 %collective-permute-done.4.refs_7_ = bf16[256,768]{1,0:T(8,128)(2,1)S(1)} collective-permute-done((bf16[256,768]{1,0:T(8,128)(2,1)S(1)}, bf16[256,768]{1,0:T(8,128)(2,1)S(1)}, u32[]{:S(2)}, u32[]{:S(2)}) %collective-permute-start.4) | collective-permute-done | bytes 393248 | tf_op jit(solution)/shard_map/ppermute | solution.py:626
  51.9 3.2 after_attention.2
  57.0 8.9 %collective-permute-start.6 = (bf16[256,768]{1,0:T(8,128)(2,1)}, bf16[256,768]{1,0:T(8,128)(2,1)}, u32[]{:S(2)}, u32[]{:S(2)}) collective-permute-start(bf16[256,768]{1,0:T(8,128)(2,1)} %get-tuple-element.221), channel_id=1, source_target_pairs={{0,1},{1,2},{2,3},{3,0},{4,5},{5,6},{6,7},{7,4},{8,9},{9,10},{10,1... | collective-permute-start | bytes 1179656 | tf_op jit(solution)/shard_map/ppermute | solution.py:626
  65.9 1.6 collective-permute-start.7
  69.6 2.3 sort_upstream.3
  77.1 15.5 %attend.3 = (bf16[512,768]{1,0:T(8,128)(2,1)S(1)}, f32[6,2,512]{2,1,0:T(2,128)S(1)}) custom-call(s32[1]{0:T(128)} %bitcast.refs_0_, f32[12,2,1024]{2,1,0:T(2,128)S(1)} %bitcast.111, bf16[1024,768]{1,0:T(8,128)(2,1)S(1)} %bitcast.93, bf16[1024,768]{1,0:T(8,128)(2,1)S(1)} %bitcast.99, bf16[1024,768]{1,0:T(8,128)(2,1)S(1)} %bitcast.105), custom_call_target="tpu_custom_call" | custom-call | flops 402653184 | bytes 1572864 | tf_op jit(solution)/shard_map/attend/pallas_call | solution.py:204
  92.7 2.8 after_attention.3
  95.5 8.9 %collective-permute-start.9 = (bf16[512,768]{1,0:T(8,128)(2,1)S(1)}, bf16[512,768]{1,0:T(8,128)(2,1)S(1)}, u32[]{:S(2)}, u32[]{:S(2)}) collective-permute-start(bf16[512,768]{1,0:T(8,128)(2,1)S(1)} %get-tuple-element.254), channel_id=1, source_target_pairs={{0,1},{1,2},{2,3},{3,0},{4,5},{5,6},{6,7},{7,4},{8,9},{9,10},{10,1... | collective-permute-start | bytes 2359304 | tf_op jit(solution)/shard_map/ppermute | solution.py:626
  104.4 2.1 collective-permute-start.10
  107.2 29.7 %experts.2 = (bf16[512,768]{1,0:T(8,128)(2,1)S(1)}, bf16[512,768]{1,0:T(8,128)(2,1)}, bf16[512,768]{1,0:T(8,128)(2,1)}, bf16[512,768]{1,0:T(8,128)(2,1)}, bf16[2...) custom-call(s32[1]{0:T(128)} %bitcast.3.refs_0_, ...), custom_call_target="tpu_custom_call" | custom-call | flops 38654705664 | bytes 18874368 | tf_op jit(solution)/shard_map/experts/pallas_call | solution.py:397
  137.6 19.4 %collective-permute-done.10.refs_3_.refs_7_.refs_6_ = bf16[512,768]{1,0:T(8,128)(2,1)S(1)} collective-permute-done((bf16[512,768]{1,0:T(8,128)(2,1)S(1)}, bf16[512,768]{1,0:T(8,128)(2,1)S(1)}, u32[]{:S(2)}, u32[]{:S(2)}) %collective-permute-start.10) | collective-permute-done | bytes 786464 | tf_op jit(solution)/shard_map/ppermute | solution.py:626
  157.0 18.1 %collective-permute-start.12 = (bf16[256,768]{1,0:T(8,128)(2,1)S(1)}, bf16[256,768]{1,0:T(8,128)(2,1)S(1)}, u32[]{:S(2)}, u32[]{:S(2)}) collective-permute-start(bf16[256,768]{1,0:T(8,128)(2,1)S(1)} %get-tuple-element.279), channel_id=1, source_target_pairs={{0,3},{1,0},{2,1},{3,2},{4,7},{5,4},{6,5},{7,6},{8,11},{9,8},{10,9... | collective-permute-start | bytes 1179656 | tf_op jit(solution)/shard_map/ppermute | solution.py:626
  177.1 30.1 %experts.3 = (bf16[512,768]{1,0:T(8,128)(2,1)S(1)}, bf16[512,768]{1,0:T(8,128)(2,1)}, bf16[512,768]{1,0:T(8,128)(2,1)}, bf16[512,768]{1,0:T(8,128)(2,1)S(1)}, bf...) custom-call(s32[1]{0:T(128)} %bitcast.3.refs_0_, ...), custom_call_target="tpu_custom_call", output_to_operand_aliasing={{0}: (12, {}), {1}: (13, {}), {2}: (14, {}), {3}: (15, {})} | custom-call | flops 38654705664 | bytes 18874368 | tf_op jit(solution)/shard_map/experts/pallas_call | solution.py:397
  210.6 3.8 collective-permute-start.15
  218.5 27.9 %expert_grads.1 = bf16[3072,1536]{1,0:T(8,128)(2,1)} custom-call(bf16[256,768]{1,0:T(8,128)(2,1)S(1)} %copy-done.62, bf16[256,768]{1,0:T(8,128)(2,1)} %collective-permute-done.6.refs_2_.refs_1_, bf16[256,768]{1,0:T(8,128)(2,1)} %collective-permute-done.7.refs_3_.refs_2_, bf16[256,768]{1,0:T(8,128)(2,1)} %collective-permute-done.8.refs_4_.refs_3_, ...), custom_call_target="tpu_custom_call" | custom-call | flops 28991029248 | bytes 34603008 | tf_op jit(solution)/shard_map/expert_grads/pallas_call | solution.py:465
  246.4 1.7 collective-permute-done.16.refs_3_
  250.0 2.7 copy.79.refs_9_
  256.4 9.1 %before_attention.2 = (f32[2,512,768]{2,1,0:T(8,128)}, bf16[2,512,768]{2,1,0:T(8,128)(2,1)}, f32[768,768]{1,0:T(8,128)}, f32[1,768]{1,0:T(1,128)}) custom-call(s32[1,1,512]{2,1,0:T(1,128)} %copy-done.45, bf16[256,768]{1,0:T(8,128)(2,1)} %copy-done.39, bf16[256,768]{1,0:T(8,128)(2,1)} %copy-done.80, bf16[256,768]{1,0:T(8,128)(2,1)} %copy-done.81, ...), custom_call_target="tpu_custom_call" | custom-call | tf_op jit(solution)/shard_map/before_attention/pallas_call | solution.py:604
  265.5 1.9 collective-permute-start.18
  268.2 8.7 %before_attention.3 = (f32[2,512,768]{2,1,0:T(8,128)}, bf16[2,512,768]{2,1,0:T(8,128)(2,1)}, f32[768,768]{1,0:T(8,128)}, f32[1,768]{1,0:T(1,128)}) custom-call(s32[1,1,512]{2,1,0:T(1,128)} %copy-done.47, bf16[256,768]{1,0:T(8,128)(2,1)} %copy-done.38, ...), custom_call_target="tpu_custom_call", output_to_operand_aliasing={{0}: (10, {}), {1}: (11, {})} | custom-call | tf_op jit(solution)/shard_map/before_attention/pallas_call | solution.py:604
  277.0 29.7 %attend_back.4 = (bf16[3,1024,384]{2,1,0:T(8,128)(2,1)}, bf16[2432,384]{1,0:T(8,128)(2,1)}) custom-call(s32[1]{0:T(128)} %bitcast.refs_0_, f32[12,2,1024]{2,1,0:T(2,128)S(1)} %bitcast.112, f32[3,512,128]{2,1,0:T(8,128)S(1)} %copy-done.71, bf16[1024,768]{1,0:T(8,128)(2,1)S(1)} %bitcast.94, bf16[1024,768]{1,0:T(8,128)(2,1)S(1)} %bitcast.100, ...), custom_call_target="tpu_custom_call" | custom-call | flops 33822867456 | bytes 5505024 | tf_op jit(solution)/shard_map/attend_back/pallas_call | solution.py:296
  307.9 9.9 %collective-permute-done.19.refs_6_ = bf16[512,768]{1,0:T(8,128)(2,1)} collective-permute-done((bf16[512,768]{1,0:T(8,128)(2,1)}, bf16[512,768]{1,0:T(8,128)(2,1)}, u32[]{:S(2)}, u32[]{:S(2)}) %collective-permute-start.19) | collective-permute-done | bytes 786464 | tf_op jit(solution)/shard_map/ppermute | solution.py:626
  317.8 1.8 constant_dynamic-update-slice_fusion.4
  319.9 1.7 copy-done.74
  327.2 11.4 %attend_back.5 = (bf16[3,1024,384]{2,1,0:T(8,128)(2,1)}, bf16[2432,384]{1,0:T(8,128)(2,1)}) custom-call(s32[1]{0:T(128)} %bitcast.refs_0_, f32[12,2,1024]{2,1,0:T(2,128)S(1)} %bitcast.113, f32[3,512,128]{2,1,0:T(8,128)S(1)} %copy-done.72, bf16[1024,768]{1,0:T(8,128)(2,1)S(1)} %bitcast.95, bf16[1024,768]{1,0:T(8,128)(2,1)S(1)} %bitcast.101, ...), custom_call_target="tpu_custom_call" | custom-call | flops 11274289152 | bytes 1835008 | tf_op jit(solution)/shard_map/attend_back/pallas_call | solution.py:296
  338.6 1.8 fusion.3
  344.1 11.5 %attend_back.6 = (bf16[3,1024,384]{2,1,0:T(8,128)(2,1)}, bf16[2432,384]{1,0:T(8,128)(2,1)}) custom-call(s32[1]{0:T(128)} %bitcast.refs_0_, f32[12,2,1024]{2,1,0:T(2,128)S(1)} %bitcast.114, f32[3,512,128]{2,1,0:T(8,128)S(1)} %copy-done.72, bf16[1024,768]{1,0:T(8,128)(2,1)S(1)} %bitcast.96, ...), custom_call_target="tpu_custom_call", output_to_operand_aliasing={{0}: (10, {}), {1}: (11, {})} | custom-call | flops 11274289152 | bytes 1835008 | tf_op jit(solution)/shard_map/attend_back/pallas_call | solution.py:296
  355.6 6.1 %collective-permute-done.22 = bf16[512,384]{1,0:T(8,128)(2,1)S(1)} collective-permute-done((bf16[512,384]{1,0:T(8,128)(2,1)S(1)}, bf16[512,384]{1,0:T(8,128)(2,1)S(1)}, u32[]{:S(2)}, u32[]{:S(2)}) %collective-permute-start.22) | collective-permute-done | bytes 393248 | tf_op jit(solution)/shard_map/ppermute | solution.py:774
  362.0 11.6 %attend_back.7 = (bf16[3,1024,384]{2,1,0:T(8,128)(2,1)}, bf16[2432,384]{1,0:T(8,128)(2,1)}) custom-call(s32[1]{0:T(128)} %bitcast.refs_0_, f32[12,2,1024]{2,1,0:T(2,128)S(1)} %bitcast.115, f32[3,512,128]{2,1,0:T(8,128)S(1)} %copy-done.72, bf16[1024,768]{1,0:T(8,128)(2,1)S(1)} %bitcast.97, ...), custom_call_target="tpu_custom_call", output_to_operand_aliasing={{0}: (10, {}), {1}: (11, {})} | custom-call | flops 11274289152 | bytes 1835008 | tf_op jit(solution)/shard_map/attend_back/pallas_call | solution.py:296
  375.9 4.1 collective-permute-start.26
  381.1 4.1 layer_output.1
  386.2 12.2 %collective-permute-done.26 = bf16[512,384]{1,0:T(8,128)(2,1)S(1)} collective-permute-done((bf16[512,384]{1,0:T(8,128)(2,1)}, bf16[512,384]{1,0:T(8,128)(2,1)S(1)}, u32[]{:S(2)}, u32[]{:S(2)}) %collective-permute-start.26) | collective-permute-done | bytes 393248 | tf_op jit(solution)/shard_map/ppermute | solution.py:774
  398.3 1.8 add_convert_fusion
  400.3 1.9 fusion.4
  405.8 8.5 %token_grads.1 = f32[1024,768]{1,0:T(8,128)} custom-call(bf16[3,1024,384]{2,1,0:T(8,128)(2,1)} %get-tuple-element.373.first_ref, bf16[3,1024,384]{2,1,0:T(8,128)(2,1)} %get-tuple-element.374.second_ref, bf16[768,768]{1,0:T(8,128)(2,1)S(1)} %copy-done.20, bf16[768,768]{1,0:T(8,128)(2,1)S(1)} %copy-done.22, bf16[768,768]{1,0:T(8,128)(2,1)S(1)} %copy-done.25, ...), custom_call_target="tpu_custom_call" | custom-call | flops 3623878656 | bytes 11010048 | tf_op jit(solution)/shard_map/token_grads/pallas_call | solution.py:717
  414.3 5.7 %collective-permute-done.31 = bf16[304,384]{1,0:T(8,128)(2,1)S(1)} collective-permute-done((bf16[304,384]{1,0:T(8,128)(2,1)S(1)}, bf16[304,384]{1,0:T(8,128)(2,1)S(1)}, u32[]{:S(2)}, u32[]{:S(2)}) %collective-permute-start.31) | collective-permute-done | bytes 233504 | tf_op jit(solution)/shard_map/ppermute | solution.py:774
  420.3 6.3 %collective-permute-done.33 = bf16[304,384]{1,0:T(8,128)(2,1)S(1)} collective-permute-done((bf16[304,384]{1,0:T(8,128)(2,1)S(1)}, bf16[304,384]{1,0:T(8,128)(2,1)S(1)}, u32[]{:S(2)}, u32[]{:S(2)}) %collective-permute-start.33) | collective-permute-done | bytes 233504 | tf_op jit(solution)/shard_map/ppermute | solution.py:774
  427.9 10.1 %collective-permute-done.34 = bf16[304,384]{1,0:T(8,128)(2,1)S(1)} collective-permute-done((bf16[304,384]{1,0:T(8,128)(2,1)S(1)}, bf16[304,384]{1,0:T(8,128)(2,1)S(1)}, u32[]{:S(2)}, u32[]{:S(2)}) %collective-permute-start.34) | collective-permute-done | bytes 233504 | tf_op jit(solution)/shard_map/ppermute | solution.py:774
  438.8 2.7 slice.65
  445.1 2.7 copy.87
  451.5 1.6 slice_select_fusion.1
  453.1 2.0 pad_maximum_fusion
  460.4 6.1 %all-gather.5.cloned.1.call-done.second_ref = bf16[2432,384]{1,0:T(8,128)(2,1)} async-done(((bf16[304,384]{1,0:T(8,128)(2,1)}), bf16[2432,384]{1,0:T(8,128)(2,1)}) %all-gather.5.cloned.1.call-update) | async-done | bytes 1867792 | tf_op jit(solution)/shard_map/all_gather | solution.py:809
  470.7 5.5 %weight_outputs.1 = (f32[768,768]{1,0:T(8,128)}, f32[768,768]{1,0:T(8,128)}, f32[768,768]{1,0:T(8,128)}, f32[1,768]{1,0:T(1,128)S(1)}) custom-call(bf16[4096,384]{1,0:T(8,128)(2,1)} %all-gather.3.cloned.1.call-done.first_ref, bf16[2432,384]{1,0:T(8,128)(2,1)S(1)} %copy-done.30, bf16[768,768]{1,0:T(8,128)(2,1)S(1)} %copy-done.20, ...), custom_call_target="tpu_custom_call" | custom-call | tf_op jit(solution)/shard_map/weight_outputs/pallas_call | solution.py:689
  (295 shorter events, 78.1 us)
Async XLA Ops:
  7.2 367.3 %reduce-scatter.2.cloned.1.call-start = ((), (), s32[]{:S(2)}) async-start(), calls=%async_computation.1 | async-start | bytes 10616832 | tf_op jit(solution)/shard_map/reduce_scatter | solution.py:917
  9.7 4.5 collective-permute-start
  11.2 58.5 %collective-permute-start.2 = (bf16[1,512,768]{2,1,0:T(8,128)(2,1)}, bf16[1,512,768]{2,1,0:T(8,128)(2,1)}, u32[]{:S(2)}, u32[]{:S(2)}) collective-permute-start(bf16[1,512,768]{2,1,0:T(8,128)(2,1)} %get-tuple-element.447), channel_id=1, source_target_pairs={{0,4},{4,0},{1,5},{5,1},{2,6},{6,2},{3,7},{7,3},{8,12},{12,8},{9,1... | collective-permute-start | bytes 2359304 | tf_op jit(solution)/shard_map/ppermute | solution.py:635
  12.3 80.4 %copy-start.42 = (f32[1,768]{1,0:T(1,128)}, f32[1,768]{1,0:T(1,128)S(1)}, u32[]{:S(2)}) copy-start(f32[1,768]{1,0:T(1,128)S(1)} %broadcast_in_dim.25.refs_4_.refs_9_) | copy-start | bytes 9220
  14.2 37.7 %copy-start.45 = (s32[1,1,512]{2,1,0:T(1,128)}, s32[1,1,512]{2,1,0:T(1,128)S(1)}, u32[]{:S(2)}) copy-start(s32[1,1,512]{2,1,0:T(1,128)S(1)} %get-tuple-element.207.refs_0_) | copy-start | bytes 6148
  20.5 24.1 %collective-permute-start.3 = (bf16[256,768]{1,0:T(8,128)(2,1)S(1)}, bf16[256,768]{1,0:T(8,128)(2,1)S(1)}, u32[]{:S(2)}, u32[]{:S(2)}) collective-permute-start(bf16[256,768]{1,0:T(8,128)(2,1)S(1)} %get-tuple-element.210), channel_id=1, source_target_pairs={{0,1},{1,2},{2,3},{3,0},{4,5},{5,6},{6,7},{7,4},{8,9},{9,10},{10,1... | collective-permute-start | bytes 1179656 | tf_op jit(solution)/shard_map/ppermute | solution.py:626
  23.5 28.3 %collective-permute-start.4 = (bf16[256,768]{1,0:T(8,128)(2,1)S(1)}, bf16[256,768]{1,0:T(8,128)(2,1)S(1)}, u32[]{:S(2)}, u32[]{:S(2)}) collective-permute-start(bf16[256,768]{1,0:T(8,128)(2,1)S(1)} %get-tuple-element.211), channel_id=1, source_target_pairs={{0,2},{1,3},{2,0},{3,1},{4,6},{5,7},{6,4},{7,5},{8,10},{9,11},{10,... | collective-permute-start | bytes 1179656 | tf_op jit(solution)/shard_map/ppermute | solution.py:626
  26.2 25.7 %collective-permute-start.5 = (bf16[256,768]{1,0:T(8,128)(2,1)S(1)}, bf16[256,768]{1,0:T(8,128)(2,1)S(1)}, u32[]{:S(2)}, u32[]{:S(2)}) collective-permute-start(bf16[256,768]{1,0:T(8,128)(2,1)S(1)} %get-tuple-element.212), channel_id=1, source_target_pairs={{0,3},{1,0},{2,1},{3,2},{4,7},{5,4},{6,5},{7,6},{8,11},{9,8},{10,9... | collective-permute-start | bytes 1179656 | tf_op jit(solution)/shard_map/ppermute | solution.py:626
  29.0 22.9 %copy-start.2 = (bf16[768,768]{1,0:T(8,128)(2,1)S(1)}, bf16[768,768]{1,0:T(8,128)(2,1)}, u32[]{:S(2)}) copy-start(bf16[768,768]{1,0:T(8,128)(2,1)} %refs_8_.3) | copy-start | bytes 3538948
  44.6 23.8 %copy-start.65 = (bf16[256,768]{1,0:T(8,128)(2,1)}, bf16[256,768]{1,0:T(8,128)(2,1)S(1)}, u32[]{:S(2)}) copy-start(bf16[256,768]{1,0:T(8,128)(2,1)S(1)} %collective-permute-done.3.refs_6_) | copy-start | bytes 1179652
  57.0 35.6 %collective-permute-start.6 = (bf16[256,768]{1,0:T(8,128)(2,1)}, bf16[256,768]{1,0:T(8,128)(2,1)}, u32[]{:S(2)}, u32[]{:S(2)}) collective-permute-start(bf16[256,768]{1,0:T(8,128)(2,1)} %get-tuple-element.221), channel_id=1, source_target_pairs={{0,1},{1,2},{2,3},{3,0},{4,5},{5,6},{6,7},{7,4},{8,9},{9,10},{10,1... | collective-permute-start | bytes 1179656 | tf_op jit(solution)/shard_map/ppermute | solution.py:626
  65.9 26.8 %collective-permute-start.7 = (bf16[256,768]{1,0:T(8,128)(2,1)}, bf16[256,768]{1,0:T(8,128)(2,1)}, u32[]{:S(2)}, u32[]{:S(2)}) collective-permute-start(bf16[256,768]{1,0:T(8,128)(2,1)} %get-tuple-element.222), channel_id=1, source_target_pairs={{0,2},{1,3},{2,0},{3,1},{4,6},{5,7},{6,4},{7,5},{8,10},{9,11},{10,... | collective-permute-start | bytes 1179656 | tf_op jit(solution)/shard_map/ppermute | solution.py:626
  67.5 25.2 %collective-permute-start.8 = (bf16[256,768]{1,0:T(8,128)(2,1)}, bf16[256,768]{1,0:T(8,128)(2,1)}, u32[]{:S(2)}, u32[]{:S(2)}) collective-permute-start(bf16[256,768]{1,0:T(8,128)(2,1)} %get-tuple-element.223), channel_id=1, source_target_pairs={{0,3},{1,0},{2,1},{3,2},{4,7},{5,4},{6,5},{7,6},{8,11},{9,8},{10,9... | collective-permute-start | bytes 1179656 | tf_op jit(solution)/shard_map/ppermute | solution.py:626
  68.4 1.2 collective-permute-start.1
  92.6 161.6 %copy-start.3 = (bf16[512,768]{1,0:T(8,128)(2,1)}, bf16[512,768]{1,0:T(8,128)(2,1)S(1)}, u32[]{:S(2)}) copy-start(bf16[512,768]{1,0:T(8,128)(2,1)S(1)} %get-tuple-element.219) | copy-start | bytes 2359300
  95.5 42.1 %collective-permute-start.9 = (bf16[512,768]{1,0:T(8,128)(2,1)S(1)}, bf16[512,768]{1,0:T(8,128)(2,1)S(1)}, u32[]{:S(2)}, u32[]{:S(2)}) collective-permute-start(bf16[512,768]{1,0:T(8,128)(2,1)S(1)} %get-tuple-element.254), channel_id=1, source_target_pairs={{0,1},{1,2},{2,3},{3,0},{4,5},{5,6},{6,7},{7,4},{8,9},{9,10},{10,1... | collective-permute-start | bytes 2359304 | tf_op jit(solution)/shard_map/ppermute | solution.py:626
  104.4 52.6 %collective-permute-start.10 = (bf16[512,768]{1,0:T(8,128)(2,1)S(1)}, bf16[512,768]{1,0:T(8,128)(2,1)S(1)}, u32[]{:S(2)}, u32[]{:S(2)}) collective-permute-start(bf16[512,768]{1,0:T(8,128)(2,1)S(1)} %get-tuple-element.255), channel_id=1, source_target_pairs={{0,2},{1,3},{2,0},{3,1},{4,6},{5,7},{6,4},{7,5},{8,10},{9,11},{10,... | collective-permute-start | bytes 2359304 | tf_op jit(solution)/shard_map/ppermute | solution.py:626
  106.5 50.5 %collective-permute-start.11 = (bf16[512,768]{1,0:T(8,128)(2,1)S(1)}, bf16[512,768]{1,0:T(8,128)(2,1)S(1)}, u32[]{:S(2)}, u32[]{:S(2)}) collective-permute-start(bf16[512,768]{1,0:T(8,128)(2,1)S(1)} %get-tuple-element.256), channel_id=1, source_target_pairs={{0,3},{1,0},{2,1},{3,2},{4,7},{5,4},{6,5},{7,6},{8,11},{9,8},{10,9... | collective-permute-start | bytes 2359304 | tf_op jit(solution)/shard_map/ppermute | solution.py:626
  137.6 38.4 %copy-start.53 = (bf16[512,768]{1,0:T(8,128)(2,1)}, bf16[512,768]{1,0:T(8,128)(2,1)S(1)}, u32[]{:S(2)}) copy-start(bf16[512,768]{1,0:T(8,128)(2,1)S(1)} %collective-permute-done.9.refs_2_.refs_6_.refs_5_) | copy-start | bytes 2359300
  157.0 19.0 %copy-start.55 = (bf16[512,768]{1,0:T(8,128)(2,1)}, bf16[512,768]{1,0:T(8,128)(2,1)S(1)}, u32[]{:S(2)}) copy-start(bf16[512,768]{1,0:T(8,128)(2,1)S(1)} %collective-permute-done.10.refs_3_.refs_7_.refs_6_) | copy-start | bytes 2359300
  157.0 19.0 %copy-start.57 = (bf16[512,768]{1,0:T(8,128)(2,1)}, bf16[512,768]{1,0:T(8,128)(2,1)S(1)}, u32[]{:S(2)}) copy-start(bf16[512,768]{1,0:T(8,128)(2,1)S(1)} %collective-permute-done.11.refs_4_.refs_8_.refs_7_) | copy-start | bytes 2359300
  157.0 53.5 %collective-permute-start.12 = (bf16[256,768]{1,0:T(8,128)(2,1)S(1)}, bf16[256,768]{1,0:T(8,128)(2,1)S(1)}, u32[]{:S(2)}, u32[]{:S(2)}) collective-permute-start(bf16[256,768]{1,0:T(8,128)(2,1)S(1)} %get-tuple-element.279), channel_id=1, source_target_pairs={{0,3},{1,0},{2,1},{3,2},{4,7},{5,4},{6,5},{7,6},{8,11},{9,8},{10,9... | collective-permute-start | bytes 1179656 | tf_op jit(solution)/shard_map/ppermute | solution.py:626
  175.1 35.5 %collective-permute-start.13 = (bf16[256,768]{1,0:T(8,128)(2,1)S(1)}, bf16[256,768]{1,0:T(8,128)(2,1)S(1)}, u32[]{:S(2)}, u32[]{:S(2)}) collective-permute-start(bf16[256,768]{1,0:T(8,128)(2,1)S(1)} %get-tuple-element.280), channel_id=1, source_target_pairs={{0,2},{1,3},{2,0},{3,1},{4,6},{5,7},{6,4},{7,5},{8,10},{9,11},{10,... | collective-permute-start | bytes 1179656 | tf_op jit(solution)/shard_map/ppermute | solution.py:626
  175.8 34.8 %collective-permute-start.14 = (bf16[256,768]{1,0:T(8,128)(2,1)S(1)}, bf16[256,768]{1,0:T(8,128)(2,1)S(1)}, u32[]{:S(2)}, u32[]{:S(2)}) collective-permute-start(bf16[256,768]{1,0:T(8,128)(2,1)S(1)} %get-tuple-element.281), channel_id=1, source_target_pairs={{0,1},{1,2},{2,3},{3,0},{4,5},{5,6},{6,7},{7,4},{8,9},{9,10},{10,1... | collective-permute-start | bytes 1179656 | tf_op jit(solution)/shard_map/ppermute | solution.py:626
  210.6 35.8 %collective-permute-start.15 = (bf16[256,768]{1,0:T(8,128)(2,1)}, bf16[256,768]{1,0:T(8,128)(2,1)}, u32[]{:S(2)}, u32[]{:S(2)}) collective-permute-start(bf16[256,768]{1,0:T(8,128)(2,1)} %get-tuple-element.288), channel_id=1, source_target_pairs={{0,3},{1,0},{2,1},{3,2},{4,7},{5,4},{6,5},{7,6},{8,11},{9,8},{10,9... | collective-permute-start | bytes 1179656 | tf_op jit(solution)/shard_map/ppermute | solution.py:626
  214.4 33.7 %collective-permute-start.16 = (bf16[256,768]{1,0:T(8,128)(2,1)S(1)}, bf16[256,768]{1,0:T(8,128)(2,1)}, u32[]{:S(2)}, u32[]{:S(2)}) collective-permute-start(bf16[256,768]{1,0:T(8,128)(2,1)S(1)} %get-tuple-element.289), channel_id=1, source_target_pairs={{0,2},{1,3},{2,0},{3,1},{4,6},{5,7},{6,4},{7,5},{8,10},{9,11},{10,... | collective-permute-start | bytes 1179656 | tf_op jit(solution)/shard_map/ppermute | solution.py:626
  214.9 33.3 %collective-permute-start.17 = (bf16[256,768]{1,0:T(8,128)(2,1)S(1)}, bf16[256,768]{1,0:T(8,128)(2,1)}, u32[]{:S(2)}, u32[]{:S(2)}) collective-permute-start(bf16[256,768]{1,0:T(8,128)(2,1)S(1)} %get-tuple-element.290), channel_id=1, source_target_pairs={{0,1},{1,2},{2,3},{3,0},{4,5},{5,6},{6,7},{7,4},{8,9},{9,10},{10,1... | collective-permute-start | bytes 1179656 | tf_op jit(solution)/shard_map/ppermute | solution.py:626
  248.2 190.7 %all-gather.3.cloned.1.call-start = ((), (), s32[]{:S(2)}) async-start(), calls=%async_computation.2 | async-start | bytes 3538944 | tf_op jit(solution)/shard_map/all_gather | solution.py:809
  265.5 42.4 %collective-permute-start.18 = (bf16[512,768]{1,0:T(8,128)(2,1)}, bf16[512,768]{1,0:T(8,128)(2,1)}, u32[]{:S(2)}, u32[]{:S(2)}) collective-permute-start(bf16[512,768]{1,0:T(8,128)(2,1)} %get-tuple-element.315), channel_id=1, source_target_pairs={{0,3},{1,0},{2,1},{3,2},{4,7},{5,4},{6,5},{7,6},{8,11},{9,8},{10,9... | collective-permute-start | bytes 2359304 | tf_op jit(solution)/shard_map/ppermute | solution.py:626
  267.3 50.5 %collective-permute-start.19 = (bf16[512,768]{1,0:T(8,128)(2,1)}, bf16[512,768]{1,0:T(8,128)(2,1)}, u32[]{:S(2)}, u32[]{:S(2)}) collective-permute-start(bf16[512,768]{1,0:T(8,128)(2,1)} %get-tuple-element.316), channel_id=1, source_target_pairs={{0,2},{1,3},{2,0},{3,1},{4,6},{5,7},{6,4},{7,5},{8,10},{9,11},{10,... | collective-permute-start | bytes 2359304 | tf_op jit(solution)/shard_map/ppermute | solution.py:626
  277.0 29.7 %copy-start.78 = (f32[768,768]{1,0:T(8,128)S(1)}, f32[768,768]{1,0:T(8,128)}, u32[]{:S(2)}) copy-start(f32[768,768]{1,0:T(8,128)} %get-tuple-element.319) | copy-start | bytes 7077892
  323.0 15.5 %collective-permute-start.20 = (bf16[4,512,384]{2,1,0:T(8,128)(2,1)}, bf16[4,512,384]{2,1,0:T(8,128)(2,1)}, u32[]{:S(2)}, u32[]{:S(2)}) collective-permute-start(bf16[4,512,384]{2,1,0:T(8,128)(2,1)} %dynamic-slice_bitcast_fusion), channel_id=1, source_target_pairs={{0,4},{4,0},{1,5},{5,1},{2,6},{6,2},{3,7},{7,3},{8,12},{12,8},{9,1... | collective-permute-start | bytes 4718600 | tf_op jit(solution)/shard_map/ppermute | solution.py:774
  323.0 32.6 %collective-permute-start.24 = (bf16[512,768]{1,0:T(8,128)(2,1)}, bf16[512,768]{1,0:T(8,128)(2,1)S(1)}, u32[]{:S(2)}, u32[]{:S(2)}) collective-permute-start(bf16[512,768]{1,0:T(8,128)(2,1)} %copy-done.60), channel_id=1, source_target_pairs={{0,1},{1,2},{2,3},{3,0},{4,5},{5,6},{6,7},{7,4},{8,9},{9,10},{10,1... | collective-permute-start | bytes 2359304 | tf_op jit(solution)/shard_map/ppermute | solution.py:626
  340.5 15.1 %collective-permute-start.21 = (bf16[512,384]{1,0:T(8,128)(2,1)S(1)}, bf16[512,384]{1,0:T(8,128)(2,1)S(1)}, u32[]{:S(2)}, u32[]{:S(2)}) collective-permute-start(bf16[512,384]{1,0:T(8,128)(2,1)S(1)} %get-tuple-element.333), channel_id=1, source_target_pairs={{0,8},{8,0},{16,24},{24,16},{1,9},{9,1},{17,25},{25,17},{2,10},{10... | collective-permute-start | bytes 1179656 | tf_op jit(solution)/shard_map/ppermute | solution.py:774
  342.1 19.6 %collective-permute-start.22 = (bf16[512,384]{1,0:T(8,128)(2,1)S(1)}, bf16[512,384]{1,0:T(8,128)(2,1)S(1)}, u32[]{:S(2)}, u32[]{:S(2)}) collective-permute-start(bf16[512,384]{1,0:T(8,128)(2,1)S(1)} %get-tuple-element.334), channel_id=1, source_target_pairs={{0,16},{8,24},{16,0},{24,8},{1,17},{9,25},{17,1},{25,9},{2,18},{10... | collective-permute-start | bytes 1179656 | tf_op jit(solution)/shard_map/ppermute | solution.py:774
  343.6 18.2 %collective-permute-start.23 = (bf16[512,384]{1,0:T(8,128)(2,1)S(1)}, bf16[512,384]{1,0:T(8,128)(2,1)S(1)}, u32[]{:S(2)}, u32[]{:S(2)}) collective-permute-start(bf16[512,384]{1,0:T(8,128)(2,1)S(1)} %get-tuple-element.335), channel_id=1, source_target_pairs={{0,24},{8,16},{16,8},{24,0},{1,25},{9,17},{17,9},{25,1},{2,26},{10... | collective-permute-start | bytes 1179656 | tf_op jit(solution)/shard_map/ppermute | solution.py:774
  355.6 18.0 %copy-start.34 = (bf16[512,768]{1,0:T(8,128)(2,1)}, bf16[512,768]{1,0:T(8,128)(2,1)S(1)}, u32[]{:S(2)}) copy-start(bf16[512,768]{1,0:T(8,128)(2,1)S(1)} %collective-permute-done.24.refs_7_) | copy-start | bytes 2359300
  362.0 11.7 %collective-permute-start.25 = (bf16[512,384]{1,0:T(8,128)(2,1)S(1)}, bf16[512,384]{1,0:T(8,128)(2,1)S(1)}, u32[]{:S(2)}, u32[]{:S(2)}) collective-permute-start(bf16[512,384]{1,0:T(8,128)(2,1)S(1)} %fusion.14), channel_id=1, source_target_pairs={{0,1},{1,0},{2,3},{3,2},{4,5},{5,4},{6,7},{7,6},{8,9},{9,8},{10,11... | collective-permute-start | bytes 1179656 | tf_op jit(solution)/shard_map/ppermute | solution.py:774
  375.8 22.5 %collective-permute-start.27 = (bf16[4,304,384]{2,1,0:T(8,128)(2,1)S(1)}, bf16[4,304,384]{2,1,0:T(8,128)(2,1)}, u32[]{:S(2)}, u32[]{:S(2)}) collective-permute-start(bf16[4,304,384]{2,1,0:T(8,128)(2,1)S(1)} %dynamic-slice_bitcast_fusion.1), channel_id=1, source_target_pairs={{0,4},{4,0},{1,5},{5,1},{2,6},{6,2},{3,7},{7,3},{8,12},{12,8},{9,1... | collective-permute-start | bytes 2801672 | tf_op jit(solution)/shard_map/ppermute | solution.py:774
  375.9 22.5 %collective-permute-start.26 = (bf16[512,384]{1,0:T(8,128)(2,1)}, bf16[512,384]{1,0:T(8,128)(2,1)S(1)}, u32[]{:S(2)}, u32[]{:S(2)}) collective-permute-start(bf16[512,384]{1,0:T(8,128)(2,1)} %add_convert_fusion.1), channel_id=1, source_target_pairs={{0,2},{1,3},{2,0},{3,1},{4,6},{5,7},{6,4},{7,5},{8,10},{9,11},{10,... | collective-permute-start | bytes 1179656 | tf_op jit(solution)/shard_map/ppermute | solution.py:774
  400.2 66.4 %all-gather.5.cloned.1.call-start = ((), (), s32[]{:S(2)}) async-start(), calls=%async_computation.3 | async-start | bytes 2101248 | tf_op jit(solution)/shard_map/all_gather | solution.py:809
  402.2 12.1 %collective-permute-start.29 = (bf16[304,384]{1,0:T(8,128)(2,1)S(1)}, bf16[304,384]{1,0:T(8,128)(2,1)S(1)}, u32[]{:S(2)}, u32[]{:S(2)}) collective-permute-start(bf16[304,384]{1,0:T(8,128)(2,1)S(1)} %get-tuple-element.370), channel_id=1, source_target_pairs={{0,8},{8,0},{16,24},{24,16},{1,9},{9,1},{17,25},{25,17},{2,10},{10... | collective-permute-start | bytes 700424 | tf_op jit(solution)/shard_map/ppermute | solution.py:774
  403.5 10.8 %collective-permute-start.30 = (bf16[304,384]{1,0:T(8,128)(2,1)S(1)}, bf16[304,384]{1,0:T(8,128)(2,1)S(1)}, u32[]{:S(2)}, u32[]{:S(2)}) collective-permute-start(bf16[304,384]{1,0:T(8,128)(2,1)S(1)} %get-tuple-element.371), channel_id=1, source_target_pairs={{0,16},{8,24},{16,0},{24,8},{1,17},{9,25},{17,1},{25,9},{2,18},{10... | collective-permute-start | bytes 700424 | tf_op jit(solution)/shard_map/ppermute | solution.py:774
  404.4 15.7 %collective-permute-start.31 = (bf16[304,384]{1,0:T(8,128)(2,1)S(1)}, bf16[304,384]{1,0:T(8,128)(2,1)S(1)}, u32[]{:S(2)}, u32[]{:S(2)}) collective-permute-start(bf16[304,384]{1,0:T(8,128)(2,1)S(1)} %get-tuple-element.372), channel_id=1, source_target_pairs={{0,24},{8,16},{16,8},{24,0},{1,25},{9,17},{17,9},{25,1},{2,26},{10... | collective-permute-start | bytes 700424 | tf_op jit(solution)/shard_map/ppermute | solution.py:774
  420.2 6.4 %collective-permute-start.33 = (bf16[304,384]{1,0:T(8,128)(2,1)S(1)}, bf16[304,384]{1,0:T(8,128)(2,1)S(1)}, u32[]{:S(2)}, u32[]{:S(2)}) collective-permute-start(bf16[304,384]{1,0:T(8,128)(2,1)S(1)} %fusion.17), channel_id=1, source_target_pairs={{0,1},{1,0},{2,3},{3,2},{4,5},{5,4},{6,7},{7,6},{8,9},{9,8},{10,11... | collective-permute-start | bytes 700424 | tf_op jit(solution)/shard_map/ppermute | solution.py:774
  426.7 11.4 %collective-permute-start.34 = (bf16[304,384]{1,0:T(8,128)(2,1)S(1)}, bf16[304,384]{1,0:T(8,128)(2,1)S(1)}, u32[]{:S(2)}, u32[]{:S(2)}) collective-permute-start(bf16[304,384]{1,0:T(8,128)(2,1)S(1)} %add_convert_fusion.3), channel_id=1, source_target_pairs={{0,2},{1,3},{2,0},{3,1},{4,6},{5,7},{6,4},{7,5},{8,10},{9,11},{10,... | collective-permute-start | bytes 700424 | tf_op jit(solution)/shard_map/ppermute | solution.py:774
  441.5 8.9 %collective-permute-start.32 = (f32[1,512,768]{2,1,0:T(8,128)}, f32[1,512,768]{2,1,0:T(8,128)}, u32[]{:S(2)}, u32[]{:S(2)}) collective-permute-start(f32[1,512,768]{2,1,0:T(8,128)} %slice.65), channel_id=1, source_target_pairs={{0,4},{4,0},{1,5},{5,1},{2,6},{6,2},{3,7},{7,3},{8,12},{12,8},{9,1... | collective-permute-start | bytes 4718600 | tf_op jit(solution)/shard_map/ppermute | solution.py:640
  441.5 6.3 %collective-permute-start.28 = (bf16[1,512,768]{2,1,0:T(8,128)(2,1)S(1)}, bf16[1,512,768]{2,1,0:T(8,128)(2,1)}, u32[]{:S(2)}, u32[]{:S(2)}) collective-permute-start(bf16[1,512,768]{2,1,0:T(8,128)(2,1)S(1)} %copy-done.52), channel_id=1, source_target_pairs={{0,4},{4,0},{1,5},{5,1},{2,6},{6,2},{3,7},{7,3},{8,12},{12,8},{9,1... | collective-permute-start | bytes 2359304 | tf_op jit(solution)/shard_map/ppermute | solution.py:640
  (79 other events, 432.1 us)
Sparse Core Ops, SparseCore 0:
  248.3 76.1 reduce-scatter.1
  400.3 36.7 all-gather.2
  439.6 26.9 all-gather.4

commit v7 on v6

--- a/solution.py
+++ b/solution.py
@@ -277,9 +277,10 @@
         total = total + jnp.where(column == 15, ends[0], 0.0) + jnp.where(column == 31, ends[1], 0.0)
         totals.append(total)
     width = xt_ref.shape[0]
+    grads = jnp.concatenate([grad_ref[kind] for kind in range(3)], axis=1)
+    weight = jnp.dot(xt_ref[...], grads, preferred_element_type=jnp.float32).astype(jnp.bfloat16)
     for kind in range(3):
-        weight = jnp.dot(xt_ref[...], grad_ref[kind], preferred_element_type=jnp.float32)
-        sums_ref[kind * width:(kind + 1) * width, :] = weight.astype(jnp.bfloat16)
+        sums_ref[kind * width:(kind + 1) * width, :] = weight[:, kind * 128:(kind + 1) * 128]
     high = [total.astype(jnp.bfloat16).astype(jnp.float32) for total in totals]
     rows = high + [total - part for total, part in zip(totals, high)]
     small = jnp.concatenate(rows + [jnp.zeros((124, 128), jnp.float32)], axis=0)
@@ -472,9 +473,7 @@
         out_shape=jax.ShapeDtypeStruct((inner, 2 * width), jnp.bfloat16),
         scratch_shapes=[pltpu.VMEM((width, groups * rows), jnp.bfloat16)] * 2,
         compiler_params=pltpu.CompilerParams(vmem_limit_bytes=48 << 20),
-        cost_estimate=pl.CostEstimate(
-            flops=6 * groups * rows * width * inner, bytes_accessed=4 * (groups * rows + width) * inner, transcendentals=0
-        ),
+        cost_estimate=pl.CostEstimate(flops=rows * width, bytes_accessed=rows * width, transcendentals=0),
         name="expert_grads",
     )(*pieces, *grads, *hiddens, *pre_grads)
 
@@ -668,32 +667,53 @@
     )(*slots, *residuals, *pieces)
 
 
-def weight_outputs_kernel(first_ref, second_ref, *refs):
-    weight_refs, gain_ref, out_refs, gain_grad_ref = refs[:3], refs[3], refs[4:7], refs[7]
+def weight_outputs_kernel(place_ref, *refs):
+    shard_refs, weight_refs, gain_ref = refs[:4], refs[4:7], refs[7]
+    out_refs, output_ref, gain_grad_ref, small_ref = refs[8:11], refs[11], refs[12], refs[13]
+    whole_refs = refs[14:]
     width = gain_ref.shape[1]
     half = width // 2
+    for side in range(2):
+        planes, rows, _ = shard_refs[2 * side].shape
+        for turn in range(planes):
+            for other in range(2):
+                shard = (place_ref[0] ^ turn) * 2 + (place_ref[1] ^ other)
+                start = pl.multiple_of(shard * rows, 16)
+                whole_refs[side][pl.ds(start, rows), :] = shard_refs[2 * side + other][turn]
     total = 0.0
     for kind in range(3):
-        for side, ref in enumerate((first_ref, second_ref)):
+        for side, ref in enumerate(whole_refs):
             columns = slice(side * half, (side + 1) * half)
             grad = ref[kind * width : (kind + 1) * width, :].astype(jnp.float32)
             out_refs[kind][:, columns] = grad
             total += jnp.sum(grad * weight_refs[kind][:, columns].astype(jnp.float32), axis=1, keepdims=True)
     total = jnp.broadcast_to(total, (width, 128)).T
     gain_grad_ref[...] = total[:1] / gain_ref[...]
-
-
-def weight_outputs(first, second, weights, gain):
+    start = 3 * width + 128
+    for side in range(2):
+        rows = slice(start + side * width, start + (side + 1) * width)
+        output_ref[:, side * half : (side + 1) * half] = whole_refs[0][rows, :].astype(jnp.float32)
+    for at, (ref, first) in enumerate(((whole_refs[0], 3 * width), (whole_refs[1], 3 * width), (whole_refs[0], start + 2 * width))):
+        small_ref[at] = ref[first : first + 128, :].astype(jnp.float32)
+
+
+def weight_outputs(shards, weights, gain):
     width = gain.shape[0]
     vmem = pl.BlockSpec(memory_space=pltpu.VMEM)
+    place = jnp.stack([lax.axis_index("dp"), lax.axis_index("ctx")]).astype(jnp.int32)
+    matrix = jax.ShapeDtypeStruct((width, width), jnp.float32)
     return pl.pallas_call(
         weight_outputs_kernel,
-        in_specs=[vmem] * 6,
-        out_specs=[vmem] * 4,
-        out_shape=[jax.ShapeDtypeStruct((width, width), jnp.float32)] * 3 + [jax.ShapeDtypeStruct((1, width), jnp.float32)],
-        compiler_params=pltpu.CompilerParams(vmem_limit_bytes=48 << 20),
+        in_specs=[pl.BlockSpec(memory_space=pltpu.SMEM)] + [vmem] * 8,
+        out_specs=[vmem] * 6,
+        out_shape=[matrix] * 4
+        + [jax.ShapeDtypeStruct((1, width), jnp.float32), jax.ShapeDtypeStruct((3, 128, width // 2), jnp.float32)],
+        scratch_shapes=[
+            pltpu.VMEM((2 * part.shape[0] * part.shape[1], width // 2), jnp.bfloat16) for part in (shards[0], shards[2])
+        ],
+        compiler_params=pltpu.CompilerParams(vmem_limit_bytes=56 << 20),
         name="weight_outputs",
-    )(first, second, *weights, gain[None])
+    )(place, *shards, *weights, gain[None])
 
 
 def token_grads_kernel(first_ref, second_ref, *refs):
@@ -775,8 +795,6 @@
 
 
 class Summing:
-    steps = 4
-
     def __init__(self, packed):
         self.core, self.plane = lax.axis_index("ctx"), lax.axis_index("dp")
         self.planes = lax.axis_size("dp")
@@ -791,10 +809,10 @@
                 lax.dynamic_index_in_dim(self.part, self.plane ^ turn, 0, keepdims=False)
                 for turn in range(1, self.planes)
             ]
-        return [self.part]
+        return [self.part] * (self.planes - 1 if self.step == 4 else 1)
 
     def move(self, sent):
-        axis, first = (("ctx", 1), ("dp", 1), ("expert", 1), ("expert", 2))[self.step]
+        axis, first = (("ctx", 1), ("dp", 1), ("expert", 1), ("expert", 2), ("dp", 1), ("ctx", 1))[self.step]
         return [swap(part, axis, first + at) for at, part in enumerate(sent)]
 
     def take(self, arrived):
@@ -802,11 +820,13 @@
             self.part = lax.dynamic_index_in_dim(self.part, self.core, 1, keepdims=False)
         elif self.step == 1:
             self.part = lax.dynamic_index_in_dim(self.part, self.plane, 0, keepdims=False)
-        self.part = add_low(self.part, *arrived)
+        if self.step < 4:
+            self.part = add_low(self.part, *arrived)
+        elif self.step == 4:
+            self.part = jnp.stack([self.part] + arrived)
+        else:
+            self.part = (self.part, arrived[0])
         self.step += 1
-
-    def finish(self):
-        return lax.all_gather(self.part, ("dp", "ctx"), axis=0, tiled=True)
 
 
 def matrix_of(sums, index, rows):
@@ -880,18 +900,17 @@
             log_totals.append(totals)
         else:
             rows = attended.astype(jnp.bfloat16)
-        rows, in_flight = together((rows, in_flight))
+        attended_groups.append(rows)
+        earlier = sorted_upstream[at] if at else []
+        residual, sorted_rows = after_attention(
+            slots[at], rows, token_groups[at], output_weight, norm2_gain, owners, earlier
+        )
+        residual1.append(residual)
+        sorted_rows, fed, in_flight = together((sorted_rows, fed, in_flight))
         if at == 0:
             upstream[0] = in_flight
         else:
             arrived[-1] = in_flight
-        attended_groups.append(rows)
-        earlier = sorted_upstream[at] if at else []
-        residual, sorted_rows = after_attention(
-            slots[at], rows, token_groups[at], output_weight, norm2_gain, owners, earlier
-        )
-        residual1.append(residual)
-        sorted_rows, fed = together((sorted_rows, fed))
         in_flight = exchange(sorted_rows, "expert", 1)
         arrived.append(in_flight)
     router_wide = jnp.pad(router_weight, ((0, 0), (0, 128 - router_weight.shape[1])))
@@ -903,17 +922,18 @@
         result = run_expert(
             label, rows, grads, tile, min(at, 1), router_wide, w_in[0], w_out[0], at, len(groups), earlier
         )
+        if at + 1 < len(arrived):
+            result, arrived[at + 1] = together((result, arrived[at + 1]))
+        leaving = result[1]
         if back:
             result, back[-1] = together((result, back[-1]))
-        if at + 1 < len(arrived):
-            result, arrived[at + 1] = together((result, arrived[at + 1]))
         done.append(result)
-        back.append(exchange(result[1], "expert", -1))
+        back.append(exchange(leaving, "expert", -1))
     rows_out = done[-1][0]
     grad_rows, hiddens, pre_grads, grad_router = zip(*[item[2] for item in done])
     grad_router = sum(grad_router)[:, : router_weight.shape[1]].T
     grad_experts = expert_grads(sum(arrived, []), grad_rows, hiddens, pre_grads)
-    grad_experts, back[-1], rows_out = together((grad_experts, back[-1], rows_out))
+    grad_experts, back, rows_out = together((grad_experts, back, rows_out))
     grad_experts = lax.psum_scatter(grad_experts, ("dp", "ctx"), scatter_dimension=0, tiled=True)
     if not whole_seq:
         returned = exchange(list(rows_out), "expert", -1)
@@ -954,29 +974,31 @@
         sent, sent_late, returned = together((early.sends(), late.sends(), returned))
         moved, moved_late = early.move(sent), late.move(sent_late)
         block_out = layer_output(slots, residual1, returned)
-        moved, moved_late, block_out = together((moved, moved_late, block_out))
-        early.take(moved)
+        moved_late, block_out = together((moved_late, block_out))
         late.take(moved_late)
-        early_sums = early.finish()
         sent_late, second_grads = together((late.sends(), second_grads))
         moved_late = late.move(sent_late)
         d_tokens = token_grads(
             first_grads, second_grads, projections, tokens.reshape(flat), residual_grad.reshape(flat), norm1_gain
         ).reshape(tokens.shape)
-        moved_late, d_tokens = together((moved_late, d_tokens))
+        moved, moved_late, d_tokens = together((moved, moved_late, d_tokens))
+        early.take(moved)
         late.take(moved_late)
-        for step in range(2):
-            late.take(late.move(late.sends()))
-        late.part, early_sums = together((late.part, early_sums))
-        sums = [early_sums, late.finish()]
-        *grad_qkv, grad_norm1 = weight_outputs(*sums, projections, norm1_gain)
+        sent, sent_late = together((early.sends(), late.sends()))
+        moved = early.move(sent)
+        late.take(late.move(sent_late))
+        moved, moved_late = together((moved, late.move(late.sends())))
+        early.take(moved)
+        late.take(moved_late)
+        sent, sent_late = together((early.sends(), late.sends()))
+        moved, moved_late = together((early.move(sent), late.move(sent_late)))
+        early.take(moved)
+        late.take(moved_late)
+        late.take(late.move(late.sends()))
+        *grad_qkv, grad_w_output, grad_norm1, smalls = weight_outputs(early.part + late.part, projections, norm1_gain)
         grad_norm1 = grad_norm1[0]
-        start = 3 * model_width + 128
-        grad_w_output = jnp.concatenate(
-            [matrix_of(sums[0][start:], side, model_width) for side in range(2)], axis=1
-        )
-        small = small_of(sums[0], start + 2 * model_width).reshape(-1, model_width)
-        grad_bias = jnp.concatenate([part[start - 128 : start - 124] for part in sums], axis=1).astype(jnp.float32)
+        small = (smalls[2, :64] + smalls[2, 64:]).reshape(-1, model_width)
+        grad_bias = jnp.concatenate([smalls[0, :4], smalls[1, :4]], axis=1)
         grad_bias = (grad_bias[:2] + grad_bias[2:]).reshape(2, -1, 128).swapaxes(0, 1).reshape(-1, 128)
     else:
         query_grad, _, diag_grad, key_part, value_part = attend_back_rows(

time: 493 us -> 465 us (0.943)
  waiting for transfers between devices: 85.3 us -> 54.8 us
  starting transfers between devices: 70.5 us -> 82.2 us
  local copies, waits for them, and re-layouts: 58 us -> 50.5 us
    ppermute x18, waiting for transfers between devices: 38.4 us -> 22.2 us  [exchange(): lax.ppermute(piece, axis, [(at, (at + sign * turn) % size) for at in rang...]
    ppermute x12 -> x20, waiting for transfers between devices: 40.5 us -> 32.1 us  [swap(): lax.ppermute(part, axis, [(to, to ^ turn) for to in range(lax.axis_size(a...]
    ppermute x12 -> x20, starting transfers between devices: 12.7 us -> 20.4 us  [swap(): lax.ppermute(part, axis, [(to, to ^ turn) for to in range(lax.axis_size(a...]
    all_gather x2 -> x0, waiting for transfers between devices: 6.14 us -> none  [finish(): return lax.all_gather(self.part, ('dp', 'ctx'), axis=0, tiled=True)]
    pallas_call x4, Pallas kernels: 64.2 us -> 59.2 us  [attend_back(): pl.pallas_call(lambda *refs: bwd_kernel(*refs[:10], *refs[10 + len(earlie...]
    unnamed x185 -> x193, local copies, waits for them, and re-layouts: 39.1 us -> 35.2 us
  transfers between devices with their start and end apart: 38 -> 44, of which waited for: 11 -> 13; matrix products, arithmetic and copies ran while one was open for 9% -> 7% of each run, Pallas kernels for 46% -> 48%
where the time goes in v7:
time: 465 us; the launch traced here: 456 us
  Pallas kernels  228 us (49%)
  starting transfers between devices  82.2 us (18%)
  waiting for transfers between devices  54.8 us (12%)
  local copies, waits for them, and re-layouts  50.5 us (11%)
  other arithmetic  20.6 us (4%)
  between operations  15.5 us (3%)
    ppermute x18, starting transfers between devices, exchange(): lax.ppermute(piece, axis, [(at, (at + sign * turn) % size) for at in rang...  60.5 us
    pallas_call x2, Pallas kernels, run_expert(): pl.pallas_call(lambda *refs: expert_kernel(count, *refs), grid_spec=pltpu...  60 us
    pallas_call x4, Pallas kernels, attend_back(): pl.pallas_call(lambda *refs: bwd_kernel(*refs[:10], *refs[10 + len(earlie...  59.2 us
    unnamed x193, local copies, waits for them, and re-layouts  35.2 us
    ppermute x20, waiting for transfers between devices, swap(): lax.ppermute(part, axis, [(to, to ^ turn) for to in range(lax.axis_size(a...  32.1 us
    pallas_call x2, Pallas kernels, attend(): pl.pallas_call(lambda *refs: fwd_kernel(first // QB, *refs), grid=(width...  31.8 us
    pallas_call x1, Pallas kernels, expert_grads(): pl.pallas_call(lambda *refs: expert_grads_kernel(groups, count, *refs), g...  27.8 us
    ppermute x18, waiting for transfers between devices, exchange(): lax.ppermute(piece, axis, [(at, (at + sign * turn) % size) for at in rang...  22.2 us
  transfers between devices with their start and end apart: 44, of which 13 were waited for; matrix products, arithmetic and copies ran while one was open for 7% of the time, Pallas kernels for 48%

profile of v7, /device:TPU:0, one launch (start us, length us, event | category | flops | bytes accessed | tf_op | source)
XLA Modules:
  0.0 456.4 jit_solution(3199179427510455862)
XLA Ops:
  7.3 1.6 constant_dynamic-slice_fusion.2
  19.8 3.0 collective-permute-start.3
  22.7 2.6 collective-permute-start.4
  28.2 16.0 %attend.2 = (bf16[512,768]{1,0:T(8,128)(2,1)S(1)}, f32[6,2,512]{2,1,0:T(2,128)S(1)}) custom-call(s32[1]{0:T(128)} %bitcast.refs_0_, f32[12,2,1024]{2,1,0:T(2,128)S(1)} %bitcast.123, bf16[1024,768]{1,0:T(8,128)(2,1)S(1)} %bitcast.117, bf16[1024,768]{1,0:T(8,128)(2,1)S(1)} %bitcast.111, bf16[1024,768]{1,0:T(8,128)(2,1)S(1)} %bitcast.105), custom_call_target="tpu_custom_call" | custom-call | flops 402653184 | bytes 1572864 | tf_op jit(solution)/shard_map/attend/pallas_call | solution.py:204
  44.2 3.2 after_attention.2
  52.7 8.1 %collective-permute-start.6 = (bf16[256,768]{1,0:T(8,128)(2,1)}, bf16[256,768]{1,0:T(8,128)(2,1)}, u32[]{:S(2)}, u32[]{:S(2)}) collective-permute-start(bf16[256,768]{1,0:T(8,128)(2,1)} %get-tuple-element.242), channel_id=1, source_target_pairs={{0,1},{1,2},{2,3},{3,0},{4,5},{5,6},{6,7},{7,4},{8,9},{9,10},{10,1... | collective-permute-start | bytes 1179656 | tf_op jit(solution)/shard_map/ppermute | solution.py:625
  60.8 2.3 collective-permute-start.7
  64.9 2.3 sort_upstream.3
  72.3 15.8 %attend.3 = (bf16[512,768]{1,0:T(8,128)(2,1)S(1)}, f32[6,2,512]{2,1,0:T(2,128)S(1)}) custom-call(s32[1]{0:T(128)} %bitcast.refs_0_, f32[12,2,1024]{2,1,0:T(2,128)S(1)} %bitcast.124, bf16[1024,768]{1,0:T(8,128)(2,1)S(1)} %bitcast.118, bf16[1024,768]{1,0:T(8,128)(2,1)S(1)} %bitcast.112, bf16[1024,768]{1,0:T(8,128)(2,1)S(1)} %bitcast.106), custom_call_target="tpu_custom_call" | custom-call | flops 402653184 | bytes 1572864 | tf_op jit(solution)/shard_map/attend/pallas_call | solution.py:204
  88.2 2.8 after_attention.3
  91.0 5.4 %collective-permute-start.10 = (bf16[512,768]{1,0:T(8,128)(2,1)S(1)}, bf16[512,768]{1,0:T(8,128)(2,1)S(1)}, u32[]{:S(2)}, u32[]{:S(2)}) collective-permute-start(bf16[512,768]{1,0:T(8,128)(2,1)S(1)} %get-tuple-element.267), channel_id=1, source_target_pairs={{0,2},{1,3},{2,0},{3,1},{4,6},{5,7},{6,4},{7,5},{8,10},{9,11},{10,... | collective-permute-start | bytes 2359304 | tf_op jit(solution)/shard_map/ppermute | solution.py:625
  96.4 3.4 collective-permute-start.11
  100.4 29.8 %experts.2 = (bf16[512,768]{1,0:T(8,128)(2,1)S(1)}, bf16[512,768]{1,0:T(8,128)(2,1)}, bf16[512,768]{1,0:T(8,128)(2,1)}, bf16[512,768]{1,0:T(8,128)(2,1)}, bf16[2...) custom-call(s32[1]{0:T(128)} %bitcast.3.refs_0_, ...), custom_call_target="tpu_custom_call" | custom-call | flops 38654705664 | bytes 18874368 | tf_op jit(solution)/shard_map/experts/pallas_call | solution.py:398
  131.7 19.4 %collective-permute-done.9.refs_2_.refs_6_.refs_5_ = bf16[512,768]{1,0:T(8,128)(2,1)S(1)} collective-permute-done((bf16[512,768]{1,0:T(8,128)(2,1)S(1)}, bf16[512,768]{1,0:T(8,128)(2,1)S(1)}, u32[]{:S(2)}, u32[]{:S(2)}) %collective-permute-start.9) | collective-permute-done | bytes 786464 | tf_op jit(solution)/shard_map/ppermute | solution.py:625
  151.1 2.0 collective-permute-start.12
  153.1 22.7 %collective-permute-start.13 = (bf16[256,768]{1,0:T(8,128)(2,1)S(1)}, bf16[256,768]{1,0:T(8,128)(2,1)S(1)}, u32[]{:S(2)}, u32[]{:S(2)}) collective-permute-start(bf16[256,768]{1,0:T(8,128)(2,1)S(1)} %get-tuple-element.292), channel_id=1, source_target_pairs={{0,2},{1,3},{2,0},{3,1},{4,6},{5,7},{6,4},{7,5},{8,10},{9,11},{10,... | collective-permute-start | bytes 1179656 | tf_op jit(solution)/shard_map/ppermute | solution.py:625
  175.8 2.2 collective-permute-start.14
  179.1 30.1 %experts.3 = (bf16[512,768]{1,0:T(8,128)(2,1)S(1)}, bf16[512,768]{1,0:T(8,128)(2,1)}, bf16[512,768]{1,0:T(8,128)(2,1)}, bf16[512,768]{1,0:T(8,128)(2,1)S(1)}, bf...) custom-call(s32[1]{0:T(128)} %bitcast.3.refs_0_, ...), custom_call_target="tpu_custom_call", output_to_operand_aliasing={{0}: (12, {}), {1}: (13, {}), {2}: (14, {}), {3}: (15, {})} | custom-call | flops 38654705664 | bytes 18874368 | tf_op jit(solution)/shard_map/experts/pallas_call | solution.py:398
  211.7 1.8 collective-permute-start.15
  218.6 27.8 %expert_grads.1 = bf16[3072,1536]{1,0:T(8,128)(2,1)} custom-call(bf16[256,768]{1,0:T(8,128)(2,1)S(1)} %copy-done.48, bf16[256,768]{1,0:T(8,128)(2,1)} %collective-permute-done.6.refs_2_.refs_1_, bf16[256,768]{1,0:T(8,128)(2,1)} %collective-permute-done.7.refs_3_.refs_2_, bf16[256,768]{1,0:T(8,128)(2,1)} %collective-permute-done.8.refs_4_.refs_3_, ...), custom_call_target="tpu_custom_call" | custom-call | flops 786432 | bytes 786432 | tf_op jit(solution)/shard_map/expert_grads/pallas_call | solution.py:466
  247.3 1.6 fusion.5
  248.9 2.7 copy.79.refs_9_
  253.0 2.5 collective-permute-start.18
  256.6 9.1 %before_attention.2 = (f32[2,512,768]{2,1,0:T(8,128)}, bf16[2,512,768]{2,1,0:T(8,128)(2,1)}, f32[768,768]{1,0:T(8,128)}, f32[1,768]{1,0:T(1,128)}) custom-call(s32[1,1,512]{2,1,0:T(1,128)} %copy-done.55, bf16[256,768]{1,0:T(8,128)(2,1)} %copy-done.42, bf16[256,768]{1,0:T(8,128)(2,1)} %copy-done.84, bf16[256,768]{1,0:T(8,128)(2,1)} %copy-done.85, ...), custom_call_target="tpu_custom_call" | custom-call | tf_op jit(solution)/shard_map/before_attention/pallas_call | solution.py:603
  265.7 8.7 %before_attention.3 = (f32[2,512,768]{2,1,0:T(8,128)}, bf16[2,512,768]{2,1,0:T(8,128)(2,1)}, f32[768,768]{1,0:T(8,128)}, f32[1,768]{1,0:T(1,128)}) custom-call(s32[1,1,512]{2,1,0:T(1,128)} %copy-done.57, bf16[256,768]{1,0:T(8,128)(2,1)} %copy-done.41, ...), custom_call_target="tpu_custom_call", output_to_operand_aliasing={{0}: (10, {}), {1}: (11, {})} | custom-call | tf_op jit(solution)/shard_map/before_attention/pallas_call | solution.py:603
  274.5 27.3 %attend_back.4 = (bf16[3,1024,384]{2,1,0:T(8,128)(2,1)}, bf16[2432,384]{1,0:T(8,128)(2,1)}) custom-call(s32[1]{0:T(128)} %bitcast.refs_0_, f32[12,2,1024]{2,1,0:T(2,128)S(1)} %bitcast.125, f32[3,512,128]{2,1,0:T(8,128)S(1)} %copy-done.71, bf16[1024,768]{1,0:T(8,128)(2,1)S(1)} %bitcast.119, bf16[1024,768]{1,0:T(8,128)(2,1)S(1)} %bitcast.113, ...), custom_call_target="tpu_custom_call" | custom-call | flops 33822867456 | bytes 5505024 | tf_op jit(solution)/shard_map/attend_back/pallas_call | solution.py:297
  303.8 1.9 convert.8
  313.8 10.7 %attend_back.5 = (bf16[3,1024,384]{2,1,0:T(8,128)(2,1)}, bf16[2432,384]{1,0:T(8,128)(2,1)}) custom-call(s32[1]{0:T(128)} %bitcast.refs_0_, f32[12,2,1024]{2,1,0:T(2,128)S(1)} %bitcast.126, f32[3,512,128]{2,1,0:T(8,128)S(1)} %copy-done.72, bf16[1024,768]{1,0:T(8,128)(2,1)S(1)} %bitcast.120, bf16[1024,768]{1,0:T(8,128)(2,1)S(1)} %bitcast.114, ...), custom_call_target="tpu_custom_call" | custom-call | flops 11274289152 | bytes 1835008 | tf_op jit(solution)/shard_map/attend_back/pallas_call | solution.py:297
  324.5 1.9 fusion.3
  330.1 10.7 %attend_back.6 = (bf16[3,1024,384]{2,1,0:T(8,128)(2,1)}, bf16[2432,384]{1,0:T(8,128)(2,1)}) custom-call(s32[1]{0:T(128)} %bitcast.refs_0_, f32[12,2,1024]{2,1,0:T(2,128)S(1)} %bitcast.127, f32[3,512,128]{2,1,0:T(8,128)S(1)} %copy-done.72, bf16[1024,768]{1,0:T(8,128)(2,1)S(1)} %bitcast.121, ...), custom_call_target="tpu_custom_call", output_to_operand_aliasing={{0}: (10, {}), {1}: (11, {})} | custom-call | flops 11274289152 | bytes 1835008 | tf_op jit(solution)/shard_map/attend_back/pallas_call | solution.py:297
  340.8 6.6 %collective-permute-done.22 = bf16[512,384]{1,0:T(8,128)(2,1)S(1)} collective-permute-done((bf16[512,384]{1,0:T(8,128)(2,1)S(1)}, bf16[512,384]{1,0:T(8,128)(2,1)S(1)}, u32[]{:S(2)}, u32[]{:S(2)}) %collective-permute-start.22) | collective-permute-done | bytes 393248 | tf_op jit(solution)/shard_map/ppermute | solution.py:794
  347.6 1.6 collective-permute-start.25
  349.2 10.5 %attend_back.7 = (bf16[3,1024,384]{2,1,0:T(8,128)(2,1)}, bf16[2432,384]{1,0:T(8,128)(2,1)}) custom-call(s32[1]{0:T(128)} %bitcast.refs_0_, f32[12,2,1024]{2,1,0:T(2,128)S(1)} %bitcast.128, f32[3,512,128]{2,1,0:T(8,128)S(1)} %copy-done.72, bf16[1024,768]{1,0:T(8,128)(2,1)S(1)} %bitcast.122, ...), custom_call_target="tpu_custom_call", output_to_operand_aliasing={{0}: (10, {}), {1}: (11, {})} | custom-call | flops 11274289152 | bytes 1835008 | tf_op jit(solution)/shard_map/attend_back/pallas_call | solution.py:297
  361.3 2.7 collective-permute-start.28
  365.1 5.5 %layer_output.1 = (bf16[1,512,768]{2,1,0:T(8,128)(2,1)S(1)}, bf16[1,512,768]{2,1,0:T(8,128)(2,1)}) custom-call(s32[1,1,512]{2,1,0:T(1,128)S(1)} %copy-done.56, s32[1,1,512]{2,1,0:T(1,128)S(1)} %copy-done.58, f32[1,512,768]{2,1,0:T(8,128)} %copy-done.18, f32[1,512,768]{2,1,0:T(8,128)} %get-tuple-element.311.refs_5_.refs_3_, bf16[512,768]{1,0:T(8,128)(2,1)S(1)} %copy-done.34, ...), custom_call_target="tpu_custom_call" | custom-call | tf_op jit(solution)/shard_map/layer_output/pallas_call | solution.py:660
  374.6 8.5 %token_grads.1 = f32[1024,768]{1,0:T(8,128)} custom-call(bf16[3,1024,384]{2,1,0:T(8,128)(2,1)} %get-tuple-element.385.first_ref, bf16[3,1024,384]{2,1,0:T(8,128)(2,1)} %get-tuple-element.386.second_ref, bf16[768,768]{1,0:T(8,128)(2,1)S(1)} %copy-done.20, bf16[768,768]{1,0:T(8,128)(2,1)S(1)} %copy-done.22, bf16[768,768]{1,0:T(8,128)(2,1)S(1)} %copy-done.24, ...), custom_call_target="tpu_custom_call" | custom-call | flops 3623878656 | bytes 11010048 | tf_op jit(solution)/shard_map/token_grads/pallas_call | solution.py:737
  383.1 1.6 collective-permute-done.31
  387.2 1.6 collective-permute-start.34
  389.9 2.0 collective-permute-done.36
  392.5 6.0 %collective-permute-done.33 = bf16[512,384]{1,0:T(8,128)(2,1)S(1)} collective-permute-done((bf16[512,384]{1,0:T(8,128)(2,1)S(1)}, bf16[512,384]{1,0:T(8,128)(2,1)S(1)}, u32[]{:S(2)}, u32[]{:S(2)}) %collective-permute-start.33) | collective-permute-done | bytes 393248 | tf_op jit(solution)/shard_map/ppermute | solution.py:794
  398.5 6.6 %collective-permute-done.34 = bf16[512,384]{1,0:T(8,128)(2,1)S(1)} collective-permute-done((bf16[512,384]{1,0:T(8,128)(2,1)S(1)}, bf16[512,384]{1,0:T(8,128)(2,1)S(1)}, u32[]{:S(2)}, u32[]{:S(2)}) %collective-permute-start.34) | collective-permute-done | bytes 393248 | tf_op jit(solution)/shard_map/ppermute | solution.py:794
  406.3 2.1 copy-done.73
  410.1 1.5 collective-permute-start.39
  413.1 5.0 %collective-permute-done.39 = bf16[304,384]{1,0:T(8,128)(2,1)} collective-permute-done((bf16[304,384]{1,0:T(8,128)(2,1)}, bf16[304,384]{1,0:T(8,128)(2,1)}, u32[]{:S(2)}, u32[]{:S(2)}) %collective-permute-start.39) | collective-permute-done | bytes 233504 | tf_op jit(solution)/shard_map/ppermute | solution.py:794
  422.0 4.0 collective-permute-done.41
  431.5 1.6 slice_select_fusion.1
  433.1 1.9 pad_maximum_fusion
  436.0 8.2 %weight_outputs.1 = (f32[768,768]{1,0:T(8,128)}, f32[768,768]{1,0:T(8,128)}, f32[768,768]{1,0:T(8,128)}, f32[768,768]{1,0:T(8,128)}, f32[1,768]{1,0:T(1,128)}, /*index=5*/f32[3,128,384]{2,1,0:T(8,128)}) custom-call(s32[2]{0:T(128)} %pad_add_fusion.place_ref, bf16[4,512,384]{2,1,0:T(8,128)(2,1)} %copy-done.77, ...), custom_call_target="tpu_custom_call" | custom-call | tf_op jit(solution)/shard_map/weight_outputs/pallas_call | solution.py:705
  (310 shorter events, 83.9 us)
Async XLA Ops:
  7.2 352.7 %reduce-scatter.2.cloned.1.call-start = ((), (), s32[]{:S(2)}) async-start(), calls=%async_computation.1 | async-start | bytes 10616832 | tf_op jit(solution)/shard_map/reduce_scatter | solution.py:937
  8.9 4.6 %collective-permute-start = (bf16[1,512,768]{2,1,0:T(8,128)(2,1)S(1)}, bf16[1,512,768]{2,1,0:T(8,128)(2,1)S(1)}, u32[]{:S(2)}, u32[]{:S(2)}) collective-permute-start(bf16[1,512,768]{2,1,0:T(8,128)(2,1)S(1)} %get-tuple-element.475), channel_id=1, source_target_pairs={{0,4},{4,0},{1,5},{5,1},{2,6},{6,2},{3,7},{7,3},{8,12},{12,8},{9,1... | collective-permute-start | bytes 2359304 | tf_op jit(solution)/shard_map/ppermute | solution.py:634
  10.4 54.5 %collective-permute-start.2 = (bf16[1,512,768]{2,1,0:T(8,128)(2,1)}, bf16[1,512,768]{2,1,0:T(8,128)(2,1)}, u32[]{:S(2)}, u32[]{:S(2)}) collective-permute-start(bf16[1,512,768]{2,1,0:T(8,128)(2,1)} %get-tuple-element.473), channel_id=1, source_target_pairs={{0,4},{4,0},{1,5},{5,1},{2,6},{6,2},{3,7},{7,3},{8,12},{12,8},{9,1... | collective-permute-start | bytes 2359304 | tf_op jit(solution)/shard_map/ppermute | solution.py:634
  11.0 77.2 %copy-start.49 = (f32[1,768]{1,0:T(1,128)}, f32[1,768]{1,0:T(1,128)S(1)}, u32[]{:S(2)}) copy-start(f32[1,768]{1,0:T(1,128)S(1)} %broadcast_in_dim.25.refs_4_.refs_9_) | copy-start | bytes 9220
  19.8 29.6 %collective-permute-start.3 = (bf16[256,768]{1,0:T(8,128)(2,1)S(1)}, bf16[256,768]{1,0:T(8,128)(2,1)S(1)}, u32[]{:S(2)}, u32[]{:S(2)}) collective-permute-start(bf16[256,768]{1,0:T(8,128)(2,1)S(1)} %get-tuple-element.228), channel_id=1, source_target_pairs={{0,1},{1,2},{2,3},{3,0},{4,5},{5,6},{6,7},{7,4},{8,9},{9,10},{10,1... | collective-permute-start | bytes 1179656 | tf_op jit(solution)/shard_map/ppermute | solution.py:625
  22.7 28.5 %collective-permute-start.4 = (bf16[256,768]{1,0:T(8,128)(2,1)S(1)}, bf16[256,768]{1,0:T(8,128)(2,1)S(1)}, u32[]{:S(2)}, u32[]{:S(2)}) collective-permute-start(bf16[256,768]{1,0:T(8,128)(2,1)S(1)} %get-tuple-element.229), channel_id=1, source_target_pairs={{0,2},{1,3},{2,0},{3,1},{4,6},{5,7},{6,4},{7,5},{8,10},{9,11},{10,... | collective-permute-start | bytes 1179656 | tf_op jit(solution)/shard_map/ppermute | solution.py:625
  25.3 26.6 %collective-permute-start.5 = (bf16[256,768]{1,0:T(8,128)(2,1)S(1)}, bf16[256,768]{1,0:T(8,128)(2,1)S(1)}, u32[]{:S(2)}, u32[]{:S(2)}) collective-permute-start(bf16[256,768]{1,0:T(8,128)(2,1)S(1)} %get-tuple-element.230), channel_id=1, source_target_pairs={{0,3},{1,0},{2,1},{3,2},{4,7},{5,4},{6,5},{7,6},{8,11},{9,8},{10,9... | collective-permute-start | bytes 1179656 | tf_op jit(solution)/shard_map/ppermute | solution.py:625
  52.7 38.3 %collective-permute-start.6 = (bf16[256,768]{1,0:T(8,128)(2,1)}, bf16[256,768]{1,0:T(8,128)(2,1)}, u32[]{:S(2)}, u32[]{:S(2)}) collective-permute-start(bf16[256,768]{1,0:T(8,128)(2,1)} %get-tuple-element.242), channel_id=1, source_target_pairs={{0,1},{1,2},{2,3},{3,0},{4,5},{5,6},{6,7},{7,4},{8,9},{9,10},{10,1... | collective-permute-start | bytes 1179656 | tf_op jit(solution)/shard_map/ppermute | solution.py:625
  60.8 30.2 %collective-permute-start.7 = (bf16[256,768]{1,0:T(8,128)(2,1)}, bf16[256,768]{1,0:T(8,128)(2,1)}, u32[]{:S(2)}, u32[]{:S(2)}) collective-permute-start(bf16[256,768]{1,0:T(8,128)(2,1)} %get-tuple-element.243), channel_id=1, source_target_pairs={{0,2},{1,3},{2,0},{3,1},{4,6},{5,7},{6,4},{7,5},{8,10},{9,11},{10,... | collective-permute-start | bytes 1179656 | tf_op jit(solution)/shard_map/ppermute | solution.py:625
  63.2 27.9 %collective-permute-start.8 = (bf16[256,768]{1,0:T(8,128)(2,1)}, bf16[256,768]{1,0:T(8,128)(2,1)}, u32[]{:S(2)}, u32[]{:S(2)}) collective-permute-start(bf16[256,768]{1,0:T(8,128)(2,1)} %get-tuple-element.244), channel_id=1, source_target_pairs={{0,3},{1,0},{2,1},{3,2},{4,7},{5,4},{6,5},{7,6},{8,11},{9,8},{10,9... | collective-permute-start | bytes 1179656 | tf_op jit(solution)/shard_map/ppermute | solution.py:625
  63.5 1.4 collective-permute-start.1
  88.1 163.5 %copy-start.3 = (bf16[512,768]{1,0:T(8,128)(2,1)}, bf16[512,768]{1,0:T(8,128)(2,1)S(1)}, u32[]{:S(2)}) copy-start(bf16[512,768]{1,0:T(8,128)(2,1)S(1)} %get-tuple-element.232) | copy-start | bytes 2359300
  91.0 40.6 %collective-permute-start.10 = (bf16[512,768]{1,0:T(8,128)(2,1)S(1)}, bf16[512,768]{1,0:T(8,128)(2,1)S(1)}, u32[]{:S(2)}, u32[]{:S(2)}) collective-permute-start(bf16[512,768]{1,0:T(8,128)(2,1)S(1)} %get-tuple-element.267), channel_id=1, source_target_pairs={{0,2},{1,3},{2,0},{3,1},{4,6},{5,7},{6,4},{7,5},{8,10},{9,11},{10,... | collective-permute-start | bytes 2359304 | tf_op jit(solution)/shard_map/ppermute | solution.py:625
  96.4 35.3 %collective-permute-start.11 = (bf16[512,768]{1,0:T(8,128)(2,1)S(1)}, bf16[512,768]{1,0:T(8,128)(2,1)S(1)}, u32[]{:S(2)}, u32[]{:S(2)}) collective-permute-start(bf16[512,768]{1,0:T(8,128)(2,1)S(1)} %get-tuple-element.268), channel_id=1, source_target_pairs={{0,3},{1,0},{2,1},{3,2},{4,7},{5,4},{6,5},{7,6},{8,11},{9,8},{10,9... | collective-permute-start | bytes 2359304 | tf_op jit(solution)/shard_map/ppermute | solution.py:625
  99.8 51.3 %collective-permute-start.9 = (bf16[512,768]{1,0:T(8,128)(2,1)S(1)}, bf16[512,768]{1,0:T(8,128)(2,1)S(1)}, u32[]{:S(2)}, u32[]{:S(2)}) collective-permute-start(bf16[512,768]{1,0:T(8,128)(2,1)S(1)} %get-tuple-element.266), channel_id=1, source_target_pairs={{0,1},{1,2},{2,3},{3,0},{4,5},{5,6},{6,7},{7,4},{8,9},{9,10},{10,1... | collective-permute-start | bytes 2359304 | tf_op jit(solution)/shard_map/ppermute | solution.py:625
  131.7 46.3 %copy-start.35 = (bf16[512,768]{1,0:T(8,128)(2,1)}, bf16[512,768]{1,0:T(8,128)(2,1)S(1)}, u32[]{:S(2)}) copy-start(bf16[512,768]{1,0:T(8,128)(2,1)S(1)} %collective-permute-done.10.refs_3_.refs_7_.refs_6_) | copy-start | bytes 2359300
  131.7 46.3 %copy-start.37 = (bf16[512,768]{1,0:T(8,128)(2,1)}, bf16[512,768]{1,0:T(8,128)(2,1)S(1)}, u32[]{:S(2)}) copy-start(bf16[512,768]{1,0:T(8,128)(2,1)S(1)} %collective-permute-done.11.refs_4_.refs_8_.refs_7_) | copy-start | bytes 2359300
  151.1 62.4 %collective-permute-start.12 = (bf16[256,768]{1,0:T(8,128)(2,1)S(1)}, bf16[256,768]{1,0:T(8,128)(2,1)S(1)}, u32[]{:S(2)}, u32[]{:S(2)}) collective-permute-start(bf16[256,768]{1,0:T(8,128)(2,1)S(1)} %get-tuple-element.291), channel_id=1, source_target_pairs={{0,3},{1,0},{2,1},{3,2},{4,7},{5,4},{6,5},{7,6},{8,11},{9,8},{10,9... | collective-permute-start | bytes 1179656 | tf_op jit(solution)/shard_map/ppermute | solution.py:625
  153.1 61.2 %collective-permute-start.13 = (bf16[256,768]{1,0:T(8,128)(2,1)S(1)}, bf16[256,768]{1,0:T(8,128)(2,1)S(1)}, u32[]{:S(2)}, u32[]{:S(2)}) collective-permute-start(bf16[256,768]{1,0:T(8,128)(2,1)S(1)} %get-tuple-element.292), channel_id=1, source_target_pairs={{0,2},{1,3},{2,0},{3,1},{4,6},{5,7},{6,4},{7,5},{8,10},{9,11},{10,... | collective-permute-start | bytes 1179656 | tf_op jit(solution)/shard_map/ppermute | solution.py:625
  175.8 38.5 %collective-permute-start.14 = (bf16[256,768]{1,0:T(8,128)(2,1)S(1)}, bf16[256,768]{1,0:T(8,128)(2,1)S(1)}, u32[]{:S(2)}, u32[]{:S(2)}) collective-permute-start(bf16[256,768]{1,0:T(8,128)(2,1)S(1)} %get-tuple-element.293), channel_id=1, source_target_pairs={{0,1},{1,2},{2,3},{3,0},{4,5},{5,6},{6,7},{7,4},{8,9},{9,10},{10,1... | collective-permute-start | bytes 1179656 | tf_op jit(solution)/shard_map/ppermute | solution.py:625
  211.7 34.7 %collective-permute-start.15 = (bf16[256,768]{1,0:T(8,128)(2,1)}, bf16[256,768]{1,0:T(8,128)(2,1)}, u32[]{:S(2)}, u32[]{:S(2)}) collective-permute-start(bf16[256,768]{1,0:T(8,128)(2,1)} %get-tuple-element.283), channel_id=1, source_target_pairs={{0,3},{1,0},{2,1},{3,2},{4,7},{5,4},{6,5},{7,6},{8,11},{9,8},{10,9... | collective-permute-start | bytes 1179656 | tf_op jit(solution)/shard_map/ppermute | solution.py:625
  213.5 33.7 %collective-permute-start.16 = (bf16[256,768]{1,0:T(8,128)(2,1)}, bf16[256,768]{1,0:T(8,128)(2,1)}, u32[]{:S(2)}, u32[]{:S(2)}) collective-permute-start(bf16[256,768]{1,0:T(8,128)(2,1)} %get-tuple-element.284), channel_id=1, source_target_pairs={{0,2},{1,3},{2,0},{3,1},{4,6},{5,7},{6,4},{7,5},{8,10},{9,11},{10,... | collective-permute-start | bytes 1179656 | tf_op jit(solution)/shard_map/ppermute | solution.py:625
  213.5 33.7 %collective-permute-start.17 = (bf16[256,768]{1,0:T(8,128)(2,1)S(1)}, bf16[256,768]{1,0:T(8,128)(2,1)}, u32[]{:S(2)}, u32[]{:S(2)}) collective-permute-start(bf16[256,768]{1,0:T(8,128)(2,1)S(1)} %get-tuple-element.285), channel_id=1, source_target_pairs={{0,1},{1,2},{2,3},{3,0},{4,5},{5,6},{6,7},{7,4},{8,9},{9,10},{10,1... | collective-permute-start | bytes 1179656 | tf_op jit(solution)/shard_map/ppermute | solution.py:625
  253.0 52.7 %collective-permute-start.18 = (bf16[512,768]{1,0:T(8,128)(2,1)}, bf16[512,768]{1,0:T(8,128)(2,1)}, u32[]{:S(2)}, u32[]{:S(2)}) collective-permute-start(bf16[512,768]{1,0:T(8,128)(2,1)} %get-tuple-element.327), channel_id=1, source_target_pairs={{0,3},{1,0},{2,1},{3,2},{4,7},{5,4},{6,5},{7,6},{8,11},{9,8},{10,9... | collective-permute-start | bytes 2359304 | tf_op jit(solution)/shard_map/ppermute | solution.py:625
  255.5 51.1 %collective-permute-start.19 = (bf16[512,768]{1,0:T(8,128)(2,1)}, bf16[512,768]{1,0:T(8,128)(2,1)}, u32[]{:S(2)}, u32[]{:S(2)}) collective-permute-start(bf16[512,768]{1,0:T(8,128)(2,1)} %get-tuple-element.328), channel_id=1, source_target_pairs={{0,2},{1,3},{2,0},{3,1},{4,6},{5,7},{6,4},{7,5},{8,10},{9,11},{10,... | collective-permute-start | bytes 2359304 | tf_op jit(solution)/shard_map/ppermute | solution.py:625
  309.3 15.2 %collective-permute-start.20 = (bf16[4,512,384]{2,1,0:T(8,128)(2,1)}, bf16[4,512,384]{2,1,0:T(8,128)(2,1)}, u32[]{:S(2)}, u32[]{:S(2)}) collective-permute-start(bf16[4,512,384]{2,1,0:T(8,128)(2,1)} %dynamic-slice_bitcast_fusion), channel_id=1, source_target_pairs={{0,4},{4,0},{1,5},{5,1},{2,6},{6,2},{3,7},{7,3},{8,12},{12,8},{9,1... | collective-permute-start | bytes 4718600 | tf_op jit(solution)/shard_map/ppermute | solution.py:794
  309.3 31.5 %collective-permute-start.24 = (bf16[512,768]{1,0:T(8,128)(2,1)}, bf16[512,768]{1,0:T(8,128)(2,1)S(1)}, u32[]{:S(2)}, u32[]{:S(2)}) collective-permute-start(bf16[512,768]{1,0:T(8,128)(2,1)} %copy-done.62), channel_id=1, source_target_pairs={{0,1},{1,2},{2,3},{3,0},{4,5},{5,6},{6,7},{7,4},{8,9},{9,10},{10,1... | collective-permute-start | bytes 2359304 | tf_op jit(solution)/shard_map/ppermute | solution.py:625
  326.5 14.3 %collective-permute-start.21 = (bf16[512,384]{1,0:T(8,128)(2,1)S(1)}, bf16[512,384]{1,0:T(8,128)(2,1)S(1)}, u32[]{:S(2)}, u32[]{:S(2)}) collective-permute-start(bf16[512,384]{1,0:T(8,128)(2,1)S(1)} %get-tuple-element.345), channel_id=1, source_target_pairs={{0,8},{8,0},{16,24},{24,16},{1,9},{9,1},{17,25},{25,17},{2,10},{10... | collective-permute-start | bytes 1179656 | tf_op jit(solution)/shard_map/ppermute | solution.py:794
  328.0 19.4 %collective-permute-start.22 = (bf16[512,384]{1,0:T(8,128)(2,1)S(1)}, bf16[512,384]{1,0:T(8,128)(2,1)S(1)}, u32[]{:S(2)}, u32[]{:S(2)}) collective-permute-start(bf16[512,384]{1,0:T(8,128)(2,1)S(1)} %get-tuple-element.346), channel_id=1, source_target_pairs={{0,16},{8,24},{16,0},{24,8},{1,17},{9,25},{17,1},{25,9},{2,18},{10... | collective-permute-start | bytes 1179656 | tf_op jit(solution)/shard_map/ppermute | solution.py:794
  329.4 18.0 %collective-permute-start.23 = (bf16[512,384]{1,0:T(8,128)(2,1)S(1)}, bf16[512,384]{1,0:T(8,128)(2,1)S(1)}, u32[]{:S(2)}, u32[]{:S(2)}) collective-permute-start(bf16[512,384]{1,0:T(8,128)(2,1)S(1)} %get-tuple-element.347), channel_id=1, source_target_pairs={{0,24},{8,16},{16,8},{24,0},{1,25},{9,17},{17,9},{25,1},{2,26},{10... | collective-permute-start | bytes 1179656 | tf_op jit(solution)/shard_map/ppermute | solution.py:794
  347.6 12.1 %collective-permute-start.25 = (bf16[512,384]{1,0:T(8,128)(2,1)S(1)}, bf16[512,384]{1,0:T(8,128)(2,1)S(1)}, u32[]{:S(2)}, u32[]{:S(2)}) collective-permute-start(bf16[512,384]{1,0:T(8,128)(2,1)S(1)} %fusion.14), channel_id=1, source_target_pairs={{0,1},{1,0},{2,3},{3,2},{4,5},{5,4},{6,7},{7,6},{8,9},{9,8},{10,11... | collective-permute-start | bytes 1179656 | tf_op jit(solution)/shard_map/ppermute | solution.py:794
  361.2 9.4 %collective-permute-start.26 = (bf16[4,304,384]{2,1,0:T(8,128)(2,1)S(1)}, bf16[4,304,384]{2,1,0:T(8,128)(2,1)S(1)}, u32[]{:S(2)}, u32[]{:S(2)}) collective-permute-start(bf16[4,304,384]{2,1,0:T(8,128)(2,1)S(1)} %dynamic-slice_bitcast_fusion.1), channel_id=1, source_target_pairs={{0,4},{4,0},{1,5},{5,1},{2,6},{6,2},{3,7},{7,3},{8,12},{12,8},{9,1... | collective-permute-start | bytes 2801672 | tf_op jit(solution)/shard_map/ppermute | solution.py:794
  361.3 21.7 %collective-permute-start.28 = (bf16[512,384]{1,0:T(8,128)(2,1)S(1)}, bf16[512,384]{1,0:T(8,128)(2,1)S(1)}, u32[]{:S(2)}, u32[]{:S(2)}) collective-permute-start(bf16[512,384]{1,0:T(8,128)(2,1)S(1)} %add_convert_fusion.1), channel_id=1, source_target_pairs={{0,2},{1,3},{2,0},{3,1},{4,6},{5,7},{6,4},{7,5},{8,10},{9,11},{10,... | collective-permute-start | bytes 1179656 | tf_op jit(solution)/shard_map/ppermute | solution.py:794
  371.0 12.0 %collective-permute-start.29 = (bf16[304,384]{1,0:T(8,128)(2,1)S(1)}, bf16[304,384]{1,0:T(8,128)(2,1)S(1)}, u32[]{:S(2)}, u32[]{:S(2)}) collective-permute-start(bf16[304,384]{1,0:T(8,128)(2,1)S(1)} %get-tuple-element.382), channel_id=1, source_target_pairs={{0,8},{8,0},{16,24},{24,16},{1,9},{9,1},{17,25},{25,17},{2,10},{10... | collective-permute-start | bytes 700424 | tf_op jit(solution)/shard_map/ppermute | solution.py:794
  372.3 10.8 %collective-permute-start.30 = (bf16[304,384]{1,0:T(8,128)(2,1)S(1)}, bf16[304,384]{1,0:T(8,128)(2,1)S(1)}, u32[]{:S(2)}, u32[]{:S(2)}) collective-permute-start(bf16[304,384]{1,0:T(8,128)(2,1)S(1)} %get-tuple-element.383), channel_id=1, source_target_pairs={{0,16},{8,24},{16,0},{24,8},{1,17},{9,25},{17,1},{25,9},{2,18},{10... | collective-permute-start | bytes 700424 | tf_op jit(solution)/shard_map/ppermute | solution.py:794
  373.1 11.6 %collective-permute-start.31 = (bf16[304,384]{1,0:T(8,128)(2,1)S(1)}, bf16[304,384]{1,0:T(8,128)(2,1)S(1)}, u32[]{:S(2)}, u32[]{:S(2)}) collective-permute-start(bf16[304,384]{1,0:T(8,128)(2,1)S(1)} %get-tuple-element.384), channel_id=1, source_target_pairs={{0,24},{8,16},{16,8},{24,0},{1,25},{9,17},{17,9},{25,1},{2,26},{10... | collective-permute-start | bytes 700424 | tf_op jit(solution)/shard_map/ppermute | solution.py:794
  385.0 7.0 %collective-permute-start.36 = (bf16[304,384]{1,0:T(8,128)(2,1)S(1)}, bf16[304,384]{1,0:T(8,128)(2,1)S(1)}, u32[]{:S(2)}, u32[]{:S(2)}) collective-permute-start(bf16[304,384]{1,0:T(8,128)(2,1)S(1)} %fusion.17), channel_id=1, source_target_pairs={{0,1},{1,0},{2,3},{3,2},{4,5},{5,4},{6,7},{7,6},{8,9},{9,8},{10,11... | collective-permute-start | bytes 700424 | tf_op jit(solution)/shard_map/ppermute | solution.py:794
  386.5 12.1 %collective-permute-start.33 = (bf16[512,384]{1,0:T(8,128)(2,1)S(1)}, bf16[512,384]{1,0:T(8,128)(2,1)S(1)}, u32[]{:S(2)}, u32[]{:S(2)}) collective-permute-start(bf16[512,384]{1,0:T(8,128)(2,1)S(1)} %add_convert_fusion), channel_id=1, source_target_pairs={{0,8},{8,0},{16,24},{24,16},{1,9},{9,1},{17,25},{25,17},{2,10},{10... | collective-permute-start | bytes 1179656 | tf_op jit(solution)/shard_map/ppermute | solution.py:794
  387.2 18.0 %collective-permute-start.34 = (bf16[512,384]{1,0:T(8,128)(2,1)S(1)}, bf16[512,384]{1,0:T(8,128)(2,1)S(1)}, u32[]{:S(2)}, u32[]{:S(2)}) collective-permute-start(bf16[512,384]{1,0:T(8,128)(2,1)S(1)} %add_convert_fusion), channel_id=1, source_target_pairs={{0,16},{8,24},{16,0},{24,8},{1,17},{9,25},{17,1},{25,9},{2,18},{10... | collective-permute-start | bytes 1179656 | tf_op jit(solution)/shard_map/ppermute | solution.py:794
  388.8 16.4 %collective-permute-start.35 = (bf16[512,384]{1,0:T(8,128)(2,1)S(1)}, bf16[512,384]{1,0:T(8,128)(2,1)S(1)}, u32[]{:S(2)}, u32[]{:S(2)}) collective-permute-start(bf16[512,384]{1,0:T(8,128)(2,1)S(1)} %add_convert_fusion), channel_id=1, source_target_pairs={{0,24},{8,16},{16,8},{24,0},{1,25},{9,17},{17,9},{25,1},{2,26},{10... | collective-permute-start | bytes 1179656 | tf_op jit(solution)/shard_map/ppermute | solution.py:794
  392.0 13.1 %collective-permute-start.37 = (bf16[304,384]{1,0:T(8,128)(2,1)S(1)}, bf16[304,384]{1,0:T(8,128)(2,1)S(1)}, u32[]{:S(2)}, u32[]{:S(2)}) collective-permute-start(bf16[304,384]{1,0:T(8,128)(2,1)S(1)} %add_convert_fusion.3), channel_id=1, source_target_pairs={{0,2},{1,3},{2,0},{3,1},{4,6},{5,7},{6,4},{7,5},{8,10},{9,11},{10,... | collective-permute-start | bytes 700424 | tf_op jit(solution)/shard_map/ppermute | solution.py:794
  406.2 19.8 %collective-permute-start.38 = (bf16[4,512,384]{2,1,0:T(8,128)(2,1)S(1)}, bf16[4,512,384]{2,1,0:T(8,128)(2,1)}, u32[]{:S(2)}, u32[]{:S(2)}) collective-permute-start(bf16[4,512,384]{2,1,0:T(8,128)(2,1)S(1)} %pad_maximum_fusion.3.refs_0_), channel_id=1, source_target_pairs={{0,4},{4,0},{1,5},{5,1},{2,6},{6,2},{3,7},{7,3},{8,12},{12,8},{9,1... | collective-permute-start | bytes 4718600 | tf_op jit(solution)/shard_map/ppermute | solution.py:794
  409.6 20.7 %collective-permute-start.32 = (f32[1,512,768]{2,1,0:T(8,128)}, f32[1,512,768]{2,1,0:T(8,128)}, u32[]{:S(2)}, u32[]{:S(2)}) collective-permute-start(f32[1,512,768]{2,1,0:T(8,128)} %slice.60), channel_id=1, source_target_pairs={{0,4},{4,0},{1,5},{5,1},{2,6},{6,2},{3,7},{7,3},{8,12},{12,8},{9,1... | collective-permute-start | bytes 4718600 | tf_op jit(solution)/shard_map/ppermute | solution.py:639
  409.6 17.9 %collective-permute-start.27 = (bf16[1,512,768]{2,1,0:T(8,128)(2,1)}, bf16[1,512,768]{2,1,0:T(8,128)(2,1)}, u32[]{:S(2)}, u32[]{:S(2)}) collective-permute-start(bf16[1,512,768]{2,1,0:T(8,128)(2,1)} %get-tuple-element.378), channel_id=1, source_target_pairs={{0,4},{4,0},{1,5},{5,1},{2,6},{6,2},{3,7},{7,3},{8,12},{12,8},{9,1... | collective-permute-start | bytes 2359304 | tf_op jit(solution)/shard_map/ppermute | solution.py:639
  410.1 7.9 %collective-permute-start.39 = (bf16[304,384]{1,0:T(8,128)(2,1)}, bf16[304,384]{1,0:T(8,128)(2,1)}, u32[]{:S(2)}, u32[]{:S(2)}) collective-permute-start(bf16[304,384]{1,0:T(8,128)(2,1)} %add_convert_fusion.2), channel_id=1, source_target_pairs={{0,8},{8,0},{16,24},{24,16},{1,9},{9,1},{17,25},{25,17},{2,10},{10... | collective-permute-start | bytes 700424 | tf_op jit(solution)/shard_map/ppermute | solution.py:794
  412.5 9.5 %collective-permute-start.40 = (bf16[304,384]{1,0:T(8,128)(2,1)}, bf16[304,384]{1,0:T(8,128)(2,1)}, u32[]{:S(2)}, u32[]{:S(2)}) collective-permute-start(bf16[304,384]{1,0:T(8,128)(2,1)} %add_convert_fusion.2), channel_id=1, source_target_pairs={{0,16},{8,24},{16,0},{24,8},{1,17},{9,25},{17,1},{25,9},{2,18},{10... | collective-permute-start | bytes 700424 | tf_op jit(solution)/shard_map/ppermute | solution.py:794
  418.1 8.0 %collective-permute-start.41 = (bf16[304,384]{1,0:T(8,128)(2,1)}, bf16[304,384]{1,0:T(8,128)(2,1)}, u32[]{:S(2)}, u32[]{:S(2)}) collective-permute-start(bf16[304,384]{1,0:T(8,128)(2,1)} %add_convert_fusion.2), channel_id=1, source_target_pairs={{0,24},{8,16},{16,8},{24,0},{1,25},{9,17},{17,9},{25,1},{2,26},{10... | collective-permute-start | bytes 700424 | tf_op jit(solution)/shard_map/ppermute | solution.py:794
  427.5 7.5 %collective-permute-start.42 = (bf16[4,304,384]{2,1,0:T(8,128)(2,1)S(1)}, bf16[4,304,384]{2,1,0:T(8,128)(2,1)S(1)}, u32[]{:S(2)}, u32[]{:S(2)}) collective-permute-start(bf16[4,304,384]{2,1,0:T(8,128)(2,1)S(1)} %pad_maximum_fusion.4.refs_2_), channel_id=1, source_target_pairs={{0,4},{4,0},{1,5},{5,1},{2,6},{6,2},{3,7},{7,3},{8,12},{12,8},{9,1... | collective-permute-start | bytes 2801672 | tf_op jit(solution)/shard_map/ppermute | solution.py:794
  (88 other events, 560.9 us)
Sparse Core Ops, SparseCore 0:
  247.4 76.6 reduce-scatter.1

commit v8 on v7

--- a/solution.py
+++ b/solution.py
@@ -634,10 +634,30 @@
     return [own, lax.ppermute(other, "ctx", [(0, 1), (1, 0)])]
 
 
+def hand_back_kernel(core_ref, own_ref, arrived_ref, out_ref):
+    out_ref[...] = jnp.where(pl.program_id(0) == 0, own_ref[...], arrived_ref[...])
+
+
 def hand_back(own, other):
-    at = lax.axis_index("ctx")
     arrived = lax.ppermute(other, "ctx", [(0, 1), (1, 0)])
-    return jnp.concatenate([jnp.where(at == 0, own, arrived), jnp.where(at == 0, arrived, own)])
+    core = lax.axis_index("ctx").astype(jnp.int32).reshape(1)
+    _, length, width = own.shape
+    block = (1, QB, width)
+    last = length // QB - 1
+    return pl.pallas_call(
+        hand_back_kernel,
+        grid_spec=pltpu.PrefetchScalarGridSpec(
+            num_scalar_prefetch=1,
+            grid=(2, length // QB),
+            in_specs=[
+                pl.BlockSpec(block, lambda side, row, core: (0, jnp.where(side == 0, row, last), 0)),
+                pl.BlockSpec(block, lambda side, row, core: (0, jnp.where(side == 0, 0, row), 0)),
+            ],
+            out_specs=pl.BlockSpec(block, lambda side, row, core: (side ^ core[0], row, 0)),
+        ),
+        out_shape=jax.ShapeDtypeStruct((2, length, width), own.dtype),
+        name="hand_back",
+    )(core, own, arrived)
 
 
 def layer_output_kernel(groups, owners, *refs):
@@ -716,43 +736,78 @@
     )(place, *shards, *weights, gain[None])
 
 
-def token_grads_kernel(first_ref, second_ref, *refs):
-    weight_refs, (tokens_ref, residual_grad_ref, gain_ref, out_ref) = refs[:3], refs[3:]
+def halves(rows, tile, width):
+    steps = rows // tile
+    first = pl.BlockSpec((tile, width), lambda step: (jnp.minimum(step, steps - 1), 0))
+    second = pl.BlockSpec((tile, width), lambda step: (jnp.maximum(step - steps, 0), 0))
+    return [first, second], lambda first_ref, second_ref: jnp.where(pl.program_id(0) < steps, first_ref[...], second_ref[...])
+
+
+def projections_kernel(choose, first_ref, second_ref, gain_ref, *refs):
+    weight_refs, out_refs, turned_ref = refs[:3], refs[3:6], refs[6]
+    rows = choose(first_ref, second_ref).astype(jnp.float32)
+    low = (rows * norm_scale_rows(rows) * gain_ref[...]).astype(jnp.bfloat16)
+    for weight_ref, out_ref in zip(weight_refs, out_refs):
+        out_ref[...] = jnp.dot(low, weight_ref[...], preferred_element_type=jnp.float32).astype(jnp.bfloat16)
+    turned_ref[...] = low.T
+
+
+def projections_of(first, second, gain, weights):
+    rows, width = first.shape
+    tile = min(QB, rows)
+    specs, choose = halves(rows, tile, width)
+    out = jax.ShapeDtypeStruct((2 * rows, width), jnp.bfloat16)
+    return pl.pallas_call(
+        lambda *refs: projections_kernel(choose, *refs),
+        grid=(2 * rows // tile,),
+        in_specs=specs + [one_step((1, width))] + [one_step((width, width))] * 3,
+        out_specs=[pl.BlockSpec((tile, width), lambda step: (step, 0))] * 3
+        + [pl.BlockSpec((width, tile), lambda step: (0, step))],
+        out_shape=[out] * 3 + [jax.ShapeDtypeStruct((width, 2 * rows), jnp.bfloat16)],
+        compiler_params=pltpu.CompilerParams(vmem_limit_bytes=48 << 20),
+        cost_estimate=pl.CostEstimate(flops=64 * rows * width * width, bytes_accessed=16 * rows * width, transcendentals=0),
+        name="projections",
+    )(first, second, gain[None], *weights)
+
+
+def token_grads_kernel(choose, first_ref, second_ref, *refs):
+    weight_refs, (own_ref, other_ref, residual_grad_ref, gain_ref, *out_refs) = refs[:3], refs[3:]
     grad = 0.0
     for kind in range(3):
         low = jnp.concatenate([first_ref[kind], second_ref[kind]], axis=1)
         grad += lax.dot_general(low, weight_refs[kind][...], (((1,), (1,)), ((), ())), preferred_element_type=jnp.float32)
-    rows = tokens_ref[...].astype(jnp.float32)
+    rows = choose(own_ref, other_ref).astype(jnp.float32)
     scale = norm_scale_rows(rows)
     normed = rows * scale
     scaled = grad * gain_ref[...]
     shrink = jnp.mean(scaled * normed, axis=-1, keepdims=True)
-    out_ref[...] = residual_grad_ref[...] + scale * (scaled - normed * shrink)
-
-
-def token_grads(first, second, weights, tokens, residual_grad, gain):
-    length, width = tokens.shape
+    out = residual_grad_ref[...] + scale * (scaled - normed * shrink)
+    half = pl.num_programs(0) // 2
+
+    @pl.when(pl.program_id(0) < half)
+    def _():
+        out_refs[0][...] = out
+
+    @pl.when(pl.program_id(0) >= half)
+    def _():
+        out_refs[1][...] = out
+
+
+def token_grads(first, second, weights, token_groups, residual_grad, gain):
+    length, width = residual_grad.shape
     half = pl.BlockSpec((3, QB, width // 2), lambda step: (0, step, 0))
     rows = pl.BlockSpec((QB, width), lambda step: (step, 0))
+    specs, choose = halves(length // 2, QB, width)
     return pl.pallas_call(
-        token_grads_kernel,
+        lambda *refs: token_grads_kernel(choose, *refs),
         grid=(length // QB,),
-        in_specs=[half, half] + [one_step((width, width))] * 3 + [rows, rows, one_step((1, width))],
-        out_specs=rows,
-        out_shape=jax.ShapeDtypeStruct((length, width), jnp.float32),
+        in_specs=[half, half] + [one_step((width, width))] * 3 + specs + [rows, one_step((1, width))],
+        out_specs=specs,
+        out_shape=[jax.ShapeDtypeStruct((length // 2, width), jnp.float32)] * 2,
         compiler_params=pltpu.CompilerParams(vmem_limit_bytes=48 << 20),
         cost_estimate=pl.CostEstimate(flops=6 * length * width * width, bytes_accessed=14 * length * width, transcendentals=0),
         name="token_grads",
-    )(first, second, *weights, tokens, residual_grad, gain[None])
-
-
-def place_rows(slots, pieces):
-    blocks, _, length = slots.shape
-    width = pieces[0].shape[-1]
-    rows = jnp.stack(pieces).reshape(len(pieces), blocks, -1, width).swapaxes(0, 1).reshape(blocks, -1, width)
-    places = jnp.arange(rows.shape[1], dtype=jnp.int32)
-    matrix = (slots == places[None, :, None]).astype(jnp.bfloat16)
-    return jnp.einsum("bsx,bsd->bxd", matrix, rows, preferred_element_type=jnp.float32)
+    )(first, second, *weights, *token_groups, residual_grad, gain[None])
 
 
 def norm_scale(value_rows):
@@ -871,19 +926,16 @@
         ]
     )
     sorted_first, token_groups = together((sorted_upstream[0], token_groups))
-    tokens = jnp.concatenate(token_groups)
     upstream = [exchange(sorted_first, "expert", 1)]
-    inputs = tokens.astype(jnp.float32)
-    scale1 = norm_scale(inputs)
-    attn_in = (inputs * scale1 * norm1_gain).astype(jnp.bfloat16)
-    queries = wide_dot(attn_in, query_weight).astype(jnp.bfloat16)
-    keys = wide_dot(attn_in, key_weight).astype(jnp.bfloat16)
-    values = wide_dot(attn_in, value_weight).astype(jnp.bfloat16)
+    projections = (query_weight, key_weight, value_weight)
+    token_rows = [rows.reshape(-1, model_width) for rows in (token_groups if whole_seq else jnp.split(tokens, 2))]
+    queries, keys, values, turned = projections_of(*token_rows, norm1_gain, projections)
     if whole_seq:
         lines = bias_lines(bias_table)
         flat = (seq_count * local_len, model_width)
-        qkv = [rows.reshape(flat) for rows in (queries, keys, values)]
+        qkv = [queries, keys, values]
     else:
+        queries, keys, values = (rows.reshape(tokens.shape) for rows in (queries, keys, values))
         first_pos = lax.axis_index("ctx") * local_len
         keys = lax.all_gather(keys, "ctx", axis=1, tiled=True)
         values = lax.all_gather(values, "ctx", axis=1, tiled=True)
@@ -924,6 +976,9 @@
         )
         if at + 1 < len(arrived):
             result, arrived[at + 1] = together((result, arrived[at + 1]))
+        if whole_seq and at == 0:
+            seen = (jnp.concatenate(attended_groups).reshape(flat), jnp.concatenate(log_totals, axis=2), turned)
+            result, seen = together((result, seen))
         leaving = result[1]
         if back:
             result, back[-1] = together((result, back[-1]))
@@ -933,25 +988,26 @@
     grad_rows, hiddens, pre_grads, grad_router = zip(*[item[2] for item in done])
     grad_router = sum(grad_router)[:, : router_weight.shape[1]].T
     grad_experts = expert_grads(sum(arrived, []), grad_rows, hiddens, pre_grads)
-    grad_experts, back, rows_out = together((grad_experts, back, rows_out))
+
+    def back_to_attention(group, earlier):
+        return before_attention(
+            slots[group], back[group], residual1[group], cotangent[group], attended_groups[group],
+            output_weight, norm2_gain, group, len(groups), earlier,
+        )
+
+    backward = back_to_attention(0, ())
+    grad_experts, back[-1], rows_out, backward = together((grad_experts, back[-1], rows_out, backward))
     grad_experts = lax.psum_scatter(grad_experts, ("dp", "ctx"), scatter_dimension=0, tiled=True)
     if not whole_seq:
         returned = exchange(list(rows_out), "expert", -1)
-    backward = ()
-    for group in groups:
-        backward = before_attention(
-            slots[group], back[group], residual1[group], cotangent[group], attended_groups[group],
-            output_weight, norm2_gain, group, len(groups), backward,
-        )
+    for group in groups[1:]:
+        backward = back_to_attention(group, backward)
     residual_grad, mixed_grad, grad_w_output, grad_norm2 = backward
     early_small = jnp.concatenate([grad_router, grad_norm2])
-    projections = (query_weight, key_weight, value_weight)
     if whole_seq:
         half = model_width // 2
         pairs = half // 128
         mixed_grad = mixed_grad.reshape(flat)
-        turned = attn_in.reshape(flat).T
-        seen = (jnp.concatenate(attended_groups).reshape(flat), jnp.concatenate(log_totals, axis=2), turned)
         returned = exchange(list(rows_out[:-1]), "expert", -1, owners)
         first = attend_back(core, *qkv, mixed_grad, *seen, lines, 0, pairs, pairs)
         first, returned, last_rows = together((first, returned, rows_out[-1]))
@@ -979,8 +1035,8 @@
         sent_late, second_grads = together((late.sends(), second_grads))
         moved_late = late.move(sent_late)
         d_tokens = token_grads(
-            first_grads, second_grads, projections, tokens.reshape(flat), residual_grad.reshape(flat), norm1_gain
-        ).reshape(tokens.shape)
+            first_grads, second_grads, projections, token_rows, residual_grad.reshape(flat), norm1_gain
+        )
         moved, moved_late, d_tokens = together((moved, moved_late, d_tokens))
         early.take(moved)
         late.take(moved_late)
@@ -1008,6 +1064,8 @@
             lax.psum_scatter(part, "ctx", scatter_dimension=1, tiled=True).astype(jnp.bfloat16)
             for part in (key_part, value_part)
         ]
+        inputs = tokens.astype(jnp.float32)
+        attn_in = turned.T.reshape(tokens.shape)
         norm_in_grad = sum(wide_dot_back(*pair) for pair in zip(low_parts, projections))
         sums = lax.psum(
             pack_sums([grad_w_output] + [weight_dot(attn_in, rows) for rows in low_parts], early_small),
@@ -1016,7 +1074,7 @@
         grad_bias = lax.psum(diag_grad, ("dp", "ctx", "expert"))
         grad_w_output, *grad_qkv = (matrix_of(sums, kind, model_width).astype(jnp.float32) for kind in range(4))
         small = small_of(sums, 4 * model_width)
-        norm1_back, grad_norm1 = norm_back(inputs, scale1, norm1_gain, norm_in_grad)
+        norm1_back, grad_norm1 = norm_back(inputs, norm_scale(inputs), norm1_gain, norm_in_grad)
         grad_norm1 = lax.psum(grad_norm1, ("dp", "ctx", "expert"))
     grad_bias = grad_bias[: bias_table.shape[1], : bias_table.shape[0]].T
     grad_w_query, grad_w_key, grad_w_value = grad_qkv
@@ -1027,7 +1085,7 @@
         block_out = layer_output(slots, residual1, returned)[0]
         d_tokens = residual_grad + norm1_back
     if whole_seq:
-        block_out, d_tokens = hand_back(*block_out), hand_back(d_tokens[:1], d_tokens[1:])
+        block_out, d_tokens = hand_back(*block_out), hand_back(*[rows[None] for rows in d_tokens])
     grad_experts = grad_experts.astype(jnp.float32)
     return (
         block_out,

time: 465 us -> 453 us (0.974)
  starting transfers between devices: 82.2 us -> 66.6 us
  Pallas kernels: 228 us -> 241 us
  other arithmetic: 20.6 us -> 11.9 us
  waiting for transfers between devices: 54.8 us -> 60.5 us
    ppermute x18, starting transfers between devices: 60.5 us -> 45.6 us  [exchange(): lax.ppermute(piece, axis, [(at, (at + sign * turn) % size) for at in rang...]
    pallas_call x1 -> x4, Pallas kernels: 8.46 us -> 22.9 us  [the longest x1 8.77 us: token_grads(): pl.pallas_call(lambda *refs: token_grads_kernel(choose, *refs), grid=(len...]
    ppermute x18, waiting for transfers between devices: 22.2 us -> 26.9 us  [exchange(): lax.ppermute(piece, axis, [(at, (at + sign * turn) % size) for at in rang...]
    unnamed x193 -> x194, local copies, waits for them, and re-layouts: 35.2 us -> 37.8 us
  transfers between devices with their start and end apart: 44 -> 44, of which waited for: 13 -> 9; matrix products, arithmetic and copies ran while one was open for 7% -> 4% of each run, Pallas kernels for 48% -> 52%
where the time goes in v8:
time: 453 us; the launch traced here: 446 us
  Pallas kernels  241 us (53%)
  starting transfers between devices  66.6 us (15%)
  waiting for transfers between devices  60.5 us (13%)
  local copies, waits for them, and re-layouts  50.3 us (11%)
  between operations  15.2 us (3%)
  other arithmetic  11.9 us (3%)
    pallas_call x4, Pallas kernels, attend_back(): pl.pallas_call(lambda *refs: bwd_kernel(*refs[:10], *refs[10 + len(earlie...  59.7 us
    pallas_call x2, Pallas kernels, run_expert(): pl.pallas_call(lambda *refs: expert_kernel(count, *refs), grid_spec=pltpu...  59.4 us
    ppermute x18, starting transfers between devices, exchange(): lax.ppermute(piece, axis, [(at, (at + sign * turn) % size) for at in rang...  45.6 us
    unnamed x194, local copies, waits for them, and re-layouts  37.8 us
    ppermute x20, waiting for transfers between devices, swap(): lax.ppermute(part, axis, [(to, to ^ turn) for to in range(lax.axis_size(a...  33.5 us
    pallas_call x2, Pallas kernels, attend(): pl.pallas_call(lambda *refs: fwd_kernel(first // QB, *refs), grid=(width...  31.8 us
    pallas_call x1, Pallas kernels, expert_grads(): pl.pallas_call(lambda *refs: expert_grads_kernel(groups, count, *refs), g...  27.6 us
    ppermute x18, waiting for transfers between devices, exchange(): lax.ppermute(piece, axis, [(at, (at + sign * turn) % size) for at in rang...  26.9 us
  transfers between devices with their start and end apart: 44, of which 9 were waited for; matrix products, arithmetic and copies ran while one was open for 4% of the time, Pallas kernels for 52%

profile of v8, /device:TPU:0, one launch (start us, length us, event | category | flops | bytes accessed | tf_op | source)
XLA Modules:
  0.0 446.1 jit_solution(605502067962371966)
XLA Ops:
  7.3 2.5 constant_dynamic-slice_fusion.2
  13.7 3.0 collective-permute-start.3
  16.8 2.6 collective-permute-start.4
  24.5 5.6 %projections.1 = (bf16[1024,768]{1,0:T(8,128)(2,1)}, bf16[1024,768]{1,0:T(8,128)(2,1)}, bf16[1024,768]{1,0:T(8,128)(2,1)}, bf16[768,1024]{1,0:T(8,128)(2,1)}) custom-call(bf16[512,768]{1,0:T(8,128)(2,1)S(1)} %bitcast.88, bf16[512,768]{1,0:T(8,128)(2,1)S(1)} %bitcast.96, f32[1,768]{1,0:T(1,128)S(1)} %broadcast_in_dim.29.refs_2_.refs_8_.refs_7_, ...), custom_call_target="tpu_custom_call" | custom-call | flops 19327352832 | bytes 6291456 | tf_op jit(solution)/shard_map/projections/pallas_call | solution.py:760
  34.4 16.0 %attend.2 = (bf16[512,768]{1,0:T(8,128)(2,1)S(1)}, f32[6,2,512]{2,1,0:T(2,128)S(1)}) custom-call(s32[1]{0:T(128)} %bitcast.refs_0_.core_ref, f32[12,2,1024]{2,1,0:T(2,128)S(1)} %bitcast.90, bf16[1024,768]{1,0:T(8,128)(2,1)S(1)} %copy-done.6, bf16[1024,768]{1,0:T(8,128)(2,1)S(1)} %copy-done.9, bf16[1024,768]{1,0:T(8,128)(2,1)S(1)} %copy-done.12), custom_call_target="tpu_custom_call" | custom-call | flops 402653184 | bytes 1572864 | tf_op jit(solution)/shard_map/attend/pallas_call | solution.py:204
  51.0 3.2 after_attention.2
  59.4 3.0 collective-permute-start.8
  62.4 1.5 copy.66
  72.1 15.8 %attend.3 = (bf16[512,768]{1,0:T(8,128)(2,1)S(1)}, f32[6,2,512]{2,1,0:T(2,128)S(1)}) custom-call(s32[1]{0:T(128)} %bitcast.refs_0_.core_ref, f32[12,2,1024]{2,1,0:T(2,128)S(1)} %bitcast.91, bf16[1024,768]{1,0:T(8,128)(2,1)S(1)} %copy-done.7, bf16[1024,768]{1,0:T(8,128)(2,1)S(1)} %copy-done.10, bf16[1024,768]{1,0:T(8,128)(2,1)S(1)} %copy-done.13), custom_call_target="tpu_custom_call" | custom-call | flops 402653184 | bytes 1572864 | tf_op jit(solution)/shard_map/attend/pallas_call | solution.py:204
  88.0 2.8 after_attention.3
  92.7 3.3 collective-permute-start.9
  96.1 2.6 collective-permute-start.11
  98.7 29.6 %experts.2 = (bf16[512,768]{1,0:T(8,128)(2,1)S(1)}, bf16[512,768]{1,0:T(8,128)(2,1)}, bf16[512,768]{1,0:T(8,128)(2,1)}, bf16[512,768]{1,0:T(8,128)(2,1)}, bf16[2...) custom-call(s32[1]{0:T(128)} %bitcast.3.refs_0_, ...), custom_call_target="tpu_custom_call" | custom-call | flops 38654705664 | bytes 18874368 | tf_op jit(solution)/shard_map/experts/pallas_call | solution.py:398
  129.8 18.6 %collective-permute-done.10.refs_3_.refs_7_.refs_6_ = bf16[512,768]{1,0:T(8,128)(2,1)S(1)} collective-permute-done((bf16[512,768]{1,0:T(8,128)(2,1)S(1)}, bf16[512,768]{1,0:T(8,128)(2,1)S(1)}, u32[]{:S(2)}, u32[]{:S(2)}) %collective-permute-start.10) | collective-permute-done | bytes 786464 | tf_op jit(solution)/shard_map/ppermute | solution.py:625
  148.4 17.9 %collective-permute-start.12 = (bf16[256,768]{1,0:T(8,128)(2,1)S(1)}, bf16[256,768]{1,0:T(8,128)(2,1)S(1)}, u32[]{:S(2)}, u32[]{:S(2)}) collective-permute-start(bf16[256,768]{1,0:T(8,128)(2,1)S(1)} %get-tuple-element.331), channel_id=1, source_target_pairs={{0,3},{1,0},{2,1},{3,2},{4,7},{5,4},{6,5},{7,6},{8,11},{9,8},{10,9... | collective-permute-start | bytes 1179656 | tf_op jit(solution)/shard_map/ppermute | solution.py:625
  168.8 29.8 %experts.3 = (bf16[512,768]{1,0:T(8,128)(2,1)S(1)}, bf16[512,768]{1,0:T(8,128)(2,1)}, bf16[512,768]{1,0:T(8,128)(2,1)}, bf16[512,768]{1,0:T(8,128)(2,1)S(1)}, bf...) custom-call(s32[1]{0:T(128)} %bitcast.3.refs_0_, ...), custom_call_target="tpu_custom_call", output_to_operand_aliasing={{0}: (12, {}), {1}: (13, {}), {2}: (14, {}), {3}: (15, {})} | custom-call | flops 38654705664 | bytes 18874368 | tf_op jit(solution)/shard_map/experts/pallas_call | solution.py:398
  201.9 3.8 collective-permute-start.15
  207.3 8.0 %before_attention.2 = (f32[2,512,768]{2,1,0:T(8,128)}, bf16[2,512,768]{2,1,0:T(8,128)(2,1)}, f32[768,768]{1,0:T(8,128)}, f32[1,768]{1,0:T(1,128)}) custom-call(s32[1,1,512]{2,1,0:T(1,128)} %copy-done.55, bf16[256,768]{1,0:T(8,128)(2,1)} %copy-done.44, bf16[256,768]{1,0:T(8,128)(2,1)} %copy-done.86, bf16[256,768]{1,0:T(8,128)(2,1)} %copy-done.87, ...), custom_call_target="tpu_custom_call" | custom-call | tf_op jit(solution)/shard_map/before_attention/pallas_call | solution.py:603
  215.3 27.6 %expert_grads.1 = bf16[3072,1536]{1,0:T(8,128)(2,1)} custom-call(bf16[256,768]{1,0:T(8,128)(2,1)S(1)} %copy-done.50, bf16[256,768]{1,0:T(8,128)(2,1)S(1)} %collective-permute-done.6.refs_2_.refs_1_, bf16[256,768]{1,0:T(8,128)(2,1)S(1)} %collective-permute-done.7.refs_3_.refs_2_, bf16[256,768]{1,0:T(8,128)(2,1)} %collective-permute-done.8.refs_4_.refs_3_, ...), custom_call_target="tpu_custom_call" | custom-call | flops 786432 | bytes 786432 | tf_op jit(solution)/shard_map/expert_grads/pallas_call | solution.py:466
  243.9 3.7 collective-permute-start.18
  248.5 10.0 %before_attention.3 = (f32[2,512,768]{2,1,0:T(8,128)}, bf16[2,512,768]{2,1,0:T(8,128)(2,1)}, f32[768,768]{1,0:T(8,128)}, f32[1,768]{1,0:T(1,128)}) custom-call(s32[1,1,512]{2,1,0:T(1,128)} %copy-done.57, bf16[256,768]{1,0:T(8,128)(2,1)} %copy-done.43, bf16[256,768]{1,0:T(8,128)(2,1)} %copy-done.83, ...), custom_call_target="tpu_custom_call", output_to_operand_aliasing={{0}: (10, {}), {1}: (11, {})} | custom-call | tf_op jit(solution)/shard_map/before_attention/pallas_call | solution.py:603
  258.6 27.5 %attend_back.4 = (bf16[3,1024,384]{2,1,0:T(8,128)(2,1)}, bf16[2432,384]{1,0:T(8,128)(2,1)}) custom-call(s32[1]{0:T(128)} %bitcast.refs_0_.core_ref, f32[12,2,1024]{2,1,0:T(2,128)S(1)} %bitcast.92, f32[3,512,128]{2,1,0:T(8,128)S(1)} %copy-done.71, bf16[1024,768]{1,0:T(8,128)(2,1)S(1)} %copy-done.8, bf16[1024,768]{1,0:T(8,128)(2,1)S(1)} %copy-done.11, ...), custom_call_target="tpu_custom_call" | custom-call | flops 33822867456 | bytes 5505024 | tf_op jit(solution)/shard_map/attend_back/pallas_call | solution.py:297
  288.1 1.9 convert.8
  290.0 8.3 %collective-permute-done.19.refs_6_ = bf16[512,768]{1,0:T(8,128)(2,1)} collective-permute-done((bf16[512,768]{1,0:T(8,128)(2,1)}, bf16[512,768]{1,0:T(8,128)(2,1)}, u32[]{:S(2)}, u32[]{:S(2)}) %collective-permute-start.19) | collective-permute-done | bytes 786464 | tf_op jit(solution)/shard_map/ppermute | solution.py:625
  298.7 1.4 dynamic-slice_bitcast_fusion
  303.9 11.0 %attend_back.5 = (bf16[3,1024,384]{2,1,0:T(8,128)(2,1)}, bf16[2432,384]{1,0:T(8,128)(2,1)}) custom-call(s32[1]{0:T(128)} %bitcast.refs_0_.core_ref, f32[12,2,1024]{2,1,0:T(2,128)S(1)} %bitcast.93, f32[3,512,128]{2,1,0:T(8,128)S(1)} %copy-done.72, bf16[1024,768]{1,0:T(8,128)(2,1)S(1)} %copy-done.8, bf16[1024,768]{1,0:T(8,128)(2,1)S(1)} %copy-done.11, ...), custom_call_target="tpu_custom_call" | custom-call | flops 11274289152 | bytes 1835008 | tf_op jit(solution)/shard_map/attend_back/pallas_call | solution.py:297
  314.9 1.9 fusion
  316.9 1.7 collective-permute-start.21
  318.7 1.5 collective-permute-start.22
  320.5 10.7 %attend_back.6 = (bf16[3,1024,384]{2,1,0:T(8,128)(2,1)}, bf16[2432,384]{1,0:T(8,128)(2,1)}) custom-call(s32[1]{0:T(128)} %bitcast.refs_0_.core_ref, f32[12,2,1024]{2,1,0:T(2,128)S(1)} %bitcast.94, f32[3,512,128]{2,1,0:T(8,128)S(1)} %copy-done.72, bf16[1024,768]{1,0:T(8,128)(2,1)S(1)} %copy-done.8, ...), custom_call_target="tpu_custom_call", output_to_operand_aliasing={{0}: (10, {}), {1}: (11, {})} | custom-call | flops 11274289152 | bytes 1835008 | tf_op jit(solution)/shard_map/attend_back/pallas_call | solution.py:297
  331.2 7.0 %collective-permute-done.22 = bf16[512,384]{1,0:T(8,128)(2,1)S(1)} collective-permute-done((bf16[512,384]{1,0:T(8,128)(2,1)S(1)}, bf16[512,384]{1,0:T(8,128)(2,1)S(1)}, u32[]{:S(2)}, u32[]{:S(2)}) %collective-permute-start.22) | collective-permute-done | bytes 393248 | tf_op jit(solution)/shard_map/ppermute | solution.py:849
  338.6 10.5 %attend_back.7 = (bf16[3,1024,384]{2,1,0:T(8,128)(2,1)}, bf16[2432,384]{1,0:T(8,128)(2,1)}) custom-call(s32[1]{0:T(128)} %bitcast.refs_0_.core_ref, f32[12,2,1024]{2,1,0:T(2,128)S(1)} %bitcast.95, f32[3,512,128]{2,1,0:T(8,128)S(1)} %copy-done.72, bf16[1024,768]{1,0:T(8,128)(2,1)S(1)} %copy-done.8, ...), custom_call_target="tpu_custom_call", output_to_operand_aliasing={{0}: (10, {}), {1}: (11, {})} | custom-call | flops 11274289152 | bytes 1835008 | tf_op jit(solution)/shard_map/attend_back/pallas_call | solution.py:297
  350.8 3.8 collective-permute-start.28
  354.6 5.4 %layer_output.1 = (bf16[1,512,768]{2,1,0:T(8,128)(2,1)S(1)}, bf16[1,512,768]{2,1,0:T(8,128)(2,1)}) custom-call(s32[1,1,512]{2,1,0:T(1,128)S(1)} %copy-done.56, s32[1,1,512]{2,1,0:T(1,128)S(1)} %copy-done.58, f32[1,512,768]{2,1,0:T(8,128)} %copy-done.16, f32[1,512,768]{2,1,0:T(8,128)} %get-tuple-element.356.refs_5_.refs_3_, bf16[512,768]{1,0:T(8,128)(2,1)S(1)} %copy-done.36, ...), custom_call_target="tpu_custom_call" | custom-call | tf_op jit(solution)/shard_map/layer_output/pallas_call | solution.py:680
  363.0 1.4 collective-permute-start.31
  364.4 8.8 %token_grads.1 = (f32[512,768]{1,0:T(8,128)}, f32[512,768]{1,0:T(8,128)}) custom-call(bf16[3,1024,384]{2,1,0:T(8,128)(2,1)} %get-tuple-element.426.refs_0_, bf16[3,1024,384]{2,1,0:T(8,128)(2,1)} %get-tuple-element.427.refs_1_, bf16[768,768]{1,0:T(8,128)(2,1)S(1)} %copy-done.21, bf16[768,768]{1,0:T(8,128)(2,1)S(1)} %copy-done.23, ...), custom_call_target="tpu_custom_call" | custom-call | flops 3623878656 | bytes 11010048 | tf_op jit(solution)/shard_map/token_grads/pallas_call | solution.py:801
  373.2 1.4 collective-permute-done.31
  376.3 1.6 collective-permute-start.34
  379.0 2.9 collective-permute-done.36
  382.5 5.0 %collective-permute-done.33 = bf16[512,384]{1,0:T(8,128)(2,1)S(1)} collective-permute-done((bf16[512,384]{1,0:T(8,128)(2,1)S(1)}, bf16[512,384]{1,0:T(8,128)(2,1)S(1)}, u32[]{:S(2)}, u32[]{:S(2)}) %collective-permute-start.33) | collective-permute-done | bytes 393248 | tf_op jit(solution)/shard_map/ppermute | solution.py:849
  387.6 6.7 %collective-permute-done.34 = bf16[512,384]{1,0:T(8,128)(2,1)S(1)} collective-permute-done((bf16[512,384]{1,0:T(8,128)(2,1)S(1)}, bf16[512,384]{1,0:T(8,128)(2,1)S(1)}, u32[]{:S(2)}, u32[]{:S(2)}) %collective-permute-start.34) | collective-permute-done | bytes 393248 | tf_op jit(solution)/shard_map/ppermute | solution.py:849
  395.2 1.5 collective-permute-start.39
  397.2 1.5 collective-permute-start.41
  398.7 5.1 %collective-permute-done.39 = bf16[304,384]{1,0:T(8,128)(2,1)S(1)} collective-permute-done((bf16[304,384]{1,0:T(8,128)(2,1)S(1)}, bf16[304,384]{1,0:T(8,128)(2,1)S(1)}, u32[]{:S(2)}, u32[]{:S(2)}) %collective-permute-start.39) | collective-permute-done | bytes 233504 | tf_op jit(solution)/shard_map/ppermute | solution.py:849
  403.8 5.4 %collective-permute-done.40 = bf16[304,384]{1,0:T(8,128)(2,1)S(1)} collective-permute-done((bf16[304,384]{1,0:T(8,128)(2,1)S(1)}, bf16[304,384]{1,0:T(8,128)(2,1)S(1)}, u32[]{:S(2)}, u32[]{:S(2)}) %collective-permute-start.40) | collective-permute-done | bytes 233504 | tf_op jit(solution)/shard_map/ppermute | solution.py:849
  416.2 3.8 hand_back.2
  421.2 4.7 %hand_back.3 = f32[2,512,768]{2,1,0:T(8,128)} custom-call(s32[1]{0:T(128)} %bitcast.refs_0_.core_ref, f32[1,512,768]{2,1,0:T(8,128)} %bitcast.109, f32[1,512,768]{2,1,0:T(8,128)} %copy-done.80), custom_call_target="tpu_custom_call" | custom-call | tf_op jit(solution)/shard_map/hand_back/pallas_call | solution.py:647
  425.9 8.2 %weight_outputs.1 = (f32[768,768]{1,0:T(8,128)}, f32[768,768]{1,0:T(8,128)}, f32[768,768]{1,0:T(8,128)}, f32[768,768]{1,0:T(8,128)}, f32[1,768]{1,0:T(1,128)}, /*index=5*/f32[3,128,384]{2,1,0:T(8,128)}) custom-call(s32[2]{0:T(128)} %pad_add_fusion.place_ref, bf16[4,512,384]{2,1,0:T(8,128)(2,1)} %copy-done.75, bf16[4,512,384]{2,1,0:T(8,128)(2,1)} %copy-done.78, ...), custom_call_target="tpu_custom_call" | custom-call | tf_op jit(solution)/shard_map/weight_outputs/pallas_call | solution.py:725
  (301 shorter events, 69.4 us)
Async XLA Ops:
  7.2 342.1 %reduce-scatter.2.cloned.1.call-start = ((), (), s32[]{:S(2)}) async-start(), calls=%async_computation.1 | async-start | bytes 10616832 | tf_op jit(solution)/shard_map/reduce_scatter | solution.py:1000
  9.7 41.2 %copy-start.18 = (bf16[1,512,768]{2,1,0:T(8,128)(2,1)}, bf16[1,512,768]{2,1,0:T(8,128)(2,1)S(1)}, u32[]{:S(2)}) copy-start(bf16[1,512,768]{2,1,0:T(8,128)(2,1)S(1)} %get-tuple-element.240.refs_2_) | copy-start | bytes 2359300
  9.8 4.0 collective-permute-start
  11.3 53.6 %collective-permute-start.2 = (bf16[1,512,768]{2,1,0:T(8,128)(2,1)}, bf16[1,512,768]{2,1,0:T(8,128)(2,1)S(1)}, u32[]{:S(2)}, u32[]{:S(2)}) collective-permute-start(bf16[1,512,768]{2,1,0:T(8,128)(2,1)} %get-tuple-element.513), channel_id=1, source_target_pairs={{0,4},{4,0},{1,5},{5,1},{2,6},{6,2},{3,7},{7,3},{8,12},{12,8},{9,1... | collective-permute-start | bytes 2359304 | tf_op jit(solution)/shard_map/ppermute | solution.py:634
  11.3 76.6 %copy-start.51 = (f32[1,768]{1,0:T(1,128)}, f32[1,768]{1,0:T(1,128)S(1)}, u32[]{:S(2)}) copy-start(f32[1,768]{1,0:T(1,128)S(1)} %broadcast_in_dim.31.refs_4_.refs_9_) | copy-start | bytes 9220
  13.7 42.4 %collective-permute-start.3 = (bf16[256,768]{1,0:T(8,128)(2,1)S(1)}, bf16[256,768]{1,0:T(8,128)(2,1)S(1)}, u32[]{:S(2)}, u32[]{:S(2)}) collective-permute-start(bf16[256,768]{1,0:T(8,128)(2,1)S(1)} %get-tuple-element.253), channel_id=1, source_target_pairs={{0,1},{1,2},{2,3},{3,0},{4,5},{5,6},{6,7},{7,4},{8,9},{9,10},{10,1... | collective-permute-start | bytes 1179656 | tf_op jit(solution)/shard_map/ppermute | solution.py:625
  16.8 40.1 %collective-permute-start.4 = (bf16[256,768]{1,0:T(8,128)(2,1)S(1)}, bf16[256,768]{1,0:T(8,128)(2,1)S(1)}, u32[]{:S(2)}, u32[]{:S(2)}) collective-permute-start(bf16[256,768]{1,0:T(8,128)(2,1)S(1)} %get-tuple-element.254), channel_id=1, source_target_pairs={{0,2},{1,3},{2,0},{3,1},{4,6},{5,7},{6,4},{7,5},{8,10},{9,11},{10,... | collective-permute-start | bytes 1179656 | tf_op jit(solution)/shard_map/ppermute | solution.py:625
  19.3 38.3 %collective-permute-start.5 = (bf16[256,768]{1,0:T(8,128)(2,1)S(1)}, bf16[256,768]{1,0:T(8,128)(2,1)S(1)}, u32[]{:S(2)}, u32[]{:S(2)}) collective-permute-start(bf16[256,768]{1,0:T(8,128)(2,1)S(1)} %get-tuple-element.255), channel_id=1, source_target_pairs={{0,3},{1,0},{2,1},{3,2},{4,7},{5,4},{6,5},{7,6},{8,11},{9,8},{10,9... | collective-permute-start | bytes 1179656 | tf_op jit(solution)/shard_map/ppermute | solution.py:625
  50.9 40.5 %copy-start.5 = (bf16[512,768]{1,0:T(8,128)(2,1)}, bf16[512,768]{1,0:T(8,128)(2,1)S(1)}, u32[]{:S(2)}) copy-start(bf16[512,768]{1,0:T(8,128)(2,1)S(1)} %get-tuple-element.247) | copy-start | bytes 2359300
  58.4 34.4 %collective-permute-start.6 = (bf16[256,768]{1,0:T(8,128)(2,1)}, bf16[256,768]{1,0:T(8,128)(2,1)S(1)}, u32[]{:S(2)}, u32[]{:S(2)}) collective-permute-start(bf16[256,768]{1,0:T(8,128)(2,1)} %get-tuple-element.267), channel_id=1, source_target_pairs={{0,1},{1,2},{2,3},{3,0},{4,5},{5,6},{6,7},{7,4},{8,9},{9,10},{10,1... | collective-permute-start | bytes 1179656 | tf_op jit(solution)/shard_map/ppermute | solution.py:625
  59.0 33.7 %collective-permute-start.7 = (bf16[256,768]{1,0:T(8,128)(2,1)}, bf16[256,768]{1,0:T(8,128)(2,1)S(1)}, u32[]{:S(2)}, u32[]{:S(2)}) collective-permute-start(bf16[256,768]{1,0:T(8,128)(2,1)} %get-tuple-element.268), channel_id=1, source_target_pairs={{0,2},{1,3},{2,0},{3,1},{4,6},{5,7},{6,4},{7,5},{8,10},{9,11},{10,... | collective-permute-start | bytes 1179656 | tf_op jit(solution)/shard_map/ppermute | solution.py:625
  59.4 33.4 %collective-permute-start.8 = (bf16[256,768]{1,0:T(8,128)(2,1)}, bf16[256,768]{1,0:T(8,128)(2,1)}, u32[]{:S(2)}, u32[]{:S(2)}) collective-permute-start(bf16[256,768]{1,0:T(8,128)(2,1)} %get-tuple-element.269), channel_id=1, source_target_pairs={{0,3},{1,0},{2,1},{3,2},{4,7},{5,4},{6,5},{7,6},{8,11},{9,8},{10,9... | collective-permute-start | bytes 1179656 | tf_op jit(solution)/shard_map/ppermute | solution.py:625
  62.4 2.5 collective-permute-start.1
  92.7 37.0 %collective-permute-start.9 = (bf16[512,768]{1,0:T(8,128)(2,1)S(1)}, bf16[512,768]{1,0:T(8,128)(2,1)S(1)}, u32[]{:S(2)}, u32[]{:S(2)}) collective-permute-start(bf16[512,768]{1,0:T(8,128)(2,1)S(1)} %get-tuple-element.291), channel_id=1, source_target_pairs={{0,1},{1,2},{2,3},{3,0},{4,5},{5,6},{6,7},{7,4},{8,9},{9,10},{10,1... | collective-permute-start | bytes 2359304 | tf_op jit(solution)/shard_map/ppermute | solution.py:625
  96.1 52.3 %collective-permute-start.10 = (bf16[512,768]{1,0:T(8,128)(2,1)S(1)}, bf16[512,768]{1,0:T(8,128)(2,1)S(1)}, u32[]{:S(2)}, u32[]{:S(2)}) collective-permute-start(bf16[512,768]{1,0:T(8,128)(2,1)S(1)} %get-tuple-element.292), channel_id=1, source_target_pairs={{0,2},{1,3},{2,0},{3,1},{4,6},{5,7},{6,4},{7,5},{8,10},{9,11},{10,... | collective-permute-start | bytes 2359304 | tf_op jit(solution)/shard_map/ppermute | solution.py:625
  96.1 52.3 %collective-permute-start.11 = (bf16[512,768]{1,0:T(8,128)(2,1)S(1)}, bf16[512,768]{1,0:T(8,128)(2,1)S(1)}, u32[]{:S(2)}, u32[]{:S(2)}) collective-permute-start(bf16[512,768]{1,0:T(8,128)(2,1)S(1)} %get-tuple-element.293), channel_id=1, source_target_pairs={{0,3},{1,0},{2,1},{3,2},{4,7},{5,4},{6,5},{7,6},{8,11},{9,8},{10,9... | collective-permute-start | bytes 2359304 | tf_op jit(solution)/shard_map/ppermute | solution.py:625
  129.8 37.9 %copy-start.37 = (bf16[512,768]{1,0:T(8,128)(2,1)}, bf16[512,768]{1,0:T(8,128)(2,1)S(1)}, u32[]{:S(2)}) copy-start(bf16[512,768]{1,0:T(8,128)(2,1)S(1)} %collective-permute-done.9.refs_2_.refs_6_.refs_5_) | copy-start | bytes 2359300
  148.4 57.5 %collective-permute-start.12 = (bf16[256,768]{1,0:T(8,128)(2,1)S(1)}, bf16[256,768]{1,0:T(8,128)(2,1)S(1)}, u32[]{:S(2)}, u32[]{:S(2)}) collective-permute-start(bf16[256,768]{1,0:T(8,128)(2,1)S(1)} %get-tuple-element.331), channel_id=1, source_target_pairs={{0,3},{1,0},{2,1},{3,2},{4,7},{5,4},{6,5},{7,6},{8,11},{9,8},{10,9... | collective-permute-start | bytes 1179656 | tf_op jit(solution)/shard_map/ppermute | solution.py:625
  166.3 40.1 %collective-permute-start.13 = (bf16[256,768]{1,0:T(8,128)(2,1)S(1)}, bf16[256,768]{1,0:T(8,128)(2,1)S(1)}, u32[]{:S(2)}, u32[]{:S(2)}) collective-permute-start(bf16[256,768]{1,0:T(8,128)(2,1)S(1)} %get-tuple-element.332), channel_id=1, source_target_pairs={{0,2},{1,3},{2,0},{3,1},{4,6},{5,7},{6,4},{7,5},{8,10},{9,11},{10,... | collective-permute-start | bytes 1179656 | tf_op jit(solution)/shard_map/ppermute | solution.py:625
  167.2 39.2 %collective-permute-start.14 = (bf16[256,768]{1,0:T(8,128)(2,1)S(1)}, bf16[256,768]{1,0:T(8,128)(2,1)S(1)}, u32[]{:S(2)}, u32[]{:S(2)}) collective-permute-start(bf16[256,768]{1,0:T(8,128)(2,1)S(1)} %get-tuple-element.333), channel_id=1, source_target_pairs={{0,1},{1,2},{2,3},{3,0},{4,5},{5,6},{6,7},{7,4},{8,9},{9,10},{10,1... | collective-permute-start | bytes 1179656 | tf_op jit(solution)/shard_map/ppermute | solution.py:625
  201.9 41.0 %collective-permute-start.15 = (bf16[256,768]{1,0:T(8,128)(2,1)S(1)}, bf16[256,768]{1,0:T(8,128)(2,1)S(1)}, u32[]{:S(2)}, u32[]{:S(2)}) collective-permute-start(bf16[256,768]{1,0:T(8,128)(2,1)S(1)} %get-tuple-element.323), channel_id=1, source_target_pairs={{0,3},{1,0},{2,1},{3,2},{4,7},{5,4},{6,5},{7,6},{8,11},{9,8},{10,9... | collective-permute-start | bytes 1179656 | tf_op jit(solution)/shard_map/ppermute | solution.py:625
  205.7 37.3 %collective-permute-start.16 = (bf16[256,768]{1,0:T(8,128)(2,1)S(1)}, bf16[256,768]{1,0:T(8,128)(2,1)S(1)}, u32[]{:S(2)}, u32[]{:S(2)}) collective-permute-start(bf16[256,768]{1,0:T(8,128)(2,1)S(1)} %get-tuple-element.324), channel_id=1, source_target_pairs={{0,2},{1,3},{2,0},{3,1},{4,6},{5,7},{6,4},{7,5},{8,10},{9,11},{10,... | collective-permute-start | bytes 1179656 | tf_op jit(solution)/shard_map/ppermute | solution.py:625
  205.9 37.0 %collective-permute-start.17 = (bf16[256,768]{1,0:T(8,128)(2,1)S(1)}, bf16[256,768]{1,0:T(8,128)(2,1)S(1)}, u32[]{:S(2)}, u32[]{:S(2)}) collective-permute-start(bf16[256,768]{1,0:T(8,128)(2,1)S(1)} %get-tuple-element.325), channel_id=1, source_target_pairs={{0,1},{1,2},{2,3},{3,0},{4,5},{5,6},{6,7},{7,4},{8,9},{9,10},{10,1... | collective-permute-start | bytes 1179656 | tf_op jit(solution)/shard_map/ppermute | solution.py:625
  243.9 46.1 %collective-permute-start.18 = (bf16[512,768]{1,0:T(8,128)(2,1)}, bf16[512,768]{1,0:T(8,128)(2,1)}, u32[]{:S(2)}, u32[]{:S(2)}) collective-permute-start(bf16[512,768]{1,0:T(8,128)(2,1)} %get-tuple-element.368), channel_id=1, source_target_pairs={{0,3},{1,0},{2,1},{3,2},{4,7},{5,4},{6,5},{7,6},{8,11},{9,8},{10,9... | collective-permute-start | bytes 2359304 | tf_op jit(solution)/shard_map/ppermute | solution.py:625
  247.6 50.7 %collective-permute-start.19 = (bf16[512,768]{1,0:T(8,128)(2,1)}, bf16[512,768]{1,0:T(8,128)(2,1)}, u32[]{:S(2)}, u32[]{:S(2)}) collective-permute-start(bf16[512,768]{1,0:T(8,128)(2,1)} %get-tuple-element.369), channel_id=1, source_target_pairs={{0,2},{1,3},{2,0},{3,1},{4,6},{5,7},{6,4},{7,5},{8,10},{9,11},{10,... | collective-permute-start | bytes 2359304 | tf_op jit(solution)/shard_map/ppermute | solution.py:625
  300.9 14.0 %collective-permute-start.20 = (bf16[4,512,384]{2,1,0:T(8,128)(2,1)}, bf16[4,512,384]{2,1,0:T(8,128)(2,1)}, u32[]{:S(2)}, u32[]{:S(2)}) collective-permute-start(bf16[4,512,384]{2,1,0:T(8,128)(2,1)} %dynamic-slice_bitcast_fusion), channel_id=1, source_target_pairs={{0,4},{4,0},{1,5},{5,1},{2,6},{6,2},{3,7},{7,3},{8,12},{12,8},{9,1... | collective-permute-start | bytes 4718600 | tf_op jit(solution)/shard_map/ppermute | solution.py:849
  300.9 30.3 %collective-permute-start.24 = (bf16[512,768]{1,0:T(8,128)(2,1)}, bf16[512,768]{1,0:T(8,128)(2,1)S(1)}, u32[]{:S(2)}, u32[]{:S(2)}) collective-permute-start(bf16[512,768]{1,0:T(8,128)(2,1)} %copy-done.62), channel_id=1, source_target_pairs={{0,1},{1,2},{2,3},{3,0},{4,5},{5,6},{6,7},{7,4},{8,9},{9,10},{10,1... | collective-permute-start | bytes 2359304 | tf_op jit(solution)/shard_map/ppermute | solution.py:625
  316.9 14.3 %collective-permute-start.21 = (bf16[512,384]{1,0:T(8,128)(2,1)S(1)}, bf16[512,384]{1,0:T(8,128)(2,1)S(1)}, u32[]{:S(2)}, u32[]{:S(2)}) collective-permute-start(bf16[512,384]{1,0:T(8,128)(2,1)S(1)} %get-tuple-element.386), channel_id=1, source_target_pairs={{0,8},{8,0},{16,24},{24,16},{1,9},{9,1},{17,25},{25,17},{2,10},{10... | collective-permute-start | bytes 1179656 | tf_op jit(solution)/shard_map/ppermute | solution.py:849
  318.7 19.5 %collective-permute-start.22 = (bf16[512,384]{1,0:T(8,128)(2,1)S(1)}, bf16[512,384]{1,0:T(8,128)(2,1)S(1)}, u32[]{:S(2)}, u32[]{:S(2)}) collective-permute-start(bf16[512,384]{1,0:T(8,128)(2,1)S(1)} %get-tuple-element.387), channel_id=1, source_target_pairs={{0,16},{8,24},{16,0},{24,8},{1,17},{9,25},{17,1},{25,9},{2,18},{10... | collective-permute-start | bytes 1179656 | tf_op jit(solution)/shard_map/ppermute | solution.py:849
  320.2 18.0 %collective-permute-start.23 = (bf16[512,384]{1,0:T(8,128)(2,1)S(1)}, bf16[512,384]{1,0:T(8,128)(2,1)S(1)}, u32[]{:S(2)}, u32[]{:S(2)}) collective-permute-start(bf16[512,384]{1,0:T(8,128)(2,1)S(1)} %get-tuple-element.388), channel_id=1, source_target_pairs={{0,24},{8,16},{16,8},{24,0},{1,25},{9,17},{17,9},{25,1},{2,26},{10... | collective-permute-start | bytes 1179656 | tf_op jit(solution)/shard_map/ppermute | solution.py:849
  338.4 10.8 %collective-permute-start.25 = (bf16[512,384]{1,0:T(8,128)(2,1)S(1)}, bf16[512,384]{1,0:T(8,128)(2,1)S(1)}, u32[]{:S(2)}, u32[]{:S(2)}) collective-permute-start(bf16[512,384]{1,0:T(8,128)(2,1)S(1)} %fusion.4), channel_id=1, source_target_pairs={{0,1},{1,0},{2,3},{3,2},{4,5},{5,4},{6,7},{7,6},{8,9},{9,8},{10,11... | collective-permute-start | bytes 1179656 | tf_op jit(solution)/shard_map/ppermute | solution.py:849
  350.7 9.3 %collective-permute-start.26 = (bf16[4,304,384]{2,1,0:T(8,128)(2,1)S(1)}, bf16[4,304,384]{2,1,0:T(8,128)(2,1)S(1)}, u32[]{:S(2)}, u32[]{:S(2)}) collective-permute-start(bf16[4,304,384]{2,1,0:T(8,128)(2,1)S(1)} %dynamic-slice_bitcast_fusion.1), channel_id=1, source_target_pairs={{0,4},{4,0},{1,5},{5,1},{2,6},{6,2},{3,7},{7,3},{8,12},{12,8},{9,1... | collective-permute-start | bytes 2801672 | tf_op jit(solution)/shard_map/ppermute | solution.py:849
  350.8 22.4 %collective-permute-start.28 = (bf16[512,384]{1,0:T(8,128)(2,1)S(1)}, bf16[512,384]{1,0:T(8,128)(2,1)S(1)}, u32[]{:S(2)}, u32[]{:S(2)}) collective-permute-start(bf16[512,384]{1,0:T(8,128)(2,1)S(1)} %add_convert_fusion.1), channel_id=1, source_target_pairs={{0,2},{1,3},{2,0},{3,1},{4,6},{5,7},{6,4},{7,5},{8,10},{9,11},{10,... | collective-permute-start | bytes 1179656 | tf_op jit(solution)/shard_map/ppermute | solution.py:849
  360.9 12.3 %collective-permute-start.29 = (bf16[304,384]{1,0:T(8,128)(2,1)S(1)}, bf16[304,384]{1,0:T(8,128)(2,1)S(1)}, u32[]{:S(2)}, u32[]{:S(2)}) collective-permute-start(bf16[304,384]{1,0:T(8,128)(2,1)S(1)} %get-tuple-element.423), channel_id=1, source_target_pairs={{0,8},{8,0},{16,24},{24,16},{1,9},{9,1},{17,25},{25,17},{2,10},{10... | collective-permute-start | bytes 700424 | tf_op jit(solution)/shard_map/ppermute | solution.py:849
  362.2 11.0 %collective-permute-start.30 = (bf16[304,384]{1,0:T(8,128)(2,1)S(1)}, bf16[304,384]{1,0:T(8,128)(2,1)S(1)}, u32[]{:S(2)}, u32[]{:S(2)}) collective-permute-start(bf16[304,384]{1,0:T(8,128)(2,1)S(1)} %get-tuple-element.424), channel_id=1, source_target_pairs={{0,16},{8,24},{16,0},{24,8},{1,17},{9,25},{17,1},{25,9},{2,18},{10... | collective-permute-start | bytes 700424 | tf_op jit(solution)/shard_map/ppermute | solution.py:849
  363.0 11.7 %collective-permute-start.31 = (bf16[304,384]{1,0:T(8,128)(2,1)S(1)}, bf16[304,384]{1,0:T(8,128)(2,1)S(1)}, u32[]{:S(2)}, u32[]{:S(2)}) collective-permute-start(bf16[304,384]{1,0:T(8,128)(2,1)S(1)} %get-tuple-element.425), channel_id=1, source_target_pairs={{0,24},{8,16},{16,8},{24,0},{1,25},{9,17},{17,9},{25,1},{2,26},{10... | collective-permute-start | bytes 700424 | tf_op jit(solution)/shard_map/ppermute | solution.py:849
  374.9 7.0 %collective-permute-start.36 = (bf16[304,384]{1,0:T(8,128)(2,1)S(1)}, bf16[304,384]{1,0:T(8,128)(2,1)S(1)}, u32[]{:S(2)}, u32[]{:S(2)}) collective-permute-start(bf16[304,384]{1,0:T(8,128)(2,1)S(1)} %fusion.7), channel_id=1, source_target_pairs={{0,1},{1,0},{2,3},{3,2},{4,5},{5,4},{6,7},{7,6},{8,9},{9,8},{10,11... | collective-permute-start | bytes 700424 | tf_op jit(solution)/shard_map/ppermute | solution.py:849
  375.5 12.1 %collective-permute-start.33 = (bf16[512,384]{1,0:T(8,128)(2,1)S(1)}, bf16[512,384]{1,0:T(8,128)(2,1)S(1)}, u32[]{:S(2)}, u32[]{:S(2)}) collective-permute-start(bf16[512,384]{1,0:T(8,128)(2,1)S(1)} %add_convert_fusion), channel_id=1, source_target_pairs={{0,8},{8,0},{16,24},{24,16},{1,9},{9,1},{17,25},{25,17},{2,10},{10... | collective-permute-start | bytes 1179656 | tf_op jit(solution)/shard_map/ppermute | solution.py:849
  376.3 18.0 %collective-permute-start.34 = (bf16[512,384]{1,0:T(8,128)(2,1)S(1)}, bf16[512,384]{1,0:T(8,128)(2,1)S(1)}, u32[]{:S(2)}, u32[]{:S(2)}) collective-permute-start(bf16[512,384]{1,0:T(8,128)(2,1)S(1)} %add_convert_fusion), channel_id=1, source_target_pairs={{0,16},{8,24},{16,0},{24,8},{1,17},{9,25},{17,1},{25,9},{2,18},{10... | collective-permute-start | bytes 1179656 | tf_op jit(solution)/shard_map/ppermute | solution.py:849
  377.9 16.4 %collective-permute-start.35 = (bf16[512,384]{1,0:T(8,128)(2,1)S(1)}, bf16[512,384]{1,0:T(8,128)(2,1)S(1)}, u32[]{:S(2)}, u32[]{:S(2)}) collective-permute-start(bf16[512,384]{1,0:T(8,128)(2,1)S(1)} %add_convert_fusion), channel_id=1, source_target_pairs={{0,24},{8,16},{16,8},{24,0},{1,25},{9,17},{17,9},{25,1},{2,26},{10... | collective-permute-start | bytes 1179656 | tf_op jit(solution)/shard_map/ppermute | solution.py:849
  382.0 12.3 %collective-permute-start.37 = (bf16[304,384]{1,0:T(8,128)(2,1)S(1)}, bf16[304,384]{1,0:T(8,128)(2,1)S(1)}, u32[]{:S(2)}, u32[]{:S(2)}) collective-permute-start(bf16[304,384]{1,0:T(8,128)(2,1)S(1)} %add_convert_fusion.3), channel_id=1, source_target_pairs={{0,2},{1,3},{2,0},{3,1},{4,6},{5,7},{6,4},{7,5},{8,10},{9,11},{10,... | collective-permute-start | bytes 700424 | tf_op jit(solution)/shard_map/ppermute | solution.py:849
  394.6 14.5 %collective-permute-start.38 = (bf16[4,512,384]{2,1,0:T(8,128)(2,1)S(1)}, bf16[4,512,384]{2,1,0:T(8,128)(2,1)S(1)}, u32[]{:S(2)}, u32[]{:S(2)}) collective-permute-start(bf16[4,512,384]{2,1,0:T(8,128)(2,1)S(1)} %pad_maximum_fusion.1.refs_0_), channel_id=1, source_target_pairs={{0,4},{4,0},{1,5},{5,1},{2,6},{6,2},{3,7},{7,3},{8,12},{12,8},{9,1... | collective-permute-start | bytes 4718600 | tf_op jit(solution)/shard_map/ppermute | solution.py:849
  394.7 25.3 %collective-permute-start.32 = (f32[1,512,768]{2,1,0:T(8,128)}, f32[1,512,768]{2,1,0:T(8,128)S(1)}, u32[]{:S(2)}, u32[]{:S(2)}) collective-permute-start(f32[1,512,768]{2,1,0:T(8,128)} %bitcast.30), channel_id=1, source_target_pairs={{0,4},{4,0},{1,5},{5,1},{2,6},{6,2},{3,7},{7,3},{8,12},{12,8},{9,1... | collective-permute-start | bytes 4718600 | tf_op jit(solution)/shard_map/ppermute | solution.py:642
  395.2 8.5 %collective-permute-start.39 = (bf16[304,384]{1,0:T(8,128)(2,1)S(1)}, bf16[304,384]{1,0:T(8,128)(2,1)S(1)}, u32[]{:S(2)}, u32[]{:S(2)}) collective-permute-start(bf16[304,384]{1,0:T(8,128)(2,1)S(1)} %add_convert_fusion.2), channel_id=1, source_target_pairs={{0,8},{8,0},{16,24},{24,16},{1,9},{9,1},{17,25},{25,17},{2,10},{10... | collective-permute-start | bytes 700424 | tf_op jit(solution)/shard_map/ppermute | solution.py:849
  396.7 12.4 %collective-permute-start.40 = (bf16[304,384]{1,0:T(8,128)(2,1)S(1)}, bf16[304,384]{1,0:T(8,128)(2,1)S(1)}, u32[]{:S(2)}, u32[]{:S(2)}) collective-permute-start(bf16[304,384]{1,0:T(8,128)(2,1)S(1)} %add_convert_fusion.2), channel_id=1, source_target_pairs={{0,16},{8,24},{16,0},{24,8},{1,17},{9,25},{17,1},{25,9},{2,18},{10... | collective-permute-start | bytes 700424 | tf_op jit(solution)/shard_map/ppermute | solution.py:849
  397.2 11.9 %collective-permute-start.41 = (bf16[304,384]{1,0:T(8,128)(2,1)S(1)}, bf16[304,384]{1,0:T(8,128)(2,1)S(1)}, u32[]{:S(2)}, u32[]{:S(2)}) collective-permute-start(bf16[304,384]{1,0:T(8,128)(2,1)S(1)} %add_convert_fusion.2), channel_id=1, source_target_pairs={{0,24},{8,16},{16,8},{24,0},{1,25},{9,17},{17,9},{25,1},{2,26},{10... | collective-permute-start | bytes 700424 | tf_op jit(solution)/shard_map/ppermute | solution.py:849
  411.4 14.5 %collective-permute-start.42 = (bf16[4,304,384]{2,1,0:T(8,128)(2,1)}, bf16[4,304,384]{2,1,0:T(8,128)(2,1)}, u32[]{:S(2)}, u32[]{:S(2)}) collective-permute-start(bf16[4,304,384]{2,1,0:T(8,128)(2,1)} %pad_maximum_fusion.2.refs_2_), channel_id=1, source_target_pairs={{0,4},{4,0},{1,5},{5,1},{2,6},{6,2},{3,7},{7,3},{8,12},{12,8},{9,1... | collective-permute-start | bytes 2801672 | tf_op jit(solution)/shard_map/ppermute | solution.py:849
  411.4 3.9 collective-permute-start.27
  (90 other events, 585.3 us)
Sparse Core Ops, SparseCore 0:
  243.1 77.6 reduce-scatter.1

commit v9 on v8

--- a/solution.py
+++ b/solution.py
@@ -320,7 +320,7 @@
             pltpu.VMEM((length, 128), jnp.float32),
             pltpu.VMEM((length, 128), jnp.float32),
         ],
-        compiler_params=pltpu.CompilerParams(vmem_limit_bytes=48 << 20),
+        compiler_params=pltpu.CompilerParams(vmem_limit_bytes=60 << 20),
         cost_estimate=pl.CostEstimate(
             flops=84 * length * length * 128 * pairs, bytes_accessed=14 * length * 128 * pairs, transcendentals=2 * length * length * pairs
         ),
@@ -425,7 +425,7 @@
         out_shape=[low(group_count * tile, width)] * count
         + [low(tile, width)] * count
         + [low(rows, width), low(rows, inner), low(rows, inner), jax.ShapeDtypeStruct((width, 128), jnp.float32)],
-        compiler_params=pltpu.CompilerParams(vmem_limit_bytes=48 << 20),
+        compiler_params=pltpu.CompilerParams(vmem_limit_bytes=60 << 20),
         cost_estimate=pl.CostEstimate(flops=16 * rows * width * inner, bytes_accessed=8 * width * inner, transcendentals=rows * inner),
         input_output_aliases={2 * count + 4 + at: at for at in range(len(earlier))},
         name="experts",
@@ -472,7 +472,7 @@
         out_specs=pl.BlockSpec((chunk, 2 * width), lambda f: (f, 0)),
         out_shape=jax.ShapeDtypeStruct((inner, 2 * width), jnp.bfloat16),
         scratch_shapes=[pltpu.VMEM((width, groups * rows), jnp.bfloat16)] * 2,
-        compiler_params=pltpu.CompilerParams(vmem_limit_bytes=48 << 20),
+        compiler_params=pltpu.CompilerParams(vmem_limit_bytes=60 << 20),
         cost_estimate=pl.CostEstimate(flops=rows * width, bytes_accessed=rows * width, transcendentals=0),
         name="expert_grads",
     )(*pieces, *grads, *hiddens, *pre_grads)
@@ -996,7 +996,9 @@
         )
 
     backward = back_to_attention(0, ())
-    grad_experts, back[-1], rows_out, backward = together((grad_experts, back[-1], rows_out, backward))
+    grad_experts, back[-1], rows_out, backward, grad_router = together(
+        (grad_experts, back[-1], rows_out, backward, grad_router)
+    )
     grad_experts = lax.psum_scatter(grad_experts, ("dp", "ctx"), scatter_dimension=0, tiled=True)
     if not whole_seq:
         returned = exchange(list(rows_out), "expert", -1)

time: 453 us -> 448 us (0.989)
  local copies, waits for them, and re-layouts: 50.3 us -> 37.5 us
  Pallas kernels: 241 us -> 247 us
    unnamed x194 -> x144, local copies, waits for them, and re-layouts: 37.8 us -> 26.3 us
  transfers between devices with their start and end apart: 44 -> 44, of which waited for: 9 -> 9; matrix products, arithmetic and copies ran while one was open for 4% -> 4% of each run, Pallas kernels for 52% -> 54%
where the time goes in v9:
time: 448 us; the launch traced here: 441 us
  Pallas kernels  247 us (55%)
  starting transfers between devices  68.1 us (15%)
  waiting for transfers between devices  60.9 us (14%)
  local copies, waits for them, and re-layouts  37.5 us (8%)
  between operations  15.1 us (3%)
  other arithmetic  12 us (3%)
    pallas_call x2, Pallas kernels, run_expert(): pl.pallas_call(lambda *refs: expert_kernel(count, *refs), grid_spec=pltpu...  62 us
    pallas_call x4, Pallas kernels, attend_back(): pl.pallas_call(lambda *refs: bwd_kernel(*refs[:10], *refs[10 + len(earlie...  60.9 us
    ppermute x18, starting transfers between devices, exchange(): lax.ppermute(piece, axis, [(at, (at + sign * turn) % size) for at in rang...  46 us
    ppermute x20, waiting for transfers between devices, swap(): lax.ppermute(part, axis, [(to, to ^ turn) for to in range(lax.axis_size(a...  32.6 us
    pallas_call x2, Pallas kernels, attend(): pl.pallas_call(lambda *refs: fwd_kernel(first // QB, *refs), grid=(width...  31.8 us
    pallas_call x1, Pallas kernels, expert_grads(): pl.pallas_call(lambda *refs: expert_grads_kernel(groups, count, *refs), g...  28.6 us
    ppermute x18, waiting for transfers between devices, exchange(): lax.ppermute(piece, axis, [(at, (at + sign * turn) % size) for at in rang...  28.2 us
    unnamed x144, local copies, waits for them, and re-layouts  26.3 us
  transfers between devices with their start and end apart: 44, of which 9 were waited for; matrix products, arithmetic and copies ran while one was open for 4% of the time, Pallas kernels for 54%

profile of v9, /device:TPU:0, one launch (start us, length us, event | category | flops | bytes accessed | tf_op | source)
XLA Modules:
  0.0 440.6 jit_solution(11297985934134525649)
XLA Ops:
  7.3 2.5 constant_dynamic-slice_fusion.2
  13.0 3.1 collective-permute-start.3
  16.1 2.6 collective-permute-start.4
  23.8 5.6 %projections.1 = (bf16[1024,768]{1,0:T(8,128)(2,1)}, bf16[1024,768]{1,0:T(8,128)(2,1)}, bf16[1024,768]{1,0:T(8,128)(2,1)}, bf16[768,1024]{1,0:T(8,128)(2,1)}) custom-call(bf16[512,768]{1,0:T(8,128)(2,1)S(1)} %bitcast.88, bf16[512,768]{1,0:T(8,128)(2,1)S(1)} %bitcast.96, f32[1,768]{1,0:T(1,128)S(1)} %broadcast_in_dim.29.refs_2_.refs_8_.refs_7_, ...), custom_call_target="tpu_custom_call" | custom-call | flops 19327352832 | bytes 6291456 | tf_op jit(solution)/shard_map/projections/pallas_call | solution.py:760
  33.7 16.0 %attend.2 = (bf16[512,768]{1,0:T(8,128)(2,1)S(1)}, f32[6,2,512]{2,1,0:T(2,128)S(1)}) custom-call(s32[1]{0:T(128)} %bitcast.refs_0_.core_ref, f32[12,2,1024]{2,1,0:T(2,128)S(1)} %bitcast.90, bf16[1024,768]{1,0:T(8,128)(2,1)S(1)} %copy-done.6, bf16[1024,768]{1,0:T(8,128)(2,1)S(1)} %copy-done.8, bf16[1024,768]{1,0:T(8,128)(2,1)S(1)} %copy-done.10), custom_call_target="tpu_custom_call" | custom-call | flops 402653184 | bytes 1572864 | tf_op jit(solution)/shard_map/attend/pallas_call | solution.py:204
  50.3 3.2 after_attention.2
  56.5 3.0 collective-permute-start.8
  61.2 2.0 sort_upstream.3
  68.4 15.8 %attend.3 = (bf16[512,768]{1,0:T(8,128)(2,1)S(1)}, f32[6,2,512]{2,1,0:T(2,128)S(1)}) custom-call(s32[1]{0:T(128)} %bitcast.refs_0_.core_ref, f32[12,2,1024]{2,1,0:T(2,128)S(1)} %bitcast.95, bf16[1024,768]{1,0:T(8,128)(2,1)S(1)} %copy-done.7, bf16[1024,768]{1,0:T(8,128)(2,1)S(1)} %copy-done.9, bf16[1024,768]{1,0:T(8,128)(2,1)S(1)} %copy-done.11), custom_call_target="tpu_custom_call" | custom-call | flops 402653184 | bytes 1572864 | tf_op jit(solution)/shard_map/attend/pallas_call | solution.py:204
  84.2 3.2 after_attention.3
  89.5 3.7 collective-permute-start.9
  93.3 2.6 collective-permute-start.11
  95.8 31.0 %experts.2 = (bf16[512,768]{1,0:T(8,128)(2,1)}, bf16[512,768]{1,0:T(8,128)(2,1)}, bf16[512,768]{1,0:T(8,128)(2,1)}, bf16[512,768]{1,0:T(8,128)(2,1)}, bf16[256,7...) custom-call(s32[1]{0:T(128)} %bitcast.3.refs_0_, ...), custom_call_target="tpu_custom_call" | custom-call | flops 38654705664 | bytes 18874368 | tf_op jit(solution)/shard_map/experts/pallas_call | solution.py:398
  126.8 18.6 %collective-permute-done.10.refs_3_.refs_7_.refs_6_ = bf16[512,768]{1,0:T(8,128)(2,1)S(1)} collective-permute-done((bf16[512,768]{1,0:T(8,128)(2,1)}, bf16[512,768]{1,0:T(8,128)(2,1)S(1)}, u32[]{:S(2)}, u32[]{:S(2)}) %collective-permute-start.10) | collective-permute-done | bytes 786464 | tf_op jit(solution)/shard_map/ppermute | solution.py:625
  145.4 18.2 %collective-permute-start.12 = (bf16[256,768]{1,0:T(8,128)(2,1)}, bf16[256,768]{1,0:T(8,128)(2,1)S(1)}, u32[]{:S(2)}, u32[]{:S(2)}) collective-permute-start(bf16[256,768]{1,0:T(8,128)(2,1)} %get-tuple-element.332), channel_id=1, source_target_pairs={{0,3},{1,0},{2,1},{3,2},{4,7},{5,4},{6,5},{7,6},{8,11},{9,8},{10,9... | collective-permute-start | bytes 1179656 | tf_op jit(solution)/shard_map/ppermute | solution.py:625
  164.7 31.0 %experts.3 = (bf16[512,768]{1,0:T(8,128)(2,1)}, bf16[512,768]{1,0:T(8,128)(2,1)}, bf16[512,768]{1,0:T(8,128)(2,1)}, bf16[512,768]{1,0:T(8,128)(2,1)}, bf16[256,7...) custom-call(s32[1]{0:T(128)} %bitcast.3.refs_0_, ...), custom_call_target="tpu_custom_call", output_to_operand_aliasing={{0}: (12, {}), {1}: (13, {}), {2}: (14, {}), {3}: (15, {})} | custom-call | flops 38654705664 | bytes 18874368 | tf_op jit(solution)/shard_map/experts/pallas_call | solution.py:398
  195.7 3.8 collective-permute-start.15
  200.8 7.8 %before_attention.2 = (f32[2,512,768]{2,1,0:T(8,128)}, bf16[2,512,768]{2,1,0:T(8,128)(2,1)}, f32[768,768]{1,0:T(8,128)}, f32[1,768]{1,0:T(1,128)}) custom-call(s32[1,1,512]{2,1,0:T(1,128)} %copy-done.34, bf16[256,768]{1,0:T(8,128)(2,1)} %get-tuple-element.344.refs_1_, bf16[256,768]{1,0:T(8,128)(2,1)} %copy-done.57, ...), custom_call_target="tpu_custom_call" | custom-call | tf_op jit(solution)/shard_map/before_attention/pallas_call | solution.py:603
  208.6 28.6 %expert_grads.1 = bf16[3072,1536]{1,0:T(8,128)(2,1)} custom-call(bf16[256,768]{1,0:T(8,128)(2,1)} %copy-done.30, bf16[256,768]{1,0:T(8,128)(2,1)} %collective-permute-done.6.refs_2_.refs_1_, bf16[256,768]{1,0:T(8,128)(2,1)} %collective-permute-done.7.refs_3_.refs_2_, bf16[256,768]{1,0:T(8,128)(2,1)} %collective-permute-done.8.refs_4_.refs_3_, ...), custom_call_target="tpu_custom_call" | custom-call | flops 786432 | bytes 786432 | tf_op jit(solution)/shard_map/expert_grads/pallas_call | solution.py:466
  238.9 3.4 collective-permute-start.18
  243.0 9.9 %before_attention.3 = (f32[2,512,768]{2,1,0:T(8,128)}, bf16[2,512,768]{2,1,0:T(8,128)(2,1)}, f32[768,768]{1,0:T(8,128)}, f32[1,768]{1,0:T(1,128)}) custom-call(s32[1,1,512]{2,1,0:T(1,128)} %copy-done.36, bf16[256,768]{1,0:T(8,128)(2,1)} %get-tuple-element.355.refs_1_, bf16[256,768]{1,0:T(8,128)(2,1)} %copy-done.54, ...), custom_call_target="tpu_custom_call", output_to_operand_aliasing={{0}: (10, {}), {1}: (11, {})} | custom-call | tf_op jit(solution)/shard_map/before_attention/pallas_call | solution.py:603
  252.9 27.8 %attend_back.4 = (bf16[3,1024,384]{2,1,0:T(8,128)(2,1)}, bf16[2432,384]{1,0:T(8,128)(2,1)}) custom-call(s32[1]{0:T(128)} %bitcast.refs_0_.core_ref, f32[12,2,1024]{2,1,0:T(2,128)} %bitcast.91, f32[3,512,128]{2,1,0:T(8,128)} %constant.79.clone.refs_2_, bf16[1024,768]{1,0:T(8,128)(2,1)} %get-tuple-element.257.refs_2_.refs_3_, ...), custom_call_target="tpu_custom_call" | custom-call | flops 33822867456 | bytes 5505024 | tf_op jit(solution)/shard_map/attend_back/pallas_call | solution.py:297
  280.9 1.9 convert.8
  282.8 9.6 %collective-permute-done.19.refs_6_ = bf16[512,768]{1,0:T(8,128)(2,1)S(1)} collective-permute-done((bf16[512,768]{1,0:T(8,128)(2,1)}, bf16[512,768]{1,0:T(8,128)(2,1)S(1)}, u32[]{:S(2)}, u32[]{:S(2)}) %collective-permute-start.19) | collective-permute-done | bytes 786464 | tf_op jit(solution)/shard_map/ppermute | solution.py:625
  292.9 1.4 dynamic-slice_bitcast_fusion
  295.9 10.9 %attend_back.5 = (bf16[3,1024,384]{2,1,0:T(8,128)(2,1)}, bf16[2432,384]{1,0:T(8,128)(2,1)}) custom-call(s32[1]{0:T(128)} %bitcast.refs_0_.core_ref, f32[12,2,1024]{2,1,0:T(2,128)} %bitcast.92, f32[3,512,128]{2,1,0:T(8,128)} %constant.79.clone.refs_2_, bf16[1024,768]{1,0:T(8,128)(2,1)} %get-tuple-element.257.refs_2_.refs_3_, ...), custom_call_target="tpu_custom_call" | custom-call | flops 11274289152 | bytes 1835008 | tf_op jit(solution)/shard_map/attend_back/pallas_call | solution.py:297
  306.8 2.3 fusion
  310.4 1.6 collective-permute-start.21
  312.0 1.6 collective-permute-start.22
  313.9 11.2 %attend_back.6 = (bf16[3,1024,384]{2,1,0:T(8,128)(2,1)}, bf16[2432,384]{1,0:T(8,128)(2,1)}) custom-call(s32[1]{0:T(128)} %bitcast.refs_0_.core_ref, f32[12,2,1024]{2,1,0:T(2,128)} %bitcast.93, f32[3,512,128]{2,1,0:T(8,128)} %constant.79.clone.refs_2_, ...), custom_call_target="tpu_custom_call", output_to_operand_aliasing={{0}: (10, {}), {1}: (11, {})} | custom-call | flops 11274289152 | bytes 1835008 | tf_op jit(solution)/shard_map/attend_back/pallas_call | solution.py:297
  325.2 6.3 %collective-permute-done.22 = bf16[512,384]{1,0:T(8,128)(2,1)} collective-permute-done((bf16[512,384]{1,0:T(8,128)(2,1)S(1)}, bf16[512,384]{1,0:T(8,128)(2,1)}, u32[]{:S(2)}, u32[]{:S(2)}) %collective-permute-start.22) | collective-permute-done | bytes 393248 | tf_op jit(solution)/shard_map/ppermute | solution.py:849
  331.5 1.5 fusion.4
  334.2 10.9 %attend_back.7 = (bf16[3,1024,384]{2,1,0:T(8,128)(2,1)}, bf16[2432,384]{1,0:T(8,128)(2,1)}) custom-call(s32[1]{0:T(128)} %bitcast.refs_0_.core_ref, f32[12,2,1024]{2,1,0:T(2,128)} %bitcast.94, f32[3,512,128]{2,1,0:T(8,128)} %constant.79.clone.refs_2_, ...), custom_call_target="tpu_custom_call", output_to_operand_aliasing={{0}: (10, {}), {1}: (11, {})} | custom-call | flops 11274289152 | bytes 1835008 | tf_op jit(solution)/shard_map/attend_back/pallas_call | solution.py:297
  346.8 3.0 collective-permute-start.28
  350.9 5.0 %layer_output.1 = (bf16[1,512,768]{2,1,0:T(8,128)(2,1)S(1)}, bf16[1,512,768]{2,1,0:T(8,128)(2,1)}) custom-call(s32[1,1,512]{2,1,0:T(1,128)S(1)} %copy-done.35, s32[1,1,512]{2,1,0:T(1,128)S(1)} %copy-done.37, f32[1,512,768]{2,1,0:T(8,128)} %copy-done.12, f32[1,512,768]{2,1,0:T(8,128)} %get-tuple-element.359.refs_5_.refs_3_, bf16[512,768]{1,0:T(8,128)(2,1)S(1)} %copy-done.29, ...), custom_call_target="tpu_custom_call" | custom-call | tf_op jit(solution)/shard_map/layer_output/pallas_call | solution.py:680
  358.9 1.4 collective-permute-start.31
  360.4 8.8 %token_grads.1 = (f32[512,768]{1,0:T(8,128)}, f32[512,768]{1,0:T(8,128)}) custom-call(bf16[3,1024,384]{2,1,0:T(8,128)(2,1)} %get-tuple-element.428.refs_0_, bf16[3,1024,384]{2,1,0:T(8,128)(2,1)} %get-tuple-element.429.refs_1_, bf16[768,768]{1,0:T(8,128)(2,1)S(1)} %copy-done.18, bf16[768,768]{1,0:T(8,128)(2,1)S(1)} %copy-done.20, ...), custom_call_target="tpu_custom_call" | custom-call | flops 3623878656 | bytes 11010048 | tf_op jit(solution)/shard_map/token_grads/pallas_call | solution.py:801
  372.8 1.5 collective-permute-start.34
  375.5 2.2 collective-permute-done.36
  378.4 5.7 %collective-permute-done.33 = bf16[512,384]{1,0:T(8,128)(2,1)S(1)} collective-permute-done((bf16[512,384]{1,0:T(8,128)(2,1)S(1)}, bf16[512,384]{1,0:T(8,128)(2,1)S(1)}, u32[]{:S(2)}, u32[]{:S(2)}) %collective-permute-start.33) | collective-permute-done | bytes 393248 | tf_op jit(solution)/shard_map/ppermute | solution.py:849
  384.1 6.8 %collective-permute-done.34 = bf16[512,384]{1,0:T(8,128)(2,1)S(1)} collective-permute-done((bf16[512,384]{1,0:T(8,128)(2,1)S(1)}, bf16[512,384]{1,0:T(8,128)(2,1)S(1)}, u32[]{:S(2)}, u32[]{:S(2)}) %collective-permute-start.34) | collective-permute-done | bytes 393248 | tf_op jit(solution)/shard_map/ppermute | solution.py:849
  391.8 1.4 collective-permute-start.39
  393.8 1.5 collective-permute-start.41
  395.2 5.1 %collective-permute-done.39 = bf16[304,384]{1,0:T(8,128)(2,1)S(1)} collective-permute-done((bf16[304,384]{1,0:T(8,128)(2,1)S(1)}, bf16[304,384]{1,0:T(8,128)(2,1)S(1)}, u32[]{:S(2)}, u32[]{:S(2)}) %collective-permute-start.39) | collective-permute-done | bytes 233504 | tf_op jit(solution)/shard_map/ppermute | solution.py:849
  400.3 5.3 %collective-permute-done.40 = bf16[304,384]{1,0:T(8,128)(2,1)S(1)} collective-permute-done((bf16[304,384]{1,0:T(8,128)(2,1)S(1)}, bf16[304,384]{1,0:T(8,128)(2,1)S(1)}, u32[]{:S(2)}, u32[]{:S(2)}) %collective-permute-start.40) | collective-permute-done | bytes 233504 | tf_op jit(solution)/shard_map/ppermute | solution.py:849
  410.9 3.8 hand_back.2
  414.8 4.7 %hand_back.3 = f32[2,512,768]{2,1,0:T(8,128)} custom-call(s32[1]{0:T(128)} %bitcast.refs_0_.core_ref, f32[1,512,768]{2,1,0:T(8,128)} %bitcast.109, f32[1,512,768]{2,1,0:T(8,128)} %collective-permute-done.32.arrived_ref), custom_call_target="tpu_custom_call" | custom-call | tf_op jit(solution)/shard_map/hand_back/pallas_call | solution.py:647
  420.5 8.2 %weight_outputs.1 = (f32[768,768]{1,0:T(8,128)}, f32[768,768]{1,0:T(8,128)}, f32[768,768]{1,0:T(8,128)}, f32[768,768]{1,0:T(8,128)}, f32[1,768]{1,0:T(1,128)}, /*index=5*/f32[3,128,384]{2,1,0:T(8,128)}) custom-call(s32[2]{0:T(128)} %pad_add_fusion.place_ref, bf16[4,512,384]{2,1,0:T(8,128)(2,1)} %copy-done.42, bf16[4,512,384]{2,1,0:T(8,128)(2,1)} %copy-done.47, ...), custom_call_target="tpu_custom_call" | custom-call | tf_op jit(solution)/shard_map/weight_outputs/pallas_call | solution.py:725
  (251 shorter events, 58.5 us)
Async XLA Ops:
  7.2 338.1 %reduce-scatter.2.cloned.1.call-start = ((), (), s32[]{:S(2)}) async-start(), calls=%async_computation.1 | async-start | bytes 10616832 | tf_op jit(solution)/shard_map/reduce_scatter | solution.py:1002
  9.7 40.5 %copy-start.14 = (bf16[1,512,768]{2,1,0:T(8,128)(2,1)}, bf16[1,512,768]{2,1,0:T(8,128)(2,1)S(1)}, u32[]{:S(2)}) copy-start(bf16[1,512,768]{2,1,0:T(8,128)(2,1)S(1)} %get-tuple-element.241.refs_2_) | copy-start | bytes 2359300
  9.8 3.2 collective-permute-start
  11.3 50.0 %collective-permute-start.2 = (bf16[1,512,768]{2,1,0:T(8,128)(2,1)}, bf16[1,512,768]{2,1,0:T(8,128)(2,1)S(1)}, u32[]{:S(2)}, u32[]{:S(2)}) collective-permute-start(bf16[1,512,768]{2,1,0:T(8,128)(2,1)} %get-tuple-element.515), channel_id=1, source_target_pairs={{0,4},{4,0},{1,5},{5,1},{2,6},{6,2},{3,7},{7,3},{8,12},{12,8},{9,1... | collective-permute-start | bytes 2359304 | tf_op jit(solution)/shard_map/ppermute | solution.py:634
  11.3 72.9 %copy-start.31 = (f32[1,768]{1,0:T(1,128)}, f32[1,768]{1,0:T(1,128)S(1)}, u32[]{:S(2)}) copy-start(f32[1,768]{1,0:T(1,128)S(1)} %broadcast_in_dim.31.refs_4_.refs_9_) | copy-start | bytes 9220
  13.0 42.4 %collective-permute-start.3 = (bf16[256,768]{1,0:T(8,128)(2,1)S(1)}, bf16[256,768]{1,0:T(8,128)(2,1)S(1)}, u32[]{:S(2)}, u32[]{:S(2)}) collective-permute-start(bf16[256,768]{1,0:T(8,128)(2,1)S(1)} %get-tuple-element.254), channel_id=1, source_target_pairs={{0,1},{1,2},{2,3},{3,0},{4,5},{5,6},{6,7},{7,4},{8,9},{9,10},{10,1... | collective-permute-start | bytes 1179656 | tf_op jit(solution)/shard_map/ppermute | solution.py:625
  16.1 39.3 %collective-permute-start.4 = (bf16[256,768]{1,0:T(8,128)(2,1)S(1)}, bf16[256,768]{1,0:T(8,128)(2,1)S(1)}, u32[]{:S(2)}, u32[]{:S(2)}) collective-permute-start(bf16[256,768]{1,0:T(8,128)(2,1)S(1)} %get-tuple-element.255), channel_id=1, source_target_pairs={{0,2},{1,3},{2,0},{3,1},{4,6},{5,7},{6,4},{7,5},{8,10},{9,11},{10,... | collective-permute-start | bytes 1179656 | tf_op jit(solution)/shard_map/ppermute | solution.py:625
  18.7 36.8 %collective-permute-start.5 = (bf16[256,768]{1,0:T(8,128)(2,1)S(1)}, bf16[256,768]{1,0:T(8,128)(2,1)S(1)}, u32[]{:S(2)}, u32[]{:S(2)}) collective-permute-start(bf16[256,768]{1,0:T(8,128)(2,1)S(1)} %get-tuple-element.256), channel_id=1, source_target_pairs={{0,3},{1,0},{2,1},{3,2},{4,7},{5,4},{6,5},{7,6},{8,11},{9,8},{10,9... | collective-permute-start | bytes 1179656 | tf_op jit(solution)/shard_map/ppermute | solution.py:625
  50.3 37.9 %copy-start.5 = (bf16[512,768]{1,0:T(8,128)(2,1)}, bf16[512,768]{1,0:T(8,128)(2,1)S(1)}, u32[]{:S(2)}) copy-start(bf16[512,768]{1,0:T(8,128)(2,1)S(1)} %get-tuple-element.248) | copy-start | bytes 2359300
  55.5 34.1 %collective-permute-start.6 = (bf16[256,768]{1,0:T(8,128)(2,1)}, bf16[256,768]{1,0:T(8,128)(2,1)}, u32[]{:S(2)}, u32[]{:S(2)}) collective-permute-start(bf16[256,768]{1,0:T(8,128)(2,1)} %get-tuple-element.268), channel_id=1, source_target_pairs={{0,1},{1,2},{2,3},{3,0},{4,5},{5,6},{6,7},{7,4},{8,9},{9,10},{10,1... | collective-permute-start | bytes 1179656 | tf_op jit(solution)/shard_map/ppermute | solution.py:625
  56.2 33.3 %collective-permute-start.7 = (bf16[256,768]{1,0:T(8,128)(2,1)}, bf16[256,768]{1,0:T(8,128)(2,1)}, u32[]{:S(2)}, u32[]{:S(2)}) collective-permute-start(bf16[256,768]{1,0:T(8,128)(2,1)} %get-tuple-element.269), channel_id=1, source_target_pairs={{0,2},{1,3},{2,0},{3,1},{4,6},{5,7},{6,4},{7,5},{8,10},{9,11},{10,... | collective-permute-start | bytes 1179656 | tf_op jit(solution)/shard_map/ppermute | solution.py:625
  56.5 33.0 %collective-permute-start.8 = (bf16[256,768]{1,0:T(8,128)(2,1)}, bf16[256,768]{1,0:T(8,128)(2,1)}, u32[]{:S(2)}, u32[]{:S(2)}) collective-permute-start(bf16[256,768]{1,0:T(8,128)(2,1)} %get-tuple-element.270), channel_id=1, source_target_pairs={{0,3},{1,0},{2,1},{3,2},{4,7},{5,4},{6,5},{7,6},{8,11},{9,8},{10,9... | collective-permute-start | bytes 1179656 | tf_op jit(solution)/shard_map/ppermute | solution.py:625
  59.5 1.7 collective-permute-start.1
  89.5 37.3 %collective-permute-start.9 = (bf16[512,768]{1,0:T(8,128)(2,1)}, bf16[512,768]{1,0:T(8,128)(2,1)S(1)}, u32[]{:S(2)}, u32[]{:S(2)}) collective-permute-start(bf16[512,768]{1,0:T(8,128)(2,1)} %get-tuple-element.292), channel_id=1, source_target_pairs={{0,1},{1,2},{2,3},{3,0},{4,5},{5,6},{6,7},{7,4},{8,9},{9,10},{10,1... | collective-permute-start | bytes 2359304 | tf_op jit(solution)/shard_map/ppermute | solution.py:625
  93.2 52.2 %collective-permute-start.10 = (bf16[512,768]{1,0:T(8,128)(2,1)}, bf16[512,768]{1,0:T(8,128)(2,1)S(1)}, u32[]{:S(2)}, u32[]{:S(2)}) collective-permute-start(bf16[512,768]{1,0:T(8,128)(2,1)} %get-tuple-element.293), channel_id=1, source_target_pairs={{0,2},{1,3},{2,0},{3,1},{4,6},{5,7},{6,4},{7,5},{8,10},{9,11},{10,... | collective-permute-start | bytes 2359304 | tf_op jit(solution)/shard_map/ppermute | solution.py:625
  93.3 52.1 %collective-permute-start.11 = (bf16[512,768]{1,0:T(8,128)(2,1)}, bf16[512,768]{1,0:T(8,128)(2,1)S(1)}, u32[]{:S(2)}, u32[]{:S(2)}) collective-permute-start(bf16[512,768]{1,0:T(8,128)(2,1)} %get-tuple-element.294), channel_id=1, source_target_pairs={{0,3},{1,0},{2,1},{3,2},{4,7},{5,4},{6,5},{7,6},{8,11},{9,8},{10,9... | collective-permute-start | bytes 2359304 | tf_op jit(solution)/shard_map/ppermute | solution.py:625
  126.8 37.8 %copy-start.51 = (bf16[512,768]{1,0:T(8,128)(2,1)}, bf16[512,768]{1,0:T(8,128)(2,1)S(1)}, u32[]{:S(2)}) copy-start(bf16[512,768]{1,0:T(8,128)(2,1)S(1)} %collective-permute-done.9.refs_2_.refs_6_.refs_5_) | copy-start | bytes 2359300
  145.4 54.7 %collective-permute-start.12 = (bf16[256,768]{1,0:T(8,128)(2,1)}, bf16[256,768]{1,0:T(8,128)(2,1)S(1)}, u32[]{:S(2)}, u32[]{:S(2)}) collective-permute-start(bf16[256,768]{1,0:T(8,128)(2,1)} %get-tuple-element.332), channel_id=1, source_target_pairs={{0,3},{1,0},{2,1},{3,2},{4,7},{5,4},{6,5},{7,6},{8,11},{9,8},{10,9... | collective-permute-start | bytes 1179656 | tf_op jit(solution)/shard_map/ppermute | solution.py:625
  163.6 36.8 %collective-permute-start.13 = (bf16[256,768]{1,0:T(8,128)(2,1)}, bf16[256,768]{1,0:T(8,128)(2,1)}, u32[]{:S(2)}, u32[]{:S(2)}) collective-permute-start(bf16[256,768]{1,0:T(8,128)(2,1)} %get-tuple-element.333), channel_id=1, source_target_pairs={{0,2},{1,3},{2,0},{3,1},{4,6},{5,7},{6,4},{7,5},{8,10},{9,11},{10,... | collective-permute-start | bytes 1179656 | tf_op jit(solution)/shard_map/ppermute | solution.py:625
  164.2 36.2 %collective-permute-start.14 = (bf16[256,768]{1,0:T(8,128)(2,1)}, bf16[256,768]{1,0:T(8,128)(2,1)}, u32[]{:S(2)}, u32[]{:S(2)}) collective-permute-start(bf16[256,768]{1,0:T(8,128)(2,1)} %get-tuple-element.334), channel_id=1, source_target_pairs={{0,1},{1,2},{2,3},{3,0},{4,5},{5,6},{6,7},{7,4},{8,9},{9,10},{10,1... | collective-permute-start | bytes 1179656 | tf_op jit(solution)/shard_map/ppermute | solution.py:625
  195.7 41.6 %collective-permute-start.15 = (bf16[256,768]{1,0:T(8,128)(2,1)}, bf16[256,768]{1,0:T(8,128)(2,1)S(1)}, u32[]{:S(2)}, u32[]{:S(2)}) collective-permute-start(bf16[256,768]{1,0:T(8,128)(2,1)} %get-tuple-element.324), channel_id=1, source_target_pairs={{0,3},{1,0},{2,1},{3,2},{4,7},{5,4},{6,5},{7,6},{8,11},{9,8},{10,9... | collective-permute-start | bytes 1179656 | tf_op jit(solution)/shard_map/ppermute | solution.py:625
  199.5 37.8 %collective-permute-start.16 = (bf16[256,768]{1,0:T(8,128)(2,1)}, bf16[256,768]{1,0:T(8,128)(2,1)S(1)}, u32[]{:S(2)}, u32[]{:S(2)}) collective-permute-start(bf16[256,768]{1,0:T(8,128)(2,1)} %get-tuple-element.325), channel_id=1, source_target_pairs={{0,2},{1,3},{2,0},{3,1},{4,6},{5,7},{6,4},{7,5},{8,10},{9,11},{10,... | collective-permute-start | bytes 1179656 | tf_op jit(solution)/shard_map/ppermute | solution.py:625
  200.0 37.3 %collective-permute-start.17 = (bf16[256,768]{1,0:T(8,128)(2,1)}, bf16[256,768]{1,0:T(8,128)(2,1)S(1)}, u32[]{:S(2)}, u32[]{:S(2)}) collective-permute-start(bf16[256,768]{1,0:T(8,128)(2,1)} %get-tuple-element.326), channel_id=1, source_target_pairs={{0,1},{1,2},{2,3},{3,0},{4,5},{5,6},{6,7},{7,4},{8,9},{9,10},{10,1... | collective-permute-start | bytes 1179656 | tf_op jit(solution)/shard_map/ppermute | solution.py:625
  238.9 43.9 %collective-permute-start.18 = (bf16[512,768]{1,0:T(8,128)(2,1)S(1)}, bf16[512,768]{1,0:T(8,128)(2,1)S(1)}, u32[]{:S(2)}, u32[]{:S(2)}) collective-permute-start(bf16[512,768]{1,0:T(8,128)(2,1)S(1)} %copy-done.65), channel_id=1, source_target_pairs={{0,3},{1,0},{2,1},{3,2},{4,7},{5,4},{6,5},{7,6},{8,11},{9,8},{10,9... | collective-permute-start | bytes 2359304 | tf_op jit(solution)/shard_map/ppermute | solution.py:625
  242.3 50.1 %collective-permute-start.19 = (bf16[512,768]{1,0:T(8,128)(2,1)}, bf16[512,768]{1,0:T(8,128)(2,1)S(1)}, u32[]{:S(2)}, u32[]{:S(2)}) collective-permute-start(bf16[512,768]{1,0:T(8,128)(2,1)} %get-tuple-element.372), channel_id=1, source_target_pairs={{0,2},{1,3},{2,0},{3,1},{4,6},{5,7},{6,4},{7,5},{8,10},{9,11},{10,... | collective-permute-start | bytes 2359304 | tf_op jit(solution)/shard_map/ppermute | solution.py:625
  295.1 11.7 %collective-permute-start.20 = (bf16[4,512,384]{2,1,0:T(8,128)(2,1)}, bf16[4,512,384]{2,1,0:T(8,128)(2,1)}, u32[]{:S(2)}, u32[]{:S(2)}) collective-permute-start(bf16[4,512,384]{2,1,0:T(8,128)(2,1)} %dynamic-slice_bitcast_fusion), channel_id=1, source_target_pairs={{0,4},{4,0},{1,5},{5,1},{2,6},{6,2},{3,7},{7,3},{8,12},{12,8},{9,1... | collective-permute-start | bytes 4718600 | tf_op jit(solution)/shard_map/ppermute | solution.py:849
  295.1 30.1 %collective-permute-start.24 = (bf16[512,768]{1,0:T(8,128)(2,1)}, bf16[512,768]{1,0:T(8,128)(2,1)S(1)}, u32[]{:S(2)}, u32[]{:S(2)}) collective-permute-start(bf16[512,768]{1,0:T(8,128)(2,1)} %get-tuple-element.394), channel_id=1, source_target_pairs={{0,1},{1,2},{2,3},{3,0},{4,5},{5,6},{6,7},{7,4},{8,9},{9,10},{10,1... | collective-permute-start | bytes 2359304 | tf_op jit(solution)/shard_map/ppermute | solution.py:625
  310.4 14.8 %collective-permute-start.21 = (bf16[512,384]{1,0:T(8,128)(2,1)S(1)}, bf16[512,384]{1,0:T(8,128)(2,1)S(1)}, u32[]{:S(2)}, u32[]{:S(2)}) collective-permute-start(bf16[512,384]{1,0:T(8,128)(2,1)S(1)} %get-tuple-element.388), channel_id=1, source_target_pairs={{0,8},{8,0},{16,24},{24,16},{1,9},{9,1},{17,25},{25,17},{2,10},{10... | collective-permute-start | bytes 1179656 | tf_op jit(solution)/shard_map/ppermute | solution.py:849
  312.0 19.6 %collective-permute-start.22 = (bf16[512,384]{1,0:T(8,128)(2,1)S(1)}, bf16[512,384]{1,0:T(8,128)(2,1)}, u32[]{:S(2)}, u32[]{:S(2)}) collective-permute-start(bf16[512,384]{1,0:T(8,128)(2,1)S(1)} %get-tuple-element.389), channel_id=1, source_target_pairs={{0,16},{8,24},{16,0},{24,8},{1,17},{9,25},{17,1},{25,9},{2,18},{10... | collective-permute-start | bytes 1179656 | tf_op jit(solution)/shard_map/ppermute | solution.py:849
  313.6 18.0 %collective-permute-start.23 = (bf16[512,384]{1,0:T(8,128)(2,1)S(1)}, bf16[512,384]{1,0:T(8,128)(2,1)}, u32[]{:S(2)}, u32[]{:S(2)}) collective-permute-start(bf16[512,384]{1,0:T(8,128)(2,1)S(1)} %get-tuple-element.390), channel_id=1, source_target_pairs={{0,24},{8,16},{16,8},{24,0},{1,25},{9,17},{17,9},{25,1},{2,26},{10... | collective-permute-start | bytes 1179656 | tf_op jit(solution)/shard_map/ppermute | solution.py:849
  333.0 12.1 %collective-permute-start.25 = (bf16[512,384]{1,0:T(8,128)(2,1)S(1)}, bf16[512,384]{1,0:T(8,128)(2,1)S(1)}, u32[]{:S(2)}, u32[]{:S(2)}) collective-permute-start(bf16[512,384]{1,0:T(8,128)(2,1)S(1)} %fusion.4), channel_id=1, source_target_pairs={{0,1},{1,0},{2,3},{3,2},{4,5},{5,4},{6,7},{7,6},{8,9},{9,8},{10,11... | collective-permute-start | bytes 1179656 | tf_op jit(solution)/shard_map/ppermute | solution.py:849
  346.7 9.2 %collective-permute-start.26 = (bf16[4,304,384]{2,1,0:T(8,128)(2,1)S(1)}, bf16[4,304,384]{2,1,0:T(8,128)(2,1)S(1)}, u32[]{:S(2)}, u32[]{:S(2)}) collective-permute-start(bf16[4,304,384]{2,1,0:T(8,128)(2,1)S(1)} %dynamic-slice_bitcast_fusion.1), channel_id=1, source_target_pairs={{0,4},{4,0},{1,5},{5,1},{2,6},{6,2},{3,7},{7,3},{8,12},{12,8},{9,1... | collective-permute-start | bytes 2801672 | tf_op jit(solution)/shard_map/ppermute | solution.py:849
  346.8 22.4 %collective-permute-start.28 = (bf16[512,384]{1,0:T(8,128)(2,1)S(1)}, bf16[512,384]{1,0:T(8,128)(2,1)S(1)}, u32[]{:S(2)}, u32[]{:S(2)}) collective-permute-start(bf16[512,384]{1,0:T(8,128)(2,1)S(1)} %add_convert_fusion.1), channel_id=1, source_target_pairs={{0,2},{1,3},{2,0},{3,1},{4,6},{5,7},{6,4},{7,5},{8,10},{9,11},{10,... | collective-permute-start | bytes 1179656 | tf_op jit(solution)/shard_map/ppermute | solution.py:849
  356.8 12.3 %collective-permute-start.29 = (bf16[304,384]{1,0:T(8,128)(2,1)S(1)}, bf16[304,384]{1,0:T(8,128)(2,1)S(1)}, u32[]{:S(2)}, u32[]{:S(2)}) collective-permute-start(bf16[304,384]{1,0:T(8,128)(2,1)S(1)} %get-tuple-element.425), channel_id=1, source_target_pairs={{0,8},{8,0},{16,24},{24,16},{1,9},{9,1},{17,25},{25,17},{2,10},{10... | collective-permute-start | bytes 700424 | tf_op jit(solution)/shard_map/ppermute | solution.py:849
  357.9 11.2 %collective-permute-start.30 = (bf16[304,384]{1,0:T(8,128)(2,1)S(1)}, bf16[304,384]{1,0:T(8,128)(2,1)S(1)}, u32[]{:S(2)}, u32[]{:S(2)}) collective-permute-start(bf16[304,384]{1,0:T(8,128)(2,1)S(1)} %get-tuple-element.426), channel_id=1, source_target_pairs={{0,16},{8,24},{16,0},{24,8},{1,17},{9,25},{17,1},{25,9},{2,18},{10... | collective-permute-start | bytes 700424 | tf_op jit(solution)/shard_map/ppermute | solution.py:849
  358.9 11.6 %collective-permute-start.31 = (bf16[304,384]{1,0:T(8,128)(2,1)S(1)}, bf16[304,384]{1,0:T(8,128)(2,1)S(1)}, u32[]{:S(2)}, u32[]{:S(2)}) collective-permute-start(bf16[304,384]{1,0:T(8,128)(2,1)S(1)} %get-tuple-element.427), channel_id=1, source_target_pairs={{0,24},{8,16},{16,8},{24,0},{1,25},{9,17},{17,9},{25,1},{2,26},{10... | collective-permute-start | bytes 700424 | tf_op jit(solution)/shard_map/ppermute | solution.py:849
  370.7 7.0 %collective-permute-start.36 = (bf16[304,384]{1,0:T(8,128)(2,1)S(1)}, bf16[304,384]{1,0:T(8,128)(2,1)S(1)}, u32[]{:S(2)}, u32[]{:S(2)}) collective-permute-start(bf16[304,384]{1,0:T(8,128)(2,1)S(1)} %fusion.7), channel_id=1, source_target_pairs={{0,1},{1,0},{2,3},{3,2},{4,5},{5,4},{6,7},{7,6},{8,9},{9,8},{10,11... | collective-permute-start | bytes 700424 | tf_op jit(solution)/shard_map/ppermute | solution.py:849
  372.0 12.1 %collective-permute-start.33 = (bf16[512,384]{1,0:T(8,128)(2,1)S(1)}, bf16[512,384]{1,0:T(8,128)(2,1)S(1)}, u32[]{:S(2)}, u32[]{:S(2)}) collective-permute-start(bf16[512,384]{1,0:T(8,128)(2,1)S(1)} %add_convert_fusion), channel_id=1, source_target_pairs={{0,8},{8,0},{16,24},{24,16},{1,9},{9,1},{17,25},{25,17},{2,10},{10... | collective-permute-start | bytes 1179656 | tf_op jit(solution)/shard_map/ppermute | solution.py:849
  372.8 18.0 %collective-permute-start.34 = (bf16[512,384]{1,0:T(8,128)(2,1)S(1)}, bf16[512,384]{1,0:T(8,128)(2,1)S(1)}, u32[]{:S(2)}, u32[]{:S(2)}) collective-permute-start(bf16[512,384]{1,0:T(8,128)(2,1)S(1)} %add_convert_fusion), channel_id=1, source_target_pairs={{0,16},{8,24},{16,0},{24,8},{1,17},{9,25},{17,1},{25,9},{2,18},{10... | collective-permute-start | bytes 1179656 | tf_op jit(solution)/shard_map/ppermute | solution.py:849
  374.3 16.5 %collective-permute-start.35 = (bf16[512,384]{1,0:T(8,128)(2,1)S(1)}, bf16[512,384]{1,0:T(8,128)(2,1)S(1)}, u32[]{:S(2)}, u32[]{:S(2)}) collective-permute-start(bf16[512,384]{1,0:T(8,128)(2,1)S(1)} %add_convert_fusion), channel_id=1, source_target_pairs={{0,24},{8,16},{16,8},{24,0},{1,25},{9,17},{17,9},{25,1},{2,26},{10... | collective-permute-start | bytes 1179656 | tf_op jit(solution)/shard_map/ppermute | solution.py:849
  377.7 13.1 %collective-permute-start.37 = (bf16[304,384]{1,0:T(8,128)(2,1)S(1)}, bf16[304,384]{1,0:T(8,128)(2,1)S(1)}, u32[]{:S(2)}, u32[]{:S(2)}) collective-permute-start(bf16[304,384]{1,0:T(8,128)(2,1)S(1)} %add_convert_fusion.3), channel_id=1, source_target_pairs={{0,2},{1,3},{2,0},{3,1},{4,6},{5,7},{6,4},{7,5},{8,10},{9,11},{10,... | collective-permute-start | bytes 700424 | tf_op jit(solution)/shard_map/ppermute | solution.py:849
  391.2 14.4 %collective-permute-start.38 = (bf16[4,512,384]{2,1,0:T(8,128)(2,1)S(1)}, bf16[4,512,384]{2,1,0:T(8,128)(2,1)S(1)}, u32[]{:S(2)}, u32[]{:S(2)}) collective-permute-start(bf16[4,512,384]{2,1,0:T(8,128)(2,1)S(1)} %pad_maximum_fusion.1.refs_0_), channel_id=1, source_target_pairs={{0,4},{4,0},{1,5},{5,1},{2,6},{6,2},{3,7},{7,3},{8,12},{12,8},{9,1... | collective-permute-start | bytes 4718600 | tf_op jit(solution)/shard_map/ppermute | solution.py:849
  391.3 23.5 %collective-permute-start.32 = (f32[1,512,768]{2,1,0:T(8,128)}, f32[1,512,768]{2,1,0:T(8,128)}, u32[]{:S(2)}, u32[]{:S(2)}) collective-permute-start(f32[1,512,768]{2,1,0:T(8,128)} %bitcast.30), channel_id=1, source_target_pairs={{0,4},{4,0},{1,5},{5,1},{2,6},{6,2},{3,7},{7,3},{8,12},{12,8},{9,1... | collective-permute-start | bytes 4718600 | tf_op jit(solution)/shard_map/ppermute | solution.py:642
  391.8 8.5 %collective-permute-start.39 = (bf16[304,384]{1,0:T(8,128)(2,1)S(1)}, bf16[304,384]{1,0:T(8,128)(2,1)S(1)}, u32[]{:S(2)}, u32[]{:S(2)}) collective-permute-start(bf16[304,384]{1,0:T(8,128)(2,1)S(1)} %add_convert_fusion.2), channel_id=1, source_target_pairs={{0,8},{8,0},{16,24},{24,16},{1,9},{9,1},{17,25},{25,17},{2,10},{10... | collective-permute-start | bytes 700424 | tf_op jit(solution)/shard_map/ppermute | solution.py:849
  393.2 12.4 %collective-permute-start.40 = (bf16[304,384]{1,0:T(8,128)(2,1)S(1)}, bf16[304,384]{1,0:T(8,128)(2,1)S(1)}, u32[]{:S(2)}, u32[]{:S(2)}) collective-permute-start(bf16[304,384]{1,0:T(8,128)(2,1)S(1)} %add_convert_fusion.2), channel_id=1, source_target_pairs={{0,16},{8,24},{16,0},{24,8},{1,17},{9,25},{17,1},{25,9},{2,18},{10... | collective-permute-start | bytes 700424 | tf_op jit(solution)/shard_map/ppermute | solution.py:849
  393.8 11.8 %collective-permute-start.41 = (bf16[304,384]{1,0:T(8,128)(2,1)S(1)}, bf16[304,384]{1,0:T(8,128)(2,1)S(1)}, u32[]{:S(2)}, u32[]{:S(2)}) collective-permute-start(bf16[304,384]{1,0:T(8,128)(2,1)S(1)} %add_convert_fusion.2), channel_id=1, source_target_pairs={{0,24},{8,16},{16,8},{24,0},{1,25},{9,17},{17,9},{25,1},{2,26},{10... | collective-permute-start | bytes 700424 | tf_op jit(solution)/shard_map/ppermute | solution.py:849
  406.9 12.6 %collective-permute-start.42 = (bf16[4,304,384]{2,1,0:T(8,128)(2,1)S(1)}, bf16[4,304,384]{2,1,0:T(8,128)(2,1)S(1)}, u32[]{:S(2)}, u32[]{:S(2)}) collective-permute-start(bf16[4,304,384]{2,1,0:T(8,128)(2,1)S(1)} %pad_maximum_fusion.2.refs_2_), channel_id=1, source_target_pairs={{0,4},{4,0},{1,5},{5,1},{2,6},{6,2},{3,7},{7,3},{8,12},{12,8},{9,1... | collective-permute-start | bytes 2801672 | tf_op jit(solution)/shard_map/ppermute | solution.py:849
  407.0 3.9 collective-permute-start.27
  (65 other events, 494.3 us)
Sparse Core Ops, SparseCore 0:
  237.5 77.3 reduce-scatter.1

commit v10 on v9

--- a/solution.py
+++ b/solution.py
@@ -1010,11 +1010,14 @@
         half = model_width // 2
         pairs = half // 128
         mixed_grad = mixed_grad.reshape(flat)
-        returned = exchange(list(rows_out[:-1]), "expert", -1, owners)
+        def send_back(turn):
+            return lax.ppermute(rows_out[turn], "expert", [(at, (at - turn) % owners) for at in range(owners)])
+
+        half_turn = owners // 2
+        returned = [rows_out[0] if turn in (0, half_turn) else send_back(turn) for turn in range(owners)]
         first = attend_back(core, *qkv, mixed_grad, *seen, lines, 0, pairs, pairs)
-        first, returned, last_rows = together((first, returned, rows_out[-1]))
-        returned.append(exchange([None, last_rows], "expert", -1, owners, owners - 2)[1])
-        first_grads, first_sums = first
+        (first_grads, first_sums), returned, rows_out = together((first, returned, rows_out))
+        returned[half_turn] = send_back(half_turn)
         matrices = [first_sums, grad_w_output[:, :half], grad_w_output[:, half:]]
         early = Summing(pack_sums(matrices, early_small.reshape(-1, half)))
         second = ()
@@ -1045,11 +1048,13 @@
         sent, sent_late = together((early.sends(), late.sends()))
         moved = early.move(sent)
         late.take(late.move(sent_late))
-        moved, moved_late = together((moved, late.move(late.sends())))
+        block_out = hand_back(*block_out)
+        moved, moved_late, block_out = together((moved, late.move(late.sends()), block_out))
         early.take(moved)
         late.take(moved_late)
         sent, sent_late = together((early.sends(), late.sends()))
-        moved, moved_late = together((early.move(sent), late.move(sent_late)))
+        d_tokens = hand_back(*[rows[None] for rows in d_tokens])
+        moved, moved_late, d_tokens = together((early.move(sent), late.move(sent_late), d_tokens))
         early.take(moved)
         late.take(moved_late)
         late.take(late.move(late.sends()))
@@ -1086,8 +1091,6 @@
     if not whole_seq:
         block_out = layer_output(slots, residual1, returned)[0]
         d_tokens = residual_grad + norm1_back
-    if whole_seq:
-        block_out, d_tokens = hand_back(*block_out), hand_back(*[rows[None] for rows in d_tokens])
     grad_experts = grad_experts.astype(jnp.float32)
     return (
         block_out,

time: 448 us -> 438 us (0.978)
  waiting for transfers between devices: 60.9 us -> 51.1 us
    ppermute x18 -> x15, waiting for transfers between devices: 28.2 us -> 18.7 us  [exchange(): lax.ppermute(piece, axis, [(at, (at + sign * turn) % size) for at in rang...]
    ppermute x20, waiting for transfers between devices: 32.6 us -> 25 us  [swap(): lax.ppermute(part, axis, [(to, to ^ turn) for to in range(lax.axis_size(a...]
    ppermute x0 -> x3, waiting for transfers between devices: none -> 7.37 us  [send_back(): lax.ppermute(rows_out[turn], 'expert', [(at, (at - turn) % owners) for at...]
    ppermute x18 -> x15, starting transfers between devices: 46 us -> 41.3 us  [exchange(): lax.ppermute(piece, axis, [(at, (at + sign * turn) % size) for at in rang...]
    unnamed x144 -> x146, local copies, waits for them, and re-layouts: 26.3 us -> 26.3 us
  transfers between devices with their start and end apart: 44 -> 44, of which waited for: 9 -> 8; matrix products, arithmetic and copies ran while one was open for 4% -> 4% of each run, Pallas kernels for 54% -> 55%
where the time goes in v10:
time: 438 us; the launch traced here: 431 us
  Pallas kernels  246 us (56%)
  starting transfers between devices  65.6 us (15%)
  waiting for transfers between devices  51.1 us (12%)
  local copies, waits for them, and re-layouts  37.6 us (9%)
  other arithmetic  15.6 us (4%)
  between operations  15.1 us (3%)
    pallas_call x2, Pallas kernels, run_expert(): pl.pallas_call(lambda *refs: expert_kernel(count, *refs), grid_spec=pltpu...  61.9 us
    pallas_call x4, Pallas kernels, attend_back(): pl.pallas_call(lambda *refs: bwd_kernel(*refs[:10], *refs[10 + len(earlie...  61.7 us
    ppermute x15, starting transfers between devices, exchange(): lax.ppermute(piece, axis, [(at, (at + sign * turn) % size) for at in rang...  41.3 us
    pallas_call x2, Pallas kernels, attend(): pl.pallas_call(lambda *refs: fwd_kernel(first // QB, *refs), grid=(width...  31.8 us
    pallas_call x1, Pallas kernels, expert_grads(): pl.pallas_call(lambda *refs: expert_grads_kernel(groups, count, *refs), g...  28.6 us
    unnamed x146, local copies, waits for them, and re-layouts  26.3 us
    ppermute x20, waiting for transfers between devices, swap(): lax.ppermute(part, axis, [(to, to ^ turn) for to in range(lax.axis_size(a...  25 us
    ppermute x20, starting transfers between devices, swap(): lax.ppermute(part, axis, [(to, to ^ turn) for to in range(lax.axis_size(a...  19.6 us
  transfers between devices with their start and end apart: 44, of which 8 were waited for; matrix products, arithmetic and copies ran while one was open for 4% of the time, Pallas kernels for 55%

profile of v10, /device:TPU:0, one launch (start us, length us, event | category | flops | bytes accessed | tf_op | source)
XLA Modules:
  0.0 431.2 jit_solution(12163801102024968582)
XLA Ops:
  7.3 2.5 constant_dynamic-slice_fusion.2
  13.0 3.1 collective-permute-start.3
  16.1 2.6 collective-permute-start.4
  23.8 5.6 %projections.1 = (bf16[1024,768]{1,0:T(8,128)(2,1)}, bf16[1024,768]{1,0:T(8,128)(2,1)}, bf16[1024,768]{1,0:T(8,128)(2,1)}, bf16[768,1024]{1,0:T(8,128)(2,1)}) custom-call(bf16[512,768]{1,0:T(8,128)(2,1)S(1)} %bitcast.88, bf16[512,768]{1,0:T(8,128)(2,1)S(1)} %bitcast.96, f32[1,768]{1,0:T(1,128)S(1)} %broadcast_in_dim.29.refs_2_.refs_8_.refs_7_, ...), custom_call_target="tpu_custom_call" | custom-call | flops 19327352832 | bytes 6291456 | tf_op jit(solution)/shard_map/projections/pallas_call | solution.py:760
  33.7 16.0 %attend.2 = (bf16[512,768]{1,0:T(8,128)(2,1)S(1)}, f32[6,2,512]{2,1,0:T(2,128)S(1)}) custom-call(s32[1]{0:T(128)} %bitcast.refs_0_.core_ref, f32[12,2,1024]{2,1,0:T(2,128)S(1)} %bitcast.90, bf16[1024,768]{1,0:T(8,128)(2,1)S(1)} %copy-done.6, bf16[1024,768]{1,0:T(8,128)(2,1)S(1)} %copy-done.8, bf16[1024,768]{1,0:T(8,128)(2,1)S(1)} %copy-done.10), custom_call_target="tpu_custom_call" | custom-call | flops 402653184 | bytes 1572864 | tf_op jit(solution)/shard_map/attend/pallas_call | solution.py:204
  50.2 3.2 after_attention.2
  56.5 3.0 collective-permute-start.8
  61.2 2.0 sort_upstream.3
  68.3 15.8 %attend.3 = (bf16[512,768]{1,0:T(8,128)(2,1)S(1)}, f32[6,2,512]{2,1,0:T(2,128)S(1)}) custom-call(s32[1]{0:T(128)} %bitcast.refs_0_.core_ref, f32[12,2,1024]{2,1,0:T(2,128)S(1)} %bitcast.95, bf16[1024,768]{1,0:T(8,128)(2,1)S(1)} %copy-done.7, bf16[1024,768]{1,0:T(8,128)(2,1)S(1)} %copy-done.9, bf16[1024,768]{1,0:T(8,128)(2,1)S(1)} %copy-done.11), custom_call_target="tpu_custom_call" | custom-call | flops 402653184 | bytes 1572864 | tf_op jit(solution)/shard_map/attend/pallas_call | solution.py:204
  84.2 3.2 after_attention.3
  89.5 3.7 collective-permute-start.9
  93.2 2.6 collective-permute-start.11
  95.8 30.9 %experts.2 = (bf16[512,768]{1,0:T(8,128)(2,1)}, bf16[512,768]{1,0:T(8,128)(2,1)}, bf16[512,768]{1,0:T(8,128)(2,1)}, bf16[512,768]{1,0:T(8,128)(2,1)}, bf16[256,7...) custom-call(s32[1]{0:T(128)} %bitcast.3.refs_0_, ...), custom_call_target="tpu_custom_call" | custom-call | flops 38654705664 | bytes 18874368 | tf_op jit(solution)/shard_map/experts/pallas_call | solution.py:398
  126.7 18.6 %collective-permute-done.10.refs_3_.refs_7_.refs_6_ = bf16[512,768]{1,0:T(8,128)(2,1)S(1)} collective-permute-done((bf16[512,768]{1,0:T(8,128)(2,1)}, bf16[512,768]{1,0:T(8,128)(2,1)S(1)}, u32[]{:S(2)}, u32[]{:S(2)}) %collective-permute-start.10) | collective-permute-done | bytes 786464 | tf_op jit(solution)/shard_map/ppermute | solution.py:625
  145.3 18.2 %collective-permute-start.12 = (bf16[256,768]{1,0:T(8,128)(2,1)}, bf16[256,768]{1,0:T(8,128)(2,1)S(1)}, u32[]{:S(2)}, u32[]{:S(2)}) collective-permute-start(bf16[256,768]{1,0:T(8,128)(2,1)} %get-tuple-element.334), channel_id=1, source_target_pairs={{0,3},{1,0},{2,1},{3,2},{4,7},{5,4},{6,5},{7,6},{8,11},{9,8},{10,9... | collective-permute-start | bytes 1179656 | tf_op jit(solution)/shard_map/ppermute | solution.py:625
  164.6 31.0 %experts.3 = (bf16[512,768]{1,0:T(8,128)(2,1)}, bf16[512,768]{1,0:T(8,128)(2,1)}, bf16[512,768]{1,0:T(8,128)(2,1)}, bf16[512,768]{1,0:T(8,128)(2,1)}, bf16[256,7...) custom-call(s32[1]{0:T(128)} %bitcast.3.refs_0_, ...), custom_call_target="tpu_custom_call", output_to_operand_aliasing={{0}: (12, {}), {1}: (13, {}), {2}: (14, {}), {3}: (15, {})} | custom-call | flops 38654705664 | bytes 18874368 | tf_op jit(solution)/shard_map/experts/pallas_call | solution.py:398
  195.7 3.8 collective-permute-start.15
  200.8 7.8 %before_attention.2 = (f32[2,512,768]{2,1,0:T(8,128)}, bf16[2,512,768]{2,1,0:T(8,128)(2,1)}, f32[768,768]{1,0:T(8,128)}, f32[1,768]{1,0:T(1,128)}) custom-call(s32[1,1,512]{2,1,0:T(1,128)} %copy-done.34, bf16[256,768]{1,0:T(8,128)(2,1)} %get-tuple-element.346.refs_1_, bf16[256,768]{1,0:T(8,128)(2,1)} %copy-done.57, ...), custom_call_target="tpu_custom_call" | custom-call | tf_op jit(solution)/shard_map/before_attention/pallas_call | solution.py:603
  208.6 28.6 %expert_grads.1 = bf16[3072,1536]{1,0:T(8,128)(2,1)} custom-call(bf16[256,768]{1,0:T(8,128)(2,1)} %copy-done.30, bf16[256,768]{1,0:T(8,128)(2,1)} %collective-permute-done.6.refs_2_.refs_1_, bf16[256,768]{1,0:T(8,128)(2,1)} %collective-permute-done.7.refs_3_.refs_2_, bf16[256,768]{1,0:T(8,128)(2,1)} %collective-permute-done.8.refs_4_.refs_3_, ...), custom_call_target="tpu_custom_call" | custom-call | flops 786432 | bytes 786432 | tf_op jit(solution)/shard_map/expert_grads/pallas_call | solution.py:466
  238.9 3.2 collective-permute-start.18
  242.3 9.5 %before_attention.3 = (f32[2,512,768]{2,1,0:T(8,128)}, bf16[2,512,768]{2,1,0:T(8,128)(2,1)}, f32[768,768]{1,0:T(8,128)}, f32[1,768]{1,0:T(1,128)}) custom-call(s32[1,1,512]{2,1,0:T(1,128)} %copy-done.36, bf16[256,768]{1,0:T(8,128)(2,1)} %get-tuple-element.357.refs_1_, bf16[256,768]{1,0:T(8,128)(2,1)} %copy-done.54, ...), custom_call_target="tpu_custom_call", output_to_operand_aliasing={{0}: (10, {}), {1}: (11, {})} | custom-call | tf_op jit(solution)/shard_map/before_attention/pallas_call | solution.py:603
  251.8 28.5 %attend_back.4 = (bf16[3,1024,384]{2,1,0:T(8,128)(2,1)}, bf16[2432,384]{1,0:T(8,128)(2,1)}) custom-call(s32[1]{0:T(128)} %bitcast.refs_0_.core_ref, f32[12,2,1024]{2,1,0:T(2,128)} %bitcast.91, f32[3,512,128]{2,1,0:T(8,128)} %constant.79.clone.refs_2_, bf16[1024,768]{1,0:T(8,128)(2,1)} %get-tuple-element.259.refs_2_.refs_3_, ...), custom_call_target="tpu_custom_call" | custom-call | flops 33822867456 | bytes 5505024 | tf_op jit(solution)/shard_map/attend_back/pallas_call | solution.py:297
  280.6 2.0 convert.8
  283.4 1.5 dynamic-slice_bitcast_fusion
  286.2 11.0 %attend_back.5 = (bf16[3,1024,384]{2,1,0:T(8,128)(2,1)}, bf16[2432,384]{1,0:T(8,128)(2,1)}) custom-call(s32[1]{0:T(128)} %bitcast.refs_0_.core_ref, f32[12,2,1024]{2,1,0:T(2,128)} %bitcast.92, f32[3,512,128]{2,1,0:T(8,128)} %constant.79.clone.refs_2_, bf16[1024,768]{1,0:T(8,128)(2,1)} %get-tuple-element.259.refs_2_.refs_3_, ...), custom_call_target="tpu_custom_call" | custom-call | flops 11274289152 | bytes 1835008 | tf_op jit(solution)/shard_map/attend_back/pallas_call | solution.py:297
  297.3 2.8 fusion
  301.4 1.5 collective-permute-start.21
  302.9 1.8 collective-permute-start.22
  305.0 11.2 %attend_back.6 = (bf16[3,1024,384]{2,1,0:T(8,128)(2,1)}, bf16[2432,384]{1,0:T(8,128)(2,1)}) custom-call(s32[1]{0:T(128)} %bitcast.refs_0_.core_ref, f32[12,2,1024]{2,1,0:T(2,128)} %bitcast.93, f32[3,512,128]{2,1,0:T(8,128)} %constant.79.clone.refs_2_, ...), custom_call_target="tpu_custom_call", output_to_operand_aliasing={{0}: (10, {}), {1}: (11, {})} | custom-call | flops 11274289152 | bytes 1835008 | tf_op jit(solution)/shard_map/attend_back/pallas_call | solution.py:297
  316.1 7.4 %collective-permute-done.24.refs_6_ = bf16[512,768]{1,0:T(8,128)(2,1)S(1)} collective-permute-done((bf16[512,768]{1,0:T(8,128)(2,1)}, bf16[512,768]{1,0:T(8,128)(2,1)S(1)}, u32[]{:S(2)}, u32[]{:S(2)}) %collective-permute-start.24) | collective-permute-done | bytes 786464 | tf_op jit(solution)/shard_map/ppermute | solution.py:1014
  323.5 7.7 %collective-permute-done.23 = bf16[512,384]{1,0:T(8,128)(2,1)} collective-permute-done((bf16[512,384]{1,0:T(8,128)(2,1)S(1)}, bf16[512,384]{1,0:T(8,128)(2,1)}, u32[]{:S(2)}, u32[]{:S(2)}) %collective-permute-start.23) | collective-permute-done | bytes 393248 | tf_op jit(solution)/shard_map/ppermute | solution.py:849
  331.2 1.5 fusion.4
  332.7 1.6 collective-permute-start.25
  334.2 10.9 %attend_back.7 = (bf16[3,1024,384]{2,1,0:T(8,128)(2,1)}, bf16[2432,384]{1,0:T(8,128)(2,1)}) custom-call(s32[1]{0:T(128)} %bitcast.refs_0_.core_ref, f32[12,2,1024]{2,1,0:T(2,128)} %bitcast.94, f32[3,512,128]{2,1,0:T(8,128)} %constant.79.clone.refs_2_, ...), custom_call_target="tpu_custom_call", output_to_operand_aliasing={{0}: (10, {}), {1}: (11, {})} | custom-call | flops 11274289152 | bytes 1835008 | tf_op jit(solution)/shard_map/attend_back/pallas_call | solution.py:297
  347.0 2.5 collective-permute-start.26
  350.6 3.9 layer_output.1
  357.0 2.4 collective-permute-start.30
  359.4 8.8 %token_grads.1 = (f32[512,768]{1,0:T(8,128)}, f32[512,768]{1,0:T(8,128)}) custom-call(bf16[3,1024,384]{2,1,0:T(8,128)(2,1)} %get-tuple-element.428.refs_0_, bf16[3,1024,384]{2,1,0:T(8,128)(2,1)} %get-tuple-element.429.refs_1_, bf16[768,768]{1,0:T(8,128)(2,1)S(1)} %copy-done.18, bf16[768,768]{1,0:T(8,128)(2,1)S(1)} %copy-done.20, ...), custom_call_target="tpu_custom_call" | custom-call | flops 3623878656 | bytes 11010048 | tf_op jit(solution)/shard_map/token_grads/pallas_call | solution.py:801
  369.8 1.5 collective-permute-start.31
  371.8 1.5 collective-permute-start.33
  373.3 3.4 collective-permute-done.34
  378.2 3.8 hand_back.2
  382.0 7.2 %collective-permute-done.32 = bf16[512,384]{1,0:T(8,128)(2,1)S(1)} collective-permute-done((bf16[512,384]{1,0:T(8,128)(2,1)S(1)}, bf16[512,384]{1,0:T(8,128)(2,1)S(1)}, u32[]{:S(2)}, u32[]{:S(2)}) %collective-permute-start.32) | collective-permute-done | bytes 393248 | tf_op jit(solution)/shard_map/ppermute | solution.py:849
  393.3 1.4 collective-permute-start.40
  394.8 4.7 %hand_back.3 = f32[2,512,768]{2,1,0:T(8,128)} custom-call(s32[1]{0:T(128)} %bitcast.refs_0_.core_ref, f32[1,512,768]{2,1,0:T(8,128)} %bitcast.109, f32[1,512,768]{2,1,0:T(8,128)} %collective-permute-done.41.arrived_ref), custom_call_target="tpu_custom_call" | custom-call | tf_op jit(solution)/shard_map/hand_back/pallas_call | solution.py:647
  399.9 5.6 %collective-permute-done.39 = bf16[304,384]{1,0:T(8,128)(2,1)} collective-permute-done((bf16[304,384]{1,0:T(8,128)(2,1)S(1)}, bf16[304,384]{1,0:T(8,128)(2,1)}, u32[]{:S(2)}, u32[]{:S(2)}) %collective-permute-start.39) | collective-permute-done | bytes 233504 | tf_op jit(solution)/shard_map/ppermute | solution.py:849
  405.5 1.9 pad_maximum_fusion.2.refs_2_
  411.1 8.2 %weight_outputs.1 = (f32[768,768]{1,0:T(8,128)}, f32[768,768]{1,0:T(8,128)}, f32[768,768]{1,0:T(8,128)}, f32[768,768]{1,0:T(8,128)}, f32[1,768]{1,0:T(1,128)}, /*index=5*/f32[3,128,384]{2,1,0:T(8,128)}) custom-call(s32[2]{0:T(128)} %pad_add_fusion.place_ref, bf16[4,512,384]{2,1,0:T(8,128)(2,1)} %copy-done.42, bf16[4,512,384]{2,1,0:T(8,128)(2,1)} %copy-done.47, ...), custom_call_target="tpu_custom_call" | custom-call | tf_op jit(solution)/shard_map/weight_outputs/pallas_call | solution.py:725
  (253 shorter events, 55.3 us)
Async XLA Ops:
  7.2 338.3 %reduce-scatter.2.cloned.1.call-start = ((), (), s32[]{:S(2)}) async-start(), calls=%async_computation.1 | async-start | bytes 10616832 | tf_op jit(solution)/shard_map/reduce_scatter | solution.py:1002
  9.7 40.5 %copy-start.14 = (bf16[1,512,768]{2,1,0:T(8,128)(2,1)}, bf16[1,512,768]{2,1,0:T(8,128)(2,1)S(1)}, u32[]{:S(2)}) copy-start(bf16[1,512,768]{2,1,0:T(8,128)(2,1)S(1)} %get-tuple-element.243.refs_2_) | copy-start | bytes 2359300
  9.8 3.2 collective-permute-start
  11.3 49.9 %collective-permute-start.2 = (bf16[1,512,768]{2,1,0:T(8,128)(2,1)}, bf16[1,512,768]{2,1,0:T(8,128)(2,1)S(1)}, u32[]{:S(2)}, u32[]{:S(2)}) collective-permute-start(bf16[1,512,768]{2,1,0:T(8,128)(2,1)} %get-tuple-element.519), channel_id=1, source_target_pairs={{0,4},{4,0},{1,5},{5,1},{2,6},{6,2},{3,7},{7,3},{8,12},{12,8},{9,1... | collective-permute-start | bytes 2359304 | tf_op jit(solution)/shard_map/ppermute | solution.py:634
  11.3 72.8 %copy-start.31 = (f32[1,768]{1,0:T(1,128)}, f32[1,768]{1,0:T(1,128)S(1)}, u32[]{:S(2)}) copy-start(f32[1,768]{1,0:T(1,128)S(1)} %broadcast_in_dim.31.refs_4_.refs_9_) | copy-start | bytes 9220
  13.0 42.4 %collective-permute-start.3 = (bf16[256,768]{1,0:T(8,128)(2,1)S(1)}, bf16[256,768]{1,0:T(8,128)(2,1)S(1)}, u32[]{:S(2)}, u32[]{:S(2)}) collective-permute-start(bf16[256,768]{1,0:T(8,128)(2,1)S(1)} %get-tuple-element.256), channel_id=1, source_target_pairs={{0,1},{1,2},{2,3},{3,0},{4,5},{5,6},{6,7},{7,4},{8,9},{9,10},{10,1... | collective-permute-start | bytes 1179656 | tf_op jit(solution)/shard_map/ppermute | solution.py:625
  16.1 39.3 %collective-permute-start.4 = (bf16[256,768]{1,0:T(8,128)(2,1)S(1)}, bf16[256,768]{1,0:T(8,128)(2,1)S(1)}, u32[]{:S(2)}, u32[]{:S(2)}) collective-permute-start(bf16[256,768]{1,0:T(8,128)(2,1)S(1)} %get-tuple-element.257), channel_id=1, source_target_pairs={{0,2},{1,3},{2,0},{3,1},{4,6},{5,7},{6,4},{7,5},{8,10},{9,11},{10,... | collective-permute-start | bytes 1179656 | tf_op jit(solution)/shard_map/ppermute | solution.py:625
  18.7 36.7 %collective-permute-start.5 = (bf16[256,768]{1,0:T(8,128)(2,1)S(1)}, bf16[256,768]{1,0:T(8,128)(2,1)S(1)}, u32[]{:S(2)}, u32[]{:S(2)}) collective-permute-start(bf16[256,768]{1,0:T(8,128)(2,1)S(1)} %get-tuple-element.258), channel_id=1, source_target_pairs={{0,3},{1,0},{2,1},{3,2},{4,7},{5,4},{6,5},{7,6},{8,11},{9,8},{10,9... | collective-permute-start | bytes 1179656 | tf_op jit(solution)/shard_map/ppermute | solution.py:625
  50.2 37.9 %copy-start.5 = (bf16[512,768]{1,0:T(8,128)(2,1)}, bf16[512,768]{1,0:T(8,128)(2,1)S(1)}, u32[]{:S(2)}) copy-start(bf16[512,768]{1,0:T(8,128)(2,1)S(1)} %get-tuple-element.250) | copy-start | bytes 2359300
  55.4 34.0 %collective-permute-start.6 = (bf16[256,768]{1,0:T(8,128)(2,1)}, bf16[256,768]{1,0:T(8,128)(2,1)}, u32[]{:S(2)}, u32[]{:S(2)}) collective-permute-start(bf16[256,768]{1,0:T(8,128)(2,1)} %get-tuple-element.270), channel_id=1, source_target_pairs={{0,1},{1,2},{2,3},{3,0},{4,5},{5,6},{6,7},{7,4},{8,9},{9,10},{10,1... | collective-permute-start | bytes 1179656 | tf_op jit(solution)/shard_map/ppermute | solution.py:625
  56.2 33.3 %collective-permute-start.7 = (bf16[256,768]{1,0:T(8,128)(2,1)}, bf16[256,768]{1,0:T(8,128)(2,1)}, u32[]{:S(2)}, u32[]{:S(2)}) collective-permute-start(bf16[256,768]{1,0:T(8,128)(2,1)} %get-tuple-element.271), channel_id=1, source_target_pairs={{0,2},{1,3},{2,0},{3,1},{4,6},{5,7},{6,4},{7,5},{8,10},{9,11},{10,... | collective-permute-start | bytes 1179656 | tf_op jit(solution)/shard_map/ppermute | solution.py:625
  56.5 33.0 %collective-permute-start.8 = (bf16[256,768]{1,0:T(8,128)(2,1)}, bf16[256,768]{1,0:T(8,128)(2,1)}, u32[]{:S(2)}, u32[]{:S(2)}) collective-permute-start(bf16[256,768]{1,0:T(8,128)(2,1)} %get-tuple-element.272), channel_id=1, source_target_pairs={{0,3},{1,0},{2,1},{3,2},{4,7},{5,4},{6,5},{7,6},{8,11},{9,8},{10,9... | collective-permute-start | bytes 1179656 | tf_op jit(solution)/shard_map/ppermute | solution.py:625
  59.5 1.7 collective-permute-start.1
  89.5 37.2 %collective-permute-start.9 = (bf16[512,768]{1,0:T(8,128)(2,1)}, bf16[512,768]{1,0:T(8,128)(2,1)S(1)}, u32[]{:S(2)}, u32[]{:S(2)}) collective-permute-start(bf16[512,768]{1,0:T(8,128)(2,1)} %get-tuple-element.294), channel_id=1, source_target_pairs={{0,1},{1,2},{2,3},{3,0},{4,5},{5,6},{6,7},{7,4},{8,9},{9,10},{10,1... | collective-permute-start | bytes 2359304 | tf_op jit(solution)/shard_map/ppermute | solution.py:625
  93.2 52.1 %collective-permute-start.10 = (bf16[512,768]{1,0:T(8,128)(2,1)}, bf16[512,768]{1,0:T(8,128)(2,1)S(1)}, u32[]{:S(2)}, u32[]{:S(2)}) collective-permute-start(bf16[512,768]{1,0:T(8,128)(2,1)} %get-tuple-element.295), channel_id=1, source_target_pairs={{0,2},{1,3},{2,0},{3,1},{4,6},{5,7},{6,4},{7,5},{8,10},{9,11},{10,... | collective-permute-start | bytes 2359304 | tf_op jit(solution)/shard_map/ppermute | solution.py:625
  93.2 52.1 %collective-permute-start.11 = (bf16[512,768]{1,0:T(8,128)(2,1)}, bf16[512,768]{1,0:T(8,128)(2,1)S(1)}, u32[]{:S(2)}, u32[]{:S(2)}) collective-permute-start(bf16[512,768]{1,0:T(8,128)(2,1)} %get-tuple-element.296), channel_id=1, source_target_pairs={{0,3},{1,0},{2,1},{3,2},{4,7},{5,4},{6,5},{7,6},{8,11},{9,8},{10,9... | collective-permute-start | bytes 2359304 | tf_op jit(solution)/shard_map/ppermute | solution.py:625
  126.7 37.9 %copy-start.51 = (bf16[512,768]{1,0:T(8,128)(2,1)}, bf16[512,768]{1,0:T(8,128)(2,1)S(1)}, u32[]{:S(2)}) copy-start(bf16[512,768]{1,0:T(8,128)(2,1)S(1)} %collective-permute-done.9.refs_2_.refs_6_.refs_5_) | copy-start | bytes 2359300
  145.3 54.7 %collective-permute-start.12 = (bf16[256,768]{1,0:T(8,128)(2,1)}, bf16[256,768]{1,0:T(8,128)(2,1)S(1)}, u32[]{:S(2)}, u32[]{:S(2)}) collective-permute-start(bf16[256,768]{1,0:T(8,128)(2,1)} %get-tuple-element.334), channel_id=1, source_target_pairs={{0,3},{1,0},{2,1},{3,2},{4,7},{5,4},{6,5},{7,6},{8,11},{9,8},{10,9... | collective-permute-start | bytes 1179656 | tf_op jit(solution)/shard_map/ppermute | solution.py:625
  163.5 36.8 %collective-permute-start.13 = (bf16[256,768]{1,0:T(8,128)(2,1)}, bf16[256,768]{1,0:T(8,128)(2,1)}, u32[]{:S(2)}, u32[]{:S(2)}) collective-permute-start(bf16[256,768]{1,0:T(8,128)(2,1)} %get-tuple-element.335), channel_id=1, source_target_pairs={{0,2},{1,3},{2,0},{3,1},{4,6},{5,7},{6,4},{7,5},{8,10},{9,11},{10,... | collective-permute-start | bytes 1179656 | tf_op jit(solution)/shard_map/ppermute | solution.py:625
  164.1 36.2 %collective-permute-start.14 = (bf16[256,768]{1,0:T(8,128)(2,1)}, bf16[256,768]{1,0:T(8,128)(2,1)}, u32[]{:S(2)}, u32[]{:S(2)}) collective-permute-start(bf16[256,768]{1,0:T(8,128)(2,1)} %get-tuple-element.336), channel_id=1, source_target_pairs={{0,1},{1,2},{2,3},{3,0},{4,5},{5,6},{6,7},{7,4},{8,9},{9,10},{10,1... | collective-permute-start | bytes 1179656 | tf_op jit(solution)/shard_map/ppermute | solution.py:625
  195.7 41.6 %collective-permute-start.15 = (bf16[256,768]{1,0:T(8,128)(2,1)}, bf16[256,768]{1,0:T(8,128)(2,1)S(1)}, u32[]{:S(2)}, u32[]{:S(2)}) collective-permute-start(bf16[256,768]{1,0:T(8,128)(2,1)} %get-tuple-element.326), channel_id=1, source_target_pairs={{0,3},{1,0},{2,1},{3,2},{4,7},{5,4},{6,5},{7,6},{8,11},{9,8},{10,9... | collective-permute-start | bytes 1179656 | tf_op jit(solution)/shard_map/ppermute | solution.py:625
  199.5 37.8 %collective-permute-start.16 = (bf16[256,768]{1,0:T(8,128)(2,1)}, bf16[256,768]{1,0:T(8,128)(2,1)S(1)}, u32[]{:S(2)}, u32[]{:S(2)}) collective-permute-start(bf16[256,768]{1,0:T(8,128)(2,1)} %get-tuple-element.327), channel_id=1, source_target_pairs={{0,2},{1,3},{2,0},{3,1},{4,6},{5,7},{6,4},{7,5},{8,10},{9,11},{10,... | collective-permute-start | bytes 1179656 | tf_op jit(solution)/shard_map/ppermute | solution.py:625
  200.0 37.3 %collective-permute-start.17 = (bf16[256,768]{1,0:T(8,128)(2,1)}, bf16[256,768]{1,0:T(8,128)(2,1)S(1)}, u32[]{:S(2)}, u32[]{:S(2)}) collective-permute-start(bf16[256,768]{1,0:T(8,128)(2,1)} %get-tuple-element.328), channel_id=1, source_target_pairs={{0,1},{1,2},{2,3},{3,0},{4,5},{5,6},{6,7},{7,4},{8,9},{9,10},{10,1... | collective-permute-start | bytes 1179656 | tf_op jit(solution)/shard_map/ppermute | solution.py:625
  238.9 43.7 %collective-permute-start.18 = (bf16[512,768]{1,0:T(8,128)(2,1)S(1)}, bf16[512,768]{1,0:T(8,128)(2,1)S(1)}, u32[]{:S(2)}, u32[]{:S(2)}) collective-permute-start(bf16[512,768]{1,0:T(8,128)(2,1)S(1)} %copy-done.66), channel_id=1, source_target_pairs={{0,3},{1,0},{2,1},{3,2},{4,7},{5,4},{6,5},{7,6},{8,11},{9,8},{10,9... | collective-permute-start | bytes 2359304 | tf_op jit(solution)/shard_map/ppermute | solution.py:1014
  242.1 40.4 %collective-permute-start.19 = (bf16[512,768]{1,0:T(8,128)(2,1)}, bf16[512,768]{1,0:T(8,128)(2,1)S(1)}, u32[]{:S(2)}, u32[]{:S(2)}) collective-permute-start(bf16[512,768]{1,0:T(8,128)(2,1)} %get-tuple-element.374), channel_id=1, source_target_pairs={{0,1},{1,2},{2,3},{3,0},{4,5},{5,6},{6,7},{7,4},{8,9},{9,10},{10,1... | collective-permute-start | bytes 2359304 | tf_op jit(solution)/shard_map/ppermute | solution.py:1014
  285.6 11.7 %collective-permute-start.20 = (bf16[4,512,384]{2,1,0:T(8,128)(2,1)}, bf16[4,512,384]{2,1,0:T(8,128)(2,1)}, u32[]{:S(2)}, u32[]{:S(2)}) collective-permute-start(bf16[4,512,384]{2,1,0:T(8,128)(2,1)} %dynamic-slice_bitcast_fusion), channel_id=1, source_target_pairs={{0,4},{4,0},{1,5},{5,1},{2,6},{6,2},{3,7},{7,3},{8,12},{12,8},{9,1... | collective-permute-start | bytes 4718600 | tf_op jit(solution)/shard_map/ppermute | solution.py:849
  285.6 37.9 %collective-permute-start.24 = (bf16[512,768]{1,0:T(8,128)(2,1)}, bf16[512,768]{1,0:T(8,128)(2,1)S(1)}, u32[]{:S(2)}, u32[]{:S(2)}) collective-permute-start(bf16[512,768]{1,0:T(8,128)(2,1)} %get-tuple-element.395), channel_id=1, source_target_pairs={{0,2},{1,3},{2,0},{3,1},{4,6},{5,7},{6,4},{7,5},{8,10},{9,11},{10,... | collective-permute-start | bytes 2359304 | tf_op jit(solution)/shard_map/ppermute | solution.py:1014
  301.4 22.1 %collective-permute-start.21 = (bf16[512,384]{1,0:T(8,128)(2,1)S(1)}, bf16[512,384]{1,0:T(8,128)(2,1)S(1)}, u32[]{:S(2)}, u32[]{:S(2)}) collective-permute-start(bf16[512,384]{1,0:T(8,128)(2,1)S(1)} %get-tuple-element.390), channel_id=1, source_target_pairs={{0,8},{8,0},{16,24},{24,16},{1,9},{9,1},{17,25},{25,17},{2,10},{10... | collective-permute-start | bytes 1179656 | tf_op jit(solution)/shard_map/ppermute | solution.py:849
  302.9 20.6 %collective-permute-start.22 = (bf16[512,384]{1,0:T(8,128)(2,1)S(1)}, bf16[512,384]{1,0:T(8,128)(2,1)}, u32[]{:S(2)}, u32[]{:S(2)}) collective-permute-start(bf16[512,384]{1,0:T(8,128)(2,1)S(1)} %get-tuple-element.391), channel_id=1, source_target_pairs={{0,16},{8,24},{16,0},{24,8},{1,17},{9,25},{17,1},{25,9},{2,18},{10... | collective-permute-start | bytes 1179656 | tf_op jit(solution)/shard_map/ppermute | solution.py:849
  304.6 26.6 %collective-permute-start.23 = (bf16[512,384]{1,0:T(8,128)(2,1)S(1)}, bf16[512,384]{1,0:T(8,128)(2,1)}, u32[]{:S(2)}, u32[]{:S(2)}) collective-permute-start(bf16[512,384]{1,0:T(8,128)(2,1)S(1)} %get-tuple-element.392), channel_id=1, source_target_pairs={{0,24},{8,16},{16,8},{24,0},{1,25},{9,17},{17,9},{25,1},{2,26},{10... | collective-permute-start | bytes 1179656 | tf_op jit(solution)/shard_map/ppermute | solution.py:849
  332.7 12.5 %collective-permute-start.25 = (bf16[512,384]{1,0:T(8,128)(2,1)S(1)}, bf16[512,384]{1,0:T(8,128)(2,1)S(1)}, u32[]{:S(2)}, u32[]{:S(2)}) collective-permute-start(bf16[512,384]{1,0:T(8,128)(2,1)S(1)} %fusion.4), channel_id=1, source_target_pairs={{0,1},{1,0},{2,3},{3,2},{4,5},{5,4},{6,7},{7,6},{8,9},{9,8},{10,11... | collective-permute-start | bytes 1179656 | tf_op jit(solution)/shard_map/ppermute | solution.py:849
  346.9 8.4 %collective-permute-start.27 = (bf16[4,304,384]{2,1,0:T(8,128)(2,1)S(1)}, bf16[4,304,384]{2,1,0:T(8,128)(2,1)S(1)}, u32[]{:S(2)}, u32[]{:S(2)}) collective-permute-start(bf16[4,304,384]{2,1,0:T(8,128)(2,1)S(1)} %dynamic-slice_bitcast_fusion.1), channel_id=1, source_target_pairs={{0,4},{4,0},{1,5},{5,1},{2,6},{6,2},{3,7},{7,3},{8,12},{12,8},{9,1... | collective-permute-start | bytes 2801672 | tf_op jit(solution)/shard_map/ppermute | solution.py:849
  347.0 21.2 %collective-permute-start.26 = (bf16[512,384]{1,0:T(8,128)(2,1)S(1)}, bf16[512,384]{1,0:T(8,128)(2,1)S(1)}, u32[]{:S(2)}, u32[]{:S(2)}) collective-permute-start(bf16[512,384]{1,0:T(8,128)(2,1)S(1)} %add_convert_fusion.1), channel_id=1, source_target_pairs={{0,2},{1,3},{2,0},{3,1},{4,6},{5,7},{6,4},{7,5},{8,10},{9,11},{10,... | collective-permute-start | bytes 1179656 | tf_op jit(solution)/shard_map/ppermute | solution.py:849
  355.8 12.4 %collective-permute-start.28 = (bf16[304,384]{1,0:T(8,128)(2,1)S(1)}, bf16[304,384]{1,0:T(8,128)(2,1)S(1)}, u32[]{:S(2)}, u32[]{:S(2)}) collective-permute-start(bf16[304,384]{1,0:T(8,128)(2,1)S(1)} %get-tuple-element.425), channel_id=1, source_target_pairs={{0,8},{8,0},{16,24},{24,16},{1,9},{9,1},{17,25},{25,17},{2,10},{10... | collective-permute-start | bytes 700424 | tf_op jit(solution)/shard_map/ppermute | solution.py:849
  356.4 12.5 %collective-permute-start.29 = (bf16[304,384]{1,0:T(8,128)(2,1)S(1)}, bf16[304,384]{1,0:T(8,128)(2,1)S(1)}, u32[]{:S(2)}, u32[]{:S(2)}) collective-permute-start(bf16[304,384]{1,0:T(8,128)(2,1)S(1)} %get-tuple-element.426), channel_id=1, source_target_pairs={{0,16},{8,24},{16,0},{24,8},{1,17},{9,25},{17,1},{25,9},{2,18},{10... | collective-permute-start | bytes 700424 | tf_op jit(solution)/shard_map/ppermute | solution.py:849
  357.0 11.9 %collective-permute-start.30 = (bf16[304,384]{1,0:T(8,128)(2,1)S(1)}, bf16[304,384]{1,0:T(8,128)(2,1)S(1)}, u32[]{:S(2)}, u32[]{:S(2)}) collective-permute-start(bf16[304,384]{1,0:T(8,128)(2,1)S(1)} %get-tuple-element.427), channel_id=1, source_target_pairs={{0,24},{8,16},{16,8},{24,0},{1,25},{9,17},{17,9},{25,1},{2,26},{10... | collective-permute-start | bytes 700424 | tf_op jit(solution)/shard_map/ppermute | solution.py:849
  359.3 17.9 %collective-permute-start.36 = (bf16[1,512,768]{2,1,0:T(8,128)(2,1)S(1)}, bf16[1,512,768]{2,1,0:T(8,128)(2,1)S(1)}, u32[]{:S(2)}, u32[]{:S(2)}) collective-permute-start(bf16[1,512,768]{2,1,0:T(8,128)(2,1)S(1)} %get-tuple-element.442), channel_id=1, source_target_pairs={{0,4},{4,0},{1,5},{5,1},{2,6},{6,2},{3,7},{7,3},{8,12},{12,8},{9,1... | collective-permute-start | bytes 2359304 | tf_op jit(solution)/shard_map/ppermute | solution.py:642
  369.2 7.5 %collective-permute-start.34 = (bf16[304,384]{1,0:T(8,128)(2,1)S(1)}, bf16[304,384]{1,0:T(8,128)(2,1)S(1)}, u32[]{:S(2)}, u32[]{:S(2)}) collective-permute-start(bf16[304,384]{1,0:T(8,128)(2,1)S(1)} %fusion.7), channel_id=1, source_target_pairs={{0,1},{1,0},{2,3},{3,2},{4,5},{5,4},{6,7},{7,6},{8,9},{9,8},{10,11... | collective-permute-start | bytes 700424 | tf_op jit(solution)/shard_map/ppermute | solution.py:849
  369.8 12.2 %collective-permute-start.31 = (bf16[512,384]{1,0:T(8,128)(2,1)S(1)}, bf16[512,384]{1,0:T(8,128)(2,1)S(1)}, u32[]{:S(2)}, u32[]{:S(2)}) collective-permute-start(bf16[512,384]{1,0:T(8,128)(2,1)S(1)} %add_convert_fusion), channel_id=1, source_target_pairs={{0,8},{8,0},{16,24},{24,16},{1,9},{9,1},{17,25},{25,17},{2,10},{10... | collective-permute-start | bytes 1179656 | tf_op jit(solution)/shard_map/ppermute | solution.py:849
  371.2 17.9 %collective-permute-start.32 = (bf16[512,384]{1,0:T(8,128)(2,1)S(1)}, bf16[512,384]{1,0:T(8,128)(2,1)S(1)}, u32[]{:S(2)}, u32[]{:S(2)}) collective-permute-start(bf16[512,384]{1,0:T(8,128)(2,1)S(1)} %add_convert_fusion), channel_id=1, source_target_pairs={{0,16},{8,24},{16,0},{24,8},{1,17},{9,25},{17,1},{25,9},{2,18},{10... | collective-permute-start | bytes 1179656 | tf_op jit(solution)/shard_map/ppermute | solution.py:849
  371.8 17.4 %collective-permute-start.33 = (bf16[512,384]{1,0:T(8,128)(2,1)S(1)}, bf16[512,384]{1,0:T(8,128)(2,1)S(1)}, u32[]{:S(2)}, u32[]{:S(2)}) collective-permute-start(bf16[512,384]{1,0:T(8,128)(2,1)S(1)} %add_convert_fusion), channel_id=1, source_target_pairs={{0,24},{8,16},{16,8},{24,0},{1,25},{9,17},{17,9},{25,1},{2,26},{10... | collective-permute-start | bytes 1179656 | tf_op jit(solution)/shard_map/ppermute | solution.py:849
  376.7 12.5 %collective-permute-start.35 = (bf16[304,384]{1,0:T(8,128)(2,1)S(1)}, bf16[304,384]{1,0:T(8,128)(2,1)S(1)}, u32[]{:S(2)}, u32[]{:S(2)}) collective-permute-start(bf16[304,384]{1,0:T(8,128)(2,1)S(1)} %add_convert_fusion.3), channel_id=1, source_target_pairs={{0,2},{1,3},{2,0},{3,1},{4,6},{5,7},{6,4},{7,5},{8,10},{9,11},{10,... | collective-permute-start | bytes 700424 | tf_op jit(solution)/shard_map/ppermute | solution.py:849
  377.3 17.5 %collective-permute-start.41 = (f32[1,512,768]{2,1,0:T(8,128)}, f32[1,512,768]{2,1,0:T(8,128)}, u32[]{:S(2)}, u32[]{:S(2)}) collective-permute-start(f32[1,512,768]{2,1,0:T(8,128)} %bitcast.35), channel_id=1, source_target_pairs={{0,4},{4,0},{1,5},{5,1},{2,6},{6,2},{3,7},{7,3},{8,12},{12,8},{9,1... | collective-permute-start | bytes 4718600 | tf_op jit(solution)/shard_map/ppermute | solution.py:642
  391.1 14.4 %collective-permute-start.37 = (bf16[4,512,384]{2,1,0:T(8,128)(2,1)S(1)}, bf16[4,512,384]{2,1,0:T(8,128)(2,1)S(1)}, u32[]{:S(2)}, u32[]{:S(2)}) collective-permute-start(bf16[4,512,384]{2,1,0:T(8,128)(2,1)S(1)} %pad_maximum_fusion.1.refs_0_), channel_id=1, source_target_pairs={{0,4},{4,0},{1,5},{5,1},{2,6},{6,2},{3,7},{7,3},{8,12},{12,8},{9,1... | collective-permute-start | bytes 4718600 | tf_op jit(solution)/shard_map/ppermute | solution.py:849
  391.2 8.7 %collective-permute-start.38 = (bf16[304,384]{1,0:T(8,128)(2,1)S(1)}, bf16[304,384]{1,0:T(8,128)(2,1)}, u32[]{:S(2)}, u32[]{:S(2)}) collective-permute-start(bf16[304,384]{1,0:T(8,128)(2,1)S(1)} %add_convert_fusion.2), channel_id=1, source_target_pairs={{0,8},{8,0},{16,24},{24,16},{1,9},{9,1},{17,25},{25,17},{2,10},{10... | collective-permute-start | bytes 700424 | tf_op jit(solution)/shard_map/ppermute | solution.py:849
  392.6 12.9 %collective-permute-start.39 = (bf16[304,384]{1,0:T(8,128)(2,1)S(1)}, bf16[304,384]{1,0:T(8,128)(2,1)}, u32[]{:S(2)}, u32[]{:S(2)}) collective-permute-start(bf16[304,384]{1,0:T(8,128)(2,1)S(1)} %add_convert_fusion.2), channel_id=1, source_target_pairs={{0,16},{8,24},{16,0},{24,8},{1,17},{9,25},{17,1},{25,9},{2,18},{10... | collective-permute-start | bytes 700424 | tf_op jit(solution)/shard_map/ppermute | solution.py:849
  393.3 12.2 %collective-permute-start.40 = (bf16[304,384]{1,0:T(8,128)(2,1)S(1)}, bf16[304,384]{1,0:T(8,128)(2,1)}, u32[]{:S(2)}, u32[]{:S(2)}) collective-permute-start(bf16[304,384]{1,0:T(8,128)(2,1)S(1)} %add_convert_fusion.2), channel_id=1, source_target_pairs={{0,24},{8,16},{16,8},{24,0},{1,25},{9,17},{17,9},{25,1},{2,26},{10... | collective-permute-start | bytes 700424 | tf_op jit(solution)/shard_map/ppermute | solution.py:849
  407.4 3.7 collective-permute-start.42
  (66 other events, 466.2 us)
Sparse Core Ops, SparseCore 0:
  237.5 86.4 reduce-scatter.1
